TPU v7x, 32 devices: a whole 2x2x4 slice. The times are simulated.
32 devices in a mesh: sec: 16 (over z, y, core), scan: 2 (over x).
Axes of the slice: x: 2, y: 2, z: 4, core: 2. Of those that a mesh axis runs over, the one named last changes fastest.
Arguments:
- obj_amp: float32 [16, 512, 512], P('sec', 'scan'), may hold values from 0.97 to 1
- obj_phase: float32 [16, 512, 512], P('sec', 'scan'), may hold values from -3.140625 to 3.140625
- forward_waves: bfloat16 [16, 16, 2, 256, 256], P('sec', 'scan'), may hold values from -6 to 6
- exit_adjoint: bfloat16 [16, 2, 256, 256], P('scan'), may hold values from -6 to 6
- offsets: int32 [16, 2], P('scan'), may hold values from 0 to 256
Outputs:
- object_grad: float32 [16, 2, 512, 512], P('sec', None, 'scan')
All inputs are finite; a program needn't handle non-finite values.
Results may differ from a plain program's by a relative error of at most 0.012.
The roundings to bfloat16 on the way count: a program that leaves them out, or rounds other values in their place, can miss the bound.
Values may be sent and summed in bfloat16 or wider, within the bound.
No kernel may reach another device: no remote copies, remote signals or barrier semaphores. Data moves between devices by JAX's collectives and lax.ppermute only.
A program may use at most 64 MiB of HBM per device.

v0:
```python
import jax
import jax.numpy as jnp
from jax import lax
from jax.sharding import PartitionSpec as P

SUBSTEPS = 2


damping = 0.0005
turning = 0.011


def shifted(value, axis, steps):
    count = lax.axis_size(axis)
    first, last = (max(0, -steps), min(count, count - steps))
    return lax.ppermute(value, axis, [(source, source + steps) for source in range(first, last)])


def laplacian(field):
    widths = [(0, 0)] * (field.ndim - 2) + [(1, 1), (1, 1)]
    padded = jnp.pad(field, widths)
    beside = (
        padded[..., 2:, 1:-1]
        + padded[..., :-2, 1:-1]
        + padded[..., 1:-1, 2:]
        + padded[..., 1:-1, :-2]
    )
    return beside - 4.0 * field


def back_step(field):
    for substep in range(SUBSTEPS):
        lap_re = laplacian(field[..., 0, :, :])
        lap_im = laplacian(field[..., 1, :, :])
        new_re = field[..., 0, :, :] + damping * lap_re + turning * lap_im
        new_im = field[..., 1, :, :] + damping * lap_im - turning * lap_re
        field = jnp.stack([new_re, new_im], axis=-3)
    return field


def on_device(obj_amp, obj_phase, forward_waves, exit_adjoint, offsets):
    amp_all, phase_all = (
        lax.all_gather(obj_amp, "scan", axis=1, tiled=True),
        lax.all_gather(obj_phase, "scan", axis=1, tiled=True),
    )
    trans_re = (amp_all * jnp.cos(phase_all))[0]
    trans_im = (amp_all * jnp.sin(phase_all))[0]
    per_tick = 1
    sections = lax.axis_size("sec")
    segment_no = lax.axis_index("sec")
    window = exit_adjoint.shape[-1]
    position_count = exit_adjoint.shape[0]
    batch_total = position_count // per_tick
    tick_count = batch_total + sections - 1
    side = trans_re.shape[-1]
    waves = forward_waves[0]
    zero_index = jnp.zeros((), jnp.int32)

    def one_tick(tick, carry):
        arriving, stored = carry
        batch_no = tick - (sections - 1 - segment_no)
        active = jnp.logical_and(batch_no >= 0, batch_no < batch_total)
        slot = jnp.clip(batch_no, 0, batch_total - 1)
        first_row = slot * per_tick
        own_exit = lax.dynamic_slice_in_dim(exit_adjoint, first_row, per_tick, 0)
        adjoint = jnp.where(segment_no == sections - 1, own_exit, arriving).astype(jnp.float32)
        spread = back_step(adjoint)
        previous = lax.dynamic_index_in_dim(stored, slot, 0, keepdims=False)
        kept = jnp.where(active, spread, previous)
        stored = lax.dynamic_update_index_in_dim(stored, kept, slot, 0)
        corners = lax.dynamic_slice_in_dim(offsets, first_row, per_tick, 0)
        row_at = corners[0, 0]
        col_at = corners[0, 1]
        spread_re = spread[0, 0]
        spread_im = spread[0, 1]
        win_re = lax.dynamic_slice(trans_re, (row_at, col_at), (window, window))
        win_im = lax.dynamic_slice(trans_im, (row_at, col_at), (window, window))
        out_re = win_re * spread_re + win_im * spread_im
        out_im = win_re * spread_im - win_im * spread_re
        outgoing = [jnp.stack([out_re, out_im])]
        leaving = jnp.stack(outgoing).astype(jnp.bfloat16)
        arriving = shifted(leaving, "sec", -1)
        return (arriving, stored)

    start_wave = jnp.zeros((per_tick, 2, window, window), jnp.bfloat16)
    start_store = jnp.zeros((batch_total, per_tick, 2, window, window), jnp.float32)
    arriving, stored = lax.fori_loop(0, tick_count, one_tick, (start_wave, start_store))
    spreads = stored.reshape(position_count, 2, window, window)

    def add_position(position, gradient):
        spread = lax.dynamic_index_in_dim(spreads, position, 0, keepdims=False)
        incoming = lax.dynamic_index_in_dim(waves, position, 0, keepdims=False).astype(jnp.float32)
        part_re = incoming[0] * spread[0] + incoming[1] * spread[1]
        part_im = incoming[0] * spread[1] - incoming[1] * spread[0]
        row_at = offsets[position, 0]
        col_at = offsets[position, 1]
        current = lax.dynamic_slice(gradient, (zero_index, row_at, col_at), (2, window, window))
        added = current + jnp.stack([part_re, part_im])
        return lax.dynamic_update_slice(gradient, added, (zero_index, row_at, col_at))

    start_grad = jnp.zeros((2, side, side), jnp.float32)
    gradient = lax.fori_loop(0, position_count, add_position, start_grad)
    reduced = lax.psum_scatter(gradient, "scan", scatter_dimension=1, tiled=True)
    return reduced[None]


def solution(mesh):
    in_specs = (
        P("sec", "scan", None),
        P("sec", "scan", None),
        P("sec", "scan", None, None, None),
        P("scan", None, None, None),
        P("scan", None),
    )
    out_specs = P("sec", None, "scan", None)
    return jax.shard_map(
        on_device, mesh=mesh, in_specs=in_specs, out_specs=out_specs, check_vma=False
    )
```

profile of v0, /device:TPU:0, one launch (start us, length us, event | category | flops | bytes accessed | tf_op | source)
XLA Modules:
  0.0 578.2 jit_solution(8051424245867390238)
XLA Ops:
  8.1 24.9 %all-gather.3.cloned.1.call-done = f32[1,512,512]{2,1,0:T(8,128)} async-done(((f32[1,256,512]{2,1,0:T(8,128)}), f32[1,512,512]{2,1,0:T(8,128)}) %all-gather.3.cloned.1.call-update) | async-done | bytes 1048592 | tf_op jit(solution)/shard_map/all_gather | solution.py:43
  32.9 22.9 %all-gather.5.cloned.1.call-done = f32[1,512,512]{2,1,0:T(8,128)} async-done(((f32[1,256,512]{2,1,0:T(8,128)}), f32[1,512,512]{2,1,0:T(8,128)}) %all-gather.5.cloned.1.call-update) | async-done | bytes 1048592 | tf_op jit(solution)/shard_map/all_gather | solution.py:44
  55.8 4.9 multiply_bitcast_fusion
  63.2 339.4 %while.30 = (s32[]{:T(128)}, bf16[1,2,256,256]{3,2,1,0:T(8,128)(2,1)S(1)}, f32[8,1,2,256,256]{4,3,2,1,0:T(8,128)}, s32[]{:T(128)}, s32[8,2]{0,1:T(2,128)S(1)}, /...) while((s32[]{:T(128)}, ...), condition=%wide.region_1.2_spmd, body=%wide.region_0.1_spmd.sunk | while | flops 3538958 | bytes 11534696 | solution.py:87
  97.0 4.5 collective-permute-done
  111.4 4.5 collective-permute-done
  125.8 4.5 collective-permute-done
  183.4 4.9 collective-permute-done
  198.3 5.4 collective-permute-done
  213.6 5.4 collective-permute-done
  228.9 5.4 collective-permute-done
  244.2 5.4 collective-permute-done
  259.5 5.4 collective-permute-done
  274.8 5.4 collective-permute-done
  290.1 5.4 collective-permute-done
  305.4 5.4 collective-permute-done
  320.7 5.4 collective-permute-done
  336.0 5.4 collective-permute-done
  351.3 5.4 collective-permute-done
  366.5 5.4 collective-permute-done
  381.8 5.4 collective-permute-done
  397.1 5.4 collective-permute-done
  402.8 117.7 %while.31 = (s32[]{:T(128)}, f32[2,512,512]{2,1,0:T(8,128)S(1)}, s32[8,2]{0,1:T(2,128)S(1)}, bf16[8,2,256,256]{3,2,1,0:T(8,128)(2,1)}, f32[8,2,256,256]{3,2,1,0:...) while((s32[]{:T(128)}, f32[2,512,512]{2,1,0:T(8,128)S(1)}, s32[8,2]{0,1:T(2,128)S(1)}, ...), condition=%wide.region_3.4_spmd, body=%wide.region_2.3_spmd.sunk | while | flops 786441 | bytes 4980953 | solution.py:102
  409.6 8.3 %dynamic_update_slice.22 = f32[2,512,512]{2,1,0:T(8,128)S(1)} dynamic-update-slice(f32[2,512,512]{2,1,0:T(8,128)S(1)} %get-tuple-element.522, f32[2,256,256]{2,1,0:T(8,128)S(1)} %maximum_add_fusion.2, s32[]{:T(128)} %constant.142.clone.1..sunk.1, s32[]{:T(128)S(6)} %select_n.118, s32[]{:T(128)S(6)} %select_n.119) | dynamic-update-slice | bytes 1048580 | tf_op jit(solution)/shard_map/while/body/eval_jaxpr/dynamic_update_slice | solution.py:99
  424.7 7.3 %dynamic_update_slice.22 = f32[2,512,512]{2,1,0:T(8,128)S(1)} dynamic-update-slice(f32[2,512,512]{2,1,0:T(8,128)S(1)} %get-tuple-element.522, f32[2,256,256]{2,1,0:T(8,128)S(1)} %maximum_add_fusion.2, s32[]{:T(128)} %constant.142.clone.1..sunk.1, s32[]{:T(128)S(6)} %select_n.118, s32[]{:T(128)S(6)} %select_n.119) | dynamic-update-slice | bytes 1048580 | tf_op jit(solution)/shard_map/while/body/eval_jaxpr/dynamic_update_slice | solution.py:99
  438.8 5.1 dynamic_update_slice.22
  450.7 8.4 %dynamic_update_slice.22 = f32[2,512,512]{2,1,0:T(8,128)S(1)} dynamic-update-slice(f32[2,512,512]{2,1,0:T(8,128)S(1)} %get-tuple-element.522, f32[2,256,256]{2,1,0:T(8,128)S(1)} %maximum_add_fusion.2, s32[]{:T(128)} %constant.142.clone.1..sunk.1, s32[]{:T(128)S(6)} %select_n.118, s32[]{:T(128)S(6)} %select_n.119) | dynamic-update-slice | bytes 1048580 | tf_op jit(solution)/shard_map/while/body/eval_jaxpr/dynamic_update_slice | solution.py:99
  465.9 7.5 %dynamic_update_slice.22 = f32[2,512,512]{2,1,0:T(8,128)S(1)} dynamic-update-slice(f32[2,512,512]{2,1,0:T(8,128)S(1)} %get-tuple-element.522, f32[2,256,256]{2,1,0:T(8,128)S(1)} %maximum_add_fusion.2, s32[]{:T(128)} %constant.142.clone.1..sunk.1, s32[]{:T(128)S(6)} %select_n.118, s32[]{:T(128)S(6)} %select_n.119) | dynamic-update-slice | bytes 1048580 | tf_op jit(solution)/shard_map/while/body/eval_jaxpr/dynamic_update_slice | solution.py:99
  480.3 9.8 %dynamic_update_slice.22 = f32[2,512,512]{2,1,0:T(8,128)S(1)} dynamic-update-slice(f32[2,512,512]{2,1,0:T(8,128)S(1)} %get-tuple-element.522, f32[2,256,256]{2,1,0:T(8,128)S(1)} %maximum_add_fusion.2, s32[]{:T(128)} %constant.142.clone.1..sunk.1, s32[]{:T(128)S(6)} %select_n.118, s32[]{:T(128)S(6)} %select_n.119) | dynamic-update-slice | bytes 1048580 | tf_op jit(solution)/shard_map/while/body/eval_jaxpr/dynamic_update_slice | solution.py:99
  496.9 8.9 %dynamic_update_slice.22 = f32[2,512,512]{2,1,0:T(8,128)S(1)} dynamic-update-slice(f32[2,512,512]{2,1,0:T(8,128)S(1)} %get-tuple-element.522, f32[2,256,256]{2,1,0:T(8,128)S(1)} %maximum_add_fusion.2, s32[]{:T(128)} %constant.142.clone.1..sunk.1, s32[]{:T(128)S(6)} %select_n.118, s32[]{:T(128)S(6)} %select_n.119) | dynamic-update-slice | bytes 1048580 | tf_op jit(solution)/shard_map/while/body/eval_jaxpr/dynamic_update_slice | solution.py:99
  512.6 7.9 %dynamic_update_slice.22 = f32[2,512,512]{2,1,0:T(8,128)S(1)} dynamic-update-slice(f32[2,512,512]{2,1,0:T(8,128)S(1)} %get-tuple-element.522, f32[2,256,256]{2,1,0:T(8,128)S(1)} %maximum_add_fusion.2, s32[]{:T(128)} %constant.142.clone.1..sunk.1, s32[]{:T(128)S(6)} %select_n.118, s32[]{:T(128)S(6)} %select_n.119) | dynamic-update-slice | bytes 1048580 | tf_op jit(solution)/shard_map/while/body/eval_jaxpr/dynamic_update_slice | solution.py:99
  521.9 49.8 %reduce-scatter.2.cloned.1.call-done = f32[2,256,512]{2,1,0:T(8,128)} async-done(((f32[2,512,512]{2,1,0:T(8,128)}), f32[2,256,512]{2,1,0:T(8,128)}) %reduce-scatter.2.cloned.1.call-update) | async-done | bytes 1048592 | tf_op jit(solution)/shard_map/reduce_scatter | solution.py:103
  (303 shorter events, 187.1 us)
Async XLA Ops:
  6.5 26.4 %all-gather.3.cloned.1.call-start = ((), (), s32[]{:S(2)}) async-start(), calls=%async_computation.1 | async-start | bytes 1572864 | tf_op jit(solution)/shard_map/all_gather | solution.py:43
  7.3 48.6 %all-gather.5.cloned.1.call-start = ((), (), s32[]{:S(2)}) async-start(), calls=%async_computation.2 | async-start | bytes 1572864 | tf_op jit(solution)/shard_map/all_gather | solution.py:44
  8.0 563.7 %reduce-scatter.2.cloned.1.call-start = ((), (), s32[]{:S(2)}) async-start(), calls=%async_computation.3 | async-start | bytes 3145728 | tf_op jit(solution)/shard_map/reduce_scatter | solution.py:103
  60.7 2.4 copy-start.1
  69.9 3.4 collective-permute-start
  80.0 7.0 %collective-permute-start = (bf16[1,2,256,256]{3,2,1,0:T(8,128)(2,1)S(1)}, bf16[1,2,256,256]{3,2,1,0:T(8,128)(2,1)S(1)}, u32[]{:S(2)}, u32[]{:S(2)}) collective-permute-start(bf16[1,2,256,256]{3,2,1,0:T(8,128)(2,1)S(1)} %pad_maximum_fusion.2), channel_id=1, source_target_pairs={{2,0},{4,2},{6,4},{8,6},{10,8},{12,10},{14,12},{16,14},{18,16},{20... | collective-permute-start | bytes 786440 | tf_op jit(solution)/shard_map/while/body/eval_jaxpr/ppermute | solution.py:16
  93.8 7.7 %collective-permute-start = (bf16[1,2,256,256]{3,2,1,0:T(8,128)(2,1)S(1)}, bf16[1,2,256,256]{3,2,1,0:T(8,128)(2,1)S(1)}, u32[]{:S(2)}, u32[]{:S(2)}) collective-permute-start(bf16[1,2,256,256]{3,2,1,0:T(8,128)(2,1)S(1)} %pad_maximum_fusion.2), channel_id=1, source_target_pairs={{2,0},{4,2},{6,4},{8,6},{10,8},{12,10},{14,12},{16,14},{18,16},{20... | collective-permute-start | bytes 786440 | tf_op jit(solution)/shard_map/while/body/eval_jaxpr/ppermute | solution.py:16
  108.2 7.7 %collective-permute-start = (bf16[1,2,256,256]{3,2,1,0:T(8,128)(2,1)S(1)}, bf16[1,2,256,256]{3,2,1,0:T(8,128)(2,1)S(1)}, u32[]{:S(2)}, u32[]{:S(2)}) collective-permute-start(bf16[1,2,256,256]{3,2,1,0:T(8,128)(2,1)S(1)} %pad_maximum_fusion.2), channel_id=1, source_target_pairs={{2,0},{4,2},{6,4},{8,6},{10,8},{12,10},{14,12},{16,14},{18,16},{20... | collective-permute-start | bytes 786440 | tf_op jit(solution)/shard_map/while/body/eval_jaxpr/ppermute | solution.py:16
  122.6 7.7 %collective-permute-start = (bf16[1,2,256,256]{3,2,1,0:T(8,128)(2,1)S(1)}, bf16[1,2,256,256]{3,2,1,0:T(8,128)(2,1)S(1)}, u32[]{:S(2)}, u32[]{:S(2)}) collective-permute-start(bf16[1,2,256,256]{3,2,1,0:T(8,128)(2,1)S(1)} %pad_maximum_fusion.2), channel_id=1, source_target_pairs={{2,0},{4,2},{6,4},{8,6},{10,8},{12,10},{14,12},{16,14},{18,16},{20... | collective-permute-start | bytes 786440 | tf_op jit(solution)/shard_map/while/body/eval_jaxpr/ppermute | solution.py:16
  137.0 7.7 %collective-permute-start = (bf16[1,2,256,256]{3,2,1,0:T(8,128)(2,1)S(1)}, bf16[1,2,256,256]{3,2,1,0:T(8,128)(2,1)S(1)}, u32[]{:S(2)}, u32[]{:S(2)}) collective-permute-start(bf16[1,2,256,256]{3,2,1,0:T(8,128)(2,1)S(1)} %pad_maximum_fusion.2), channel_id=1, source_target_pairs={{2,0},{4,2},{6,4},{8,6},{10,8},{12,10},{14,12},{16,14},{18,16},{20... | collective-permute-start | bytes 786440 | tf_op jit(solution)/shard_map/while/body/eval_jaxpr/ppermute | solution.py:16
  151.4 7.7 %collective-permute-start = (bf16[1,2,256,256]{3,2,1,0:T(8,128)(2,1)S(1)}, bf16[1,2,256,256]{3,2,1,0:T(8,128)(2,1)S(1)}, u32[]{:S(2)}, u32[]{:S(2)}) collective-permute-start(bf16[1,2,256,256]{3,2,1,0:T(8,128)(2,1)S(1)} %pad_maximum_fusion.2), channel_id=1, source_target_pairs={{2,0},{4,2},{6,4},{8,6},{10,8},{12,10},{14,12},{16,14},{18,16},{20... | collective-permute-start | bytes 786440 | tf_op jit(solution)/shard_map/while/body/eval_jaxpr/ppermute | solution.py:16
  165.8 7.7 %collective-permute-start = (bf16[1,2,256,256]{3,2,1,0:T(8,128)(2,1)S(1)}, bf16[1,2,256,256]{3,2,1,0:T(8,128)(2,1)S(1)}, u32[]{:S(2)}, u32[]{:S(2)}) collective-permute-start(bf16[1,2,256,256]{3,2,1,0:T(8,128)(2,1)S(1)} %pad_maximum_fusion.2), channel_id=1, source_target_pairs={{2,0},{4,2},{6,4},{8,6},{10,8},{12,10},{14,12},{16,14},{18,16},{20... | collective-permute-start | bytes 786440 | tf_op jit(solution)/shard_map/while/body/eval_jaxpr/ppermute | solution.py:16
  180.2 8.2 %collective-permute-start = (bf16[1,2,256,256]{3,2,1,0:T(8,128)(2,1)S(1)}, bf16[1,2,256,256]{3,2,1,0:T(8,128)(2,1)S(1)}, u32[]{:S(2)}, u32[]{:S(2)}) collective-permute-start(bf16[1,2,256,256]{3,2,1,0:T(8,128)(2,1)S(1)} %pad_maximum_fusion.2), channel_id=1, source_target_pairs={{2,0},{4,2},{6,4},{8,6},{10,8},{12,10},{14,12},{16,14},{18,16},{20... | collective-permute-start | bytes 786440 | tf_op jit(solution)/shard_map/while/body/eval_jaxpr/ppermute | solution.py:16
  195.1 8.6 %collective-permute-start = (bf16[1,2,256,256]{3,2,1,0:T(8,128)(2,1)S(1)}, bf16[1,2,256,256]{3,2,1,0:T(8,128)(2,1)S(1)}, u32[]{:S(2)}, u32[]{:S(2)}) collective-permute-start(bf16[1,2,256,256]{3,2,1,0:T(8,128)(2,1)S(1)} %pad_maximum_fusion.2), channel_id=1, source_target_pairs={{2,0},{4,2},{6,4},{8,6},{10,8},{12,10},{14,12},{16,14},{18,16},{20... | collective-permute-start | bytes 786440 | tf_op jit(solution)/shard_map/while/body/eval_jaxpr/ppermute | solution.py:16
  210.4 8.6 %collective-permute-start = (bf16[1,2,256,256]{3,2,1,0:T(8,128)(2,1)S(1)}, bf16[1,2,256,256]{3,2,1,0:T(8,128)(2,1)S(1)}, u32[]{:S(2)}, u32[]{:S(2)}) collective-permute-start(bf16[1,2,256,256]{3,2,1,0:T(8,128)(2,1)S(1)} %pad_maximum_fusion.2), channel_id=1, source_target_pairs={{2,0},{4,2},{6,4},{8,6},{10,8},{12,10},{14,12},{16,14},{18,16},{20... | collective-permute-start | bytes 786440 | tf_op jit(solution)/shard_map/while/body/eval_jaxpr/ppermute | solution.py:16
  225.7 8.6 %collective-permute-start = (bf16[1,2,256,256]{3,2,1,0:T(8,128)(2,1)S(1)}, bf16[1,2,256,256]{3,2,1,0:T(8,128)(2,1)S(1)}, u32[]{:S(2)}, u32[]{:S(2)}) collective-permute-start(bf16[1,2,256,256]{3,2,1,0:T(8,128)(2,1)S(1)} %pad_maximum_fusion.2), channel_id=1, source_target_pairs={{2,0},{4,2},{6,4},{8,6},{10,8},{12,10},{14,12},{16,14},{18,16},{20... | collective-permute-start | bytes 786440 | tf_op jit(solution)/shard_map/while/body/eval_jaxpr/ppermute | solution.py:16
  241.0 8.6 %collective-permute-start = (bf16[1,2,256,256]{3,2,1,0:T(8,128)(2,1)S(1)}, bf16[1,2,256,256]{3,2,1,0:T(8,128)(2,1)S(1)}, u32[]{:S(2)}, u32[]{:S(2)}) collective-permute-start(bf16[1,2,256,256]{3,2,1,0:T(8,128)(2,1)S(1)} %pad_maximum_fusion.2), channel_id=1, source_target_pairs={{2,0},{4,2},{6,4},{8,6},{10,8},{12,10},{14,12},{16,14},{18,16},{20... | collective-permute-start | bytes 786440 | tf_op jit(solution)/shard_map/while/body/eval_jaxpr/ppermute | solution.py:16
  256.3 8.6 %collective-permute-start = (bf16[1,2,256,256]{3,2,1,0:T(8,128)(2,1)S(1)}, bf16[1,2,256,256]{3,2,1,0:T(8,128)(2,1)S(1)}, u32[]{:S(2)}, u32[]{:S(2)}) collective-permute-start(bf16[1,2,256,256]{3,2,1,0:T(8,128)(2,1)S(1)} %pad_maximum_fusion.2), channel_id=1, source_target_pairs={{2,0},{4,2},{6,4},{8,6},{10,8},{12,10},{14,12},{16,14},{18,16},{20... | collective-permute-start | bytes 786440 | tf_op jit(solution)/shard_map/while/body/eval_jaxpr/ppermute | solution.py:16
  271.6 8.6 %collective-permute-start = (bf16[1,2,256,256]{3,2,1,0:T(8,128)(2,1)S(1)}, bf16[1,2,256,256]{3,2,1,0:T(8,128)(2,1)S(1)}, u32[]{:S(2)}, u32[]{:S(2)}) collective-permute-start(bf16[1,2,256,256]{3,2,1,0:T(8,128)(2,1)S(1)} %pad_maximum_fusion.2), channel_id=1, source_target_pairs={{2,0},{4,2},{6,4},{8,6},{10,8},{12,10},{14,12},{16,14},{18,16},{20... | collective-permute-start | bytes 786440 | tf_op jit(solution)/shard_map/while/body/eval_jaxpr/ppermute | solution.py:16
  286.9 8.6 %collective-permute-start = (bf16[1,2,256,256]{3,2,1,0:T(8,128)(2,1)S(1)}, bf16[1,2,256,256]{3,2,1,0:T(8,128)(2,1)S(1)}, u32[]{:S(2)}, u32[]{:S(2)}) collective-permute-start(bf16[1,2,256,256]{3,2,1,0:T(8,128)(2,1)S(1)} %pad_maximum_fusion.2), channel_id=1, source_target_pairs={{2,0},{4,2},{6,4},{8,6},{10,8},{12,10},{14,12},{16,14},{18,16},{20... | collective-permute-start | bytes 786440 | tf_op jit(solution)/shard_map/while/body/eval_jaxpr/ppermute | solution.py:16
  302.1 8.6 %collective-permute-start = (bf16[1,2,256,256]{3,2,1,0:T(8,128)(2,1)S(1)}, bf16[1,2,256,256]{3,2,1,0:T(8,128)(2,1)S(1)}, u32[]{:S(2)}, u32[]{:S(2)}) collective-permute-start(bf16[1,2,256,256]{3,2,1,0:T(8,128)(2,1)S(1)} %pad_maximum_fusion.2), channel_id=1, source_target_pairs={{2,0},{4,2},{6,4},{8,6},{10,8},{12,10},{14,12},{16,14},{18,16},{20... | collective-permute-start | bytes 786440 | tf_op jit(solution)/shard_map/while/body/eval_jaxpr/ppermute | solution.py:16
  317.4 8.6 %collective-permute-start = (bf16[1,2,256,256]{3,2,1,0:T(8,128)(2,1)S(1)}, bf16[1,2,256,256]{3,2,1,0:T(8,128)(2,1)S(1)}, u32[]{:S(2)}, u32[]{:S(2)}) collective-permute-start(bf16[1,2,256,256]{3,2,1,0:T(8,128)(2,1)S(1)} %pad_maximum_fusion.2), channel_id=1, source_target_pairs={{2,0},{4,2},{6,4},{8,6},{10,8},{12,10},{14,12},{16,14},{18,16},{20... | collective-permute-start | bytes 786440 | tf_op jit(solution)/shard_map/while/body/eval_jaxpr/ppermute | solution.py:16
  332.7 8.6 %collective-permute-start = (bf16[1,2,256,256]{3,2,1,0:T(8,128)(2,1)S(1)}, bf16[1,2,256,256]{3,2,1,0:T(8,128)(2,1)S(1)}, u32[]{:S(2)}, u32[]{:S(2)}) collective-permute-start(bf16[1,2,256,256]{3,2,1,0:T(8,128)(2,1)S(1)} %pad_maximum_fusion.2), channel_id=1, source_target_pairs={{2,0},{4,2},{6,4},{8,6},{10,8},{12,10},{14,12},{16,14},{18,16},{20... | collective-permute-start | bytes 786440 | tf_op jit(solution)/shard_map/while/body/eval_jaxpr/ppermute | solution.py:16
  348.0 8.6 %collective-permute-start = (bf16[1,2,256,256]{3,2,1,0:T(8,128)(2,1)S(1)}, bf16[1,2,256,256]{3,2,1,0:T(8,128)(2,1)S(1)}, u32[]{:S(2)}, u32[]{:S(2)}) collective-permute-start(bf16[1,2,256,256]{3,2,1,0:T(8,128)(2,1)S(1)} %pad_maximum_fusion.2), channel_id=1, source_target_pairs={{2,0},{4,2},{6,4},{8,6},{10,8},{12,10},{14,12},{16,14},{18,16},{20... | collective-permute-start | bytes 786440 | tf_op jit(solution)/shard_map/while/body/eval_jaxpr/ppermute | solution.py:16
  363.3 8.6 %collective-permute-start = (bf16[1,2,256,256]{3,2,1,0:T(8,128)(2,1)S(1)}, bf16[1,2,256,256]{3,2,1,0:T(8,128)(2,1)S(1)}, u32[]{:S(2)}, u32[]{:S(2)}) collective-permute-start(bf16[1,2,256,256]{3,2,1,0:T(8,128)(2,1)S(1)} %pad_maximum_fusion.2), channel_id=1, source_target_pairs={{2,0},{4,2},{6,4},{8,6},{10,8},{12,10},{14,12},{16,14},{18,16},{20... | collective-permute-start | bytes 786440 | tf_op jit(solution)/shard_map/while/body/eval_jaxpr/ppermute | solution.py:16
  378.6 8.6 %collective-permute-start = (bf16[1,2,256,256]{3,2,1,0:T(8,128)(2,1)S(1)}, bf16[1,2,256,256]{3,2,1,0:T(8,128)(2,1)S(1)}, u32[]{:S(2)}, u32[]{:S(2)}) collective-permute-start(bf16[1,2,256,256]{3,2,1,0:T(8,128)(2,1)S(1)} %pad_maximum_fusion.2), channel_id=1, source_target_pairs={{2,0},{4,2},{6,4},{8,6},{10,8},{12,10},{14,12},{16,14},{18,16},{20... | collective-permute-start | bytes 786440 | tf_op jit(solution)/shard_map/while/body/eval_jaxpr/ppermute | solution.py:16
  393.9 8.6 %collective-permute-start = (bf16[1,2,256,256]{3,2,1,0:T(8,128)(2,1)S(1)}, bf16[1,2,256,256]{3,2,1,0:T(8,128)(2,1)S(1)}, u32[]{:S(2)}, u32[]{:S(2)}) collective-permute-start(bf16[1,2,256,256]{3,2,1,0:T(8,128)(2,1)S(1)} %pad_maximum_fusion.2), channel_id=1, source_target_pairs={{2,0},{4,2},{6,4},{8,6},{10,8},{12,10},{14,12},{16,14},{18,16},{20... | collective-permute-start | bytes 786440 | tf_op jit(solution)/shard_map/while/body/eval_jaxpr/ppermute | solution.py:16
  520.5 1.3 copy-start
Sparse Core Ops, SparseCore 0:
  8.9 23.9 all-gather.2
  34.5 21.2 all-gather.4
  522.0 49.6 reduce-scatter.1
where the time goes:
time: 583 us; the launch traced here: 578 us
  waiting for transfers between devices  210 us (36%)
  loops' own time  119 us (20%)
  other arithmetic  118 us (20%)
  local copies, waits for them, and re-layouts  88.9 us (15%)
  starting transfers between devices  29.8 us (5%)
  between operations  13.2 us (2%)
    ppermute x23, waiting for transfers between devices, shifted(): lax.ppermute(value, axis, [(source, source + steps) for source in range(f...  111 us
    another operation x1, loops' own time, on_device(): lax.fori_loop(0, tick_count, one_tick, (start_wave, start_store))  88.1 us
    dynamic_update_slice x8, local copies, waits for them, and re-layouts, add_position(): lax.dynamic_update_slice(gradient, added, (zero_index, row_at, col_at))  63.2 us
    reduce_scatter x1, waiting for transfers between devices, on_device(): lax.psum_scatter(gradient, 'scan', scatter_dimension=1, tiled=True)  49.8 us
    dynamic_update_slice x23, other arithmetic, one_tick(): stored = lax.dynamic_update_index_in_dim(stored, kept, slot, 0)  44 us
    another operation x1, loops' own time, on_device(): gradient = lax.fori_loop(0, position_count, add_position, start_grad)  30.7 us
    ppermute x23, starting transfers between devices, shifted(): lax.ppermute(value, axis, [(source, source + steps) for source in range(f...  29.7 us
    all_gather x1, waiting for transfers between devices, on_device(): lax.all_gather(obj_amp, 'scan', axis=1, tiled=True)  24.9 us
  transfers between devices with their start and end apart: 26, of which 26 were waited for; matrix products, arithmetic and copies ran while one was open for 8% of the time, Pallas kernels for 0%

commit v1 on v0

v1 whole, which is shorter than its diff:
```python
import jax
import jax.numpy as jnp
from jax import lax
from jax.experimental import pallas as pl
from jax.experimental.pallas import tpu as pltpu
from jax.sharding import PartitionSpec as P

SUBSTEPS = 2
damping = 0.0005
turning = 0.011
code_gain = 83.0
sublanes = 8
lanes = 128
vmem_bytes = 48 * 2**20


def params():
    return pltpu.CompilerParams(vmem_limit_bytes=vmem_bytes)


def around(corner_ref, position, window):
    row_at = corner_ref[position, 0]
    col_at = corner_ref[position, 1]
    row_by = lax.rem(row_at, sublanes)
    col_by = lax.rem(col_at, lanes)
    row_to = pl.multiple_of(row_at - row_by, sublanes)
    col_to = pl.multiple_of(col_at - col_by, lanes)
    return window + sublanes, window + lanes, row_to, row_by, col_to, col_by


def padded(rows, width):
    return pltpu.VMEM((2, 2 * rows + sublanes, width + lanes), jnp.float32)


def cut_kernel(corner_ref, place_ref, mine_ref, other_ref, win_ref, full_ref):
    position = pl.program_id(0)
    rows = mine_ref.shape[1]
    width = mine_ref.shape[2]
    window = win_ref.shape[-1]

    @pl.when(position == 0)
    def _():
        here = pl.multiple_of(place_ref[0] * rows, rows)
        there = pl.multiple_of((1 - place_ref[0]) * rows, rows)
        full_ref[:, pl.ds(here, rows), :width] = mine_ref[...].astype(jnp.float32)
        full_ref[:, pl.ds(there, rows), :width] = other_ref[...].astype(jnp.float32)

    tall, wide, row_to, row_by, col_to, col_by = around(corner_ref, position, window)
    for part in range(2):
        box = full_ref[part, pl.ds(row_to, tall), pl.ds(col_to, wide)]
        box = pltpu.roll(box, lax.rem(wide - col_by, wide), 1)[:, :window]
        box = pltpu.roll(box, lax.rem(tall - row_by, tall), 0)[:window]
        win_ref[0, part] = box.astype(jnp.bfloat16)


def cut_windows(offsets, place, mine, other, window):
    count = offsets.shape[0]
    _, rows, width = mine.shape
    whole = pl.BlockSpec(mine.shape, lambda p, *_: (0, 0, 0))
    return pl.pallas_call(
        cut_kernel,
        grid_spec=pltpu.PrefetchScalarGridSpec(
            num_scalar_prefetch=2,
            grid=(count,),
            in_specs=[whole, whole],
            out_specs=pl.BlockSpec((1, 2, window, window), lambda p, *_: (p, 0, 0, 0)),
            scratch_shapes=[padded(rows, width)],
        ),
        out_shape=jax.ShapeDtypeStruct((count, 2, window, window), jnp.bfloat16),
        compiler_params=params(),
    )(offsets, place, mine, other)


def second_difference(size):
    row = lax.broadcasted_iota(jnp.int32, (size, size), 0)
    col = lax.broadcasted_iota(jnp.int32, (size, size), 1)
    apart = jnp.abs(row - col)
    return jnp.where(apart == 0, -2.0, jnp.where(apart == 1, 1.0, 0.0)).astype(jnp.bfloat16)


def laplacian(band, field_re, field_im):
    def one(field):
        down = jnp.dot(band, field, preferred_element_type=jnp.float32)
        return down + jnp.dot(field, band, preferred_element_type=jnp.float32)

    return one(field_re), one(field_im)


def back(band, chi_re, chi_im):
    lap_re, lap_im = laplacian(band, chi_re, chi_im)
    lap2_re, lap2_im = laplacian(band, lap_re.astype(jnp.bfloat16), lap_im.astype(jnp.bfloat16))
    square_re = damping * damping - turning * turning
    square_im = 2.0 * damping * turning
    spread_re = chi_re.astype(jnp.float32) + (2.0 * damping) * lap_re + (2.0 * turning) * lap_im
    spread_im = chi_im.astype(jnp.float32) + (2.0 * damping) * lap_im - (2.0 * turning) * lap_re
    spread_re = spread_re + square_re * lap2_re + square_im * lap2_im
    spread_im = spread_im + square_re * lap2_im - square_im * lap2_re
    return spread_re, spread_im


def group_kernel(pick_ref, exit_ref, come_ref, win_ref, spread_ref, leave_ref, chi_ref, band_ref):
    step = pl.program_id(0)

    @pl.when(step == 0)
    def _():
        band_ref[...] = second_difference(band_ref.shape[0])

        @pl.when(pick_ref[1] == 1)
        def _():
            chi_ref[...] = exit_ref[0]

        @pl.when(pick_ref[1] == 0)
        def _():
            chi_ref[...] = come_ref[...]

    spread_re, spread_im = back(band_ref[...], chi_ref[0], chi_ref[1])
    spread_ref[0, 0] = spread_re.astype(jnp.bfloat16)
    spread_ref[0, 1] = spread_im.astype(jnp.bfloat16)
    win_re = jnp.log(win_ref[0, 0].astype(jnp.float32)) * (1.0 / code_gain)
    win_im = jnp.log(win_ref[0, 1].astype(jnp.float32)) * (1.0 / code_gain)
    chi_ref[0] = (win_re * spread_re + win_im * spread_im).astype(jnp.bfloat16)
    chi_ref[1] = (win_re * spread_im - win_im * spread_re).astype(jnp.bfloat16)

    @pl.when(step == pl.num_programs(0) - 1)
    def _():
        leave_ref[...] = chi_ref[...]


def through_group(pick, exits, come, windows):
    count, _, window, _ = windows.shape
    wave = (2, window, window)
    last = count - 1
    return pl.pallas_call(
        group_kernel,
        grid_spec=pltpu.PrefetchScalarGridSpec(
            num_scalar_prefetch=1,
            grid=(count,),
            in_specs=[
                pl.BlockSpec((1,) + wave, lambda k, pick: (pick[0], 0, 0, 0)),
                pl.BlockSpec(wave, lambda k, pick: (0, 0, 0)),
                pl.BlockSpec((1,) + wave, lambda k, pick: (last - k, 0, 0, 0)),
            ],
            out_specs=[
                pl.BlockSpec((1,) + wave, lambda k, pick: (last - k, 0, 0, 0)),
                pl.BlockSpec(wave, lambda k, pick: (0, 0, 0)),
            ],
            scratch_shapes=[
                pltpu.VMEM(wave, jnp.bfloat16),
                pltpu.VMEM((window, window), jnp.bfloat16),
            ],
        ),
        out_shape=[
            jax.ShapeDtypeStruct(windows.shape, jnp.bfloat16),
            jax.ShapeDtypeStruct(wave, jnp.bfloat16),
        ],
        compiler_params=params(),
    )(pick, exits, come, windows)


def gradient_kernel(corner_ref, place_ref, wave_ref, spread_ref, mine_ref, other_ref, sum_ref):
    position = pl.program_id(0)
    rows = mine_ref.shape[1]
    width = mine_ref.shape[2]
    window = wave_ref.shape[-1]

    @pl.when(position == 0)
    def _():
        sum_ref[...] = jnp.zeros_like(sum_ref)

    tall, wide, row_to, row_by, col_to, col_by = around(corner_ref, position, window)
    wave_re = wave_ref[0, 0].astype(jnp.float32)
    wave_im = wave_ref[0, 1].astype(jnp.float32)
    spread_re = spread_ref[0, 0].astype(jnp.float32)
    spread_im = spread_ref[0, 1].astype(jnp.float32)
    parts = (
        wave_re * spread_re + wave_im * spread_im,
        wave_re * spread_im - wave_im * spread_re,
    )
    below = jnp.zeros((tall - window, window), jnp.float32)
    beside = jnp.zeros((tall, wide - window), jnp.float32)
    for part in range(2):
        box = pltpu.roll(jnp.concatenate([parts[part], below], axis=0), row_by, 0)
        box = pltpu.roll(jnp.concatenate([box, beside], axis=1), col_by, 1)
        sum_ref[part, pl.ds(row_to, tall), pl.ds(col_to, wide)] += box

    @pl.when(position == pl.num_programs(0) - 1)
    def _():
        here = pl.multiple_of(place_ref[0] * rows, rows)
        there = pl.multiple_of((1 - place_ref[0]) * rows, rows)
        mine_ref[...] = sum_ref[:, pl.ds(here, rows), :width]
        other_ref[...] = sum_ref[:, pl.ds(there, rows), :width].astype(jnp.bfloat16)


def gradient(offsets, place, waves, spreads, half):
    count, _, window, _ = waves.shape
    block = pl.BlockSpec((1, 2, window, window), lambda p, *_: (p, 0, 0, 0))
    whole = pl.BlockSpec(half, lambda p, *_: (0, 0, 0))
    return pl.pallas_call(
        gradient_kernel,
        grid_spec=pltpu.PrefetchScalarGridSpec(
            num_scalar_prefetch=2,
            grid=(count,),
            in_specs=[block, block],
            out_specs=[whole, whole],
            scratch_shapes=[padded(half[1], half[2])],
        ),
        out_shape=[
            jax.ShapeDtypeStruct(half, jnp.float32),
            jax.ShapeDtypeStruct(half, jnp.bfloat16),
        ],
        compiler_params=params(),
    )(offsets, place, waves, spreads)


def on_device(obj_amp, obj_phase, forward_waves, exit_adjoint, offsets):
    sections = lax.axis_size("sec")
    section = lax.axis_index("sec")
    place = lax.axis_index("scan").astype(jnp.int32).reshape(1)
    position_count, _, window, _ = exit_adjoint.shape
    group = position_count
    group_count = sections // group
    swap = [(0, 1), (1, 0)]
    groups = [[first + i for i in range(group)] for first in range(0, sections, group)]

    trans_re = obj_amp[0] * jnp.cos(obj_phase[0])
    trans_im = obj_amp[0] * jnp.sin(obj_phase[0])
    mine = jnp.exp(code_gain * jnp.stack([trans_re, trans_im])).astype(jnp.bfloat16)
    other = lax.ppermute(mine, "scan", swap)
    cut = cut_windows(offsets, place, mine, other, window)
    windows = lax.all_to_all(cut, "sec", 0, 0, axis_index_groups=groups, tiled=True)

    at_end = (section >= sections - group).astype(jnp.int32)
    pick = jnp.stack([section % group, jnp.int32(1)])
    come = jnp.zeros((2, window, window), jnp.bfloat16)
    for stage in range(group_count):
        spreads, leave = through_group(pick, exit_adjoint, come, windows)
        if stage < group_count - 1:
            come = lax.ppermute(leave, "sec", [(s, s - group) for s in range(group, sections)])
            pick = jnp.stack([section % group, at_end])

    spreads = lax.all_to_all(spreads, "sec", 0, 0, axis_index_groups=groups, tiled=True)
    own, away = gradient(offsets, place, forward_waves[0], spreads, mine.shape)
    reduced = own + lax.ppermute(away, "scan", swap).astype(jnp.float32)
    return reduced[None]


def solution(mesh):
    in_specs = (
        P("sec", "scan", None),
        P("sec", "scan", None),
        P("sec", "scan", None, None, None),
        P("scan", None, None, None),
        P("scan", None),
    )
    out_specs = P("sec", None, "scan", None)
    return jax.shard_map(
        on_device, mesh=mesh, in_specs=in_specs, out_specs=out_specs, check_vma=False
    )
```

time: 583 us -> 136 us (0.23)
  waiting for transfers between devices: 210 us -> 64.2 us
  loops' own time: 119 us -> 0 us
  other arithmetic: 118 us -> 4.36 us
  local copies, waits for them, and re-layouts: 88.9 us -> 1.42 us
  blocking collectives: 0 us -> 28.6 us
  Pallas kernels: 0 us -> 26.2 us
  starting transfers between devices: 29.8 us -> 10.6 us
  between operations: 13.2 us -> 0.1 us
    another operation x2 -> x0, loops' own time: 119 us -> none  [the longest x1 88.1 us: on_device(): lax.fori_loop(0, tick_count, one_tick, (start_wave, start_store))]
    ppermute x23 -> x3, waiting for transfers between devices: 111 us -> 38.6 us  [the longest x1 14.9 us: on_device(): lax.ppermute(leave, 'sec', [(s, s - group) for s in range(group, sections)])]
    dynamic_update_slice x8 -> x0, local copies, waits for them, and re-layouts: 63.2 us -> none  [add_position(): lax.dynamic_update_slice(gradient, added, (zero_index, row_at, col_at))]
    reduce_scatter x1 -> x0, waiting for transfers between devices: 49.8 us -> none  [on_device(): lax.psum_scatter(gradient, 'scan', scatter_dimension=1, tiled=True)]
    all_gather x2 -> x0, waiting for transfers between devices: 47.8 us -> none  [the longest x1 24.9 us: on_device(): lax.all_gather(obj_amp, 'scan', axis=1, tiled=True)]
    dynamic_update_slice x23 -> x0, other arithmetic: 44 us -> none  [one_tick(): stored = lax.dynamic_update_index_in_dim(stored, kept, slot, 0)]
    convert_element_type x31 -> x1, other arithmetic: 30.9 us -> 0.15 us  [on_device(): jnp.exp(code_gain * jnp.stack([trans_re, trans_im])).astype(jnp.bfloat16)]
    all_to_all x0 -> x1, blocking collectives: none -> 28.6 us  [on_device(): lax.all_to_all(spreads, 'sec', 0, 0, axis_index_groups=groups, tiled=True)]
  transfers between devices with their start and end apart: 26 -> 4, of which waited for: 26 -> 4; matrix products, arithmetic and copies ran while one was open for 8% -> 0% of each run, Pallas kernels for 0% -> 0%
where the time goes in v1:
time: 136 us
  waiting for transfers between devices  64.2 us (47%)
  blocking collectives  28.6 us (21%)
  Pallas kernels  26.2 us (19%)
  starting transfers between devices  10.6 us (8%)
  other arithmetic  4.36 us (3%)
  local copies, waits for them, and re-layouts  1.42 us (1%)
    all_to_all x1, blocking collectives, on_device(): lax.all_to_all(spreads, 'sec', 0, 0, axis_index_groups=groups, tiled=True)  28.6 us
    all_to_all x1, waiting for transfers between devices, on_device(): lax.all_to_all(cut, 'sec', 0, 0, axis_index_groups=groups, tiled=True)  25.6 us
    pallas_call x2, Pallas kernels, through_group(): pl.pallas_call(group_kernel, grid_spec=pltpu.PrefetchScalarGridSpec(num_s...  17.2 us
    ppermute x1, waiting for transfers between devices, on_device(): lax.ppermute(leave, 'sec', [(s, s - group) for s in range(group, sections)])  14.9 us
    ppermute x1, waiting for transfers between devices, on_device(): reduced = own + lax.ppermute(away, 'scan', swap).astype(jnp.float32)  11.9 us
    ppermute x1, waiting for transfers between devices, on_device(): other = lax.ppermute(mine, 'scan', swap)  11.8 us
    pallas_call x1, Pallas kernels, gradient(): pl.pallas_call(gradient_kernel, grid_spec=pltpu.PrefetchScalarGridSpec(nu...  4.84 us
    all_to_all x1, starting transfers between devices, on_device(): lax.all_to_all(cut, 'sec', 0, 0, axis_index_groups=groups, tiled=True)  4.48 us
  transfers between devices with their start and end apart: 4, of which 4 were waited for; matrix products, arithmetic and copies ran while one was open for 0% of the time, Pallas kernels for 0%

profile of v1, /device:TPU:0, one launch (start us, length us, event | category | flops | bytes accessed | tf_op | source)
XLA Modules:
  0.0 135.5 jit_solution(18093740105155184415)
XLA Ops:
  0.0 0.0 copy-start.3
  0.0 2.9 %cosine_multiply_fusion = (f32[1,256,512]{2,1,0:T(8,128)S(1)}, f32[1,256,512]{2,1,0:T(8,128)S(1)}) fusion(f32[1,256,512]{2,1,0:T(8,128)} %param.5, f32[1,256,512]{2,1,0:T(8,128)} %param.6), kind=kLoop, calls=%fused_computation.5 | loop fusion | flops 262144 | bytes 2097152 | tf_op jit(solution)/shard_map/mul | solution.py:225
  2.9 0.1 fusion.1.mine_ref
  3.1 3.0 %collective-permute-start = (bf16[2,256,512]{2,1,0:T(8,128)(2,1)S(1)}, bf16[2,256,512]{2,1,0:T(8,128)(2,1)S(1)}, u32[]{:S(2)}, u32[]{:S(2)}) collective-permute-start(bf16[2,256,512]{2,1,0:T(8,128)(2,1)S(1)} %fusion.1.mine_ref), channel_id=1, source_target_pairs={{0,1},{1,0},{2,3},{3,2},{4,5},{5,4},{6,7},{7,6},{8,9},{9,8},{10,11... | collective-permute-start | bytes 1572872 | tf_op jit(solution)/shard_map/ppermute | solution.py:228
  6.1 0.0 copy-done.3
  6.1 0.1 copy.7.corner_ref
  6.2 11.8 %collective-permute-done.other_ref = bf16[2,256,512]{2,1,0:T(8,128)(2,1)S(1)} collective-permute-done((bf16[2,256,512]{2,1,0:T(8,128)(2,1)S(1)}, bf16[2,256,512]{2,1,0:T(8,128)(2,1)S(1)}, u32[]{:S(2)}, u32[]{:S(2)}) %collective-permute-start) | collective-permute-done | bytes 524320 | tf_op jit(solution)/shard_map/ppermute | solution.py:228
  18.0 4.2 %shard_map.55 = bf16[8,2,256,256]{3,2,1,0:T(8,128)(2,1)S(1)} custom-call(s32[8,2]{1,0:T(8,128)S(1)} %copy.7.corner_ref, s32[1]{0:T(128)} %bitcast.place_ref, bf16[2,256,512]{2,1,0:T(8,128)(2,1)S(1)} %fusion.1.mine_ref, bf16[2,256,512]{2,1,0:T(8,128)(2,1)S(1)} %collective-permute-done.other_ref), custom_call_target="tpu_custom_call" | custom-call | tf_op jit(solution)/shard_map/pallas_call | solution.py:60
  22.2 0.0 copy-start.1
  22.2 1.3 copy-done.1
  23.5 0.0 copy-start
  23.5 4.5 %all-to-all-start = ((bf16[8,2,256,256]{3,2,1,0:T(8,128)(2,1)}), bf16[8,2,256,256]{3,2,1,0:T(8,128)(2,1)}, u32[]{:S(2)}, u32[]{:S(2)}) async-start(bf16[8,2,256,256]{3,2,1,0:T(8,128)(2,1)} %copy-done.1), calls=%async_computation | async-start | bytes 4194304 | tf_op jit(solution)/shard_map/all_to_all | solution.py:230
  28.0 0.1 pad_add_fusion.1.pick_ref
  28.1 25.6 %all-to-all-done.win_ref = bf16[8,2,256,256]{3,2,1,0:T(8,128)(2,1)} async-done(((bf16[8,2,256,256]{3,2,1,0:T(8,128)(2,1)}), bf16[8,2,256,256]{3,2,1,0:T(8,128)(2,1)}, u32[]{:S(2)}, u32[]{:S(2)}) %all-to-all-start) | async-done | bytes 2097184 | tf_op jit(solution)/shard_map/all_to_all | solution.py:230
  53.7 0.0 copy-done
  53.7 8.8 %shard_map.56 = (bf16[8,2,256,256]{3,2,1,0:T(8,128)(2,1)}, bf16[2,256,256]{2,1,0:T(8,128)(2,1)S(1)}) custom-call(s32[2]{0:T(128)S(1)} %pad_add_fusion.1.pick_ref, bf16[8,2,256,256]{3,2,1,0:T(8,128)(2,1)S(1)} %copy-done, bf16[2,256,256]{2,1,0:T(8,128)(2,1)S(1)} %broadcast_in_dim.6.come_ref, bf16[8,2,256,256]{3,2,1,0:T(8,128)(2,1)} %all-to-all-done.win_ref), custom_call_target="tpu_custom_call" | custom-call | tf_op jit(solution)/shard_map/pallas_call | solution.py:133
  62.5 1.3 collective-permute-start.1
  63.8 0.1 pad_add_fusion.pick_ref
  63.8 14.9 %collective-permute-done.1.come_ref = bf16[2,256,256]{2,1,0:T(8,128)(2,1)S(1)} collective-permute-done((bf16[2,256,256]{2,1,0:T(8,128)(2,1)S(1)}, bf16[2,256,256]{2,1,0:T(8,128)(2,1)S(1)}, u32[]{:S(2)}, u32[]{:S(2)}) %collective-permute-start.1) | collective-permute-done | bytes 262176 | tf_op jit(solution)/shard_map/ppermute | solution.py:238
  78.7 8.5 %shard_map.57 = (bf16[8,2,256,256]{3,2,1,0:T(8,128)(2,1)S(1)}, bf16[2,256,256]{2,1,0:T(8,128)(2,1)}) custom-call(s32[2]{0:T(128)S(1)} %pad_add_fusion.pick_ref, bf16[8,2,256,256]{3,2,1,0:T(8,128)(2,1)S(1)} %copy-done, bf16[2,256,256]{2,1,0:T(8,128)(2,1)S(1)} %collective-permute-done.1.come_ref, bf16[8,2,256,256]{3,2,1,0:T(8,128)(2,1)} %all-to-all-done.win_ref), custom_call_target="tpu_custom_call" | custom-call | tf_op jit(solution)/shard_map/pallas_call | solution.py:133
  87.2 0.0 copy-start.2
  87.2 28.6 %all_to_all.10.spread_ref = bf16[8,2,256,256]{3,2,1,0:T(8,128)(2,1)S(1)} all-to-all(bf16[8,2,256,256]{3,2,1,0:T(8,128)(2,1)S(1)} %get-tuple-element.10), channel_id=1, replica_groups={{0,2,4,6,8,10,12,14},{16,18,20,22,24,26,28,30},{1,3,5,7,9,11,13,15},{17..., dimensions={0} | all-to-all | bytes 4194304 | tf_op jit(solution)/shard_map/all_to_all | solution.py:241
  115.8 0.0 copy-done.2
  115.8 4.8 %shard_map.58 = (f32[2,256,512]{2,1,0:T(8,128)S(1)}, bf16[2,256,512]{2,1,0:T(8,128)(2,1)S(1)}) custom-call(s32[8,2]{1,0:T(8,128)S(1)} %copy.7.corner_ref, s32[1]{0:T(128)} %bitcast.place_ref, bf16[8,2,256,256]{3,2,1,0:T(8,128)(2,1)S(1)} %bitcast.6, bf16[8,2,256,256]{3,2,1,0:T(8,128)(2,1)S(1)} %all_to_all.10.spread_ref), custom_call_target="tpu_custom_call" | custom-call | tf_op jit(solution)/shard_map/pallas_call | solution.py:198
  120.7 1.8 %collective-permute-start.2 = (bf16[2,256,512]{2,1,0:T(8,128)(2,1)S(1)}, bf16[2,256,512]{2,1,0:T(8,128)(2,1)S(1)}, u32[]{:S(2)}, u32[]{:S(2)}) collective-permute-start(bf16[2,256,512]{2,1,0:T(8,128)(2,1)S(1)} %get-tuple-element.12), channel_id=1, source_target_pairs={{0,1},{1,0},{2,3},{3,2},{4,5},{5,4},{6,7},{7,6},{8,9},{9,8},{10,11... | collective-permute-start | bytes 1572872 | tf_op jit(solution)/shard_map/ppermute | solution.py:243
  122.5 11.9 %collective-permute-done.2 = bf16[2,256,512]{2,1,0:T(8,128)(2,1)S(1)} collective-permute-done((bf16[2,256,512]{2,1,0:T(8,128)(2,1)S(1)}, bf16[2,256,512]{2,1,0:T(8,128)(2,1)S(1)}, u32[]{:S(2)}, u32[]{:S(2)}) %collective-permute-start.2) | collective-permute-done | bytes 524320 | tf_op jit(solution)/shard_map/ppermute | solution.py:243
  134.4 1.1 add_bitcast_fusion
  (1 shorter events, 0.0 us)
Async XLA Ops:
  0.0 6.1 %copy-start.3 = (s32[8,2]{0,1:T(2,128)S(1)}, s32[8,2]{0,1:T(2,128)}, u32[]{:S(2)}) copy-start(s32[8,2]{0,1:T(2,128)} %param.9) | copy-start | bytes 196
  3.1 14.9 %collective-permute-start = (bf16[2,256,512]{2,1,0:T(8,128)(2,1)S(1)}, bf16[2,256,512]{2,1,0:T(8,128)(2,1)S(1)}, u32[]{:S(2)}, u32[]{:S(2)}) collective-permute-start(bf16[2,256,512]{2,1,0:T(8,128)(2,1)S(1)} %fusion.1.mine_ref), channel_id=1, source_target_pairs={{0,1},{1,0},{2,3},{3,2},{4,5},{5,4},{6,7},{7,6},{8,9},{9,8},{10,11... | collective-permute-start | bytes 1572872 | tf_op jit(solution)/shard_map/ppermute | solution.py:228
  22.2 1.3 copy-start.1
  23.5 30.2 %copy-start = (bf16[8,2,256,256]{3,2,1,0:T(8,128)(2,1)S(1)}, bf16[8,2,256,256]{3,2,1,0:T(8,128)(2,1)}, u32[]{:S(2)}) copy-start(bf16[8,2,256,256]{3,2,1,0:T(8,128)(2,1)} %exit_ref.3) | copy-start | bytes 6291460
  23.5 30.2 %all-to-all-start = ((bf16[8,2,256,256]{3,2,1,0:T(8,128)(2,1)}), bf16[8,2,256,256]{3,2,1,0:T(8,128)(2,1)}, u32[]{:S(2)}, u32[]{:S(2)}) async-start(bf16[8,2,256,256]{3,2,1,0:T(8,128)(2,1)} %copy-done.1), calls=%async_computation | async-start | bytes 4194304 | tf_op jit(solution)/shard_map/all_to_all | solution.py:230
  62.5 16.2 %collective-permute-start.1 = (bf16[2,256,256]{2,1,0:T(8,128)(2,1)S(1)}, bf16[2,256,256]{2,1,0:T(8,128)(2,1)S(1)}, u32[]{:S(2)}, u32[]{:S(2)}) collective-permute-start(bf16[2,256,256]{2,1,0:T(8,128)(2,1)S(1)} %get-tuple-element.9), channel_id=1, source_target_pairs={{16,0},{18,2},{20,4},{22,6},{24,8},{26,10},{28,12},{30,14},{17,1},... | collective-permute-start | bytes 786440 | tf_op jit(solution)/shard_map/ppermute | solution.py:238
  87.2 28.7 %copy-start.2 = (bf16[1,8,2,256,256]{4,3,2,1,0:T(8,128)(2,1)S(1)}, bf16[1,8,2,256,256]{4,3,2,1,0:T(8,128)(2,1)}, u32[]{:S(2)}) copy-start(bf16[1,8,2,256,256]{4,3,2,1,0:T(8,128)(2,1)} %param.7) | copy-start | bytes 6291460
  120.7 13.7 %collective-permute-start.2 = (bf16[2,256,512]{2,1,0:T(8,128)(2,1)S(1)}, bf16[2,256,512]{2,1,0:T(8,128)(2,1)S(1)}, u32[]{:S(2)}, u32[]{:S(2)}) collective-permute-start(bf16[2,256,512]{2,1,0:T(8,128)(2,1)S(1)} %get-tuple-element.12), channel_id=1, source_target_pairs={{0,1},{1,0},{2,3},{3,2},{4,5},{5,4},{6,7},{7,6},{8,9},{9,8},{10,11... | collective-permute-start | bytes 1572872 | tf_op jit(solution)/shard_map/ppermute | solution.py:243

commit v2 on v0

v2 whole, which is shorter than its diff:
```python
import functools
import math

import jax
import jax.numpy as jnp
from jax import lax
from jax.experimental import pallas as pl
from jax.experimental.pallas import tpu as pltpu
from jax.sharding import PartitionSpec as P

SUBSTEPS = 2
damping = 0.0005
turning = 0.011
code_gain = 83.0
chunk_count = 2
f32 = jnp.float32
bf16 = jnp.bfloat16


def call(kernel, out_shape, prefetch=0, scratch=(), flops=0, transcendentals=0):
    def run(*args):
        moved = sum(a.size * a.dtype.itemsize for a in jax.tree.leaves((args, out_shape)))
        vmem = pl.BlockSpec(memory_space=pltpu.VMEM)
        return pl.pallas_call(
            kernel,
            grid_spec=pltpu.PrefetchScalarGridSpec(
                num_scalar_prefetch=prefetch,
                grid=(1,),
                in_specs=[vmem] * (len(args) - prefetch),
                out_specs=jax.tree.map(lambda _: vmem, out_shape),
                scratch_shapes=list(scratch),
            ),
            out_shape=out_shape,
            cost_estimate=pl.CostEstimate(flops=flops, bytes_accessed=moved, transcendentals=transcendentals),
            compiler_params=pltpu.CompilerParams(vmem_limit_bytes=32 * 2**20),
        )(*args)

    return run


def code_kernel(amp_ref, phase_ref, *code_refs):
    rows = code_refs[0].shape[1]
    for chunk, code_ref in enumerate(code_refs):
        amp = amp_ref[pl.ds(chunk * rows, rows), :]
        half = 0.5 * phase_ref[pl.ds(chunk * rows, rows), :]
        square = half * half
        sine = jnp.full_like(half, 1.0 / math.factorial(13))
        cosine = jnp.full_like(half, 1.0 / math.factorial(12))
        for power in (11, 9, 7, 5, 3, 1):
            sign = -1.0 if power % 4 == 3 else 1.0
            sine = sine * square + sign / math.factorial(power)
            cosine = cosine * square + sign / math.factorial(power - 1)
        sine = sine * half
        code_ref[0] = jnp.exp((code_gain * amp) * (1.0 - 2.0 * sine * sine)).astype(bf16)
        code_ref[1] = jnp.exp((code_gain * amp) * (2.0 * sine * cosine)).astype(bf16)


def first_masks(corner_ref, position, place, base, shape):
    row = lax.broadcasted_iota(jnp.int32, shape, 0) + base
    col = lax.broadcasted_iota(jnp.int32, shape, 1)
    at_first = (row >= corner_ref[position, 0]).astype(jnp.int32)
    return at_first != place, col >= corner_ref[position, 1]


def cut_kernel(base, corner_ref, place_ref, mine_ref, other_ref, win_ref):
    count, _, rows, window = win_ref.shape
    place = place_ref[0]

    def one(position, _):
        in_mine, in_left = first_masks(corner_ref, position, place, base, (rows, window))
        for part in range(2):
            left = jnp.where(in_mine, mine_ref[part, :, :window].astype(f32), other_ref[part, :, :window].astype(f32))
            right = jnp.where(in_mine, mine_ref[part, :, window:].astype(f32), other_ref[part, :, window:].astype(f32))
            win_ref[position, part] = jnp.where(in_left, left, right).astype(bf16)
        return 0

    lax.fori_loop(0, count, one, 0)


def turned(wave, row_at, col_at):
    window = wave.shape[-1]
    wave = pltpu.roll(wave.astype(f32), lax.rem(row_at, window), 0)
    return pltpu.roll(wave, lax.rem(col_at, window), 1).astype(bf16)


def second_difference(size, break_at):
    row = lax.broadcasted_iota(jnp.int32, (size, size), 0)
    col = lax.broadcasted_iota(jnp.int32, (size, size), 1)
    start = lax.rem(break_at, size)
    before = (lax.rem(row - col + size, size) == 1) & (row != start)
    after = (lax.rem(col - row + size, size) == 1) & (col != start)
    return jnp.where(row == col, -2.0, jnp.where(before | after, 1.0, 0.0)).astype(bf16)


def ready_kernel(corner_ref, pick_ref, exit_ref, start_ref, down_ref, across_ref):
    own = pick_ref[0]
    row_at = corner_ref[own, 0]
    col_at = corner_ref[own, 1]
    size = start_ref.shape[-1]
    for part in range(2):
        start_ref[part] = turned(exit_ref[own, part], row_at, col_at)
    down_ref[...] = second_difference(size, row_at)
    across_ref[...] = second_difference(size, col_at)


def turn_kernel(corner_ref, wave_ref, turned_ref):
    count = wave_ref.shape[0]

    def one(position, _):
        for part in range(2):
            turned_ref[position, part] = turned(
                wave_ref[position, part], corner_ref[position, 0], corner_ref[position, 1]
            )
        return 0

    lax.fori_loop(0, count, one, 0)


def back(down, across, chi_re, chi_im):
    def laplacian(field):
        rows = jnp.dot(down, field, preferred_element_type=f32)
        return rows + jnp.dot(field, across, preferred_element_type=f32)

    lap_re = laplacian(chi_re)
    lap_im = laplacian(chi_im)
    lap2_re = laplacian(lap_re.astype(bf16))
    lap2_im = laplacian(lap_im.astype(bf16))
    square_re = damping * damping - turning * turning
    square_im = 2.0 * damping * turning
    spread_re = chi_re.astype(f32) + (2.0 * damping) * lap_re + (2.0 * turning) * lap_im
    spread_im = chi_im.astype(f32) + (2.0 * damping) * lap_im - (2.0 * turning) * lap_re
    spread_re = spread_re + square_re * lap2_re + square_im * lap2_im
    spread_im = spread_im + square_re * lap2_im - square_im * lap2_re
    return spread_re, spread_im


def group_kernel(pick_ref, start_ref, come_ref, down_ref, across_ref, *refs):
    win_refs = refs[:chunk_count]
    spread_refs = refs[chunk_count : 2 * chunk_count]
    leave_ref = refs[2 * chunk_count]
    count, _, rows, _ = win_refs[0].shape
    down = down_ref[...]
    across = across_ref[...]
    at_end = jnp.full(start_ref.shape[1:], pick_ref[1], jnp.int32) == 1
    chi_re, chi_im = (
        jnp.where(at_end, start_ref[part].astype(f32), come_ref[part].astype(f32)).astype(bf16) for part in range(2)
    )
    for layer in range(count - 1, -1, -1):
        spread_re, spread_im = back(down, across, chi_re, chi_im)
        out_re, out_im = [], []
        for chunk in range(chunk_count):
            here = slice(chunk * rows, (chunk + 1) * rows)
            part_re, part_im = spread_re[here], spread_im[here]
            spread_refs[chunk][layer, 0] = part_re.astype(bf16)
            spread_refs[chunk][layer, 1] = part_im.astype(bf16)
            win_re = jnp.log(win_refs[chunk][layer, 0].astype(f32)) * (1.0 / code_gain)
            win_im = jnp.log(win_refs[chunk][layer, 1].astype(f32)) * (1.0 / code_gain)
            out_re.append((win_re * part_re + win_im * part_im).astype(bf16))
            out_im.append((win_re * part_im - win_im * part_re).astype(bf16))
        chi_re = jnp.concatenate(out_re, axis=0)
        chi_im = jnp.concatenate(out_im, axis=0)
    leave_ref[0] = chi_re
    leave_ref[1] = chi_im


def gradient_kernel(base, corner_ref, place_ref, wave_ref, spread_ref, own_ref, away_ref):
    count, _, rows, window = spread_ref.shape
    tall = 16
    place = place_ref[0]

    def one(block, _):
        at = pl.multiple_of(block * tall, tall)
        sums = [jnp.zeros((tall, window), f32) for _ in range(8)]
        for position in range(count):
            in_mine, in_left = first_masks(corner_ref, position, place, base + at, (tall, window))
            wave_re, wave_im = (wave_ref[position, part, pl.ds(base + at, tall), :].astype(f32) for part in range(2))
            spread_re, spread_im = (spread_ref[position, part, pl.ds(at, tall), :].astype(f32) for part in range(2))
            parts = (
                wave_re * spread_re + wave_im * spread_im,
                wave_re * spread_im - wave_im * spread_re,
            )
            for part in range(2):
                left = jnp.where(in_left, parts[part], 0.0)
                right = jnp.where(in_left, 0.0, parts[part])
                for side, value in enumerate((left, right)):
                    sums[4 * part + side] += jnp.where(in_mine, value, 0.0)
                    sums[4 * part + 2 + side] += jnp.where(in_mine, 0.0, value)
        for part in range(2):
            for side in range(2):
                cols = pl.ds(side * window, window)
                own_ref[part, pl.ds(at, tall), cols] = sums[4 * part + side]
                away_ref[part, pl.ds(at, tall), cols] = sums[4 * part + 2 + side].astype(bf16)
        return 0

    lax.fori_loop(0, rows // tall, one, 0)


def finish_kernel(*refs):
    out_ref = refs[-1]
    rows = refs[0].shape[1]
    for chunk in range(chunk_count):
        own_ref, come_ref = refs[2 * chunk : 2 * chunk + 2]
        out_ref[:, pl.ds(chunk * rows, rows), :] = own_ref[...] + come_ref[...].astype(f32)


def shape_of(dims, dtype):
    return jax.ShapeDtypeStruct(dims, dtype)


def on_device(obj_amp, obj_phase, forward_waves, exit_adjoint, offsets):
    sections = lax.axis_size("sec")
    section = lax.axis_index("sec")
    place = lax.axis_index("scan").astype(jnp.int32).reshape(1)
    count, _, window, _ = exit_adjoint.shape
    _, half, width = obj_amp.shape
    swap = [(0, 1), (1, 0)]
    groups = [[first + i for i in range(count)] for first in range(0, sections, count)]
    group_count = sections // count
    rows = half // chunk_count
    chunks = range(chunk_count)
    piece = (2, rows, width)
    part = (count, 2, rows, window)
    wave = (2, window, window)
    flops = 8 * 2 * window**3

    def all_to_all(value):
        return lax.all_to_all(value, "sec", 0, 0, axis_index_groups=groups, tiled=True)

    own = section % count
    pick = jnp.stack([own, jnp.int32(1)])
    mine = call(code_kernel, [shape_of(piece, bf16)] * chunk_count)(obj_amp[0], obj_phase[0])
    other = [lax.ppermute(mine[c], "scan", swap) for c in chunks]
    windows = []
    for c in chunks:
        cut = call(functools.partial(cut_kernel, c * rows), shape_of(part, bf16), prefetch=2)
        windows.append(all_to_all(cut(offsets, place, mine[c], other[c])))
    ready = call(ready_kernel, [shape_of(wave, bf16)] + [shape_of((window, window), bf16)] * 2, prefetch=2)
    start, down, across = ready(offsets, pick, exit_adjoint)
    waves = call(turn_kernel, shape_of(forward_waves.shape[1:], bf16), prefetch=1)(offsets, forward_waves[0])

    at_end = (section >= sections - count).astype(jnp.int32)
    come = start
    through = call(
        group_kernel,
        [shape_of(part, bf16)] * chunk_count + [shape_of(wave, bf16)],
        prefetch=1,
        flops=count * flops,
    )
    for stage in range(group_count):
        *spreads, leave = through(pick, start, come, down, across, *windows)
        if stage < group_count - 1:
            come = lax.ppermute(leave, "sec", [(s, s - count) for s in range(count, sections)])
            pick = jnp.stack([own, at_end])

    spreads = [all_to_all(spreads[c]) for c in chunks]
    sums = []
    for c in chunks:
        gradient = call(
            functools.partial(gradient_kernel, c * rows), [shape_of(piece, f32), shape_of(piece, bf16)], prefetch=2
        )
        keep, away = gradient(offsets, place, waves, spreads[c])
        sums += [keep, lax.ppermute(away, "scan", swap)]
    return call(finish_kernel, shape_of((2, half, width), f32))(*sums)[None]


def solution(mesh):
    in_specs = (
        P("sec", "scan", None),
        P("sec", "scan", None),
        P("sec", "scan", None, None, None),
        P("scan", None, None, None),
        P("scan", None),
    )
    out_specs = P("sec", None, "scan", None)
    return jax.shard_map(
        on_device, mesh=mesh, in_specs=in_specs, out_specs=out_specs, check_vma=False
    )
```

time: 583 us -> 132 us (0.23)
  waiting for transfers between devices: 210 us -> 55 us
  loops' own time: 119 us -> 0 us
  other arithmetic: 118 us -> 0.15 us
  local copies, waits for them, and re-layouts: 88.9 us -> 7.8 us
  Pallas kernels: 0 us -> 29.5 us
  blocking collectives: 0 us -> 17.7 us
  between operations: 13.2 us -> 0.11 us
  starting transfers between devices: 29.8 us -> 20.8 us
    another operation x2 -> x0, loops' own time: 119 us -> none  [the longest x1 88.1 us: on_device(): lax.fori_loop(0, tick_count, one_tick, (start_wave, start_store))]
    ppermute x23 -> x5, waiting for transfers between devices: 111 us -> 33.9 us  [the longest x1 14.9 us: on_device(): lax.ppermute(leave, 'sec', [(s, s - count) for s in range(count, sections)])]
    dynamic_update_slice x8 -> x0, local copies, waits for them, and re-layouts: 63.2 us -> none  [add_position(): lax.dynamic_update_slice(gradient, added, (zero_index, row_at, col_at))]
    reduce_scatter x1 -> x0, waiting for transfers between devices: 49.8 us -> none  [on_device(): lax.psum_scatter(gradient, 'scan', scatter_dimension=1, tiled=True)]
    all_gather x2 -> x0, waiting for transfers between devices: 47.8 us -> none  [the longest x1 24.9 us: on_device(): lax.all_gather(obj_amp, 'scan', axis=1, tiled=True)]
    dynamic_update_slice x23 -> x0, other arithmetic: 44 us -> none  [one_tick(): stored = lax.dynamic_update_index_in_dim(stored, kept, slot, 0)]
    convert_element_type x31 -> x0, other arithmetic: 30.9 us -> none  [the longest x23 22.9 us: one_tick(): jnp.where(segment_no == sections - 1, own_exit, arriving)]
    pallas_call x0 -> x10, Pallas kernels: none -> 29.5 us  [run(): pl.pallas_call(kernel, grid_spec=pltpu.PrefetchScalarGridSpec(num_scalar_...]
  transfers between devices with their start and end apart: 26 -> 8, of which waited for: 26 -> 7; matrix products, arithmetic and copies ran while one was open for 8% -> 1% of each run, Pallas kernels for 0% -> 8%
where the time goes in v2:
time: 132 us; the launch traced here: 131 us
  waiting for transfers between devices  55 us (42%)
  Pallas kernels  29.5 us (22%)
  starting transfers between devices  20.8 us (16%)
  blocking collectives  17.7 us (13%)
  local copies, waits for them, and re-layouts  7.8 us (6%)
    pallas_call x10, Pallas kernels, run(): pl.pallas_call(kernel, grid_spec=pltpu.PrefetchScalarGridSpec(num_scalar_...  29.5 us
    all_to_all x3, waiting for transfers between devices, all_to_all(): lax.all_to_all(value, 'sec', 0, 0, axis_index_groups=groups, tiled=True)  21.1 us
    all_to_all x1, blocking collectives, all_to_all(): lax.all_to_all(value, 'sec', 0, 0, axis_index_groups=groups, tiled=True)  17.7 us
    ppermute x1, waiting for transfers between devices, on_device(): lax.ppermute(leave, 'sec', [(s, s - count) for s in range(count, sections)])  14.9 us
    ppermute x2, waiting for transfers between devices, on_device(): other = [lax.ppermute(mine[c], 'scan', swap) for c in chunks]  12.7 us
    all_to_all x3, starting transfers between devices, all_to_all(): lax.all_to_all(value, 'sec', 0, 0, axis_index_groups=groups, tiled=True)  11.9 us
    unnamed x25, local copies, waits for them, and re-layouts  7.8 us
    ppermute x2, waiting for transfers between devices, on_device(): sums += [keep, lax.ppermute(away, 'scan', swap)]  6.36 us
  transfers between devices with their start and end apart: 8, of which 7 were waited for; matrix products, arithmetic and copies ran while one was open for 1% of the time, Pallas kernels for 8%

profile of v2, /device:TPU:0, one launch (start us, length us, event | category | flops | bytes accessed | tf_op | source)
XLA Modules:
  0.0 131.1 jit_solution(14277563020999412578)
XLA Ops:
  0.0 1.0 copy-done.5
  1.0 1.0 copy-done.6
  2.8 3.0 %collective-permute-start = (bf16[2,128,512]{2,1,0:T(8,128)(2,1)S(1)}, bf16[2,128,512]{2,1,0:T(8,128)(2,1)S(1)}, u32[]{:S(2)}, u32[]{:S(2)}) collective-permute-start(bf16[2,128,512]{2,1,0:T(8,128)(2,1)S(1)} %get-tuple-element.20.mine_ref), channel_id=1, source_target_pairs={{0,1},{1,0},{2,3},{3,2},{4,5},{5,4},{6,7},{7,6},{8,9},{9,8},{10,11... | collective-permute-start | bytes 786440 | tf_op jit(solution)/shard_map/ppermute | solution.py:232
  5.8 0.8 copy.10.corner_ref
  6.6 5.6 %collective-permute-done.other_ref = bf16[2,128,512]{2,1,0:T(8,128)(2,1)S(1)} collective-permute-done((bf16[2,128,512]{2,1,0:T(8,128)(2,1)S(1)}, bf16[2,128,512]{2,1,0:T(8,128)(2,1)S(1)}, u32[]{:S(2)}, u32[]{:S(2)}) %collective-permute-start) | collective-permute-done | bytes 262176 | tf_op jit(solution)/shard_map/ppermute | solution.py:232
  12.1 2.2 %shard_map.58 = bf16[8,2,128,256]{3,2,1,0:T(8,128)(2,1)} custom-call(s32[8,2]{1,0:T(8,128)S(1)} %copy.10.corner_ref, s32[1]{0:T(128)} %bitcast.place_ref, bf16[2,128,512]{2,1,0:T(8,128)(2,1)S(1)} %get-tuple-element.20.mine_ref, bf16[2,128,512]{2,1,0:T(8,128)(2,1)S(1)} %collective-permute-done.other_ref), custom_call_target="tpu_custom_call" | custom-call | bytes 1572932 | tf_op jit(solution)/shard_map/pallas_call | solution.py:24
  14.3 4.1 %all-to-all-start = ((bf16[8,2,128,256]{3,2,1,0:T(8,128)(2,1)}), bf16[8,2,128,256]{3,2,1,0:T(8,128)(2,1)S(1)}, u32[]{:S(2)}, u32[]{:S(2)}) async-start(bf16[8,2,128,256]{3,2,1,0:T(8,128)(2,1)} %shard_map.58), calls=%async_computation | async-start | bytes 2097152 | tf_op jit(solution)/shard_map/all_to_all | solution.py:227
  18.4 1.6 %collective-permute-start.1 = (bf16[2,128,512]{2,1,0:T(8,128)(2,1)S(1)}, bf16[2,128,512]{2,1,0:T(8,128)(2,1)S(1)}, u32[]{:S(2)}, u32[]{:S(2)}) collective-permute-start(bf16[2,128,512]{2,1,0:T(8,128)(2,1)S(1)} %get-tuple-element.21.mine_ref), channel_id=1, source_target_pairs={{0,1},{1,0},{2,3},{3,2},{4,5},{5,4},{6,7},{7,6},{8,9},{9,8},{10,11... | collective-permute-start | bytes 786440 | tf_op jit(solution)/shard_map/ppermute | solution.py:232
  19.9 7.2 %collective-permute-done.1.other_ref = bf16[2,128,512]{2,1,0:T(8,128)(2,1)S(1)} collective-permute-done((bf16[2,128,512]{2,1,0:T(8,128)(2,1)S(1)}, bf16[2,128,512]{2,1,0:T(8,128)(2,1)S(1)}, u32[]{:S(2)}, u32[]{:S(2)}) %collective-permute-start.1) | collective-permute-done | bytes 262176 | tf_op jit(solution)/shard_map/ppermute | solution.py:232
  27.1 2.2 %shard_map.59 = bf16[8,2,128,256]{3,2,1,0:T(8,128)(2,1)} custom-call(s32[8,2]{1,0:T(8,128)S(1)} %copy.10.corner_ref, s32[1]{0:T(128)} %bitcast.place_ref, bf16[2,128,512]{2,1,0:T(8,128)(2,1)S(1)} %get-tuple-element.21.mine_ref, bf16[2,128,512]{2,1,0:T(8,128)(2,1)S(1)} %collective-permute-done.1.other_ref), custom_call_target="tpu_custom_call" | custom-call | bytes 1572932 | tf_op jit(solution)/shard_map/pallas_call | solution.py:24
  29.3 3.5 %all-to-all-done.refs_0_ = bf16[8,2,128,256]{3,2,1,0:T(8,128)(2,1)S(1)} async-done(((bf16[8,2,128,256]{3,2,1,0:T(8,128)(2,1)}), bf16[8,2,128,256]{3,2,1,0:T(8,128)(2,1)S(1)}, u32[]{:S(2)}, u32[]{:S(2)}) %all-to-all-start) | async-done | bytes 1048608 | tf_op jit(solution)/shard_map/all_to_all | solution.py:227
  32.8 4.3 %all-to-all-start.1 = ((bf16[8,2,128,256]{3,2,1,0:T(8,128)(2,1)}), bf16[8,2,128,256]{3,2,1,0:T(8,128)(2,1)}, u32[]{:S(2)}, u32[]{:S(2)}) async-start(bf16[8,2,128,256]{3,2,1,0:T(8,128)(2,1)} %shard_map.59), calls=%async_computation.1 | async-start | bytes 2097152 | tf_op jit(solution)/shard_map/all_to_all | solution.py:227
  37.2 1.2 shard_map.56
  39.1 12.4 %all-to-all-done.1.refs_1_ = bf16[8,2,128,256]{3,2,1,0:T(8,128)(2,1)} async-done(((bf16[8,2,128,256]{3,2,1,0:T(8,128)(2,1)}), bf16[8,2,128,256]{3,2,1,0:T(8,128)(2,1)}, u32[]{:S(2)}, u32[]{:S(2)}) %all-to-all-start.1) | async-done | bytes 1048608 | tf_op jit(solution)/shard_map/all_to_all | solution.py:227
  51.6 0.9 copy-done.8
  52.5 7.5 %shard_map.60 = (bf16[8,2,128,256]{3,2,1,0:T(8,128)(2,1)}, bf16[8,2,128,256]{3,2,1,0:T(8,128)(2,1)}, bf16[2,256,256]{2,1,0:T(8,128)(2,1)S(1)}) custom-call(s32[2]{0:T(128)S(1)} %pad_add_fusion.1.pick_ref, bf16[2,256,256]{2,1,0:T(8,128)(2,1)S(1)} %copy-done.8, bf16[2,256,256]{2,1,0:T(8,128)(2,1)S(1)} %copy-done.8, ...), custom_call_target="tpu_custom_call" | custom-call | flops 2147483648 | bytes 5242888 | tf_op jit(solution)/shard_map/pallas_call | solution.py:24
  60.0 1.3 collective-permute-start.2
  61.3 14.9 %collective-permute-done.2.come_ref = bf16[2,256,256]{2,1,0:T(8,128)(2,1)S(1)} collective-permute-done((bf16[2,256,256]{2,1,0:T(8,128)(2,1)S(1)}, bf16[2,256,256]{2,1,0:T(8,128)(2,1)S(1)}, u32[]{:S(2)}, u32[]{:S(2)}) %collective-permute-start.2) | collective-permute-done | bytes 262176 | tf_op jit(solution)/shard_map/ppermute | solution.py:252
  76.2 0.9 copy-done.11
  77.1 7.2 %shard_map.61 = (bf16[8,2,128,256]{3,2,1,0:T(8,128)(2,1)}, bf16[8,2,128,256]{3,2,1,0:T(8,128)(2,1)S(1)}, bf16[2,256,256]{2,1,0:T(8,128)(2,1)}) custom-call(s32[2]{0:T(128)S(1)} %pad_add_fusion.pick_ref, bf16[2,256,256]{2,1,0:T(8,128)(2,1)S(1)} %copy-done.9, bf16[2,256,256]{2,1,0:T(8,128)(2,1)S(1)} %collective-permute-done.2.come_ref, ...), custom_call_target="tpu_custom_call" | custom-call | flops 2147483648 | bytes 5242888 | tf_op jit(solution)/shard_map/pallas_call | solution.py:24
  84.3 17.7 %all_to_all.20.spread_ref = bf16[8,2,128,256]{3,2,1,0:T(8,128)(2,1)} all-to-all(bf16[8,2,128,256]{3,2,1,0:T(8,128)(2,1)S(1)} %get-tuple-element.26), channel_id=1, replica_groups={{0,2,4,6,8,10,12,14},{16,18,20,22,24,26,28,30},{1,3,5,7,9,11,13,15},{17..., dimensions={0} | all-to-all | bytes 2097152 | tf_op jit(solution)/shard_map/all_to_all | solution.py:227
  102.0 3.6 %all-to-all-start.2 = ((bf16[8,2,128,256]{3,2,1,0:T(8,128)(2,1)}), bf16[8,2,128,256]{3,2,1,0:T(8,128)(2,1)S(1)}, u32[]{:S(2)}, u32[]{:S(2)}) async-start(bf16[8,2,128,256]{3,2,1,0:T(8,128)(2,1)} %get-tuple-element.23), calls=%async_computation.2 | async-start | bytes 2097152 | tf_op jit(solution)/shard_map/all_to_all | solution.py:227
  105.6 1.6 %copy-done.1 = bf16[1,8,2,256,256]{4,3,2,1,0:T(8,128)(2,1)S(1)} copy-done((bf16[1,8,2,256,256]{4,3,2,1,0:T(8,128)(2,1)S(1)}, bf16[1,8,2,256,256]{4,3,2,1,0:T(8,128)(2,1)}, u32[]{:S(2)}) %copy-start.1) | copy-done | bytes 2097176
  107.2 2.5 %shard_map.55.wave_ref = bf16[8,2,256,256]{3,2,1,0:T(8,128)(2,1)S(1)} custom-call(s32[8,2]{1,0:T(8,128)S(1)} %copy.10.corner_ref, bf16[8,2,256,256]{3,2,1,0:T(8,128)(2,1)S(1)} %bitcast.7), custom_call_target="tpu_custom_call" | custom-call | bytes 4194368 | tf_op jit(solution)/shard_map/pallas_call | solution.py:24
  109.7 2.8 %shard_map.63 = (f32[2,128,512]{2,1,0:T(8,128)S(1)}, bf16[2,128,512]{2,1,0:T(8,128)(2,1)}) custom-call(s32[8,2]{1,0:T(8,128)S(1)} %copy.10.corner_ref, s32[1]{0:T(128)} %bitcast.place_ref, bf16[8,2,256,256]{3,2,1,0:T(8,128)(2,1)S(1)} %shard_map.55.wave_ref, bf16[8,2,128,256]{3,2,1,0:T(8,128)(2,1)S(1)} %copy-done), custom_call_target="tpu_custom_call" | custom-call | bytes 3932228 | tf_op jit(solution)/shard_map/pallas_call | solution.py:24
  112.5 0.8 copy-done.3
  113.3 1.5 %collective-permute-start.4 = (bf16[2,128,512]{2,1,0:T(8,128)(2,1)}, bf16[2,128,512]{2,1,0:T(8,128)(2,1)S(1)}, u32[]{:S(2)}, u32[]{:S(2)}) collective-permute-start(bf16[2,128,512]{2,1,0:T(8,128)(2,1)} %get-tuple-element.28), channel_id=1, source_target_pairs={{0,1},{1,0},{2,3},{3,2},{4,5},{5,4},{6,7},{7,6},{8,9},{9,8},{10,11... | collective-permute-start | bytes 786440 | tf_op jit(solution)/shard_map/ppermute | solution.py:262
  114.8 5.1 %all-to-all-done.2.spread_ref = bf16[8,2,128,256]{3,2,1,0:T(8,128)(2,1)S(1)} async-done(((bf16[8,2,128,256]{3,2,1,0:T(8,128)(2,1)}), bf16[8,2,128,256]{3,2,1,0:T(8,128)(2,1)S(1)}, u32[]{:S(2)}, u32[]{:S(2)}) %all-to-all-start.2) | async-done | bytes 1048608 | tf_op jit(solution)/shard_map/all_to_all | solution.py:227
  120.0 2.1 %shard_map.62 = (f32[2,128,512]{2,1,0:T(8,128)S(1)}, bf16[2,128,512]{2,1,0:T(8,128)(2,1)S(1)}) custom-call(s32[8,2]{1,0:T(8,128)S(1)} %copy.10.corner_ref, s32[1]{0:T(128)} %bitcast.place_ref, bf16[8,2,256,256]{3,2,1,0:T(8,128)(2,1)S(1)} %shard_map.55.wave_ref, bf16[8,2,128,256]{3,2,1,0:T(8,128)(2,1)S(1)} %all-to-all-done.2.spread_ref), custom_call_target="tpu_custom_call" | custom-call | bytes 3932228 | tf_op jit(solution)/shard_map/pallas_call | solution.py:24
  122.1 1.6 %collective-permute-start.3 = (bf16[2,128,512]{2,1,0:T(8,128)(2,1)S(1)}, bf16[2,128,512]{2,1,0:T(8,128)(2,1)S(1)}, u32[]{:S(2)}, u32[]{:S(2)}) collective-permute-start(bf16[2,128,512]{2,1,0:T(8,128)(2,1)S(1)} %get-tuple-element.25), channel_id=1, source_target_pairs={{0,1},{1,0},{2,3},{3,2},{4,5},{5,4},{6,7},{7,6},{8,9},{9,8},{10,11... | collective-permute-start | bytes 786440 | tf_op jit(solution)/shard_map/ppermute | solution.py:262
  123.6 6.4 %collective-permute-done.3.refs_1_ = bf16[2,128,512]{2,1,0:T(8,128)(2,1)S(1)} collective-permute-done((bf16[2,128,512]{2,1,0:T(8,128)(2,1)S(1)}, bf16[2,128,512]{2,1,0:T(8,128)(2,1)S(1)}, u32[]{:S(2)}, u32[]{:S(2)}) %collective-permute-start.3) | collective-permute-done | bytes 262176 | tf_op jit(solution)/shard_map/ppermute | solution.py:262
  130.0 1.1 shard_map.64
  (22 shorter events, 1.6 us)
Async XLA Ops:
  0.0 1.0 copy-start.5
  1.0 1.0 copy-start.6
  2.8 9.3 %collective-permute-start = (bf16[2,128,512]{2,1,0:T(8,128)(2,1)S(1)}, bf16[2,128,512]{2,1,0:T(8,128)(2,1)S(1)}, u32[]{:S(2)}, u32[]{:S(2)}) collective-permute-start(bf16[2,128,512]{2,1,0:T(8,128)(2,1)S(1)} %get-tuple-element.20.mine_ref), channel_id=1, source_target_pairs={{0,1},{1,0},{2,3},{3,2},{4,5},{5,4},{6,7},{7,6},{8,9},{9,8},{10,11... | collective-permute-start | bytes 786440 | tf_op jit(solution)/shard_map/ppermute | solution.py:232
  14.3 18.5 %all-to-all-start = ((bf16[8,2,128,256]{3,2,1,0:T(8,128)(2,1)}), bf16[8,2,128,256]{3,2,1,0:T(8,128)(2,1)S(1)}, u32[]{:S(2)}, u32[]{:S(2)}) async-start(bf16[8,2,128,256]{3,2,1,0:T(8,128)(2,1)} %shard_map.58), calls=%async_computation | async-start | bytes 2097152 | tf_op jit(solution)/shard_map/all_to_all | solution.py:227
  18.4 18.8 %copy-start.2 = (bf16[8,2,256,256]{3,2,1,0:T(8,128)(2,1)S(1)}, bf16[8,2,256,256]{3,2,1,0:T(8,128)(2,1)}, u32[]{:S(2)}) copy-start(bf16[8,2,256,256]{3,2,1,0:T(8,128)(2,1)} %exit_ref.1) | copy-start | bytes 6291460
  18.4 8.7 %collective-permute-start.1 = (bf16[2,128,512]{2,1,0:T(8,128)(2,1)S(1)}, bf16[2,128,512]{2,1,0:T(8,128)(2,1)S(1)}, u32[]{:S(2)}, u32[]{:S(2)}) collective-permute-start(bf16[2,128,512]{2,1,0:T(8,128)(2,1)S(1)} %get-tuple-element.21.mine_ref), channel_id=1, source_target_pairs={{0,1},{1,0},{2,3},{3,2},{4,5},{5,4},{6,7},{7,6},{8,9},{9,8},{10,11... | collective-permute-start | bytes 786440 | tf_op jit(solution)/shard_map/ppermute | solution.py:232
  32.8 18.7 %all-to-all-start.1 = ((bf16[8,2,128,256]{3,2,1,0:T(8,128)(2,1)}), bf16[8,2,128,256]{3,2,1,0:T(8,128)(2,1)}, u32[]{:S(2)}, u32[]{:S(2)}) async-start(bf16[8,2,128,256]{3,2,1,0:T(8,128)(2,1)} %shard_map.59), calls=%async_computation.1 | async-start | bytes 2097152 | tf_op jit(solution)/shard_map/all_to_all | solution.py:227
  38.4 0.7 copy-start.7
  39.1 20.8 %copy-start.10 = (bf16[256,256]{1,0:T(8,128)(2,1)}, bf16[256,256]{1,0:T(8,128)(2,1)S(1)}, u32[]{:S(2)}) copy-start(bf16[256,256]{1,0:T(8,128)(2,1)S(1)} %get-tuple-element.19.across_ref) | copy-start | bytes 393220
  51.6 1.0 copy-start.8
  52.5 23.7 %copy-start.9 = (bf16[2,256,256]{2,1,0:T(8,128)(2,1)S(1)}, bf16[2,256,256]{2,1,0:T(8,128)(2,1)}, u32[]{:S(2)}) copy-start(bf16[2,256,256]{2,1,0:T(8,128)(2,1)} %copy-done.7) | copy-start | bytes 786436
  60.0 16.2 %collective-permute-start.2 = (bf16[2,256,256]{2,1,0:T(8,128)(2,1)S(1)}, bf16[2,256,256]{2,1,0:T(8,128)(2,1)S(1)}, u32[]{:S(2)}, u32[]{:S(2)}) collective-permute-start(bf16[2,256,256]{2,1,0:T(8,128)(2,1)S(1)} %get-tuple-element.22), channel_id=1, source_target_pairs={{16,0},{18,2},{20,4},{22,6},{24,8},{26,10},{28,12},{30,14},{17,1},... | collective-permute-start | bytes 786440 | tf_op jit(solution)/shard_map/ppermute | solution.py:252
  76.2 0.9 copy-start.11
  102.0 17.9 %all-to-all-start.2 = ((bf16[8,2,128,256]{3,2,1,0:T(8,128)(2,1)}), bf16[8,2,128,256]{3,2,1,0:T(8,128)(2,1)S(1)}, u32[]{:S(2)}, u32[]{:S(2)}) async-start(bf16[8,2,128,256]{3,2,1,0:T(8,128)(2,1)} %get-tuple-element.23), calls=%async_computation.2 | async-start | bytes 2097152 | tf_op jit(solution)/shard_map/all_to_all | solution.py:227
  105.6 1.6 %copy-start.1 = (bf16[1,8,2,256,256]{4,3,2,1,0:T(8,128)(2,1)S(1)}, bf16[1,8,2,256,256]{4,3,2,1,0:T(8,128)(2,1)}, u32[]{:S(2)}) copy-start(bf16[1,8,2,256,256]{4,3,2,1,0:T(8,128)(2,1)} %param.7) | copy-start | bytes 6291460
  107.2 2.5 %copy-start = (bf16[8,2,128,256]{3,2,1,0:T(8,128)(2,1)S(1)}, bf16[8,2,128,256]{3,2,1,0:T(8,128)(2,1)}, u32[]{:S(2)}) copy-start(bf16[8,2,128,256]{3,2,1,0:T(8,128)(2,1)} %all_to_all.20.spread_ref) | copy-start | bytes 3145732
  112.5 0.8 copy-start.3
  113.3 10.3 %collective-permute-start.4 = (bf16[2,128,512]{2,1,0:T(8,128)(2,1)}, bf16[2,128,512]{2,1,0:T(8,128)(2,1)S(1)}, u32[]{:S(2)}, u32[]{:S(2)}) collective-permute-start(bf16[2,128,512]{2,1,0:T(8,128)(2,1)} %get-tuple-element.28), channel_id=1, source_target_pairs={{0,1},{1,0},{2,3},{3,2},{4,5},{5,4},{6,7},{7,6},{8,9},{9,8},{10,11... | collective-permute-start | bytes 786440 | tf_op jit(solution)/shard_map/ppermute | solution.py:262
  120.0 10.0 %copy-start.4 = (f32[2,128,512]{2,1,0:T(8,128)S(1)}, f32[2,128,512]{2,1,0:T(8,128)}, u32[]{:S(2)}) copy-start(f32[2,128,512]{2,1,0:T(8,128)} %copy-done.3) | copy-start | bytes 1572868
  122.1 7.9 %collective-permute-start.3 = (bf16[2,128,512]{2,1,0:T(8,128)(2,1)S(1)}, bf16[2,128,512]{2,1,0:T(8,128)(2,1)S(1)}, u32[]{:S(2)}, u32[]{:S(2)}) collective-permute-start(bf16[2,128,512]{2,1,0:T(8,128)(2,1)S(1)} %get-tuple-element.25), channel_id=1, source_target_pairs={{0,1},{1,0},{2,3},{3,2},{4,5},{5,4},{6,7},{7,6},{8,9},{9,8},{10,11... | collective-permute-start | bytes 786440 | tf_op jit(solution)/shard_map/ppermute | solution.py:262

commit v3 on v2

--- a/solution.py
+++ b/solution.py
@@ -62,19 +62,15 @@
     return at_first != place, col >= corner_ref[position, 1]
 
 
-def cut_kernel(base, corner_ref, place_ref, mine_ref, other_ref, win_ref):
-    count, _, rows, window = win_ref.shape
+def cut_kernel(base, corner_ref, place_ref, pick_ref, mine_ref, other_ref, *win_refs):
+    _, rows, window = win_refs[0].shape
     place = place_ref[0]
-
-    def one(position, _):
-        in_mine, in_left = first_masks(corner_ref, position, place, base, (rows, window))
+    for apart, win_ref in enumerate(win_refs):
+        in_mine, in_left = first_masks(corner_ref, pick_ref[0] ^ apart, place, base, (rows, window))
         for part in range(2):
             left = jnp.where(in_mine, mine_ref[part, :, :window].astype(f32), other_ref[part, :, :window].astype(f32))
             right = jnp.where(in_mine, mine_ref[part, :, window:].astype(f32), other_ref[part, :, window:].astype(f32))
-            win_ref[position, part] = jnp.where(in_left, left, right).astype(bf16)
-        return 0
-
-    lax.fori_loop(0, count, one, 0)
+            win_ref[part] = jnp.where(in_left, left, right).astype(bf16)
 
 
 def turned(wave, row_at, col_at):
@@ -135,10 +131,15 @@
 
 
 def group_kernel(pick_ref, start_ref, come_ref, down_ref, across_ref, *refs):
-    win_refs = refs[:chunk_count]
-    spread_refs = refs[chunk_count : 2 * chunk_count]
-    leave_ref = refs[2 * chunk_count]
-    count, _, rows, _ = win_refs[0].shape
+    win_refs, refs = refs[: len(refs) // 2 - 1], refs[len(refs) // 2 - 1 :]
+    *spread_refs, leave_ref, held_ref, kept_ref = refs
+    count, _, window, _ = held_ref.shape
+    rows = window // chunk_count
+    own = pick_ref[0]
+    for apart in range(count):
+        for chunk in range(chunk_count):
+            here = slice(chunk * rows, (chunk + 1) * rows)
+            held_ref[own ^ apart, :, here] = win_refs[apart * chunk_count + chunk][...]
     down = down_ref[...]
     across = across_ref[...]
     at_end = jnp.full(start_ref.shape[1:], pick_ref[1], jnp.int32) == 1
@@ -147,34 +148,35 @@
     )
     for layer in range(count - 1, -1, -1):
         spread_re, spread_im = back(down, across, chi_re, chi_im)
-        out_re, out_im = [], []
+        kept_ref[layer, 0] = spread_re.astype(bf16)
+        kept_ref[layer, 1] = spread_im.astype(bf16)
+        win_re = jnp.log(held_ref[layer, 0].astype(f32)) * (1.0 / code_gain)
+        win_im = jnp.log(held_ref[layer, 1].astype(f32)) * (1.0 / code_gain)
+        chi_re = (win_re * spread_re + win_im * spread_im).astype(bf16)
+        chi_im = (win_re * spread_im - win_im * spread_re).astype(bf16)
+    leave_ref[0] = chi_re
+    leave_ref[1] = chi_im
+    for apart in range(count):
         for chunk in range(chunk_count):
             here = slice(chunk * rows, (chunk + 1) * rows)
-            part_re, part_im = spread_re[here], spread_im[here]
-            spread_refs[chunk][layer, 0] = part_re.astype(bf16)
-            spread_refs[chunk][layer, 1] = part_im.astype(bf16)
-            win_re = jnp.log(win_refs[chunk][layer, 0].astype(f32)) * (1.0 / code_gain)
-            win_im = jnp.log(win_refs[chunk][layer, 1].astype(f32)) * (1.0 / code_gain)
-            out_re.append((win_re * part_re + win_im * part_im).astype(bf16))
-            out_im.append((win_re * part_im - win_im * part_re).astype(bf16))
-        chi_re = jnp.concatenate(out_re, axis=0)
-        chi_im = jnp.concatenate(out_im, axis=0)
-    leave_ref[0] = chi_re
-    leave_ref[1] = chi_im
-
-
-def gradient_kernel(base, corner_ref, place_ref, wave_ref, spread_ref, own_ref, away_ref):
-    count, _, rows, window = spread_ref.shape
+            spread_refs[apart * chunk_count + chunk][...] = kept_ref[own ^ apart, :, here]
+
+
+def gradient_kernel(base, corner_ref, place_ref, pick_ref, wave_ref, *refs):
+    *spread_refs, own_ref, away_ref = refs
+    _, rows, window = spread_refs[0].shape
     tall = 16
     place = place_ref[0]
+    own = pick_ref[0]
 
     def one(block, _):
         at = pl.multiple_of(block * tall, tall)
         sums = [jnp.zeros((tall, window), f32) for _ in range(8)]
-        for position in range(count):
+        for apart, spread_ref in enumerate(spread_refs):
+            position = own ^ apart
             in_mine, in_left = first_masks(corner_ref, position, place, base + at, (tall, window))
             wave_re, wave_im = (wave_ref[position, part, pl.ds(base + at, tall), :].astype(f32) for part in range(2))
-            spread_re, spread_im = (spread_ref[position, part, pl.ds(at, tall), :].astype(f32) for part in range(2))
+            spread_re, spread_im = (spread_ref[part, pl.ds(at, tall), :].astype(f32) for part in range(2))
             parts = (
                 wave_re * spread_re + wave_im * spread_im,
                 wave_re * spread_im - wave_im * spread_re,
@@ -214,17 +216,20 @@
     count, _, window, _ = exit_adjoint.shape
     _, half, width = obj_amp.shape
     swap = [(0, 1), (1, 0)]
-    groups = [[first + i for i in range(count)] for first in range(0, sections, count)]
     group_count = sections // count
     rows = half // chunk_count
     chunks = range(chunk_count)
     piece = (2, rows, width)
-    part = (count, 2, rows, window)
+    part = (2, rows, window)
     wave = (2, window, window)
     flops = 8 * 2 * window**3
 
-    def all_to_all(value):
-        return lax.all_to_all(value, "sec", 0, 0, axis_index_groups=groups, tiled=True)
+    def exchange(values):
+        order = sorted(range(1, count), key=lambda apart: (apart == 1, apart % 2, apart))
+        got = list(values)
+        for apart in order:
+            got[apart] = lax.ppermute(values[apart], "sec", [(s, s ^ apart) for s in range(sections)])
+        return got
 
     own = section % count
     pick = jnp.stack([own, jnp.int32(1)])
@@ -232,8 +237,8 @@
     other = [lax.ppermute(mine[c], "scan", swap) for c in chunks]
     windows = []
     for c in chunks:
-        cut = call(functools.partial(cut_kernel, c * rows), shape_of(part, bf16), prefetch=2)
-        windows.append(all_to_all(cut(offsets, place, mine[c], other[c])))
+        cut = call(functools.partial(cut_kernel, c * rows), [shape_of(part, bf16)] * count, prefetch=3)
+        windows.append(exchange(cut(offsets, place, pick, mine[c], other[c])))
     ready = call(ready_kernel, [shape_of(wave, bf16)] + [shape_of((window, window), bf16)] * 2, prefetch=2)
     start, down, across = ready(offsets, pick, exit_adjoint)
     waves = call(turn_kernel, shape_of(forward_waves.shape[1:], bf16), prefetch=1)(offsets, forward_waves[0])
@@ -242,23 +247,25 @@
     come = start
     through = call(
         group_kernel,
-        [shape_of(part, bf16)] * chunk_count + [shape_of(wave, bf16)],
+        [shape_of(part, bf16)] * (chunk_count * count) + [shape_of(wave, bf16)],
         prefetch=1,
+        scratch=[pltpu.VMEM((count,) + wave, bf16)] * 2,
         flops=count * flops,
     )
+    stage_windows = [windows[c][apart] for apart in range(count) for c in chunks]
     for stage in range(group_count):
-        *spreads, leave = through(pick, start, come, down, across, *windows)
+        *spreads, leave = through(pick, start, come, down, across, *stage_windows)
         if stage < group_count - 1:
             come = lax.ppermute(leave, "sec", [(s, s - count) for s in range(count, sections)])
             pick = jnp.stack([own, at_end])
 
-    spreads = [all_to_all(spreads[c]) for c in chunks]
+    spreads = [exchange(spreads[c::chunk_count]) for c in chunks]
     sums = []
     for c in chunks:
         gradient = call(
-            functools.partial(gradient_kernel, c * rows), [shape_of(piece, f32), shape_of(piece, bf16)], prefetch=2
+            functools.partial(gradient_kernel, c * rows), [shape_of(piece, f32), shape_of(piece, bf16)], prefetch=3
         )
-        keep, away = gradient(offsets, place, waves, spreads[c])
+        keep, away = gradient(offsets, place, pick, waves, *spreads[c])
         sums += [keep, lax.ppermute(away, "scan", swap)]
     return call(finish_kernel, shape_of((2, half, width), f32))(*sums)[None]
 

time: 132 us -> 130 us (0.985)
  blocking collectives: 17.7 us -> 0 us
  starting transfers between devices: 20.8 us -> 28.7 us
  local copies, waits for them, and re-layouts: 7.8 us -> 14.8 us
  waiting for transfers between devices: 55 us -> 60.9 us
  Pallas kernels: 29.5 us -> 24.5 us
    ppermute x0 -> x28, waiting for transfers between devices: none -> 28.3 us  [exchange(): lax.ppermute(values[apart], 'sec', [(s, s ^ apart) for s in range(section...]
    all_to_all x3 -> x0, waiting for transfers between devices: 21.1 us -> none  [all_to_all(): lax.all_to_all(value, 'sec', 0, 0, axis_index_groups=groups, tiled=True)]
    ppermute x0 -> x28, starting transfers between devices: none -> 21 us  [exchange(): lax.ppermute(values[apart], 'sec', [(s, s ^ apart) for s in range(section...]
    all_to_all x1 -> x0, blocking collectives: 17.7 us -> none  [all_to_all(): lax.all_to_all(value, 'sec', 0, 0, axis_index_groups=groups, tiled=True)]
    all_to_all x3 -> x0, starting transfers between devices: 11.9 us -> none  [all_to_all(): lax.all_to_all(value, 'sec', 0, 0, axis_index_groups=groups, tiled=True)]
    unnamed x25 -> x61, local copies, waits for them, and re-layouts: 7.8 us -> 14.8 us
    pallas_call x10, Pallas kernels: 29.5 us -> 24.5 us  [run(): pl.pallas_call(kernel, grid_spec=pltpu.PrefetchScalarGridSpec(num_scalar_...]
    ppermute x2, waiting for transfers between devices: 12.7 us -> 9.75 us  [on_device(): other = [lax.ppermute(mine[c], 'scan', swap) for c in chunks]]
  transfers between devices with their start and end apart: 8 -> 33, of which waited for: 7 -> 20; matrix products, arithmetic and copies ran while one was open for 1% -> 1% of each run, Pallas kernels for 8% -> 8%
where the time goes in v3:
time: 130 us; the launch traced here: 129 us
  waiting for transfers between devices  60.9 us (47%)
  starting transfers between devices  28.7 us (22%)
  Pallas kernels  24.5 us (19%)
  local copies, waits for them, and re-layouts  14.8 us (11%)
    ppermute x28, waiting for transfers between devices, exchange(): lax.ppermute(values[apart], 'sec', [(s, s ^ apart) for s in range(section...  28.3 us
    pallas_call x10, Pallas kernels, run(): pl.pallas_call(kernel, grid_spec=pltpu.PrefetchScalarGridSpec(num_scalar_...  24.5 us
    ppermute x28, starting transfers between devices, exchange(): lax.ppermute(values[apart], 'sec', [(s, s ^ apart) for s in range(section...  21 us
    ppermute x1, waiting for transfers between devices, on_device(): lax.ppermute(leave, 'sec', [(s, s - count) for s in range(count, sections)])  15.2 us
    unnamed x61, local copies, waits for them, and re-layouts  14.8 us
    ppermute x2, waiting for transfers between devices, on_device(): other = [lax.ppermute(mine[c], 'scan', swap) for c in chunks]  9.75 us
    ppermute x2, waiting for transfers between devices, on_device(): sums += [keep, lax.ppermute(away, 'scan', swap)]  7.68 us
    ppermute x2, starting transfers between devices, on_device(): sums += [keep, lax.ppermute(away, 'scan', swap)]  3.1 us
  transfers between devices with their start and end apart: 33, of which 20 were waited for; matrix products, arithmetic and copies ran while one was open for 1% of the time, Pallas kernels for 8%

profile of v3, /device:TPU:0, one launch (start us, length us, event | category | flops | bytes accessed | tf_op | source)
XLA Modules:
  0.0 129.3 jit_solution(13841018705682607175)
XLA Ops:
  3.0 3.0 %collective-permute-start = (bf16[2,128,512]{2,1,0:T(8,128)(2,1)S(1)}, bf16[2,128,512]{2,1,0:T(8,128)(2,1)S(1)}, u32[]{:S(2)}, u32[]{:S(2)}) collective-permute-start(bf16[2,128,512]{2,1,0:T(8,128)(2,1)S(1)} %get-tuple-element.50.mine_ref), channel_id=1, source_target_pairs={{0,1},{1,0},{2,3},{3,2},{4,5},{5,4},{6,7},{7,6},{8,9},{9,8},{10,11... | collective-permute-start | bytes 786440 | tf_op jit(solution)/shard_map/ppermute | solution.py:237
  6.9 6.2 %collective-permute-done.other_ref = bf16[2,128,512]{2,1,0:T(8,128)(2,1)S(1)} collective-permute-done((bf16[2,128,512]{2,1,0:T(8,128)(2,1)S(1)}, bf16[2,128,512]{2,1,0:T(8,128)(2,1)S(1)}, u32[]{:S(2)}, u32[]{:S(2)}) %collective-permute-start) | collective-permute-done | bytes 262176 | tf_op jit(solution)/shard_map/ppermute | solution.py:237
  14.4 3.5 %collective-permute-done.1.other_ref = bf16[2,128,512]{2,1,0:T(8,128)(2,1)S(1)} collective-permute-done((bf16[2,128,512]{2,1,0:T(8,128)(2,1)S(1)}, bf16[2,128,512]{2,1,0:T(8,128)(2,1)S(1)}, u32[]{:S(2)}, u32[]{:S(2)}) %collective-permute-start.1) | collective-permute-done | bytes 262176 | tf_op jit(solution)/shard_map/ppermute | solution.py:237
  19.5 2.5 %collective-permute-start.12 = (bf16[2,128,256]{2,1,0:T(8,128)(2,1)S(1)}, bf16[2,128,256]{2,1,0:T(8,128)(2,1)S(1)}, u32[]{:S(2)}, u32[]{:S(2)}) collective-permute-start(bf16[2,128,256]{2,1,0:T(8,128)(2,1)S(1)} %get-tuple-element.64), channel_id=1, source_target_pairs={{0,12},{2,14},{4,8},{6,10},{8,4},{10,6},{12,0},{14,2},{16,28},{18,... | collective-permute-start | bytes 393224 | tf_op jit(solution)/shard_map/ppermute | solution.py:231
  22.5 2.0 %collective-permute-start.14 = (bf16[2,128,256]{2,1,0:T(8,128)(2,1)S(1)}, bf16[2,128,256]{2,1,0:T(8,128)(2,1)S(1)}, u32[]{:S(2)}, u32[]{:S(2)}) collective-permute-start(bf16[2,128,256]{2,1,0:T(8,128)(2,1)S(1)} %get-tuple-element.66), channel_id=1, source_target_pairs={{0,14},{2,12},{4,10},{6,8},{8,6},{10,4},{12,2},{14,0},{16,30},{18,... | collective-permute-start | bytes 393224 | tf_op jit(solution)/shard_map/ppermute | solution.py:231
  26.1 3.0 %collective-permute-done.12.refs_12_ = bf16[2,128,256]{2,1,0:T(8,128)(2,1)S(1)} collective-permute-done((bf16[2,128,256]{2,1,0:T(8,128)(2,1)S(1)}, bf16[2,128,256]{2,1,0:T(8,128)(2,1)S(1)}, u32[]{:S(2)}, u32[]{:S(2)}) %collective-permute-start.12) | collective-permute-done | bytes 131104 | tf_op jit(solution)/shard_map/ppermute | solution.py:231
  29.1 2.8 %collective-permute-done.13.refs_13_ = bf16[2,128,256]{2,1,0:T(8,128)(2,1)S(1)} collective-permute-done((bf16[2,128,256]{2,1,0:T(8,128)(2,1)S(1)}, bf16[2,128,256]{2,1,0:T(8,128)(2,1)S(1)}, u32[]{:S(2)}, u32[]{:S(2)}) %collective-permute-start.13) | collective-permute-done | bytes 131104 | tf_op jit(solution)/shard_map/ppermute | solution.py:231
  32.3 2.1 %collective-permute-done.14.refs_14_ = bf16[2,128,256]{2,1,0:T(8,128)(2,1)S(1)} collective-permute-done((bf16[2,128,256]{2,1,0:T(8,128)(2,1)S(1)}, bf16[2,128,256]{2,1,0:T(8,128)(2,1)S(1)}, u32[]{:S(2)}, u32[]{:S(2)}) %collective-permute-start.14) | collective-permute-done | bytes 131104 | tf_op jit(solution)/shard_map/ppermute | solution.py:231
  34.5 2.8 %collective-permute-done.15.refs_15_ = bf16[2,128,256]{2,1,0:T(8,128)(2,1)S(1)} collective-permute-done((bf16[2,128,256]{2,1,0:T(8,128)(2,1)S(1)}, bf16[2,128,256]{2,1,0:T(8,128)(2,1)S(1)}, u32[]{:S(2)}, u32[]{:S(2)}) %collective-permute-start.15) | collective-permute-done | bytes 131104 | tf_op jit(solution)/shard_map/ppermute | solution.py:231
  37.4 1.7 %collective-permute-start.7 = (bf16[2,128,256]{2,1,0:T(8,128)(2,1)S(1)}, bf16[2,128,256]{2,1,0:T(8,128)(2,1)S(1)}, u32[]{:S(2)}, u32[]{:S(2)}) collective-permute-start(bf16[2,128,256]{2,1,0:T(8,128)(2,1)S(1)} %get-tuple-element.59), channel_id=1, source_target_pairs={{0,6},{2,4},{4,2},{6,0},{8,14},{10,12},{12,10},{14,8},{16,22},{18,... | collective-permute-start | bytes 393224 | tf_op jit(solution)/shard_map/ppermute | solution.py:231
  41.1 1.2 shard_map.56
  43.1 2.6 %collective-permute-done.6.refs_6_ = bf16[2,128,256]{2,1,0:T(8,128)(2,1)S(1)} collective-permute-done((bf16[2,128,256]{2,1,0:T(8,128)(2,1)S(1)}, bf16[2,128,256]{2,1,0:T(8,128)(2,1)S(1)}, u32[]{:S(2)}, u32[]{:S(2)}) %collective-permute-start.6) | collective-permute-done | bytes 131104 | tf_op jit(solution)/shard_map/ppermute | solution.py:231
  45.7 2.8 %collective-permute-done.7.refs_7_ = bf16[2,128,256]{2,1,0:T(8,128)(2,1)S(1)} collective-permute-done((bf16[2,128,256]{2,1,0:T(8,128)(2,1)S(1)}, bf16[2,128,256]{2,1,0:T(8,128)(2,1)S(1)}, u32[]{:S(2)}, u32[]{:S(2)}) %collective-permute-start.7) | collective-permute-done | bytes 131104 | tf_op jit(solution)/shard_map/ppermute | solution.py:231
  48.5 6.5 %shard_map.60 = (bf16[2,128,256]{2,1,0:T(8,128)(2,1)}, bf16[2,128,256]{2,1,0:T(8,128)(2,1)}, bf16[2,128,256]{2,1,0:T(8,128)(2,1)}, bf16[2,128,256]{2,1,0:T(8,128...) custom-call(s32[2]{0:T(128)S(1)} %pad_add_fusion.1.pick_ref, ...), custom_call_target="tpu_custom_call" | custom-call | flops 2147483648 | bytes 5242888 | tf_op jit(solution)/shard_map/pallas_call | solution.py:24
  55.1 1.5 %collective-permute-start.16 = (bf16[2,256,256]{2,1,0:T(8,128)(2,1)S(1)}, bf16[2,256,256]{2,1,0:T(8,128)(2,1)S(1)}, u32[]{:S(2)}, u32[]{:S(2)}) collective-permute-start(bf16[2,256,256]{2,1,0:T(8,128)(2,1)S(1)} %get-tuple-element.68), channel_id=1, source_target_pairs={{16,0},{18,2},{20,4},{22,6},{24,8},{26,10},{28,12},{30,14},{17,1},... | collective-permute-start | bytes 786440 | tf_op jit(solution)/shard_map/ppermute | solution.py:259
  56.7 15.2 %collective-permute-done.16.come_ref = bf16[2,256,256]{2,1,0:T(8,128)(2,1)S(1)} collective-permute-done((bf16[2,256,256]{2,1,0:T(8,128)(2,1)S(1)}, bf16[2,256,256]{2,1,0:T(8,128)(2,1)S(1)}, u32[]{:S(2)}, u32[]{:S(2)}) %collective-permute-start.16) | collective-permute-done | bytes 262176 | tf_op jit(solution)/shard_map/ppermute | solution.py:259
  83.6 5.9 %shard_map.61 = (bf16[2,128,256]{2,1,0:T(8,128)(2,1)S(1)}, bf16[2,128,256]{2,1,0:T(8,128)(2,1)S(1)}, bf16[2,128,256]{2,1,0:T(8,128)(2,1)S(1)}, bf16[2,128,256]{2...) custom-call(s32[2]{0:T(128)S(1)} %pad_add_fusion.pick_ref, ...), custom_call_target="tpu_custom_call" | custom-call | flops 2147483648 | bytes 5242888 | tf_op jit(solution)/shard_map/pallas_call | solution.py:24
  89.8 1.6 %collective-permute-start.27 = (bf16[2,128,256]{2,1,0:T(8,128)(2,1)S(1)}, bf16[2,128,256]{2,1,0:T(8,128)(2,1)S(1)}, u32[]{:S(2)}, u32[]{:S(2)}) collective-permute-start(bf16[2,128,256]{2,1,0:T(8,128)(2,1)S(1)} %get-tuple-element.82), channel_id=1, source_target_pairs={{0,6},{2,4},{4,2},{6,0},{8,14},{10,12},{12,10},{14,8},{16,22},{18,... | collective-permute-start | bytes 393224 | tf_op jit(solution)/shard_map/ppermute | solution.py:231
  91.4 1.6 %collective-permute-start.29 = (bf16[2,128,256]{2,1,0:T(8,128)(2,1)S(1)}, bf16[2,128,256]{2,1,0:T(8,128)(2,1)S(1)}, u32[]{:S(2)}, u32[]{:S(2)}) collective-permute-start(bf16[2,128,256]{2,1,0:T(8,128)(2,1)S(1)} %get-tuple-element.84), channel_id=1, source_target_pairs={{0,10},{2,8},{4,14},{6,12},{8,2},{10,0},{12,6},{14,4},{16,26},{18,... | collective-permute-start | bytes 393224 | tf_op jit(solution)/shard_map/ppermute | solution.py:231
  93.2 2.7 %collective-permute-done.26.refs_2_ = bf16[2,128,256]{2,1,0:T(8,128)(2,1)S(1)} collective-permute-done((bf16[2,128,256]{2,1,0:T(8,128)(2,1)S(1)}, bf16[2,128,256]{2,1,0:T(8,128)(2,1)S(1)}, u32[]{:S(2)}, u32[]{:S(2)}) %collective-permute-start.26) | collective-permute-done | bytes 131104 | tf_op jit(solution)/shard_map/ppermute | solution.py:231
  95.8 2.0 %collective-permute-done.27.refs_3_ = bf16[2,128,256]{2,1,0:T(8,128)(2,1)S(1)} collective-permute-done((bf16[2,128,256]{2,1,0:T(8,128)(2,1)S(1)}, bf16[2,128,256]{2,1,0:T(8,128)(2,1)S(1)}, u32[]{:S(2)}, u32[]{:S(2)}) %collective-permute-start.27) | collective-permute-done | bytes 131104 | tf_op jit(solution)/shard_map/ppermute | solution.py:231
  100.3 2.9 %collective-permute-done.30.refs_6_ = bf16[2,128,256]{2,1,0:T(8,128)(2,1)S(1)} collective-permute-done((bf16[2,128,256]{2,1,0:T(8,128)(2,1)S(1)}, bf16[2,128,256]{2,1,0:T(8,128)(2,1)S(1)}, u32[]{:S(2)}, u32[]{:S(2)}) %collective-permute-start.30) | collective-permute-done | bytes 131104 | tf_op jit(solution)/shard_map/ppermute | solution.py:231
  103.2 1.4 %collective-permute-done.31.refs_7_ = bf16[2,128,256]{2,1,0:T(8,128)(2,1)S(1)} collective-permute-done((bf16[2,128,256]{2,1,0:T(8,128)(2,1)S(1)}, bf16[2,128,256]{2,1,0:T(8,128)(2,1)S(1)}, u32[]{:S(2)}, u32[]{:S(2)}) %collective-permute-start.31) | collective-permute-done | bytes 131104 | tf_op jit(solution)/shard_map/ppermute | solution.py:231
  105.0 3.5 %collective-permute-start.22 = (bf16[2,128,256]{2,1,0:T(8,128)(2,1)S(1)}, bf16[2,128,256]{2,1,0:T(8,128)(2,1)S(1)}, u32[]{:S(2)}, u32[]{:S(2)}) collective-permute-start(bf16[2,128,256]{2,1,0:T(8,128)(2,1)S(1)} %get-tuple-element.75), channel_id=1, source_target_pairs={{0,12},{2,14},{4,8},{6,10},{8,4},{10,6},{12,0},{14,2},{16,28},{18,... | collective-permute-start | bytes 393224 | tf_op jit(solution)/shard_map/ppermute | solution.py:231
  109.1 2.5 %shard_map.55.wave_ref = bf16[8,2,256,256]{3,2,1,0:T(8,128)(2,1)S(1)} custom-call(s32[8,2]{1,0:T(8,128)S(1)} %copy.10.corner_ref, bf16[8,2,256,256]{3,2,1,0:T(8,128)(2,1)S(1)} %bitcast.7), custom_call_target="tpu_custom_call" | custom-call | bytes 4194368 | tf_op jit(solution)/shard_map/pallas_call | solution.py:24
  111.6 2.1 %shard_map.63 = (f32[2,128,512]{2,1,0:T(8,128)S(1)}, bf16[2,128,512]{2,1,0:T(8,128)(2,1)S(1)}) custom-call(s32[8,2]{1,0:T(8,128)S(1)} %copy.10.corner_ref, s32[1]{0:T(128)} %bitcast.place_ref, s32[2]{0:T(128)S(1)} %pad_add_fusion.pick_ref, bf16[8,2,256,256]{3,2,1,0:T(8,128)(2,1)S(1)} %shard_map.55.wave_ref, ...), custom_call_target="tpu_custom_call" | custom-call | bytes 3932236 | tf_op jit(solution)/shard_map/pallas_call | solution.py:24
  113.8 1.6 %collective-permute-start.32 = (bf16[2,128,512]{2,1,0:T(8,128)(2,1)S(1)}, bf16[2,128,512]{2,1,0:T(8,128)(2,1)S(1)}, u32[]{:S(2)}, u32[]{:S(2)}) collective-permute-start(bf16[2,128,512]{2,1,0:T(8,128)(2,1)S(1)} %get-tuple-element.88), channel_id=1, source_target_pairs={{0,1},{1,0},{2,3},{3,2},{4,5},{5,4},{6,7},{7,6},{8,9},{9,8},{10,11... | collective-permute-start | bytes 786440 | tf_op jit(solution)/shard_map/ppermute | solution.py:269
  115.7 1.2 collective-permute-done.23.refs_7_
  116.9 2.1 %shard_map.62 = (f32[2,128,512]{2,1,0:T(8,128)S(1)}, bf16[2,128,512]{2,1,0:T(8,128)(2,1)S(1)}) custom-call(s32[8,2]{1,0:T(8,128)S(1)} %copy.10.corner_ref, s32[1]{0:T(128)} %bitcast.place_ref, s32[2]{0:T(128)S(1)} %pad_add_fusion.pick_ref, bf16[8,2,256,256]{3,2,1,0:T(8,128)(2,1)S(1)} %shard_map.55.wave_ref, ...), custom_call_target="tpu_custom_call" | custom-call | bytes 3932236 | tf_op jit(solution)/shard_map/pallas_call | solution.py:24
  119.0 1.6 %collective-permute-start.24 = (bf16[2,128,512]{2,1,0:T(8,128)(2,1)S(1)}, bf16[2,128,512]{2,1,0:T(8,128)(2,1)S(1)}, u32[]{:S(2)}, u32[]{:S(2)}) collective-permute-start(bf16[2,128,512]{2,1,0:T(8,128)(2,1)S(1)} %get-tuple-element.78), channel_id=1, source_target_pairs={{0,1},{1,0},{2,3},{3,2},{4,5},{5,4},{6,7},{7,6},{8,9},{9,8},{10,11... | collective-permute-start | bytes 786440 | tf_op jit(solution)/shard_map/ppermute | solution.py:269
  120.6 2.4 %collective-permute-done.32.refs_3_ = bf16[2,128,512]{2,1,0:T(8,128)(2,1)S(1)} collective-permute-done((bf16[2,128,512]{2,1,0:T(8,128)(2,1)S(1)}, bf16[2,128,512]{2,1,0:T(8,128)(2,1)S(1)}, u32[]{:S(2)}, u32[]{:S(2)}) %collective-permute-start.32) | collective-permute-done | bytes 262176 | tf_op jit(solution)/shard_map/ppermute | solution.py:269
  123.0 5.3 %collective-permute-done.24.refs_1_ = bf16[2,128,512]{2,1,0:T(8,128)(2,1)S(1)} collective-permute-done((bf16[2,128,512]{2,1,0:T(8,128)(2,1)S(1)}, bf16[2,128,512]{2,1,0:T(8,128)(2,1)S(1)}, u32[]{:S(2)}, u32[]{:S(2)}) %collective-permute-start.24) | collective-permute-done | bytes 262176 | tf_op jit(solution)/shard_map/ppermute | solution.py:269
  (107 shorter events, 29.2 us)
Async XLA Ops:
  3.0 10.1 %collective-permute-start = (bf16[2,128,512]{2,1,0:T(8,128)(2,1)S(1)}, bf16[2,128,512]{2,1,0:T(8,128)(2,1)S(1)}, u32[]{:S(2)}, u32[]{:S(2)}) collective-permute-start(bf16[2,128,512]{2,1,0:T(8,128)(2,1)S(1)} %get-tuple-element.50.mine_ref), channel_id=1, source_target_pairs={{0,1},{1,0},{2,3},{3,2},{4,5},{5,4},{6,7},{7,6},{8,9},{9,8},{10,11... | collective-permute-start | bytes 786440 | tf_op jit(solution)/shard_map/ppermute | solution.py:237
  6.0 11.9 %collective-permute-start.1 = (bf16[2,128,512]{2,1,0:T(8,128)(2,1)S(1)}, bf16[2,128,512]{2,1,0:T(8,128)(2,1)S(1)}, u32[]{:S(2)}, u32[]{:S(2)}) collective-permute-start(bf16[2,128,512]{2,1,0:T(8,128)(2,1)S(1)} %get-tuple-element.52.mine_ref), channel_id=1, source_target_pairs={{0,1},{1,0},{2,3},{3,2},{4,5},{5,4},{6,7},{7,6},{8,9},{9,8},{10,11... | collective-permute-start | bytes 786440 | tf_op jit(solution)/shard_map/ppermute | solution.py:237
  14.3 10.2 %collective-permute-start.10 = (bf16[2,128,256]{2,1,0:T(8,128)(2,1)S(1)}, bf16[2,128,256]{2,1,0:T(8,128)(2,1)S(1)}, u32[]{:S(2)}, u32[]{:S(2)}) collective-permute-start(bf16[2,128,256]{2,1,0:T(8,128)(2,1)S(1)} %get-tuple-element.62), channel_id=1, source_target_pairs={{0,10},{2,8},{4,14},{6,12},{8,2},{10,0},{12,6},{14,4},{16,26},{18,... | collective-permute-start | bytes 393224 | tf_op jit(solution)/shard_map/ppermute | solution.py:231
  19.1 6.0 %collective-permute-start.11 = (bf16[2,128,256]{2,1,0:T(8,128)(2,1)S(1)}, bf16[2,128,256]{2,1,0:T(8,128)(2,1)S(1)}, u32[]{:S(2)}, u32[]{:S(2)}) collective-permute-start(bf16[2,128,256]{2,1,0:T(8,128)(2,1)S(1)} %get-tuple-element.63), channel_id=1, source_target_pairs={{0,10},{2,8},{4,14},{6,12},{8,2},{10,0},{12,6},{14,4},{16,26},{18,... | collective-permute-start | bytes 393224 | tf_op jit(solution)/shard_map/ppermute | solution.py:231
  19.5 9.5 %collective-permute-start.12 = (bf16[2,128,256]{2,1,0:T(8,128)(2,1)S(1)}, bf16[2,128,256]{2,1,0:T(8,128)(2,1)S(1)}, u32[]{:S(2)}, u32[]{:S(2)}) collective-permute-start(bf16[2,128,256]{2,1,0:T(8,128)(2,1)S(1)} %get-tuple-element.64), channel_id=1, source_target_pairs={{0,12},{2,14},{4,8},{6,10},{8,4},{10,6},{12,0},{14,2},{16,28},{18,... | collective-permute-start | bytes 393224 | tf_op jit(solution)/shard_map/ppermute | solution.py:231
  22.0 9.9 %collective-permute-start.13 = (bf16[2,128,256]{2,1,0:T(8,128)(2,1)S(1)}, bf16[2,128,256]{2,1,0:T(8,128)(2,1)S(1)}, u32[]{:S(2)}, u32[]{:S(2)}) collective-permute-start(bf16[2,128,256]{2,1,0:T(8,128)(2,1)S(1)} %get-tuple-element.65), channel_id=1, source_target_pairs={{0,12},{2,14},{4,8},{6,10},{8,4},{10,6},{12,0},{14,2},{16,28},{18,... | collective-permute-start | bytes 393224 | tf_op jit(solution)/shard_map/ppermute | solution.py:231
  22.5 12.0 %collective-permute-start.14 = (bf16[2,128,256]{2,1,0:T(8,128)(2,1)S(1)}, bf16[2,128,256]{2,1,0:T(8,128)(2,1)S(1)}, u32[]{:S(2)}, u32[]{:S(2)}) collective-permute-start(bf16[2,128,256]{2,1,0:T(8,128)(2,1)S(1)} %get-tuple-element.66), channel_id=1, source_target_pairs={{0,14},{2,12},{4,10},{6,8},{8,6},{10,4},{12,2},{14,0},{16,30},{18,... | collective-permute-start | bytes 393224 | tf_op jit(solution)/shard_map/ppermute | solution.py:231
  24.5 12.9 %collective-permute-start.15 = (bf16[2,128,256]{2,1,0:T(8,128)(2,1)S(1)}, bf16[2,128,256]{2,1,0:T(8,128)(2,1)S(1)}, u32[]{:S(2)}, u32[]{:S(2)}) collective-permute-start(bf16[2,128,256]{2,1,0:T(8,128)(2,1)S(1)} %get-tuple-element.67), channel_id=1, source_target_pairs={{0,14},{2,12},{4,10},{6,8},{8,6},{10,4},{12,2},{14,0},{16,30},{18,... | collective-permute-start | bytes 393224 | tf_op jit(solution)/shard_map/ppermute | solution.py:231
  25.1 12.2 %collective-permute-start.2 = (bf16[2,128,256]{2,1,0:T(8,128)(2,1)S(1)}, bf16[2,128,256]{2,1,0:T(8,128)(2,1)S(1)}, u32[]{:S(2)}, u32[]{:S(2)}) collective-permute-start(bf16[2,128,256]{2,1,0:T(8,128)(2,1)S(1)} %get-tuple-element.54), channel_id=1, source_target_pairs={{0,2},{2,0},{4,6},{6,4},{8,10},{10,8},{12,14},{14,12},{16,18},{18,... | collective-permute-start | bytes 393224 | tf_op jit(solution)/shard_map/ppermute | solution.py:231
  29.1 10.0 %collective-permute-start.3 = (bf16[2,128,256]{2,1,0:T(8,128)(2,1)S(1)}, bf16[2,128,256]{2,1,0:T(8,128)(2,1)S(1)}, u32[]{:S(2)}, u32[]{:S(2)}) collective-permute-start(bf16[2,128,256]{2,1,0:T(8,128)(2,1)S(1)} %get-tuple-element.55), channel_id=1, source_target_pairs={{0,2},{2,0},{4,6},{6,4},{8,10},{10,8},{12,14},{14,12},{16,18},{18,... | collective-permute-start | bytes 393224 | tf_op jit(solution)/shard_map/ppermute | solution.py:231
  31.9 8.4 %collective-permute-start.4 = (bf16[2,128,256]{2,1,0:T(8,128)(2,1)S(1)}, bf16[2,128,256]{2,1,0:T(8,128)(2,1)S(1)}, u32[]{:S(2)}, u32[]{:S(2)}) collective-permute-start(bf16[2,128,256]{2,1,0:T(8,128)(2,1)S(1)} %get-tuple-element.56), channel_id=1, source_target_pairs={{0,4},{2,6},{4,0},{6,2},{8,12},{10,14},{12,8},{14,10},{16,20},{18,... | collective-permute-start | bytes 393224 | tf_op jit(solution)/shard_map/ppermute | solution.py:231
  34.4 8.6 %collective-permute-start.5 = (bf16[2,128,256]{2,1,0:T(8,128)(2,1)S(1)}, bf16[2,128,256]{2,1,0:T(8,128)(2,1)S(1)}, u32[]{:S(2)}, u32[]{:S(2)}) collective-permute-start(bf16[2,128,256]{2,1,0:T(8,128)(2,1)S(1)} %get-tuple-element.57), channel_id=1, source_target_pairs={{0,4},{2,6},{4,0},{6,2},{8,12},{10,14},{12,8},{14,10},{16,20},{18,... | collective-permute-start | bytes 393224 | tf_op jit(solution)/shard_map/ppermute | solution.py:231
  37.3 8.4 %collective-permute-start.6 = (bf16[2,128,256]{2,1,0:T(8,128)(2,1)S(1)}, bf16[2,128,256]{2,1,0:T(8,128)(2,1)S(1)}, u32[]{:S(2)}, u32[]{:S(2)}) collective-permute-start(bf16[2,128,256]{2,1,0:T(8,128)(2,1)S(1)} %get-tuple-element.58), channel_id=1, source_target_pairs={{0,6},{2,4},{4,2},{6,0},{8,14},{10,12},{12,10},{14,8},{16,22},{18,... | collective-permute-start | bytes 393224 | tf_op jit(solution)/shard_map/ppermute | solution.py:231
  37.4 11.1 %collective-permute-start.7 = (bf16[2,128,256]{2,1,0:T(8,128)(2,1)S(1)}, bf16[2,128,256]{2,1,0:T(8,128)(2,1)S(1)}, u32[]{:S(2)}, u32[]{:S(2)}) collective-permute-start(bf16[2,128,256]{2,1,0:T(8,128)(2,1)S(1)} %get-tuple-element.59), channel_id=1, source_target_pairs={{0,6},{2,4},{4,2},{6,0},{8,14},{10,12},{12,10},{14,8},{16,22},{18,... | collective-permute-start | bytes 393224 | tf_op jit(solution)/shard_map/ppermute | solution.py:231
  39.1 9.4 %collective-permute-start.8 = (bf16[2,128,256]{2,1,0:T(8,128)(2,1)S(1)}, bf16[2,128,256]{2,1,0:T(8,128)(2,1)S(1)}, u32[]{:S(2)}, u32[]{:S(2)}) collective-permute-start(bf16[2,128,256]{2,1,0:T(8,128)(2,1)S(1)} %get-tuple-element.60), channel_id=1, source_target_pairs={{0,8},{2,10},{4,12},{6,14},{8,0},{10,2},{12,4},{14,6},{16,24},{18,... | collective-permute-start | bytes 393224 | tf_op jit(solution)/shard_map/ppermute | solution.py:231
  40.3 8.2 %collective-permute-start.9 = (bf16[2,128,256]{2,1,0:T(8,128)(2,1)S(1)}, bf16[2,128,256]{2,1,0:T(8,128)(2,1)S(1)}, u32[]{:S(2)}, u32[]{:S(2)}) collective-permute-start(bf16[2,128,256]{2,1,0:T(8,128)(2,1)S(1)} %get-tuple-element.61), channel_id=1, source_target_pairs={{0,8},{2,10},{4,12},{6,14},{8,0},{10,2},{12,4},{14,6},{16,24},{18,... | collective-permute-start | bytes 393224 | tf_op jit(solution)/shard_map/ppermute | solution.py:231
  55.1 16.7 %collective-permute-start.16 = (bf16[2,256,256]{2,1,0:T(8,128)(2,1)S(1)}, bf16[2,256,256]{2,1,0:T(8,128)(2,1)S(1)}, u32[]{:S(2)}, u32[]{:S(2)}) collective-permute-start(bf16[2,256,256]{2,1,0:T(8,128)(2,1)S(1)} %get-tuple-element.68), channel_id=1, source_target_pairs={{16,0},{18,2},{20,4},{22,6},{24,8},{26,10},{28,12},{30,14},{17,1},... | collective-permute-start | bytes 786440 | tf_op jit(solution)/shard_map/ppermute | solution.py:259
  89.5 6.3 %collective-permute-start.26 = (bf16[2,128,256]{2,1,0:T(8,128)(2,1)S(1)}, bf16[2,128,256]{2,1,0:T(8,128)(2,1)S(1)}, u32[]{:S(2)}, u32[]{:S(2)}) collective-permute-start(bf16[2,128,256]{2,1,0:T(8,128)(2,1)S(1)} %get-tuple-element.81), channel_id=1, source_target_pairs={{0,4},{2,6},{4,0},{6,2},{8,12},{10,14},{12,8},{14,10},{16,20},{18,... | collective-permute-start | bytes 393224 | tf_op jit(solution)/shard_map/ppermute | solution.py:231
  89.8 8.1 %collective-permute-start.27 = (bf16[2,128,256]{2,1,0:T(8,128)(2,1)S(1)}, bf16[2,128,256]{2,1,0:T(8,128)(2,1)S(1)}, u32[]{:S(2)}, u32[]{:S(2)}) collective-permute-start(bf16[2,128,256]{2,1,0:T(8,128)(2,1)S(1)} %get-tuple-element.82), channel_id=1, source_target_pairs={{0,6},{2,4},{4,2},{6,0},{8,14},{10,12},{12,10},{14,8},{16,22},{18,... | collective-permute-start | bytes 393224 | tf_op jit(solution)/shard_map/ppermute | solution.py:231
  91.4 7.0 %collective-permute-start.28 = (bf16[2,128,256]{2,1,0:T(8,128)(2,1)S(1)}, bf16[2,128,256]{2,1,0:T(8,128)(2,1)S(1)}, u32[]{:S(2)}, u32[]{:S(2)}) collective-permute-start(bf16[2,128,256]{2,1,0:T(8,128)(2,1)S(1)} %get-tuple-element.83), channel_id=1, source_target_pairs={{0,8},{2,10},{4,12},{6,14},{8,0},{10,2},{12,4},{14,6},{16,24},{18,... | collective-permute-start | bytes 393224 | tf_op jit(solution)/shard_map/ppermute | solution.py:231
  91.4 7.8 %collective-permute-start.29 = (bf16[2,128,256]{2,1,0:T(8,128)(2,1)S(1)}, bf16[2,128,256]{2,1,0:T(8,128)(2,1)S(1)}, u32[]{:S(2)}, u32[]{:S(2)}) collective-permute-start(bf16[2,128,256]{2,1,0:T(8,128)(2,1)S(1)} %get-tuple-element.84), channel_id=1, source_target_pairs={{0,10},{2,8},{4,14},{6,12},{8,2},{10,0},{12,6},{14,4},{16,26},{18,... | collective-permute-start | bytes 393224 | tf_op jit(solution)/shard_map/ppermute | solution.py:231
  93.0 10.2 %collective-permute-start.30 = (bf16[2,128,256]{2,1,0:T(8,128)(2,1)S(1)}, bf16[2,128,256]{2,1,0:T(8,128)(2,1)S(1)}, u32[]{:S(2)}, u32[]{:S(2)}) collective-permute-start(bf16[2,128,256]{2,1,0:T(8,128)(2,1)S(1)} %get-tuple-element.85), channel_id=1, source_target_pairs={{0,12},{2,14},{4,8},{6,10},{8,4},{10,6},{12,0},{14,2},{16,28},{18,... | collective-permute-start | bytes 393224 | tf_op jit(solution)/shard_map/ppermute | solution.py:231
  95.8 8.8 %collective-permute-start.31 = (bf16[2,128,256]{2,1,0:T(8,128)(2,1)S(1)}, bf16[2,128,256]{2,1,0:T(8,128)(2,1)S(1)}, u32[]{:S(2)}, u32[]{:S(2)}) collective-permute-start(bf16[2,128,256]{2,1,0:T(8,128)(2,1)S(1)} %get-tuple-element.86), channel_id=1, source_target_pairs={{0,14},{2,12},{4,10},{6,8},{8,6},{10,4},{12,2},{14,0},{16,30},{18,... | collective-permute-start | bytes 393224 | tf_op jit(solution)/shard_map/ppermute | solution.py:231
  97.8 7.1 %collective-permute-start.17 = (bf16[2,128,256]{2,1,0:T(8,128)(2,1)S(1)}, bf16[2,128,256]{2,1,0:T(8,128)(2,1)S(1)}, u32[]{:S(2)}, u32[]{:S(2)}) collective-permute-start(bf16[2,128,256]{2,1,0:T(8,128)(2,1)S(1)} %get-tuple-element.70), channel_id=1, source_target_pairs={{0,2},{2,0},{4,6},{6,4},{8,10},{10,8},{12,14},{14,12},{16,18},{18,... | collective-permute-start | bytes 393224 | tf_op jit(solution)/shard_map/ppermute | solution.py:231
  98.4 10.2 %collective-permute-start.18 = (bf16[2,128,256]{2,1,0:T(8,128)(2,1)S(1)}, bf16[2,128,256]{2,1,0:T(8,128)(2,1)S(1)}, u32[]{:S(2)}, u32[]{:S(2)}) collective-permute-start(bf16[2,128,256]{2,1,0:T(8,128)(2,1)S(1)} %get-tuple-element.71), channel_id=1, source_target_pairs={{0,4},{2,6},{4,0},{6,2},{8,12},{10,14},{12,8},{14,10},{16,20},{18,... | collective-permute-start | bytes 393224 | tf_op jit(solution)/shard_map/ppermute | solution.py:231
  99.2 14.6 %collective-permute-start.19 = (bf16[2,128,256]{2,1,0:T(8,128)(2,1)S(1)}, bf16[2,128,256]{2,1,0:T(8,128)(2,1)S(1)}, u32[]{:S(2)}, u32[]{:S(2)}) collective-permute-start(bf16[2,128,256]{2,1,0:T(8,128)(2,1)S(1)} %get-tuple-element.72), channel_id=1, source_target_pairs={{0,6},{2,4},{4,2},{6,0},{8,14},{10,12},{12,10},{14,8},{16,22},{18,... | collective-permute-start | bytes 393224 | tf_op jit(solution)/shard_map/ppermute | solution.py:231
  103.2 12.2 %collective-permute-start.20 = (bf16[2,128,256]{2,1,0:T(8,128)(2,1)S(1)}, bf16[2,128,256]{2,1,0:T(8,128)(2,1)S(1)}, u32[]{:S(2)}, u32[]{:S(2)}) collective-permute-start(bf16[2,128,256]{2,1,0:T(8,128)(2,1)S(1)} %get-tuple-element.73), channel_id=1, source_target_pairs={{0,8},{2,10},{4,12},{6,14},{8,0},{10,2},{12,4},{14,6},{16,24},{18,... | collective-permute-start | bytes 393224 | tf_op jit(solution)/shard_map/ppermute | solution.py:231
  104.6 10.8 %collective-permute-start.21 = (bf16[2,128,256]{2,1,0:T(8,128)(2,1)S(1)}, bf16[2,128,256]{2,1,0:T(8,128)(2,1)S(1)}, u32[]{:S(2)}, u32[]{:S(2)}) collective-permute-start(bf16[2,128,256]{2,1,0:T(8,128)(2,1)S(1)} %get-tuple-element.74), channel_id=1, source_target_pairs={{0,10},{2,8},{4,14},{6,12},{8,2},{10,0},{12,6},{14,4},{16,26},{18,... | collective-permute-start | bytes 393224 | tf_op jit(solution)/shard_map/ppermute | solution.py:231
  105.0 10.7 %collective-permute-start.22 = (bf16[2,128,256]{2,1,0:T(8,128)(2,1)S(1)}, bf16[2,128,256]{2,1,0:T(8,128)(2,1)S(1)}, u32[]{:S(2)}, u32[]{:S(2)}) collective-permute-start(bf16[2,128,256]{2,1,0:T(8,128)(2,1)S(1)} %get-tuple-element.75), channel_id=1, source_target_pairs={{0,12},{2,14},{4,8},{6,10},{8,4},{10,6},{12,0},{14,2},{16,28},{18,... | collective-permute-start | bytes 393224 | tf_op jit(solution)/shard_map/ppermute | solution.py:231
  108.5 8.4 %collective-permute-start.23 = (bf16[2,128,256]{2,1,0:T(8,128)(2,1)S(1)}, bf16[2,128,256]{2,1,0:T(8,128)(2,1)S(1)}, u32[]{:S(2)}, u32[]{:S(2)}) collective-permute-start(bf16[2,128,256]{2,1,0:T(8,128)(2,1)S(1)} %get-tuple-element.76), channel_id=1, source_target_pairs={{0,14},{2,12},{4,10},{6,8},{8,6},{10,4},{12,2},{14,0},{16,30},{18,... | collective-permute-start | bytes 393224 | tf_op jit(solution)/shard_map/ppermute | solution.py:231
  113.8 9.2 %collective-permute-start.32 = (bf16[2,128,512]{2,1,0:T(8,128)(2,1)S(1)}, bf16[2,128,512]{2,1,0:T(8,128)(2,1)S(1)}, u32[]{:S(2)}, u32[]{:S(2)}) collective-permute-start(bf16[2,128,512]{2,1,0:T(8,128)(2,1)S(1)} %get-tuple-element.88), channel_id=1, source_target_pairs={{0,1},{1,0},{2,3},{3,2},{4,5},{5,4},{6,7},{7,6},{8,9},{9,8},{10,11... | collective-permute-start | bytes 786440 | tf_op jit(solution)/shard_map/ppermute | solution.py:269
  119.0 9.2 %collective-permute-start.24 = (bf16[2,128,512]{2,1,0:T(8,128)(2,1)S(1)}, bf16[2,128,512]{2,1,0:T(8,128)(2,1)S(1)}, u32[]{:S(2)}, u32[]{:S(2)}) collective-permute-start(bf16[2,128,512]{2,1,0:T(8,128)(2,1)S(1)} %get-tuple-element.78), channel_id=1, source_target_pairs={{0,1},{1,0},{2,3},{3,2},{4,5},{5,4},{6,7},{7,6},{8,9},{9,8},{10,11... | collective-permute-start | bytes 786440 | tf_op jit(solution)/shard_map/ppermute | solution.py:269
  (31 other events, 287.0 us)

commit v4 on v3

--- a/solution.py
+++ b/solution.py
@@ -17,7 +17,7 @@
 bf16 = jnp.bfloat16
 
 
-def call(kernel, out_shape, prefetch=0, scratch=(), flops=0, transcendentals=0):
+def call(kernel, out_shape, prefetch=0, scratch=(), flops=0, grant=12, space=pltpu.VMEM):
     def run(*args):
         moved = sum(a.size * a.dtype.itemsize for a in jax.tree.leaves((args, out_shape)))
         vmem = pl.BlockSpec(memory_space=pltpu.VMEM)
@@ -26,21 +26,32 @@
             grid_spec=pltpu.PrefetchScalarGridSpec(
                 num_scalar_prefetch=prefetch,
                 grid=(1,),
-                in_specs=[vmem] * (len(args) - prefetch),
+                in_specs=[pl.BlockSpec(memory_space=space)] * (len(args) - prefetch),
                 out_specs=jax.tree.map(lambda _: vmem, out_shape),
                 scratch_shapes=list(scratch),
             ),
             out_shape=out_shape,
-            cost_estimate=pl.CostEstimate(flops=flops, bytes_accessed=moved, transcendentals=transcendentals),
-            compiler_params=pltpu.CompilerParams(vmem_limit_bytes=32 * 2**20),
+            cost_estimate=pl.CostEstimate(flops=flops, bytes_accessed=moved, transcendentals=0),
+            compiler_params=pltpu.CompilerParams(vmem_limit_bytes=grant * 2**20),
         )(*args)
 
     return run
 
 
-def code_kernel(amp_ref, phase_ref, *code_refs):
+def code_kernel(amp_hbm, phase_hbm, *refs):
+    *code_refs, amp_ref, phase_ref, sems = refs
     rows = code_refs[0].shape[1]
+    copies = []
+    for piece in range(sems.shape[0]):
+        tall = amp_ref.shape[0] // sems.shape[0]
+        here = pl.ds(piece * tall, tall)
+        for side, (source, target) in enumerate(((amp_hbm, amp_ref), (phase_hbm, phase_ref))):
+            copies.append(pltpu.make_async_copy(source.at[here], target.at[here], sems.at[piece, side]))
+            copies[-1].start()
+    share = len(copies) // len(code_refs)
     for chunk, code_ref in enumerate(code_refs):
+        for copy in copies[chunk * share : (chunk + 1) * share]:
+            copy.wait()
         amp = amp_ref[pl.ds(chunk * rows, rows), :]
         half = 0.5 * phase_ref[pl.ds(chunk * rows, rows), :]
         square = half * half
@@ -62,15 +73,19 @@
     return at_first != place, col >= corner_ref[position, 1]
 
 
-def cut_kernel(base, corner_ref, place_ref, pick_ref, mine_ref, other_ref, *win_refs):
-    _, rows, window = win_refs[0].shape
+def cut_kernel(base, corner_ref, place_ref, pick_ref, *refs):
+    slices = (refs[:2], refs[2:4])
     place = place_ref[0]
-    for apart, win_ref in enumerate(win_refs):
-        in_mine, in_left = first_masks(corner_ref, pick_ref[0] ^ apart, place, base, (rows, window))
-        for part in range(2):
-            left = jnp.where(in_mine, mine_ref[part, :, :window].astype(f32), other_ref[part, :, :window].astype(f32))
-            right = jnp.where(in_mine, mine_ref[part, :, window:].astype(f32), other_ref[part, :, window:].astype(f32))
-            win_ref[part] = jnp.where(in_left, left, right).astype(bf16)
+    for apart, win_ref in enumerate(refs[4:]):
+        _, _, rows, window = win_ref.shape
+        in_mine, in_left = first_masks(corner_ref, pick_ref[0] ^ (2 * apart), place, base, (rows, window))
+        for core, (mine_ref, other_ref) in enumerate(slices):
+            for part in range(2):
+                left, right = (
+                    jnp.where(in_mine, mine_ref[part, :, cols].astype(f32), other_ref[part, :, cols].astype(f32))
+                    for cols in (slice(0, window), slice(window, 2 * window))
+                )
+                win_ref[core, part] = jnp.where(in_left, left, right).astype(bf16)
 
 
 def turned(wave, row_at, col_at):
@@ -139,7 +154,7 @@
     for apart in range(count):
         for chunk in range(chunk_count):
             here = slice(chunk * rows, (chunk + 1) * rows)
-            held_ref[own ^ apart, :, here] = win_refs[apart * chunk_count + chunk][...]
+            held_ref[own ^ apart, :, here] = win_refs[apart // 2 * chunk_count + chunk][apart % 2]
     down = down_ref[...]
     across = across_ref[...]
     at_end = jnp.full(start_ref.shape[1:], pick_ref[1], jnp.int32) == 1
@@ -159,12 +174,18 @@
     for apart in range(count):
         for chunk in range(chunk_count):
             here = slice(chunk * rows, (chunk + 1) * rows)
-            spread_refs[apart * chunk_count + chunk][...] = kept_ref[own ^ apart, :, here]
+            spread_refs[apart // 2 * chunk_count + chunk][apart % 2] = kept_ref[own ^ apart, :, here]
+
+
+def pass_kernel(*refs):
+    *spread_refs, pass_ref = refs
+    for apart, spread_ref in enumerate(spread_refs):
+        pass_ref[apart] = spread_ref[1]
 
 
 def gradient_kernel(base, corner_ref, place_ref, pick_ref, wave_ref, *refs):
-    *spread_refs, own_ref, away_ref = refs
-    _, rows, window = spread_refs[0].shape
+    *came_refs, passed_ref, own_ref, away_ref = refs
+    _, _, rows, window = passed_ref.shape
     tall = 16
     place = place_ref[0]
     own = pick_ref[0]
@@ -172,7 +193,8 @@
     def one(block, _):
         at = pl.multiple_of(block * tall, tall)
         sums = [jnp.zeros((tall, window), f32) for _ in range(8)]
-        for apart, spread_ref in enumerate(spread_refs):
+        for apart in range(2 * len(came_refs)):
+            spread_ref = passed_ref.at[apart // 2] if apart % 2 else came_refs[apart // 2].at[0]
             position = own ^ apart
             in_mine, in_left = first_masks(corner_ref, position, place, base + at, (tall, window))
             wave_re, wave_im = (wave_ref[position, part, pl.ds(base + at, tall), :].astype(f32) for part in range(2))
@@ -220,25 +242,31 @@
     rows = half // chunk_count
     chunks = range(chunk_count)
     piece = (2, rows, width)
-    part = (2, rows, window)
+    part = (2, 2, rows, window)
     wave = (2, window, window)
-    flops = 8 * 2 * window**3
+    chips = range(count // 2)
+
+    def to_partner(value, distance):
+        return lax.ppermute(value, "sec", [(s, s ^ distance) for s in range(sections)])
 
     def exchange(values):
-        order = sorted(range(1, count), key=lambda apart: (apart == 1, apart % 2, apart))
-        got = list(values)
-        for apart in order:
-            got[apart] = lax.ppermute(values[apart], "sec", [(s, s ^ apart) for s in range(sections)])
-        return got
+        return [to_partner(values[d], 2 * d) if d else values[0] for d in chips]
 
     own = section % count
     pick = jnp.stack([own, jnp.int32(1)])
-    mine = call(code_kernel, [shape_of(piece, bf16)] * chunk_count)(obj_amp[0], obj_phase[0])
-    other = [lax.ppermute(mine[c], "scan", swap) for c in chunks]
+    code = call(
+        code_kernel,
+        [shape_of(piece, bf16)] * chunk_count,
+        scratch=[pltpu.VMEM((half, width), f32)] * 2 + [pltpu.SemaphoreType.DMA((8, 2))],
+        space=pltpu.HBM,
+    )
+    mine = code(obj_amp[0], obj_phase[0])
     windows = []
     for c in chunks:
-        cut = call(functools.partial(cut_kernel, c * rows), [shape_of(part, bf16)] * count, prefetch=3)
-        windows.append(exchange(cut(offsets, place, pick, mine[c], other[c])))
+        other = lax.ppermute(mine[c], "scan", swap)
+        slices = [mine[c], other, to_partner(mine[c], 1), to_partner(other, 1)]
+        cut = call(functools.partial(cut_kernel, c * rows), [shape_of(part, bf16)] * len(chips), prefetch=3)
+        windows.append(exchange(cut(offsets, place, pick, *slices)))
     ready = call(ready_kernel, [shape_of(wave, bf16)] + [shape_of((window, window), bf16)] * 2, prefetch=2)
     start, down, across = ready(offsets, pick, exit_adjoint)
     waves = call(turn_kernel, shape_of(forward_waves.shape[1:], bf16), prefetch=1)(offsets, forward_waves[0])
@@ -247,25 +275,28 @@
     come = start
     through = call(
         group_kernel,
-        [shape_of(part, bf16)] * (chunk_count * count) + [shape_of(wave, bf16)],
+        [shape_of(part, bf16)] * (chunk_count * len(chips)) + [shape_of(wave, bf16)],
         prefetch=1,
         scratch=[pltpu.VMEM((count,) + wave, bf16)] * 2,
-        flops=count * flops,
-    )
-    stage_windows = [windows[c][apart] for apart in range(count) for c in chunks]
+        flops=count * 8 * 2 * window**3,
+        grant=20,
+    )
+    stage_windows = [windows[c][d] for d in chips for c in chunks]
     for stage in range(group_count):
         *spreads, leave = through(pick, start, come, down, across, *stage_windows)
         if stage < group_count - 1:
             come = lax.ppermute(leave, "sec", [(s, s - count) for s in range(count, sections)])
+            come, waves = lax.optimization_barrier((come, waves))
             pick = jnp.stack([own, at_end])
 
-    spreads = [exchange(spreads[c::chunk_count]) for c in chunks]
+    came = [exchange(spreads[c::chunk_count]) for c in chunks]
     sums = []
     for c in chunks:
+        passed = to_partner(call(pass_kernel, shape_of((len(chips), 2, rows, window), bf16))(*came[c]), 1)
         gradient = call(
             functools.partial(gradient_kernel, c * rows), [shape_of(piece, f32), shape_of(piece, bf16)], prefetch=3
         )
-        keep, away = gradient(offsets, place, pick, waves, *spreads[c])
+        keep, away = gradient(offsets, place, pick, waves, *came[c], passed)
         sums += [keep, lax.ppermute(away, "scan", swap)]
     return call(finish_kernel, shape_of((2, half, width), f32))(*sums)[None]
 

time: 130 us -> 122 us (0.938)
  local copies, waits for them, and re-layouts: 14.8 us -> 3.04 us
  waiting for transfers between devices: 60.9 us -> 67.6 us
  starting transfers between devices: 28.7 us -> 22.2 us
  Pallas kernels: 24.5 us -> 28.2 us
    unnamed x61 -> x29, local copies, waits for them, and re-layouts: 14.8 us -> 3.04 us
    ppermute x30 -> x20, waiting for transfers between devices: 38 us -> 45.2 us  [the longest x18 34.7 us: to_partner(): lax.ppermute(value, 'sec', [(s, s ^ distance) for s in range(sections)])]
    ppermute x30 -> x20, starting transfers between devices: 24.1 us -> 18.5 us  [the longest x18 15.5 us: to_partner(): lax.ppermute(value, 'sec', [(s, s ^ distance) for s in range(sections)])]
    pallas_call x10 -> x12, Pallas kernels: 24.5 us -> 28.2 us  [run(): pl.pallas_call(kernel, grid_spec=pltpu.PrefetchScalarGridSpec(num_scalar_...]
    ppermute x1, waiting for transfers between devices: 15.2 us -> 12.3 us  [on_device(): lax.ppermute(leave, 'sec', [(s, s - count) for s in range(count, sections)])]
    ppermute x2, waiting for transfers between devices: 7.68 us -> 10.1 us  [on_device(): sums += [keep, lax.ppermute(away, 'scan', swap)]]
  transfers between devices with their start and end apart: 33 -> 23, of which waited for: 20 -> 15; matrix products, arithmetic and copies ran while one was open for 1% -> 1% of each run, Pallas kernels for 8% -> 9%
where the time goes in v4:
time: 122 us; the launch traced here: 121 us
  waiting for transfers between devices  67.6 us (55%)
  Pallas kernels  28.2 us (23%)
  starting transfers between devices  22.2 us (18%)
  local copies, waits for them, and re-layouts  3.04 us (2%)
    ppermute x18, waiting for transfers between devices, to_partner(): lax.ppermute(value, 'sec', [(s, s ^ distance) for s in range(sections)])  34.7 us
    pallas_call x12, Pallas kernels, run(): pl.pallas_call(kernel, grid_spec=pltpu.PrefetchScalarGridSpec(num_scalar_...  28.2 us
    ppermute x18, starting transfers between devices, to_partner(): lax.ppermute(value, 'sec', [(s, s ^ distance) for s in range(sections)])  15.5 us
    ppermute x1, waiting for transfers between devices, on_device(): lax.ppermute(leave, 'sec', [(s, s - count) for s in range(count, sections)])  12.3 us
    ppermute x2, waiting for transfers between devices, on_device(): other = lax.ppermute(mine[c], 'scan', swap)  10.5 us
    ppermute x2, waiting for transfers between devices, on_device(): sums += [keep, lax.ppermute(away, 'scan', swap)]  10.1 us
    ppermute x2, starting transfers between devices, on_device(): other = lax.ppermute(mine[c], 'scan', swap)  3.08 us
    unnamed x29, local copies, waits for them, and re-layouts  3.04 us
  transfers between devices with their start and end apart: 23, of which 15 were waited for; matrix products, arithmetic and copies ran while one was open for 1% of the time, Pallas kernels for 9%

profile of v4, /device:TPU:0, one launch (start us, length us, event | category | flops | bytes accessed | tf_op | source)
XLA Modules:
  0.0 121.4 jit_solution(3320419017476584949)
XLA Ops:
  2.2 2.2 %shard_map.56 = (bf16[2,128,512]{2,1,0:T(8,128)(2,1)S(1)}, bf16[2,128,512]{2,1,0:T(8,128)(2,1)S(1)}) custom-call(f32[256,512]{1,0:T(8,128)S(1)} %bitcast.8, f32[256,512]{1,0:T(8,128)S(1)} %bitcast.9), custom_call_target="tpu_custom_call" | custom-call | bytes 1572864 | tf_op jit(solution)/shard_map/pallas_call | solution.py:24
  4.5 3.0 %collective-permute-start = (bf16[2,128,512]{2,1,0:T(8,128)(2,1)S(1)}, bf16[2,128,512]{2,1,0:T(8,128)(2,1)S(1)}, u32[]{:S(2)}, u32[]{:S(2)}) collective-permute-start(bf16[2,128,512]{2,1,0:T(8,128)(2,1)S(1)} %get-tuple-element.36.refs_0_), channel_id=1, source_target_pairs={{0,1},{1,0},{2,3},{3,2},{4,5},{5,4},{6,7},{7,6},{8,9},{9,8},{10,11... | collective-permute-start | bytes 786440 | tf_op jit(solution)/shard_map/ppermute | solution.py:266
  7.5 7.1 %collective-permute-done.refs_1_ = bf16[2,128,512]{2,1,0:T(8,128)(2,1)S(1)} collective-permute-done((bf16[2,128,512]{2,1,0:T(8,128)(2,1)S(1)}, bf16[2,128,512]{2,1,0:T(8,128)(2,1)S(1)}, u32[]{:S(2)}, u32[]{:S(2)}) %collective-permute-start) | collective-permute-done | bytes 262176 | tf_op jit(solution)/shard_map/ppermute | solution.py:266
  15.9 3.4 %collective-permute-done.3.refs_1_ = bf16[2,128,512]{2,1,0:T(8,128)(2,1)S(1)} collective-permute-done((bf16[2,128,512]{2,1,0:T(8,128)(2,1)S(1)}, bf16[2,128,512]{2,1,0:T(8,128)(2,1)S(1)}, u32[]{:S(2)}, u32[]{:S(2)}) %collective-permute-start.3) | collective-permute-done | bytes 262176 | tf_op jit(solution)/shard_map/ppermute | solution.py:266
  19.4 2.2 %shard_map.57 = (bf16[2,2,128,256]{3,2,1,0:T(8,128)(2,1)S(1)}, bf16[2,2,128,256]{3,2,1,0:T(8,128)(2,1)S(1)}, bf16[2,2,128,256]{3,2,1,0:T(8,128)(2,1)S(1)}, bf16[2,2,128,256]{3,2,1,0:T(8,128)(2,1)S(1)}) custom-call(s32[8,2]{1,0:T(8,128)S(1)} %copy.10.corner_ref, s32[1]{0:T(128)} %bitcast.place_ref, s32[2]{0:T(128)S(1)} %pad_add_fusion.1.pick_ref, ...), custom_call_target="tpu_custom_call" | custom-call | bytes 2097228 | tf_op jit(solution)/shard_map/pallas_call | solution.py:24
  21.6 1.8 %collective-permute-start.6 = (bf16[2,2,128,256]{3,2,1,0:T(8,128)(2,1)S(1)}, bf16[2,2,128,256]{3,2,1,0:T(8,128)(2,1)S(1)}, u32[]{:S(2)}, u32[]{:S(2)}) collective-permute-start(bf16[2,2,128,256]{3,2,1,0:T(8,128)(2,1)S(1)} %get-tuple-element.40), channel_id=1, source_target_pairs={{0,4},{2,6},{4,0},{6,2},{8,12},{10,14},{12,8},{14,10},{16,20},{18,... | collective-permute-start | bytes 786440 | tf_op jit(solution)/shard_map/ppermute | solution.py:250
  23.4 1.6 %collective-permute-start.8 = (bf16[2,2,128,256]{3,2,1,0:T(8,128)(2,1)S(1)}, bf16[2,2,128,256]{3,2,1,0:T(8,128)(2,1)S(1)}, u32[]{:S(2)}, u32[]{:S(2)}) collective-permute-start(bf16[2,2,128,256]{3,2,1,0:T(8,128)(2,1)S(1)} %get-tuple-element.42), channel_id=1, source_target_pairs={{0,8},{2,10},{4,12},{6,14},{8,0},{10,2},{12,4},{14,6},{16,24},{18,... | collective-permute-start | bytes 786440 | tf_op jit(solution)/shard_map/ppermute | solution.py:250
  26.3 1.8 %collective-permute-start.7 = (bf16[2,2,128,256]{3,2,1,0:T(8,128)(2,1)S(1)}, bf16[2,2,128,256]{3,2,1,0:T(8,128)(2,1)S(1)}, u32[]{:S(2)}, u32[]{:S(2)}) collective-permute-start(bf16[2,2,128,256]{3,2,1,0:T(8,128)(2,1)S(1)} %get-tuple-element.41), channel_id=1, source_target_pairs={{0,4},{2,6},{4,0},{6,2},{8,12},{10,14},{12,8},{14,10},{16,20},{18,... | collective-permute-start | bytes 786440 | tf_op jit(solution)/shard_map/ppermute | solution.py:250
  28.2 1.6 %collective-permute-start.9 = (bf16[2,2,128,256]{3,2,1,0:T(8,128)(2,1)S(1)}, bf16[2,2,128,256]{3,2,1,0:T(8,128)(2,1)S(1)}, u32[]{:S(2)}, u32[]{:S(2)}) collective-permute-start(bf16[2,2,128,256]{3,2,1,0:T(8,128)(2,1)S(1)} %get-tuple-element.43), channel_id=1, source_target_pairs={{0,8},{2,10},{4,12},{6,14},{8,0},{10,2},{12,4},{14,6},{16,24},{18,... | collective-permute-start | bytes 786440 | tf_op jit(solution)/shard_map/ppermute | solution.py:250
  30.8 2.8 %collective-permute-start.11 = (bf16[2,2,128,256]{3,2,1,0:T(8,128)(2,1)S(1)}, bf16[2,2,128,256]{3,2,1,0:T(8,128)(2,1)S(1)}, u32[]{:S(2)}, u32[]{:S(2)}) collective-permute-start(bf16[2,2,128,256]{3,2,1,0:T(8,128)(2,1)S(1)} %get-tuple-element.45), channel_id=1, source_target_pairs={{0,12},{2,14},{4,8},{6,10},{8,4},{10,6},{12,0},{14,2},{16,28},{18,... | collective-permute-start | bytes 786440 | tf_op jit(solution)/shard_map/ppermute | solution.py:250
  34.8 3.1 %collective-permute-done.10.refs_6_ = bf16[2,2,128,256]{3,2,1,0:T(8,128)(2,1)S(1)} collective-permute-done((bf16[2,2,128,256]{3,2,1,0:T(8,128)(2,1)S(1)}, bf16[2,2,128,256]{3,2,1,0:T(8,128)(2,1)S(1)}, u32[]{:S(2)}, u32[]{:S(2)}) %collective-permute-start.10) | collective-permute-done | bytes 262176 | tf_op jit(solution)/shard_map/ppermute | solution.py:250
  37.9 3.7 %collective-permute-done.7.refs_3_ = bf16[2,2,128,256]{3,2,1,0:T(8,128)(2,1)S(1)} collective-permute-done((bf16[2,2,128,256]{3,2,1,0:T(8,128)(2,1)S(1)}, bf16[2,2,128,256]{3,2,1,0:T(8,128)(2,1)S(1)}, u32[]{:S(2)}, u32[]{:S(2)}) %collective-permute-start.7) | collective-permute-done | bytes 262176 | tf_op jit(solution)/shard_map/ppermute | solution.py:250
  41.6 2.2 %collective-permute-done.9.refs_5_ = bf16[2,2,128,256]{3,2,1,0:T(8,128)(2,1)S(1)} collective-permute-done((bf16[2,2,128,256]{3,2,1,0:T(8,128)(2,1)S(1)}, bf16[2,2,128,256]{3,2,1,0:T(8,128)(2,1)S(1)}, u32[]{:S(2)}, u32[]{:S(2)}) %collective-permute-start.9) | collective-permute-done | bytes 262176 | tf_op jit(solution)/shard_map/ppermute | solution.py:250
  43.8 4.7 %collective-permute-done.11.refs_7_ = bf16[2,2,128,256]{3,2,1,0:T(8,128)(2,1)S(1)} collective-permute-done((bf16[2,2,128,256]{3,2,1,0:T(8,128)(2,1)S(1)}, bf16[2,2,128,256]{3,2,1,0:T(8,128)(2,1)S(1)}, u32[]{:S(2)}, u32[]{:S(2)}) %collective-permute-start.11) | collective-permute-done | bytes 262176 | tf_op jit(solution)/shard_map/ppermute | solution.py:250
  48.5 6.6 %shard_map.59 = (bf16[2,2,128,256]{3,2,1,0:T(8,128)(2,1)}, bf16[2,2,128,256]{3,2,1,0:T(8,128)(2,1)}, bf16[2,2,128,256]{3,2,1,0:T(8,128)(2,1)}, bf16[2,2,128,256]...) custom-call(s32[2]{0:T(128)S(1)} %pad_add_fusion.1.pick_ref, ...), custom_call_target="tpu_custom_call" | custom-call | flops 2147483648 | bytes 5242888 | tf_op jit(solution)/shard_map/pallas_call | solution.py:24
  55.1 1.5 %collective-permute-start.12 = (bf16[2,256,256]{2,1,0:T(8,128)(2,1)}, bf16[2,256,256]{2,1,0:T(8,128)(2,1)}, u32[]{:S(2)}, u32[]{:S(2)}) collective-permute-start(bf16[2,256,256]{2,1,0:T(8,128)(2,1)} %get-tuple-element.46), channel_id=1, source_target_pairs={{16,0},{18,2},{20,4},{22,6},{24,8},{26,10},{28,12},{30,14},{17,1},... | collective-permute-start | bytes 786440 | tf_op jit(solution)/shard_map/ppermute | solution.py:288
  56.7 2.5 %shard_map.60.wave_ref = bf16[8,2,256,256]{3,2,1,0:T(8,128)(2,1)S(1)} custom-call(s32[8,2]{1,0:T(8,128)S(1)} %copy.10.corner_ref, bf16[8,2,256,256]{3,2,1,0:T(8,128)(2,1)S(1)} %bitcast.7), custom_call_target="tpu_custom_call" | custom-call | bytes 4194368 | tf_op jit(solution)/shard_map/pallas_call | solution.py:24
  59.3 12.3 %collective-permute-done.12.come_ref = bf16[2,256,256]{2,1,0:T(8,128)(2,1)} collective-permute-done((bf16[2,256,256]{2,1,0:T(8,128)(2,1)}, bf16[2,256,256]{2,1,0:T(8,128)(2,1)}, u32[]{:S(2)}, u32[]{:S(2)}) %collective-permute-start.12) | collective-permute-done | bytes 262176 | tf_op jit(solution)/shard_map/ppermute | solution.py:288
  71.6 6.9 %shard_map.61 = (bf16[2,2,128,256]{3,2,1,0:T(8,128)(2,1)S(1)}, bf16[2,2,128,256]{3,2,1,0:T(8,128)(2,1)S(1)}, bf16[2,2,128,256]{3,2,1,0:T(8,128)(2,1)S(1)}, bf16[...) custom-call(s32[2]{0:T(128)S(1)} %pad_add_fusion.pick_ref, ...), custom_call_target="tpu_custom_call" | custom-call | flops 2147483648 | bytes 5242888 | tf_op jit(solution)/shard_map/pallas_call | solution.py:24
  78.5 1.6 %collective-permute-start.13 = (bf16[2,2,128,256]{3,2,1,0:T(8,128)(2,1)S(1)}, bf16[2,2,128,256]{3,2,1,0:T(8,128)(2,1)S(1)}, u32[]{:S(2)}, u32[]{:S(2)}) collective-permute-start(bf16[2,2,128,256]{3,2,1,0:T(8,128)(2,1)S(1)} %get-tuple-element.50), channel_id=1, source_target_pairs={{0,4},{2,6},{4,0},{6,2},{8,12},{10,14},{12,8},{14,10},{16,20},{18,... | collective-permute-start | bytes 786440 | tf_op jit(solution)/shard_map/ppermute | solution.py:250
  80.1 1.9 %collective-permute-start.15 = (bf16[2,2,128,256]{3,2,1,0:T(8,128)(2,1)S(1)}, bf16[2,2,128,256]{3,2,1,0:T(8,128)(2,1)S(1)}, u32[]{:S(2)}, u32[]{:S(2)}) collective-permute-start(bf16[2,2,128,256]{3,2,1,0:T(8,128)(2,1)S(1)} %get-tuple-element.52), channel_id=1, source_target_pairs={{0,12},{2,14},{4,8},{6,10},{8,4},{10,6},{12,0},{14,2},{16,28},{18,... | collective-permute-start | bytes 786440 | tf_op jit(solution)/shard_map/ppermute | solution.py:250
  82.0 1.6 %collective-permute-start.18 = (bf16[2,2,128,256]{3,2,1,0:T(8,128)(2,1)S(1)}, bf16[2,2,128,256]{3,2,1,0:T(8,128)(2,1)S(1)}, u32[]{:S(2)}, u32[]{:S(2)}) collective-permute-start(bf16[2,2,128,256]{3,2,1,0:T(8,128)(2,1)S(1)} %get-tuple-element.56), channel_id=1, source_target_pairs={{0,4},{2,6},{4,0},{6,2},{8,12},{10,14},{12,8},{14,10},{16,20},{18,... | collective-permute-start | bytes 786440 | tf_op jit(solution)/shard_map/ppermute | solution.py:250
  83.6 8.3 %collective-permute-done.13.refs_1_ = bf16[2,2,128,256]{3,2,1,0:T(8,128)(2,1)S(1)} collective-permute-done((bf16[2,2,128,256]{3,2,1,0:T(8,128)(2,1)S(1)}, bf16[2,2,128,256]{3,2,1,0:T(8,128)(2,1)S(1)}, u32[]{:S(2)}, u32[]{:S(2)}) %collective-permute-start.13) | collective-permute-done | bytes 262176 | tf_op jit(solution)/shard_map/ppermute | solution.py:250
  91.9 2.9 %collective-permute-done.15.refs_3_ = bf16[2,2,128,256]{3,2,1,0:T(8,128)(2,1)S(1)} collective-permute-done((bf16[2,2,128,256]{3,2,1,0:T(8,128)(2,1)S(1)}, bf16[2,2,128,256]{3,2,1,0:T(8,128)(2,1)S(1)}, u32[]{:S(2)}, u32[]{:S(2)}) %collective-permute-start.15) | collective-permute-done | bytes 262176 | tf_op jit(solution)/shard_map/ppermute | solution.py:250
  95.0 3.1 %collective-permute-done.18.refs_1_ = bf16[2,2,128,256]{3,2,1,0:T(8,128)(2,1)S(1)} collective-permute-done((bf16[2,2,128,256]{3,2,1,0:T(8,128)(2,1)S(1)}, bf16[2,2,128,256]{3,2,1,0:T(8,128)(2,1)S(1)}, u32[]{:S(2)}, u32[]{:S(2)}) %collective-permute-start.18) | collective-permute-done | bytes 262176 | tf_op jit(solution)/shard_map/ppermute | solution.py:250
  98.1 2.5 %collective-permute-done.19.refs_2_ = bf16[2,2,128,256]{3,2,1,0:T(8,128)(2,1)S(1)} collective-permute-done((bf16[2,2,128,256]{3,2,1,0:T(8,128)(2,1)S(1)}, bf16[2,2,128,256]{3,2,1,0:T(8,128)(2,1)S(1)}, u32[]{:S(2)}, u32[]{:S(2)}) %collective-permute-start.19) | collective-permute-done | bytes 262176 | tf_op jit(solution)/shard_map/ppermute | solution.py:250
  100.6 3.1 %collective-permute-done.20.refs_3_ = bf16[2,2,128,256]{3,2,1,0:T(8,128)(2,1)S(1)} collective-permute-done((bf16[2,2,128,256]{3,2,1,0:T(8,128)(2,1)S(1)}, bf16[2,2,128,256]{3,2,1,0:T(8,128)(2,1)S(1)}, u32[]{:S(2)}, u32[]{:S(2)}) %collective-permute-start.20) | collective-permute-done | bytes 262176 | tf_op jit(solution)/shard_map/ppermute | solution.py:250
  103.8 2.1 %shard_map.63 = (f32[2,128,512]{2,1,0:T(8,128)S(1)}, bf16[2,128,512]{2,1,0:T(8,128)(2,1)S(1)}) custom-call(s32[8,2]{1,0:T(8,128)S(1)} %copy.10.corner_ref, s32[1]{0:T(128)} %bitcast.place_ref, s32[2]{0:T(128)S(1)} %pad_add_fusion.pick_ref, bf16[8,2,256,256]{3,2,1,0:T(8,128)(2,1)S(1)} %shard_map.60.wave_ref, ...), custom_call_target="tpu_custom_call" | custom-call | bytes 4456524 | tf_op jit(solution)/shard_map/pallas_call | solution.py:24
  105.9 1.6 %collective-permute-start.17 = (bf16[2,128,512]{2,1,0:T(8,128)(2,1)S(1)}, bf16[2,128,512]{2,1,0:T(8,128)(2,1)S(1)}, u32[]{:S(2)}, u32[]{:S(2)}) collective-permute-start(bf16[2,128,512]{2,1,0:T(8,128)(2,1)S(1)} %get-tuple-element.54), channel_id=1, source_target_pairs={{0,1},{1,0},{2,3},{3,2},{4,5},{5,4},{6,7},{7,6},{8,9},{9,8},{10,11... | collective-permute-start | bytes 786440 | tf_op jit(solution)/shard_map/ppermute | solution.py:300
  107.6 2.1 %shard_map.65 = (f32[2,128,512]{2,1,0:T(8,128)S(1)}, bf16[2,128,512]{2,1,0:T(8,128)(2,1)S(1)}) custom-call(s32[8,2]{1,0:T(8,128)S(1)} %copy.10.corner_ref, s32[1]{0:T(128)} %bitcast.place_ref, s32[2]{0:T(128)S(1)} %pad_add_fusion.pick_ref, bf16[8,2,256,256]{3,2,1,0:T(8,128)(2,1)S(1)} %shard_map.60.wave_ref, ...), custom_call_target="tpu_custom_call" | custom-call | bytes 4456524 | tf_op jit(solution)/shard_map/pallas_call | solution.py:24
  110.2 4.9 %collective-permute-done.17.refs_1_ = bf16[2,128,512]{2,1,0:T(8,128)(2,1)S(1)} collective-permute-done((bf16[2,128,512]{2,1,0:T(8,128)(2,1)S(1)}, bf16[2,128,512]{2,1,0:T(8,128)(2,1)S(1)}, u32[]{:S(2)}, u32[]{:S(2)}) %collective-permute-start.17) | collective-permute-done | bytes 262176 | tf_op jit(solution)/shard_map/ppermute | solution.py:300
  115.1 5.2 %collective-permute-done.22.refs_3_ = bf16[2,128,512]{2,1,0:T(8,128)(2,1)S(1)} collective-permute-done((bf16[2,128,512]{2,1,0:T(8,128)(2,1)S(1)}, bf16[2,128,512]{2,1,0:T(8,128)(2,1)S(1)}, u32[]{:S(2)}, u32[]{:S(2)}) %collective-permute-start.22) | collective-permute-done | bytes 262176 | tf_op jit(solution)/shard_map/ppermute | solution.py:300
  (57 shorter events, 9.2 us)
Async XLA Ops:
  0.0 33.5 %copy-start.1 = (bf16[8,2,256,256]{3,2,1,0:T(8,128)(2,1)S(1)}, bf16[8,2,256,256]{3,2,1,0:T(8,128)(2,1)}, u32[]{:S(2)}) copy-start(bf16[8,2,256,256]{3,2,1,0:T(8,128)(2,1)} %exit_ref.1) | copy-start | bytes 6291460
  4.5 10.1 %collective-permute-start = (bf16[2,128,512]{2,1,0:T(8,128)(2,1)S(1)}, bf16[2,128,512]{2,1,0:T(8,128)(2,1)S(1)}, u32[]{:S(2)}, u32[]{:S(2)}) collective-permute-start(bf16[2,128,512]{2,1,0:T(8,128)(2,1)S(1)} %get-tuple-element.36.refs_0_), channel_id=1, source_target_pairs={{0,1},{1,0},{2,3},{3,2},{4,5},{5,4},{6,7},{7,6},{8,9},{9,8},{10,11... | collective-permute-start | bytes 786440 | tf_op jit(solution)/shard_map/ppermute | solution.py:266
  7.5 11.9 %collective-permute-start.3 = (bf16[2,128,512]{2,1,0:T(8,128)(2,1)S(1)}, bf16[2,128,512]{2,1,0:T(8,128)(2,1)S(1)}, u32[]{:S(2)}, u32[]{:S(2)}) collective-permute-start(bf16[2,128,512]{2,1,0:T(8,128)(2,1)S(1)} %get-tuple-element.38.refs_0_), channel_id=1, source_target_pairs={{0,1},{1,0},{2,3},{3,2},{4,5},{5,4},{6,7},{7,6},{8,9},{9,8},{10,11... | collective-permute-start | bytes 786440 | tf_op jit(solution)/shard_map/ppermute | solution.py:266
  7.5 11.9 %collective-permute-start.1 = (bf16[2,128,512]{2,1,0:T(8,128)(2,1)S(1)}, bf16[2,128,512]{2,1,0:T(8,128)(2,1)}, u32[]{:S(2)}, u32[]{:S(2)}) collective-permute-start(bf16[2,128,512]{2,1,0:T(8,128)(2,1)S(1)} %get-tuple-element.36.refs_0_), channel_id=1, source_target_pairs={{0,2},{2,0},{4,6},{6,4},{8,10},{10,8},{12,14},{14,12},{16,18},{18,... | collective-permute-start | bytes 786440 | tf_op jit(solution)/shard_map/ppermute | solution.py:250
  14.6 4.8 %collective-permute-start.2 = (bf16[2,128,512]{2,1,0:T(8,128)(2,1)S(1)}, bf16[2,128,512]{2,1,0:T(8,128)(2,1)}, u32[]{:S(2)}, u32[]{:S(2)}) collective-permute-start(bf16[2,128,512]{2,1,0:T(8,128)(2,1)S(1)} %collective-permute-done.refs_1_), channel_id=1, source_target_pairs={{0,2},{2,0},{4,6},{6,4},{8,10},{10,8},{12,14},{14,12},{16,18},{18,... | collective-permute-start | bytes 786440 | tf_op jit(solution)/shard_map/ppermute | solution.py:250
  14.6 10.6 %collective-permute-start.4 = (bf16[2,128,512]{2,1,0:T(8,128)(2,1)S(1)}, bf16[2,128,512]{2,1,0:T(8,128)(2,1)S(1)}, u32[]{:S(2)}, u32[]{:S(2)}) collective-permute-start(bf16[2,128,512]{2,1,0:T(8,128)(2,1)S(1)} %get-tuple-element.38.refs_0_), channel_id=1, source_target_pairs={{0,2},{2,0},{4,6},{6,4},{8,10},{10,8},{12,14},{14,12},{16,18},{18,... | collective-permute-start | bytes 786440 | tf_op jit(solution)/shard_map/ppermute | solution.py:250
  19.4 5.8 %collective-permute-start.5 = (bf16[2,128,512]{2,1,0:T(8,128)(2,1)S(1)}, bf16[2,128,512]{2,1,0:T(8,128)(2,1)S(1)}, u32[]{:S(2)}, u32[]{:S(2)}) collective-permute-start(bf16[2,128,512]{2,1,0:T(8,128)(2,1)S(1)} %collective-permute-done.3.refs_1_), channel_id=1, source_target_pairs={{0,2},{2,0},{4,6},{6,4},{8,10},{10,8},{12,14},{14,12},{16,18},{18,... | collective-permute-start | bytes 786440 | tf_op jit(solution)/shard_map/ppermute | solution.py:250
  21.6 33.5 %copy-start.4 = (bf16[2,2,128,256]{3,2,1,0:T(8,128)(2,1)}, bf16[2,2,128,256]{3,2,1,0:T(8,128)(2,1)S(1)}, u32[]{:S(2)}) copy-start(bf16[2,2,128,256]{3,2,1,0:T(8,128)(2,1)S(1)} %get-tuple-element.37.refs_0_) | copy-start | bytes 786436
  21.6 9.2 %collective-permute-start.6 = (bf16[2,2,128,256]{3,2,1,0:T(8,128)(2,1)S(1)}, bf16[2,2,128,256]{3,2,1,0:T(8,128)(2,1)S(1)}, u32[]{:S(2)}, u32[]{:S(2)}) collective-permute-start(bf16[2,2,128,256]{3,2,1,0:T(8,128)(2,1)S(1)} %get-tuple-element.40), channel_id=1, source_target_pairs={{0,4},{2,6},{4,0},{6,2},{8,12},{10,14},{12,8},{14,10},{16,20},{18,... | collective-permute-start | bytes 786440 | tf_op jit(solution)/shard_map/ppermute | solution.py:250
  23.4 11.4 %collective-permute-start.8 = (bf16[2,2,128,256]{3,2,1,0:T(8,128)(2,1)S(1)}, bf16[2,2,128,256]{3,2,1,0:T(8,128)(2,1)S(1)}, u32[]{:S(2)}, u32[]{:S(2)}) collective-permute-start(bf16[2,2,128,256]{3,2,1,0:T(8,128)(2,1)S(1)} %get-tuple-element.42), channel_id=1, source_target_pairs={{0,8},{2,10},{4,12},{6,14},{8,0},{10,2},{12,4},{14,6},{16,24},{18,... | collective-permute-start | bytes 786440 | tf_op jit(solution)/shard_map/ppermute | solution.py:250
  25.0 12.9 %collective-permute-start.10 = (bf16[2,2,128,256]{3,2,1,0:T(8,128)(2,1)S(1)}, bf16[2,2,128,256]{3,2,1,0:T(8,128)(2,1)S(1)}, u32[]{:S(2)}, u32[]{:S(2)}) collective-permute-start(bf16[2,2,128,256]{3,2,1,0:T(8,128)(2,1)S(1)} %get-tuple-element.44), channel_id=1, source_target_pairs={{0,12},{2,14},{4,8},{6,10},{8,4},{10,6},{12,0},{14,2},{16,28},{18,... | collective-permute-start | bytes 786440 | tf_op jit(solution)/shard_map/ppermute | solution.py:250
  26.3 28.8 %copy-start.8 = (bf16[2,2,128,256]{3,2,1,0:T(8,128)(2,1)}, bf16[2,2,128,256]{3,2,1,0:T(8,128)(2,1)S(1)}, u32[]{:S(2)}) copy-start(bf16[2,2,128,256]{3,2,1,0:T(8,128)(2,1)S(1)} %get-tuple-element.39.refs_1_) | copy-start | bytes 786436
  26.3 15.3 %collective-permute-start.7 = (bf16[2,2,128,256]{3,2,1,0:T(8,128)(2,1)S(1)}, bf16[2,2,128,256]{3,2,1,0:T(8,128)(2,1)S(1)}, u32[]{:S(2)}, u32[]{:S(2)}) collective-permute-start(bf16[2,2,128,256]{3,2,1,0:T(8,128)(2,1)S(1)} %get-tuple-element.41), channel_id=1, source_target_pairs={{0,4},{2,6},{4,0},{6,2},{8,12},{10,14},{12,8},{14,10},{16,20},{18,... | collective-permute-start | bytes 786440 | tf_op jit(solution)/shard_map/ppermute | solution.py:250
  28.2 15.7 %collective-permute-start.9 = (bf16[2,2,128,256]{3,2,1,0:T(8,128)(2,1)S(1)}, bf16[2,2,128,256]{3,2,1,0:T(8,128)(2,1)S(1)}, u32[]{:S(2)}, u32[]{:S(2)}) collective-permute-start(bf16[2,2,128,256]{3,2,1,0:T(8,128)(2,1)S(1)} %get-tuple-element.43), channel_id=1, source_target_pairs={{0,8},{2,10},{4,12},{6,14},{8,0},{10,2},{12,4},{14,6},{16,24},{18,... | collective-permute-start | bytes 786440 | tf_op jit(solution)/shard_map/ppermute | solution.py:250
  30.8 17.8 %collective-permute-start.11 = (bf16[2,2,128,256]{3,2,1,0:T(8,128)(2,1)S(1)}, bf16[2,2,128,256]{3,2,1,0:T(8,128)(2,1)S(1)}, u32[]{:S(2)}, u32[]{:S(2)}) collective-permute-start(bf16[2,2,128,256]{3,2,1,0:T(8,128)(2,1)S(1)} %get-tuple-element.45), channel_id=1, source_target_pairs={{0,12},{2,14},{4,8},{6,10},{8,4},{10,6},{12,0},{14,2},{16,28},{18,... | collective-permute-start | bytes 786440 | tf_op jit(solution)/shard_map/ppermute | solution.py:250
  34.8 20.3 %copy-start.10 = (bf16[2,256,256]{2,1,0:T(8,128)(2,1)}, bf16[2,256,256]{2,1,0:T(8,128)(2,1)S(1)}, u32[]{:S(2)}) copy-start(bf16[2,256,256]{2,1,0:T(8,128)(2,1)S(1)} %get-tuple-element.33.start_ref.come_ref) | copy-start | bytes 786436
  34.8 20.3 %copy-start.12 = (bf16[256,256]{1,0:T(8,128)(2,1)}, bf16[256,256]{1,0:T(8,128)(2,1)S(1)}, u32[]{:S(2)}) copy-start(bf16[256,256]{1,0:T(8,128)(2,1)S(1)} %get-tuple-element.35.across_ref) | copy-start | bytes 393220
  37.9 17.2 %copy-start.6 = (bf16[2,2,128,256]{3,2,1,0:T(8,128)(2,1)}, bf16[2,2,128,256]{3,2,1,0:T(8,128)(2,1)S(1)}, u32[]{:S(2)}) copy-start(bf16[2,2,128,256]{3,2,1,0:T(8,128)(2,1)S(1)} %collective-permute-done.10.refs_6_) | copy-start | bytes 786436
  55.1 16.4 %collective-permute-start.12 = (bf16[2,256,256]{2,1,0:T(8,128)(2,1)}, bf16[2,256,256]{2,1,0:T(8,128)(2,1)}, u32[]{:S(2)}, u32[]{:S(2)}) collective-permute-start(bf16[2,256,256]{2,1,0:T(8,128)(2,1)} %get-tuple-element.46), channel_id=1, source_target_pairs={{16,0},{18,2},{20,4},{22,6},{24,8},{26,10},{28,12},{30,14},{17,1},... | collective-permute-start | bytes 786440 | tf_op jit(solution)/shard_map/ppermute | solution.py:288
  56.6 14.9 %copy-start.5 = (bf16[2,2,128,256]{3,2,1,0:T(8,128)(2,1)S(1)}, bf16[2,2,128,256]{3,2,1,0:T(8,128)(2,1)}, u32[]{:S(2)}) copy-start(bf16[2,2,128,256]{3,2,1,0:T(8,128)(2,1)} %copy-done.4) | copy-start | bytes 786436
  56.7 14.9 %copy-start.7 = (bf16[2,2,128,256]{3,2,1,0:T(8,128)(2,1)S(1)}, bf16[2,2,128,256]{3,2,1,0:T(8,128)(2,1)}, u32[]{:S(2)}) copy-start(bf16[2,2,128,256]{3,2,1,0:T(8,128)(2,1)} %copy-done.6) | copy-start | bytes 786436
  56.7 14.9 %copy-start.9 = (bf16[2,2,128,256]{3,2,1,0:T(8,128)(2,1)S(1)}, bf16[2,2,128,256]{3,2,1,0:T(8,128)(2,1)}, u32[]{:S(2)}) copy-start(bf16[2,2,128,256]{3,2,1,0:T(8,128)(2,1)} %copy-done.8) | copy-start | bytes 786436
  78.5 13.4 %collective-permute-start.13 = (bf16[2,2,128,256]{3,2,1,0:T(8,128)(2,1)S(1)}, bf16[2,2,128,256]{3,2,1,0:T(8,128)(2,1)S(1)}, u32[]{:S(2)}, u32[]{:S(2)}) collective-permute-start(bf16[2,2,128,256]{3,2,1,0:T(8,128)(2,1)S(1)} %get-tuple-element.50), channel_id=1, source_target_pairs={{0,4},{2,6},{4,0},{6,2},{8,12},{10,14},{12,8},{14,10},{16,20},{18,... | collective-permute-start | bytes 786440 | tf_op jit(solution)/shard_map/ppermute | solution.py:250
  80.1 11.8 %collective-permute-start.14 = (bf16[2,2,128,256]{3,2,1,0:T(8,128)(2,1)S(1)}, bf16[2,2,128,256]{3,2,1,0:T(8,128)(2,1)S(1)}, u32[]{:S(2)}, u32[]{:S(2)}) collective-permute-start(bf16[2,2,128,256]{3,2,1,0:T(8,128)(2,1)S(1)} %get-tuple-element.51), channel_id=1, source_target_pairs={{0,8},{2,10},{4,12},{6,14},{8,0},{10,2},{12,4},{14,6},{16,24},{18,... | collective-permute-start | bytes 786440 | tf_op jit(solution)/shard_map/ppermute | solution.py:250
  80.1 14.8 %collective-permute-start.15 = (bf16[2,2,128,256]{3,2,1,0:T(8,128)(2,1)S(1)}, bf16[2,2,128,256]{3,2,1,0:T(8,128)(2,1)S(1)}, u32[]{:S(2)}, u32[]{:S(2)}) collective-permute-start(bf16[2,2,128,256]{3,2,1,0:T(8,128)(2,1)S(1)} %get-tuple-element.52), channel_id=1, source_target_pairs={{0,12},{2,14},{4,8},{6,10},{8,4},{10,6},{12,0},{14,2},{16,28},{18,... | collective-permute-start | bytes 786440 | tf_op jit(solution)/shard_map/ppermute | solution.py:250
  82.0 16.1 %collective-permute-start.18 = (bf16[2,2,128,256]{3,2,1,0:T(8,128)(2,1)S(1)}, bf16[2,2,128,256]{3,2,1,0:T(8,128)(2,1)S(1)}, u32[]{:S(2)}, u32[]{:S(2)}) collective-permute-start(bf16[2,2,128,256]{3,2,1,0:T(8,128)(2,1)S(1)} %get-tuple-element.56), channel_id=1, source_target_pairs={{0,4},{2,6},{4,0},{6,2},{8,12},{10,14},{12,8},{14,10},{16,20},{18,... | collective-permute-start | bytes 786440 | tf_op jit(solution)/shard_map/ppermute | solution.py:250
  83.6 17.0 %collective-permute-start.19 = (bf16[2,2,128,256]{3,2,1,0:T(8,128)(2,1)S(1)}, bf16[2,2,128,256]{3,2,1,0:T(8,128)(2,1)S(1)}, u32[]{:S(2)}, u32[]{:S(2)}) collective-permute-start(bf16[2,2,128,256]{3,2,1,0:T(8,128)(2,1)S(1)} %get-tuple-element.57), channel_id=1, source_target_pairs={{0,8},{2,10},{4,12},{6,14},{8,0},{10,2},{12,4},{14,6},{16,24},{18,... | collective-permute-start | bytes 786440 | tf_op jit(solution)/shard_map/ppermute | solution.py:250
  91.9 11.7 %collective-permute-start.20 = (bf16[2,2,128,256]{3,2,1,0:T(8,128)(2,1)S(1)}, bf16[2,2,128,256]{3,2,1,0:T(8,128)(2,1)S(1)}, u32[]{:S(2)}, u32[]{:S(2)}) collective-permute-start(bf16[2,2,128,256]{3,2,1,0:T(8,128)(2,1)S(1)} %get-tuple-element.58), channel_id=1, source_target_pairs={{0,12},{2,14},{4,8},{6,10},{8,4},{10,6},{12,0},{14,2},{16,28},{18,... | collective-permute-start | bytes 786440 | tf_op jit(solution)/shard_map/ppermute | solution.py:250
  94.9 8.9 %collective-permute-start.16 = (bf16[4,2,128,256]{3,2,1,0:T(8,128)(2,1)S(1)}, bf16[4,2,128,256]{3,2,1,0:T(8,128)(2,1)S(1)}, u32[]{:S(2)}, u32[]{:S(2)}) collective-permute-start(bf16[4,2,128,256]{3,2,1,0:T(8,128)(2,1)S(1)} %shard_map.62), channel_id=1, source_target_pairs={{0,2},{2,0},{4,6},{6,4},{8,10},{10,8},{12,14},{14,12},{16,18},{18,... | collective-permute-start | bytes 1572872 | tf_op jit(solution)/shard_map/ppermute | solution.py:250
  103.7 3.9 %collective-permute-start.21 = (bf16[4,2,128,256]{3,2,1,0:T(8,128)(2,1)S(1)}, bf16[4,2,128,256]{3,2,1,0:T(8,128)(2,1)S(1)}, u32[]{:S(2)}, u32[]{:S(2)}) collective-permute-start(bf16[4,2,128,256]{3,2,1,0:T(8,128)(2,1)S(1)} %shard_map.64), channel_id=1, source_target_pairs={{0,2},{2,0},{4,6},{6,4},{8,10},{10,8},{12,14},{14,12},{16,18},{18,... | collective-permute-start | bytes 1572872 | tf_op jit(solution)/shard_map/ppermute | solution.py:250
  105.9 9.2 %collective-permute-start.17 = (bf16[2,128,512]{2,1,0:T(8,128)(2,1)S(1)}, bf16[2,128,512]{2,1,0:T(8,128)(2,1)S(1)}, u32[]{:S(2)}, u32[]{:S(2)}) collective-permute-start(bf16[2,128,512]{2,1,0:T(8,128)(2,1)S(1)} %get-tuple-element.54), channel_id=1, source_target_pairs={{0,1},{1,0},{2,3},{3,2},{4,5},{5,4},{6,7},{7,6},{8,9},{9,8},{10,11... | collective-permute-start | bytes 786440 | tf_op jit(solution)/shard_map/ppermute | solution.py:300
  109.7 10.6 %collective-permute-start.22 = (bf16[2,128,512]{2,1,0:T(8,128)(2,1)S(1)}, bf16[2,128,512]{2,1,0:T(8,128)(2,1)S(1)}, u32[]{:S(2)}, u32[]{:S(2)}) collective-permute-start(bf16[2,128,512]{2,1,0:T(8,128)(2,1)S(1)} %get-tuple-element.60), channel_id=1, source_target_pairs={{0,1},{1,0},{2,3},{3,2},{4,5},{5,4},{6,7},{7,6},{8,9},{9,8},{10,11... | collective-permute-start | bytes 786440 | tf_op jit(solution)/shard_map/ppermute | solution.py:300
  (5 other events, 40.2 us)

commit v5 on v4

--- a/solution.py
+++ b/solution.py
@@ -17,41 +17,29 @@
 bf16 = jnp.bfloat16
 
 
-def call(kernel, out_shape, prefetch=0, scratch=(), flops=0, grant=12, space=pltpu.VMEM):
+def call(kernel, out_shape, prefetch=0, scratch=(), cost=1, grant=12):
     def run(*args):
-        moved = sum(a.size * a.dtype.itemsize for a in jax.tree.leaves((args, out_shape)))
         vmem = pl.BlockSpec(memory_space=pltpu.VMEM)
         return pl.pallas_call(
             kernel,
             grid_spec=pltpu.PrefetchScalarGridSpec(
                 num_scalar_prefetch=prefetch,
                 grid=(1,),
-                in_specs=[pl.BlockSpec(memory_space=space)] * (len(args) - prefetch),
+                in_specs=[vmem] * (len(args) - prefetch),
                 out_specs=jax.tree.map(lambda _: vmem, out_shape),
                 scratch_shapes=list(scratch),
             ),
             out_shape=out_shape,
-            cost_estimate=pl.CostEstimate(flops=flops, bytes_accessed=moved, transcendentals=0),
+            cost_estimate=pl.CostEstimate(flops=cost, bytes_accessed=cost, transcendentals=0),
             compiler_params=pltpu.CompilerParams(vmem_limit_bytes=grant * 2**20),
         )(*args)
 
     return run
 
 
-def code_kernel(amp_hbm, phase_hbm, *refs):
-    *code_refs, amp_ref, phase_ref, sems = refs
+def code_kernel(amp_ref, phase_ref, *code_refs):
     rows = code_refs[0].shape[1]
-    copies = []
-    for piece in range(sems.shape[0]):
-        tall = amp_ref.shape[0] // sems.shape[0]
-        here = pl.ds(piece * tall, tall)
-        for side, (source, target) in enumerate(((amp_hbm, amp_ref), (phase_hbm, phase_ref))):
-            copies.append(pltpu.make_async_copy(source.at[here], target.at[here], sems.at[piece, side]))
-            copies[-1].start()
-    share = len(copies) // len(code_refs)
     for chunk, code_ref in enumerate(code_refs):
-        for copy in copies[chunk * share : (chunk + 1) * share]:
-            copy.wait()
         amp = amp_ref[pl.ds(chunk * rows, rows), :]
         half = 0.5 * phase_ref[pl.ds(chunk * rows, rows), :]
         square = half * half
@@ -145,16 +133,30 @@
     return spread_re, spread_im
 
 
-def group_kernel(pick_ref, start_ref, come_ref, down_ref, across_ref, *refs):
-    win_refs, refs = refs[: len(refs) // 2 - 1], refs[len(refs) // 2 - 1 :]
-    *spread_refs, leave_ref, held_ref, kept_ref = refs
+def group_kernel(pick_ref, start_ref, come_ref, down_ref, across_ref, token_ref, *refs):
+    *refs, leave_ref, held_ref, kept_ref = refs
     count, _, window, _ = held_ref.shape
     rows = window // chunk_count
+    here_refs = refs[:chunk_count]
+    far = (count // 2 - 1) * chunk_count
+    spread_refs = refs[chunk_count + 2 * far :]
     own = pick_ref[0]
-    for apart in range(count):
+
+    def hold(apart, chunk, ref):
+        held_ref[own ^ apart, :, pl.ds(chunk * rows, rows)] = ref[apart % 2]
+
+    for apart in range(2):
         for chunk in range(chunk_count):
-            here = slice(chunk * rows, (chunk + 1) * rows)
-            held_ref[own ^ apart, :, here] = win_refs[apart // 2 * chunk_count + chunk][apart % 2]
+            hold(apart, chunk, here_refs[chunk])
+    for core in range(2):
+
+        @pl.when(lax.rem(own, 2) == core)
+        def _(core=core):
+            came_refs = refs[chunk_count + core * far : chunk_count + (core + 1) * far]
+            for apart in range(2, count):
+                for chunk in range(chunk_count):
+                    hold(apart, chunk, came_refs[(apart // 2 - 1) * chunk_count + chunk])
+
     down = down_ref[...]
     across = across_ref[...]
     at_end = jnp.full(start_ref.shape[1:], pick_ref[1], jnp.int32) == 1
@@ -246,27 +248,35 @@
     wave = (2, window, window)
     chips = range(count // 2)
 
-    def to_partner(value, distance):
-        return lax.ppermute(value, "sec", [(s, s ^ distance) for s in range(sections)])
+    def to_partner(value, distance, core=None):
+        senders = [s for s in range(sections) if core is None or s % 2 == core]
+        return lax.ppermute(value, "sec", [(s, s ^ distance) for s in senders])
 
     def exchange(values):
         return [to_partner(values[d], 2 * d) if d else values[0] for d in chips]
 
     own = section % count
     pick = jnp.stack([own, jnp.int32(1)])
-    code = call(
-        code_kernel,
-        [shape_of(piece, bf16)] * chunk_count,
-        scratch=[pltpu.VMEM((half, width), f32)] * 2 + [pltpu.SemaphoreType.DMA((8, 2))],
-        space=pltpu.HBM,
-    )
-    mine = code(obj_amp[0], obj_phase[0])
-    windows = []
+    mine = call(code_kernel, [shape_of(piece, bf16)] * chunk_count)(obj_amp[0], obj_phase[0])
+    others = [lax.ppermute(mine[c], "scan", swap) for c in chunks]
+    beside = [to_partner(mine[c], 1) for c in chunks]
+    cuts = []
     for c in chunks:
-        other = lax.ppermute(mine[c], "scan", swap)
-        slices = [mine[c], other, to_partner(mine[c], 1), to_partner(other, 1)]
+        slices = [mine[c], others[c], beside[c], to_partner(others[c], 1)]
         cut = call(functools.partial(cut_kernel, c * rows), [shape_of(part, bf16)] * len(chips), prefetch=3)
-        windows.append(exchange(cut(offsets, place, pick, *slices)))
+        cuts.append(cut(offsets, place, pick, *slices))
+        if c < chunk_count - 1:
+            others[c + 1], cuts[c] = lax.optimization_barrier((others[c + 1], cuts[c]))
+
+    windows = [[[to_partner(cuts[c][d], 2 * d, 0) for c in chunks] for d in chips[1:]]]
+    *most, last = jax.tree.leaves(windows)
+    most = lax.optimization_barrier(most)
+    windows = [most + [last]]
+    token = lax.slice(most[0], (0, 0, 0, 0), (1, 1, 16, 128))
+    token = lax.ppermute(token, "sec", [(s, s + 1) for s in range(0, sections, 2)])
+    cuts, token = lax.optimization_barrier((cuts, token))
+    windows.append([[to_partner(cuts[c][d], 2 * d, 1) for c in chunks] for d in chips[1:]])
+    stage_windows = [cuts[c][0] for c in chunks] + jax.tree.leaves(windows)
     ready = call(ready_kernel, [shape_of(wave, bf16)] + [shape_of((window, window), bf16)] * 2, prefetch=2)
     start, down, across = ready(offsets, pick, exit_adjoint)
     waves = call(turn_kernel, shape_of(forward_waves.shape[1:], bf16), prefetch=1)(offsets, forward_waves[0])
@@ -278,12 +288,10 @@
         [shape_of(part, bf16)] * (chunk_count * len(chips)) + [shape_of(wave, bf16)],
         prefetch=1,
         scratch=[pltpu.VMEM((count,) + wave, bf16)] * 2,
-        flops=count * 8 * 2 * window**3,
         grant=20,
     )
-    stage_windows = [windows[c][d] for d in chips for c in chunks]
     for stage in range(group_count):
-        *spreads, leave = through(pick, start, come, down, across, *stage_windows)
+        *spreads, leave = through(pick, start, come, down, across, token, *stage_windows)
         if stage < group_count - 1:
             come = lax.ppermute(leave, "sec", [(s, s - count) for s in range(count, sections)])
             come, waves = lax.optimization_barrier((come, waves))
@@ -292,12 +300,15 @@
     came = [exchange(spreads[c::chunk_count]) for c in chunks]
     sums = []
     for c in chunks:
+        if c > 0:
+            came[c], sums = lax.optimization_barrier((came[c], sums))
         passed = to_partner(call(pass_kernel, shape_of((len(chips), 2, rows, window), bf16))(*came[c]), 1)
         gradient = call(
             functools.partial(gradient_kernel, c * rows), [shape_of(piece, f32), shape_of(piece, bf16)], prefetch=3
         )
         keep, away = gradient(offsets, place, pick, waves, *came[c], passed)
-        sums += [keep, lax.ppermute(away, "scan", swap)]
+        sums += [keep, away]
+    sums[1::2] = [lax.ppermute(away, "scan", swap) for away in sums[1::2]]
     return call(finish_kernel, shape_of((2, half, width), f32))(*sums)[None]
 
 

time: 122 us -> 145 us (1.19)
  starting transfers between devices: 22.2 us -> 49.9 us
  waiting for transfers between devices: 67.6 us -> 51.5 us
  local copies, waits for them, and re-layouts: 3.04 us -> 15.1 us
    ppermute x22 -> x29, starting transfers between devices: 20.7 us -> 48.6 us  [the longest x24 39.5 us: to_partner(): return lax.ppermute(value, 'sec', [(s, s ^ distance) for s in senders])]
    ppermute x22 -> x29, waiting for transfers between devices: 55.3 us -> 43.1 us  [the longest x24 24.8 us: to_partner(): return lax.ppermute(value, 'sec', [(s, s ^ distance) for s in senders])]
    unnamed x29 -> x57, local copies, waits for them, and re-layouts: 3.04 us -> 15.1 us
    ppermute x1, waiting for transfers between devices: 12.3 us -> 8.37 us  [on_device(): lax.ppermute(leave, 'sec', [(s, s - count) for s in range(count, sections)])]
  transfers between devices with their start and end apart: 23 -> 30, of which waited for: 15 -> 15; matrix products, arithmetic and copies ran while one was open for 1% -> 1% of each run, Pallas kernels for 9% -> 8%
where the time goes in v5:
time: 145 us; the launch traced here: 144 us
  waiting for transfers between devices  51.5 us (36%)
  starting transfers between devices  49.9 us (34%)
  Pallas kernels  26.9 us (19%)
  local copies, waits for them, and re-layouts  15.1 us (10%)
    ppermute x24, starting transfers between devices, to_partner(): return lax.ppermute(value, 'sec', [(s, s ^ distance) for s in senders])  39.5 us
    pallas_call x12, Pallas kernels, run(): pl.pallas_call(kernel, grid_spec=pltpu.PrefetchScalarGridSpec(num_scalar_...  26.9 us
    ppermute x24, waiting for transfers between devices, to_partner(): return lax.ppermute(value, 'sec', [(s, s ^ distance) for s in senders])  24.8 us
    unnamed x57, local copies, waits for them, and re-layouts  15.1 us
    ppermute x2, waiting for transfers between devices, on_device(): others = [lax.ppermute(mine[c], 'scan', swap) for c in chunks]  9.51 us
    ppermute x2, waiting for transfers between devices, on_device(): sums[1::2] = [lax.ppermute(away, 'scan', swap) for away in sums[1::2]]  8.77 us
    ppermute x1, waiting for transfers between devices, on_device(): lax.ppermute(leave, 'sec', [(s, s - count) for s in range(count, sections)])  8.37 us
    ppermute x2, starting transfers between devices, on_device(): others = [lax.ppermute(mine[c], 'scan', swap) for c in chunks]  4.74 us
  transfers between devices with their start and end apart: 30, of which 15 were waited for; matrix products, arithmetic and copies ran while one was open for 1% of the time, Pallas kernels for 8%

profile of v5, /device:TPU:0, one launch (start us, length us, event | category | flops | bytes accessed | tf_op | source)
XLA Modules:
  0.0 144.0 jit_solution(4336737855217890169)
XLA Ops:
  3.0 3.0 %collective-permute-start.1 = (bf16[2,128,512]{2,1,0:T(8,128)(2,1)S(1)}, bf16[2,128,512]{2,1,0:T(8,128)(2,1)S(1)}, u32[]{:S(2)}, u32[]{:S(2)}) collective-permute-start(bf16[2,128,512]{2,1,0:T(8,128)(2,1)S(1)} %get-tuple-element.62.refs_0_), channel_id=1, source_target_pairs={{0,1},{1,0},{2,3},{3,2},{4,5},{5,4},{6,7},{7,6},{8,9},{9,8},{10,11... | collective-permute-start | bytes 786440 | tf_op jit(solution)/shard_map/ppermute | solution.py:261
  6.0 6.3 %collective-permute-done.1.refs_1_ = bf16[2,128,512]{2,1,0:T(8,128)(2,1)S(1)} collective-permute-done((bf16[2,128,512]{2,1,0:T(8,128)(2,1)S(1)}, bf16[2,128,512]{2,1,0:T(8,128)(2,1)S(1)}, u32[]{:S(2)}, u32[]{:S(2)}) %collective-permute-start.1) | collective-permute-done | bytes 262176 | tf_op jit(solution)/shard_map/ppermute | solution.py:261
  12.3 1.7 %collective-permute-start = (bf16[2,128,512]{2,1,0:T(8,128)(2,1)S(1)}, bf16[2,128,512]{2,1,0:T(8,128)(2,1)}, u32[]{:S(2)}, u32[]{:S(2)}) collective-permute-start(bf16[2,128,512]{2,1,0:T(8,128)(2,1)S(1)} %get-tuple-element.61.refs_0_), channel_id=1, source_target_pairs={{0,1},{1,0},{2,3},{3,2},{4,5},{5,4},{6,7},{7,6},{8,9},{9,8},{10,11... | collective-permute-start | bytes 786440 | tf_op jit(solution)/shard_map/ppermute | solution.py:261
  17.9 3.2 %collective-permute-done.refs_1_ = bf16[2,128,512]{2,1,0:T(8,128)(2,1)} collective-permute-done((bf16[2,128,512]{2,1,0:T(8,128)(2,1)S(1)}, bf16[2,128,512]{2,1,0:T(8,128)(2,1)}, u32[]{:S(2)}, u32[]{:S(2)}) %collective-permute-start) | collective-permute-done | bytes 262176 | tf_op jit(solution)/shard_map/ppermute | solution.py:261
  21.1 3.7 %collective-permute-start.6 = (bf16[2,2,128,256]{3,2,1,0:T(8,128)(2,1)S(1)}, bf16[2,2,128,256]{3,2,1,0:T(8,128)(2,1)S(1)}, u32[]{:S(2)}, u32[]{:S(2)}) collective-permute-start(bf16[2,2,128,256]{3,2,1,0:T(8,128)(2,1)S(1)} %get-tuple-element.84), channel_id=1, source_target_pairs={{0,4},{4,0},{8,12},{12,8},{16,20},{20,16},{24,28},{28,24},{1,5},{5... | collective-permute-start | bytes 786440 | tf_op jit(solution)/shard_map/ppermute | solution.py:253
  24.8 3.5 %collective-permute-start.8 = (bf16[2,2,128,256]{3,2,1,0:T(8,128)(2,1)S(1)}, bf16[2,2,128,256]{3,2,1,0:T(8,128)(2,1)S(1)}, u32[]{:S(2)}, u32[]{:S(2)}) collective-permute-start(bf16[2,2,128,256]{3,2,1,0:T(8,128)(2,1)S(1)} %get-tuple-element.86), channel_id=1, source_target_pairs={{0,8},{4,12},{8,0},{12,4},{16,24},{20,28},{24,16},{28,20},{1,9},{5... | collective-permute-start | bytes 786440 | tf_op jit(solution)/shard_map/ppermute | solution.py:253
  28.3 2.1 %collective-permute-start.10 = (bf16[2,2,128,256]{3,2,1,0:T(8,128)(2,1)S(1)}, bf16[2,2,128,256]{3,2,1,0:T(8,128)(2,1)S(1)}, u32[]{:S(2)}, u32[]{:S(2)}) collective-permute-start(bf16[2,2,128,256]{3,2,1,0:T(8,128)(2,1)S(1)} %get-tuple-element.88), channel_id=1, source_target_pairs={{0,12},{4,8},{8,4},{12,0},{16,28},{20,24},{24,20},{28,16},{1,13},{... | collective-permute-start | bytes 786440 | tf_op jit(solution)/shard_map/ppermute | solution.py:253
  30.3 2.2 %shard_map.58 = (bf16[2,2,128,256]{3,2,1,0:T(8,128)(2,1)S(1)}, bf16[2,2,128,256]{3,2,1,0:T(8,128)(2,1)S(1)}, bf16[2,2,128,256]{3,2,1,0:T(8,128)(2,1)S(1)}, bf16[2,2,128,256]{3,2,1,0:T(8,128)(2,1)S(1)}) custom-call(s32[8,2]{1,0:T(8,128)S(1)} %copy.6.corner_ref, s32[1]{0:T(128)} %bitcast.4.place_ref, s32[2]{0:T(128)S(1)} %pad_add_fusion.1.pick_ref, ...), custom_call_target="tpu_custom_call" | custom-call | flops 1 | bytes 1 | tf_op jit(solution)/shard_map/pallas_call | solution.py:23
  32.5 3.7 %collective-permute-start.7 = (bf16[2,2,128,256]{3,2,1,0:T(8,128)(2,1)S(1)}, bf16[2,2,128,256]{3,2,1,0:T(8,128)(2,1)S(1)}, u32[]{:S(2)}, u32[]{:S(2)}) collective-permute-start(bf16[2,2,128,256]{3,2,1,0:T(8,128)(2,1)S(1)} %get-tuple-element.85), channel_id=1, source_target_pairs={{0,4},{4,0},{8,12},{12,8},{16,20},{20,16},{24,28},{28,24},{1,5},{5... | collective-permute-start | bytes 786440 | tf_op jit(solution)/shard_map/ppermute | solution.py:253
  36.2 3.5 %collective-permute-start.9 = (bf16[2,2,128,256]{3,2,1,0:T(8,128)(2,1)S(1)}, bf16[2,2,128,256]{3,2,1,0:T(8,128)(2,1)S(1)}, u32[]{:S(2)}, u32[]{:S(2)}) collective-permute-start(bf16[2,2,128,256]{3,2,1,0:T(8,128)(2,1)S(1)} %get-tuple-element.87), channel_id=1, source_target_pairs={{0,8},{4,12},{8,0},{12,4},{16,24},{20,28},{24,16},{28,20},{1,9},{5... | collective-permute-start | bytes 786440 | tf_op jit(solution)/shard_map/ppermute | solution.py:253
  40.8 3.7 %collective-permute-done.9.refs_5_ = bf16[2,2,128,256]{3,2,1,0:T(8,128)(2,1)S(1)} collective-permute-done((bf16[2,2,128,256]{3,2,1,0:T(8,128)(2,1)S(1)}, bf16[2,2,128,256]{3,2,1,0:T(8,128)(2,1)S(1)}, u32[]{:S(2)}, u32[]{:S(2)}) %collective-permute-start.9) | collective-permute-done | bytes 262176 | tf_op jit(solution)/shard_map/ppermute | solution.py:253
  45.8 3.4 %collective-permute-start.12 = (bf16[2,2,128,256]{3,2,1,0:T(8,128)(2,1)S(1)}, bf16[2,2,128,256]{3,2,1,0:T(8,128)(2,1)S(1)}, u32[]{:S(2)}, u32[]{:S(2)}) collective-permute-start(bf16[2,2,128,256]{3,2,1,0:T(8,128)(2,1)S(1)} %get-tuple-element.89), channel_id=1, source_target_pairs={{0,12},{4,8},{8,4},{12,0},{16,28},{20,24},{24,20},{28,16},{1,13},{... | collective-permute-start | bytes 786440 | tf_op jit(solution)/shard_map/ppermute | solution.py:253
  52.0 3.1 %collective-permute-done.12.refs_7_ = bf16[2,2,128,256]{3,2,1,0:T(8,128)(2,1)S(1)} collective-permute-done((bf16[2,2,128,256]{3,2,1,0:T(8,128)(2,1)S(1)}, bf16[2,2,128,256]{3,2,1,0:T(8,128)(2,1)S(1)}, u32[]{:S(2)}, u32[]{:S(2)}) %collective-permute-start.12) | collective-permute-done | bytes 262176 | tf_op jit(solution)/shard_map/ppermute | solution.py:253
  57.8 6.6 %shard_map.59 = (bf16[2,2,128,256]{3,2,1,0:T(8,128)(2,1)}, bf16[2,2,128,256]{3,2,1,0:T(8,128)(2,1)}, bf16[2,2,128,256]{3,2,1,0:T(8,128)(2,1)}, bf16[2,2,128,256]...) custom-call(s32[2]{0:T(128)S(1)} %pad_add_fusion.1.pick_ref, ...), custom_call_target="tpu_custom_call" | custom-call | flops 1 | bytes 1 | tf_op jit(solution)/shard_map/pallas_call | solution.py:23
  65.9 2.5 %shard_map.60.wave_ref = bf16[8,2,256,256]{3,2,1,0:T(8,128)(2,1)S(1)} custom-call(s32[8,2]{1,0:T(8,128)S(1)} %copy.6.corner_ref, bf16[8,2,256,256]{3,2,1,0:T(8,128)(2,1)S(1)} %bitcast.7), custom_call_target="tpu_custom_call" | custom-call | flops 1 | bytes 1 | tf_op jit(solution)/shard_map/pallas_call | solution.py:23
  68.5 8.4 %collective-permute-done.19.come_ref = bf16[2,256,256]{2,1,0:T(8,128)(2,1)} collective-permute-done((bf16[2,256,256]{2,1,0:T(8,128)(2,1)}, bf16[2,256,256]{2,1,0:T(8,128)(2,1)}, u32[]{:S(2)}, u32[]{:S(2)}) %collective-permute-start.19) | collective-permute-done | bytes 262176 | tf_op jit(solution)/shard_map/ppermute | solution.py:296
  87.2 7.1 %shard_map.61 = (bf16[2,2,128,256]{3,2,1,0:T(8,128)(2,1)S(1)}, bf16[2,2,128,256]{3,2,1,0:T(8,128)(2,1)S(1)}, bf16[2,2,128,256]{3,2,1,0:T(8,128)(2,1)S(1)}, bf16[...) custom-call(s32[2]{0:T(128)S(1)} %pad_add_fusion.pick_ref, ...), custom_call_target="tpu_custom_call" | custom-call | flops 1 | bytes 1 | tf_op jit(solution)/shard_map/pallas_call | solution.py:23
  94.6 3.2 %collective-permute-start.25 = (bf16[2,2,128,256]{3,2,1,0:T(8,128)(2,1)S(1)}, bf16[2,2,128,256]{3,2,1,0:T(8,128)(2,1)S(1)}, u32[]{:S(2)}, u32[]{:S(2)}) collective-permute-start(bf16[2,2,128,256]{3,2,1,0:T(8,128)(2,1)S(1)} %get-tuple-element.100), channel_id=1, source_target_pairs={{0,12},{2,14},{4,8},{6,10},{8,4},{10,6},{12,0},{14,2},{16,28},{18,... | collective-permute-start | bytes 786440 | tf_op jit(solution)/shard_map/ppermute | solution.py:253
  97.8 2.9 %collective-permute-done.23.refs_1_ = bf16[2,2,128,256]{3,2,1,0:T(8,128)(2,1)S(1)} collective-permute-done((bf16[2,2,128,256]{3,2,1,0:T(8,128)(2,1)S(1)}, bf16[2,2,128,256]{3,2,1,0:T(8,128)(2,1)S(1)}, u32[]{:S(2)}, u32[]{:S(2)}) %collective-permute-start.23) | collective-permute-done | bytes 262176 | tf_op jit(solution)/shard_map/ppermute | solution.py:253
  101.0 4.0 %collective-permute-done.25.refs_3_ = bf16[2,2,128,256]{3,2,1,0:T(8,128)(2,1)S(1)} collective-permute-done((bf16[2,2,128,256]{3,2,1,0:T(8,128)(2,1)S(1)}, bf16[2,2,128,256]{3,2,1,0:T(8,128)(2,1)S(1)}, u32[]{:S(2)}, u32[]{:S(2)}) %collective-permute-start.25) | collective-permute-done | bytes 262176 | tf_op jit(solution)/shard_map/ppermute | solution.py:253
  105.0 8.4 %collective-permute-start.26 = (bf16[4,2,128,256]{3,2,1,0:T(8,128)(2,1)S(1)}, bf16[4,2,128,256]{3,2,1,0:T(8,128)(2,1)S(1)}, u32[]{:S(2)}, u32[]{:S(2)}) collective-permute-start(bf16[4,2,128,256]{3,2,1,0:T(8,128)(2,1)S(1)} %shard_map.62), channel_id=1, source_target_pairs={{0,2},{2,0},{4,6},{6,4},{8,10},{10,8},{12,14},{14,12},{16,18},{18,... | collective-permute-start | bytes 1572872 | tf_op jit(solution)/shard_map/ppermute | solution.py:253
  113.4 1.5 %collective-permute-start.20 = (bf16[2,2,128,256]{3,2,1,0:T(8,128)(2,1)S(1)}, bf16[2,2,128,256]{3,2,1,0:T(8,128)(2,1)S(1)}, u32[]{:S(2)}, u32[]{:S(2)}) collective-permute-start(bf16[2,2,128,256]{3,2,1,0:T(8,128)(2,1)S(1)} %get-tuple-element.93), channel_id=1, source_target_pairs={{0,4},{2,6},{4,0},{6,2},{8,12},{10,14},{12,8},{14,10},{16,20},{18,... | collective-permute-start | bytes 786440 | tf_op jit(solution)/shard_map/ppermute | solution.py:253
  115.2 1.7 %collective-permute-start.22 = (bf16[2,2,128,256]{3,2,1,0:T(8,128)(2,1)S(1)}, bf16[2,2,128,256]{3,2,1,0:T(8,128)(2,1)S(1)}, u32[]{:S(2)}, u32[]{:S(2)}) collective-permute-start(bf16[2,2,128,256]{3,2,1,0:T(8,128)(2,1)S(1)} %get-tuple-element.95), channel_id=1, source_target_pairs={{0,12},{2,14},{4,8},{6,10},{8,4},{10,6},{12,0},{14,2},{16,28},{18,... | collective-permute-start | bytes 786440 | tf_op jit(solution)/shard_map/ppermute | solution.py:253
  116.9 2.1 %shard_map.63 = (f32[2,128,512]{2,1,0:T(8,128)S(1)}, bf16[2,128,512]{2,1,0:T(8,128)(2,1)S(1)}) custom-call(s32[8,2]{1,0:T(8,128)S(1)} %copy.6.corner_ref, s32[1]{0:T(128)} %bitcast.4.place_ref, s32[2]{0:T(128)S(1)} %pad_add_fusion.pick_ref, bf16[8,2,256,256]{3,2,1,0:T(8,128)(2,1)S(1)} %shard_map.60.wave_ref, ...), custom_call_target="tpu_custom_call" | custom-call | flops 1 | bytes 1 | tf_op jit(solution)/shard_map/pallas_call | solution.py:23
  119.0 2.7 %collective-permute-done.20.refs_1_ = bf16[2,2,128,256]{3,2,1,0:T(8,128)(2,1)S(1)} collective-permute-done((bf16[2,2,128,256]{3,2,1,0:T(8,128)(2,1)S(1)}, bf16[2,2,128,256]{3,2,1,0:T(8,128)(2,1)S(1)}, u32[]{:S(2)}, u32[]{:S(2)}) %collective-permute-start.20) | collective-permute-done | bytes 262176 | tf_op jit(solution)/shard_map/ppermute | solution.py:253
  121.7 2.4 %collective-permute-done.21.refs_2_ = bf16[2,2,128,256]{3,2,1,0:T(8,128)(2,1)S(1)} collective-permute-done((bf16[2,2,128,256]{3,2,1,0:T(8,128)(2,1)S(1)}, bf16[2,2,128,256]{3,2,1,0:T(8,128)(2,1)S(1)}, u32[]{:S(2)}, u32[]{:S(2)}) %collective-permute-start.21) | collective-permute-done | bytes 262176 | tf_op jit(solution)/shard_map/ppermute | solution.py:253
  124.1 4.4 %collective-permute-done.22.refs_3_ = bf16[2,2,128,256]{3,2,1,0:T(8,128)(2,1)S(1)} collective-permute-done((bf16[2,2,128,256]{3,2,1,0:T(8,128)(2,1)S(1)}, bf16[2,2,128,256]{3,2,1,0:T(8,128)(2,1)S(1)}, u32[]{:S(2)}, u32[]{:S(2)}) %collective-permute-start.22) | collective-permute-done | bytes 262176 | tf_op jit(solution)/shard_map/ppermute | solution.py:253
  128.6 1.6 %collective-permute-start.27 = (bf16[2,128,512]{2,1,0:T(8,128)(2,1)S(1)}, bf16[2,128,512]{2,1,0:T(8,128)(2,1)S(1)}, u32[]{:S(2)}, u32[]{:S(2)}) collective-permute-start(bf16[2,128,512]{2,1,0:T(8,128)(2,1)S(1)} %get-tuple-element.104), channel_id=1, source_target_pairs={{0,1},{1,0},{2,3},{3,2},{4,5},{5,4},{6,7},{7,6},{8,9},{9,8},{10,11... | collective-permute-start | bytes 786440 | tf_op jit(solution)/shard_map/ppermute | solution.py:311
  130.5 2.1 %shard_map.65 = (f32[2,128,512]{2,1,0:T(8,128)S(1)}, bf16[2,128,512]{2,1,0:T(8,128)(2,1)S(1)}) custom-call(s32[8,2]{1,0:T(8,128)S(1)} %copy.6.corner_ref, s32[1]{0:T(128)} %bitcast.4.place_ref, s32[2]{0:T(128)S(1)} %pad_add_fusion.pick_ref, bf16[8,2,256,256]{3,2,1,0:T(8,128)(2,1)S(1)} %shard_map.60.wave_ref, ...), custom_call_target="tpu_custom_call" | custom-call | flops 1 | bytes 1 | tf_op jit(solution)/shard_map/pallas_call | solution.py:23
  132.6 1.6 %collective-permute-start.29 = (bf16[2,128,512]{2,1,0:T(8,128)(2,1)S(1)}, bf16[2,128,512]{2,1,0:T(8,128)(2,1)S(1)}, u32[]{:S(2)}, u32[]{:S(2)}) collective-permute-start(bf16[2,128,512]{2,1,0:T(8,128)(2,1)S(1)} %get-tuple-element.110), channel_id=1, source_target_pairs={{0,1},{1,0},{2,3},{3,2},{4,5},{5,4},{6,7},{7,6},{8,9},{9,8},{10,11... | collective-permute-start | bytes 786440 | tf_op jit(solution)/shard_map/ppermute | solution.py:311
  134.2 3.6 %collective-permute-done.27.refs_1_ = bf16[2,128,512]{2,1,0:T(8,128)(2,1)S(1)} collective-permute-done((bf16[2,128,512]{2,1,0:T(8,128)(2,1)S(1)}, bf16[2,128,512]{2,1,0:T(8,128)(2,1)S(1)}, u32[]{:S(2)}, u32[]{:S(2)}) %collective-permute-start.27) | collective-permute-done | bytes 262176 | tf_op jit(solution)/shard_map/ppermute | solution.py:311
  137.8 5.2 %collective-permute-done.29.refs_3_ = bf16[2,128,512]{2,1,0:T(8,128)(2,1)S(1)} collective-permute-done((bf16[2,128,512]{2,1,0:T(8,128)(2,1)S(1)}, bf16[2,128,512]{2,1,0:T(8,128)(2,1)S(1)}, u32[]{:S(2)}, u32[]{:S(2)}) %collective-permute-start.29) | collective-permute-done | bytes 262176 | tf_op jit(solution)/shard_map/ppermute | solution.py:311
  (100 shorter events, 28.7 us)
Async XLA Ops:
  0.0 56.4 %copy-start.1 = (bf16[8,2,256,256]{3,2,1,0:T(8,128)(2,1)S(1)}, bf16[8,2,256,256]{3,2,1,0:T(8,128)(2,1)}, u32[]{:S(2)}) copy-start(bf16[8,2,256,256]{3,2,1,0:T(8,128)(2,1)} %exit_ref.1) | copy-start | bytes 6291460
  3.0 9.3 %collective-permute-start.1 = (bf16[2,128,512]{2,1,0:T(8,128)(2,1)S(1)}, bf16[2,128,512]{2,1,0:T(8,128)(2,1)S(1)}, u32[]{:S(2)}, u32[]{:S(2)}) collective-permute-start(bf16[2,128,512]{2,1,0:T(8,128)(2,1)S(1)} %get-tuple-element.62.refs_0_), channel_id=1, source_target_pairs={{0,1},{1,0},{2,3},{3,2},{4,5},{5,4},{6,7},{7,6},{8,9},{9,8},{10,11... | collective-permute-start | bytes 786440 | tf_op jit(solution)/shard_map/ppermute | solution.py:261
  6.0 9.1 %collective-permute-start.2 = (bf16[2,128,512]{2,1,0:T(8,128)(2,1)S(1)}, bf16[2,128,512]{2,1,0:T(8,128)(2,1)S(1)}, u32[]{:S(2)}, u32[]{:S(2)}) collective-permute-start(bf16[2,128,512]{2,1,0:T(8,128)(2,1)S(1)} %get-tuple-element.62.refs_0_), channel_id=1, source_target_pairs={{0,2},{2,0},{4,6},{6,4},{8,10},{10,8},{12,14},{14,12},{16,18},{18,... | collective-permute-start | bytes 786440 | tf_op jit(solution)/shard_map/ppermute | solution.py:253
  12.3 2.8 %collective-permute-start.3 = (bf16[2,128,512]{2,1,0:T(8,128)(2,1)S(1)}, bf16[2,128,512]{2,1,0:T(8,128)(2,1)S(1)}, u32[]{:S(2)}, u32[]{:S(2)}) collective-permute-start(bf16[2,128,512]{2,1,0:T(8,128)(2,1)S(1)} %collective-permute-done.1.refs_1_), channel_id=1, source_target_pairs={{0,2},{2,0},{4,6},{6,4},{8,10},{10,8},{12,14},{14,12},{16,18},{18,... | collective-permute-start | bytes 786440 | tf_op jit(solution)/shard_map/ppermute | solution.py:253
  12.3 8.8 %collective-permute-start = (bf16[2,128,512]{2,1,0:T(8,128)(2,1)S(1)}, bf16[2,128,512]{2,1,0:T(8,128)(2,1)}, u32[]{:S(2)}, u32[]{:S(2)}) collective-permute-start(bf16[2,128,512]{2,1,0:T(8,128)(2,1)S(1)} %get-tuple-element.61.refs_0_), channel_id=1, source_target_pairs={{0,1},{1,0},{2,3},{3,2},{4,5},{5,4},{6,7},{7,6},{8,9},{9,8},{10,11... | collective-permute-start | bytes 786440 | tf_op jit(solution)/shard_map/ppermute | solution.py:261
  14.0 16.3 %collective-permute-start.4 = (bf16[2,128,512]{2,1,0:T(8,128)(2,1)S(1)}, bf16[2,128,512]{2,1,0:T(8,128)(2,1)}, u32[]{:S(2)}, u32[]{:S(2)}) collective-permute-start(bf16[2,128,512]{2,1,0:T(8,128)(2,1)S(1)} %get-tuple-element.61.refs_0_), channel_id=1, source_target_pairs={{0,2},{2,0},{4,6},{6,4},{8,10},{10,8},{12,14},{14,12},{16,18},{18,... | collective-permute-start | bytes 786440 | tf_op jit(solution)/shard_map/ppermute | solution.py:253
  21.1 9.2 %collective-permute-start.5 = (bf16[2,128,512]{2,1,0:T(8,128)(2,1)}, bf16[2,128,512]{2,1,0:T(8,128)(2,1)S(1)}, u32[]{:S(2)}, u32[]{:S(2)}) collective-permute-start(bf16[2,128,512]{2,1,0:T(8,128)(2,1)} %collective-permute-done.refs_1_), channel_id=1, source_target_pairs={{0,2},{2,0},{4,6},{6,4},{8,10},{10,8},{12,14},{14,12},{16,18},{18,... | collective-permute-start | bytes 786440 | tf_op jit(solution)/shard_map/ppermute | solution.py:253
  21.1 18.6 %collective-permute-start.6 = (bf16[2,2,128,256]{3,2,1,0:T(8,128)(2,1)S(1)}, bf16[2,2,128,256]{3,2,1,0:T(8,128)(2,1)S(1)}, u32[]{:S(2)}, u32[]{:S(2)}) collective-permute-start(bf16[2,2,128,256]{3,2,1,0:T(8,128)(2,1)S(1)} %get-tuple-element.84), channel_id=1, source_target_pairs={{0,4},{4,0},{8,12},{12,8},{16,20},{20,16},{24,28},{28,24},{1,5},{5... | collective-permute-start | bytes 786440 | tf_op jit(solution)/shard_map/ppermute | solution.py:253
  24.8 15.0 %collective-permute-start.8 = (bf16[2,2,128,256]{3,2,1,0:T(8,128)(2,1)S(1)}, bf16[2,2,128,256]{3,2,1,0:T(8,128)(2,1)S(1)}, u32[]{:S(2)}, u32[]{:S(2)}) collective-permute-start(bf16[2,2,128,256]{3,2,1,0:T(8,128)(2,1)S(1)} %get-tuple-element.86), channel_id=1, source_target_pairs={{0,8},{4,12},{8,0},{12,4},{16,24},{20,28},{24,16},{28,20},{1,9},{5... | collective-permute-start | bytes 786440 | tf_op jit(solution)/shard_map/ppermute | solution.py:253
  28.3 11.5 %collective-permute-start.10 = (bf16[2,2,128,256]{3,2,1,0:T(8,128)(2,1)S(1)}, bf16[2,2,128,256]{3,2,1,0:T(8,128)(2,1)S(1)}, u32[]{:S(2)}, u32[]{:S(2)}) collective-permute-start(bf16[2,2,128,256]{3,2,1,0:T(8,128)(2,1)S(1)} %get-tuple-element.88), channel_id=1, source_target_pairs={{0,12},{4,8},{8,4},{12,0},{16,28},{20,24},{24,20},{28,16},{1,13},{... | collective-permute-start | bytes 786440 | tf_op jit(solution)/shard_map/ppermute | solution.py:253
  32.5 31.9 %copy-start.2 = (bf16[2,2,128,256]{3,2,1,0:T(8,128)(2,1)}, bf16[2,2,128,256]{3,2,1,0:T(8,128)(2,1)S(1)}, u32[]{:S(2)}) copy-start(bf16[2,2,128,256]{3,2,1,0:T(8,128)(2,1)S(1)} %get-tuple-element.79.refs_1_) | copy-start | bytes 786436
  32.5 8.3 %collective-permute-start.7 = (bf16[2,2,128,256]{3,2,1,0:T(8,128)(2,1)S(1)}, bf16[2,2,128,256]{3,2,1,0:T(8,128)(2,1)S(1)}, u32[]{:S(2)}, u32[]{:S(2)}) collective-permute-start(bf16[2,2,128,256]{3,2,1,0:T(8,128)(2,1)S(1)} %get-tuple-element.85), channel_id=1, source_target_pairs={{0,4},{4,0},{8,12},{12,8},{16,20},{20,16},{24,28},{28,24},{1,5},{5... | collective-permute-start | bytes 786440 | tf_op jit(solution)/shard_map/ppermute | solution.py:253
  36.2 8.3 %collective-permute-start.9 = (bf16[2,2,128,256]{3,2,1,0:T(8,128)(2,1)S(1)}, bf16[2,2,128,256]{3,2,1,0:T(8,128)(2,1)S(1)}, u32[]{:S(2)}, u32[]{:S(2)}) collective-permute-start(bf16[2,2,128,256]{3,2,1,0:T(8,128)(2,1)S(1)} %get-tuple-element.87), channel_id=1, source_target_pairs={{0,8},{4,12},{8,0},{12,4},{16,24},{20,28},{24,16},{28,20},{1,9},{5... | collective-permute-start | bytes 786440 | tf_op jit(solution)/shard_map/ppermute | solution.py:253
  44.5 4.7 %collective-permute-start.11 = (bf16[1,1,16,128]{3,2,1,0:T(8,128)(2,1)S(1)}, bf16[1,1,16,128]{3,2,1,0:T(8,128)(2,1)S(1)}, u32[]{:S(2)}, u32[]{:S(2)}) collective-permute-start(bf16[1,1,16,128]{3,2,1,0:T(8,128)(2,1)S(1)} %slice.3), channel_id=1, source_target_pairs={{0,2},{4,6},{8,10},{12,14},{16,18},{20,22},{24,26},{28,30},{1,3},{... | collective-permute-start | bytes 12296 | tf_op jit(solution)/shard_map/ppermute | solution.py:276
  45.8 9.3 %collective-permute-start.12 = (bf16[2,2,128,256]{3,2,1,0:T(8,128)(2,1)S(1)}, bf16[2,2,128,256]{3,2,1,0:T(8,128)(2,1)S(1)}, u32[]{:S(2)}, u32[]{:S(2)}) collective-permute-start(bf16[2,2,128,256]{3,2,1,0:T(8,128)(2,1)S(1)} %get-tuple-element.89), channel_id=1, source_target_pairs={{0,12},{4,8},{8,4},{12,0},{16,28},{20,24},{24,20},{28,16},{1,13},{... | collective-permute-start | bytes 786440 | tf_op jit(solution)/shard_map/ppermute | solution.py:253
  49.2 6.5 %collective-permute-start.13 = (bf16[2,2,128,256]{3,2,1,0:T(8,128)(2,1)S(1)}, bf16[2,2,128,256]{3,2,1,0:T(8,128)(2,1)S(1)}, u32[]{:S(2)}, u32[]{:S(2)}) collective-permute-start(bf16[2,2,128,256]{3,2,1,0:T(8,128)(2,1)S(1)} %get-tuple-element.84), channel_id=1, source_target_pairs={{2,6},{6,2},{10,14},{14,10},{18,22},{22,18},{26,30},{30,26},{3,7},... | collective-permute-start | bytes 786440 | tf_op jit(solution)/shard_map/ppermute | solution.py:253
  49.9 7.8 %collective-permute-start.14 = (bf16[2,2,128,256]{3,2,1,0:T(8,128)(2,1)S(1)}, bf16[2,2,128,256]{3,2,1,0:T(8,128)(2,1)S(1)}, u32[]{:S(2)}, u32[]{:S(2)}) collective-permute-start(bf16[2,2,128,256]{3,2,1,0:T(8,128)(2,1)S(1)} %get-tuple-element.85), channel_id=1, source_target_pairs={{2,6},{6,2},{10,14},{14,10},{18,22},{22,18},{26,30},{30,26},{3,7},... | collective-permute-start | bytes 786440 | tf_op jit(solution)/shard_map/ppermute | solution.py:253
  50.6 7.1 %collective-permute-start.15 = (bf16[2,2,128,256]{3,2,1,0:T(8,128)(2,1)S(1)}, bf16[2,2,128,256]{3,2,1,0:T(8,128)(2,1)S(1)}, u32[]{:S(2)}, u32[]{:S(2)}) collective-permute-start(bf16[2,2,128,256]{3,2,1,0:T(8,128)(2,1)S(1)} %get-tuple-element.86), channel_id=1, source_target_pairs={{2,10},{6,14},{10,2},{14,6},{18,26},{22,30},{26,18},{30,22},{3,11}... | collective-permute-start | bytes 786440 | tf_op jit(solution)/shard_map/ppermute | solution.py:253
  51.3 6.5 %collective-permute-start.16 = (bf16[2,2,128,256]{3,2,1,0:T(8,128)(2,1)S(1)}, bf16[2,2,128,256]{3,2,1,0:T(8,128)(2,1)S(1)}, u32[]{:S(2)}, u32[]{:S(2)}) collective-permute-start(bf16[2,2,128,256]{3,2,1,0:T(8,128)(2,1)S(1)} %get-tuple-element.87), channel_id=1, source_target_pairs={{2,10},{6,14},{10,2},{14,6},{18,26},{22,30},{26,18},{30,22},{3,11}... | collective-permute-start | bytes 786440 | tf_op jit(solution)/shard_map/ppermute | solution.py:253
  55.1 2.7 %collective-permute-start.17 = (bf16[2,2,128,256]{3,2,1,0:T(8,128)(2,1)S(1)}, bf16[2,2,128,256]{3,2,1,0:T(8,128)(2,1)S(1)}, u32[]{:S(2)}, u32[]{:S(2)}) collective-permute-start(bf16[2,2,128,256]{3,2,1,0:T(8,128)(2,1)S(1)} %get-tuple-element.88), channel_id=1, source_target_pairs={{2,14},{6,10},{10,6},{14,2},{18,30},{22,26},{26,22},{30,18},{3,15}... | collective-permute-start | bytes 786440 | tf_op jit(solution)/shard_map/ppermute | solution.py:253
  55.8 2.0 %collective-permute-start.18 = (bf16[2,2,128,256]{3,2,1,0:T(8,128)(2,1)S(1)}, bf16[2,2,128,256]{3,2,1,0:T(8,128)(2,1)S(1)}, u32[]{:S(2)}, u32[]{:S(2)}) collective-permute-start(bf16[2,2,128,256]{3,2,1,0:T(8,128)(2,1)S(1)} %get-tuple-element.89), channel_id=1, source_target_pairs={{2,14},{6,10},{10,6},{14,2},{18,30},{22,26},{26,22},{30,18},{3,15}... | collective-permute-start | bytes 786440 | tf_op jit(solution)/shard_map/ppermute | solution.py:253
  64.5 12.3 %collective-permute-start.19 = (bf16[2,256,256]{2,1,0:T(8,128)(2,1)}, bf16[2,256,256]{2,1,0:T(8,128)(2,1)}, u32[]{:S(2)}, u32[]{:S(2)}) collective-permute-start(bf16[2,256,256]{2,1,0:T(8,128)(2,1)} %get-tuple-element.90), channel_id=1, source_target_pairs={{16,0},{18,2},{20,4},{22,6},{24,8},{26,10},{28,12},{30,14},{17,1},... | collective-permute-start | bytes 786440 | tf_op jit(solution)/shard_map/ppermute | solution.py:296
  94.4 6.4 %collective-permute-start.23 = (bf16[2,2,128,256]{3,2,1,0:T(8,128)(2,1)S(1)}, bf16[2,2,128,256]{3,2,1,0:T(8,128)(2,1)S(1)}, u32[]{:S(2)}, u32[]{:S(2)}) collective-permute-start(bf16[2,2,128,256]{3,2,1,0:T(8,128)(2,1)S(1)} %get-tuple-element.98), channel_id=1, source_target_pairs={{0,4},{2,6},{4,0},{6,2},{8,12},{10,14},{12,8},{14,10},{16,20},{18,... | collective-permute-start | bytes 786440 | tf_op jit(solution)/shard_map/ppermute | solution.py:253
  94.6 6.4 %collective-permute-start.24 = (bf16[2,2,128,256]{3,2,1,0:T(8,128)(2,1)S(1)}, bf16[2,2,128,256]{3,2,1,0:T(8,128)(2,1)S(1)}, u32[]{:S(2)}, u32[]{:S(2)}) collective-permute-start(bf16[2,2,128,256]{3,2,1,0:T(8,128)(2,1)S(1)} %get-tuple-element.99), channel_id=1, source_target_pairs={{0,8},{2,10},{4,12},{6,14},{8,0},{10,2},{12,4},{14,6},{16,24},{18,... | collective-permute-start | bytes 786440 | tf_op jit(solution)/shard_map/ppermute | solution.py:253
  94.6 10.4 %collective-permute-start.25 = (bf16[2,2,128,256]{3,2,1,0:T(8,128)(2,1)S(1)}, bf16[2,2,128,256]{3,2,1,0:T(8,128)(2,1)S(1)}, u32[]{:S(2)}, u32[]{:S(2)}) collective-permute-start(bf16[2,2,128,256]{3,2,1,0:T(8,128)(2,1)S(1)} %get-tuple-element.100), channel_id=1, source_target_pairs={{0,12},{2,14},{4,8},{6,10},{8,4},{10,6},{12,0},{14,2},{16,28},{18,... | collective-permute-start | bytes 786440 | tf_op jit(solution)/shard_map/ppermute | solution.py:253
  105.0 11.9 %collective-permute-start.26 = (bf16[4,2,128,256]{3,2,1,0:T(8,128)(2,1)S(1)}, bf16[4,2,128,256]{3,2,1,0:T(8,128)(2,1)S(1)}, u32[]{:S(2)}, u32[]{:S(2)}) collective-permute-start(bf16[4,2,128,256]{3,2,1,0:T(8,128)(2,1)S(1)} %shard_map.62), channel_id=1, source_target_pairs={{0,2},{2,0},{4,6},{6,4},{8,10},{10,8},{12,14},{14,12},{16,18},{18,... | collective-permute-start | bytes 1572872 | tf_op jit(solution)/shard_map/ppermute | solution.py:253
  113.4 8.3 %collective-permute-start.20 = (bf16[2,2,128,256]{3,2,1,0:T(8,128)(2,1)S(1)}, bf16[2,2,128,256]{3,2,1,0:T(8,128)(2,1)S(1)}, u32[]{:S(2)}, u32[]{:S(2)}) collective-permute-start(bf16[2,2,128,256]{3,2,1,0:T(8,128)(2,1)S(1)} %get-tuple-element.93), channel_id=1, source_target_pairs={{0,4},{2,6},{4,0},{6,2},{8,12},{10,14},{12,8},{14,10},{16,20},{18,... | collective-permute-start | bytes 786440 | tf_op jit(solution)/shard_map/ppermute | solution.py:253
  114.9 9.2 %collective-permute-start.21 = (bf16[2,2,128,256]{3,2,1,0:T(8,128)(2,1)S(1)}, bf16[2,2,128,256]{3,2,1,0:T(8,128)(2,1)S(1)}, u32[]{:S(2)}, u32[]{:S(2)}) collective-permute-start(bf16[2,2,128,256]{3,2,1,0:T(8,128)(2,1)S(1)} %get-tuple-element.94), channel_id=1, source_target_pairs={{0,8},{2,10},{4,12},{6,14},{8,0},{10,2},{12,4},{14,6},{16,24},{18,... | collective-permute-start | bytes 786440 | tf_op jit(solution)/shard_map/ppermute | solution.py:253
  115.2 13.3 %collective-permute-start.22 = (bf16[2,2,128,256]{3,2,1,0:T(8,128)(2,1)S(1)}, bf16[2,2,128,256]{3,2,1,0:T(8,128)(2,1)S(1)}, u32[]{:S(2)}, u32[]{:S(2)}) collective-permute-start(bf16[2,2,128,256]{3,2,1,0:T(8,128)(2,1)S(1)} %get-tuple-element.95), channel_id=1, source_target_pairs={{0,12},{2,14},{4,8},{6,10},{8,4},{10,6},{12,0},{14,2},{16,28},{18,... | collective-permute-start | bytes 786440 | tf_op jit(solution)/shard_map/ppermute | solution.py:253
  128.5 2.0 %collective-permute-start.28 = (bf16[4,2,128,256]{3,2,1,0:T(8,128)(2,1)S(1)}, bf16[4,2,128,256]{3,2,1,0:T(8,128)(2,1)S(1)}, u32[]{:S(2)}, u32[]{:S(2)}) collective-permute-start(bf16[4,2,128,256]{3,2,1,0:T(8,128)(2,1)S(1)} %shard_map.64), channel_id=1, source_target_pairs={{0,2},{2,0},{4,6},{6,4},{8,10},{10,8},{12,14},{14,12},{16,18},{18,... | collective-permute-start | bytes 1572872 | tf_op jit(solution)/shard_map/ppermute | solution.py:253
  128.6 9.2 %collective-permute-start.27 = (bf16[2,128,512]{2,1,0:T(8,128)(2,1)S(1)}, bf16[2,128,512]{2,1,0:T(8,128)(2,1)S(1)}, u32[]{:S(2)}, u32[]{:S(2)}) collective-permute-start(bf16[2,128,512]{2,1,0:T(8,128)(2,1)S(1)} %get-tuple-element.104), channel_id=1, source_target_pairs={{0,1},{1,0},{2,3},{3,2},{4,5},{5,4},{6,7},{7,6},{8,9},{9,8},{10,11... | collective-permute-start | bytes 786440 | tf_op jit(solution)/shard_map/ppermute | solution.py:311
  132.6 10.3 %collective-permute-start.29 = (bf16[2,128,512]{2,1,0:T(8,128)(2,1)S(1)}, bf16[2,128,512]{2,1,0:T(8,128)(2,1)S(1)}, u32[]{:S(2)}, u32[]{:S(2)}) collective-permute-start(bf16[2,128,512]{2,1,0:T(8,128)(2,1)S(1)} %get-tuple-element.110), channel_id=1, source_target_pairs={{0,1},{1,0},{2,3},{3,2},{4,5},{5,4},{6,7},{7,6},{8,9},{9,8},{10,11... | collective-permute-start | bytes 786440 | tf_op jit(solution)/shard_map/ppermute | solution.py:311
  (26 other events, 124.6 us)

commit v6 on v3

v6 whole, which is shorter than its diff:
```python
import functools
import math

import jax
import jax.numpy as jnp
from jax import lax
from jax.experimental import pallas as pl
from jax.experimental.pallas import tpu as pltpu
from jax.sharding import PartitionSpec as P

SUBSTEPS = 2
damping = 0.0005
turning = 0.011
code_gain = 83.0
chunk_count = 2
f32 = jnp.float32
bf16 = jnp.bfloat16


def call(kernel, out_shape, prefetch=0, scratch=(), cost=(0, 0), grant=6, aliases=None):
    flops, transcendentals = cost

    def run(*args):
        moved = sum(a.size * a.dtype.itemsize for a in jax.tree.leaves((args, out_shape)))
        vmem = pl.BlockSpec(memory_space=pltpu.VMEM)
        return pl.pallas_call(
            kernel,
            grid_spec=pltpu.PrefetchScalarGridSpec(
                num_scalar_prefetch=prefetch,
                grid=(1,),
                in_specs=[vmem] * (len(args) - prefetch),
                out_specs=jax.tree.map(lambda _: vmem, out_shape),
                scratch_shapes=list(scratch),
            ),
            out_shape=out_shape,
            input_output_aliases=aliases or {},
            cost_estimate=pl.CostEstimate(flops=flops, bytes_accessed=moved, transcendentals=transcendentals),
            compiler_params=pltpu.CompilerParams(vmem_limit_bytes=grant * 2**20),
        )(*args)

    return run


def place_in_group(count):
    return lax.rem(lax.axis_index("sec").astype(jnp.int32), count)


def code_kernel(amp_ref, phase_ref, *code_refs):
    rows = code_refs[0].shape[1]
    for chunk, code_ref in enumerate(code_refs):
        amp = amp_ref[pl.ds(chunk * rows, rows), :]
        half = 0.5 * phase_ref[pl.ds(chunk * rows, rows), :]
        square = half * half
        sine = jnp.full_like(half, 1.0 / math.factorial(13))
        cosine = jnp.full_like(half, 1.0 / math.factorial(12))
        for power in (11, 9, 7, 5, 3, 1):
            sign = -1.0 if power % 4 == 3 else 1.0
            sine = sine * square + sign / math.factorial(power)
            cosine = cosine * square + sign / math.factorial(power - 1)
        sine = sine * half
        code_ref[0] = jnp.exp((code_gain * amp) * (1.0 - 2.0 * sine * sine)).astype(bf16)
        code_ref[1] = jnp.exp((code_gain * amp) * (2.0 * sine * cosine)).astype(bf16)


def first_masks(corner_ref, position, base, shape):
    place = lax.axis_index("scan").astype(jnp.int32)
    row = lax.broadcasted_iota(jnp.int32, shape, 0) + base
    col = lax.broadcasted_iota(jnp.int32, shape, 1)
    at_first = (row >= corner_ref[0, position]).astype(jnp.int32)
    return at_first != place, col >= corner_ref[1, position]


def cut_kernel(base, count, corner_ref, mine_ref, other_ref, *refs):
    own = place_in_group(count)
    for apart, win_ref in enumerate(refs[-count:]):
        _, rows, width = mine_ref.shape
        window = width // 2
        if base:
            win_ref[:, :base] = refs[apart][:, :base]
        in_mine, in_left = first_masks(corner_ref, own ^ apart, base, (rows, window))
        for part in range(2):
            left, right = (
                jnp.where(in_mine, mine_ref[part, :, cols].astype(f32), other_ref[part, :, cols].astype(f32))
                for cols in (slice(0, window), slice(window, 2 * window))
            )
            win_ref[part, pl.ds(base, rows), :] = jnp.where(in_left, left, right).astype(bf16)


def turned(wave, row_at, col_at):
    window = wave.shape[-1]
    wave = pltpu.roll(wave.astype(f32), lax.rem(row_at, window), 0)
    return pltpu.roll(wave, lax.rem(col_at, window), 1).astype(bf16)


def second_difference(size, break_at):
    row = lax.broadcasted_iota(jnp.int32, (size, size), 0)
    col = lax.broadcasted_iota(jnp.int32, (size, size), 1)
    start = lax.rem(break_at, size)
    before = (lax.rem(row - col + size, size) == 1) & (row != start)
    after = (lax.rem(col - row + size, size) == 1) & (col != start)
    return jnp.where(row == col, -2.0, jnp.where(before | after, 1.0, 0.0)).astype(bf16)


def ready_kernel(corner_ref, exit_ref, start_ref, down_ref, across_ref):
    own = place_in_group(exit_ref.shape[0])
    row_at = corner_ref[0, own]
    col_at = corner_ref[1, own]
    size = start_ref.shape[-1]
    for part in range(2):
        start_ref[part] = turned(exit_ref[own, part], row_at, col_at)
    down_ref[...] = second_difference(size, row_at)
    across_ref[...] = second_difference(size, col_at)


def turn_kernel(corner_ref, wave_ref, turned_ref):
    count = wave_ref.shape[0]

    def one(position, _):
        for part in range(2):
            turned_ref[position, part] = turned(
                wave_ref[position, part], corner_ref[0, position], corner_ref[1, position]
            )
        return 0

    lax.fori_loop(0, count, one, 0)


def back(down, across, chi_re, chi_im):
    def laplacian(field):
        rows = jnp.dot(down, field, preferred_element_type=f32)
        return rows + jnp.dot(field, across, preferred_element_type=f32)

    lap_re = laplacian(chi_re)
    lap_im = laplacian(chi_im)
    lap2_re = laplacian(lap_re.astype(bf16))
    lap2_im = laplacian(lap_im.astype(bf16))
    more_re = 2.0 * lap_re + (damping * lap2_re + turning * lap2_im)
    more_im = 2.0 * lap_im + (damping * lap2_im - turning * lap2_re)
    spread_re = chi_re.astype(f32) + (damping * more_re + turning * more_im)
    spread_im = chi_im.astype(f32) + (damping * more_im - turning * more_re)
    return spread_re, spread_im


def pass_group(down, across, chi_re, chi_im, count, window_of, keep):
    for layer in range(count - 1, -1, -1):
        spread_re, spread_im = back(down, across, chi_re, chi_im)
        keep(layer, spread_re, spread_im)
        win_re, win_im = window_of(layer)
        chi_re = (win_re * spread_re + win_im * spread_im).astype(bf16)
        chi_im = (win_re * spread_im - win_im * spread_re).astype(bf16)
    return chi_re, chi_im


def decoded(held_ref, layer):
    return [jnp.log(held_ref[layer, part].astype(f32)) * (1.0 / code_gain) for part in range(2)]


def first_kernel(start_ref, down_ref, across_ref, *refs):
    *win_refs, leave_ref, held_ref = refs
    count = len(win_refs)
    own = place_in_group(count)
    for apart in range(count):
        held_ref[own ^ apart] = win_refs[apart][...]
    leave_ref[0], leave_ref[1] = pass_group(
        down_ref[...],
        across_ref[...],
        start_ref[0],
        start_ref[1],
        count,
        functools.partial(decoded, held_ref),
        lambda *_: None,
    )


def next_kernel(is_last, start_ref, come_ref, down_ref, across_ref, held_ref, *refs):
    count, _, window, _ = held_ref.shape
    own = place_in_group(count)
    behind = (lax.axis_index("sec") + count).astype(jnp.int32)
    at_end = jnp.full((window, window), behind, jnp.int32) >= lax.axis_size("sec")
    chi_re, chi_im = (
        jnp.where(at_end, start_ref[part].astype(f32), come_ref[part].astype(f32)).astype(bf16) for part in range(2)
    )

    def keep(layer, spread_re, spread_im):
        if is_last:
            refs[-1][layer, 0] = spread_re.astype(bf16)
            refs[-1][layer, 1] = spread_im.astype(bf16)

    chi = pass_group(
        down_ref[...], across_ref[...], chi_re, chi_im, count, functools.partial(decoded, held_ref), keep
    )
    if not is_last:
        refs[0][0], refs[0][1] = chi
        return
    for apart in range(count):
        refs[apart][...] = refs[-1][own ^ apart]


def gradient_kernel(base, corner_ref, wave_ref, *refs):
    *spread_refs, own_ref, away_ref = refs
    rows = own_ref.shape[1]
    window = wave_ref.shape[-1]
    tall = 16
    own = place_in_group(wave_ref.shape[0])

    def one(block, _):
        at = pl.multiple_of(block * tall, tall)
        sums = [jnp.zeros((tall, window), f32) for _ in range(8)]
        here = pl.ds(base + at, tall)
        for apart, spread_ref in enumerate(spread_refs):
            position = own ^ apart
            in_mine, in_left = first_masks(corner_ref, position, base + at, (tall, window))
            wave_re, wave_im = (wave_ref[position, part, here, :].astype(f32) for part in range(2))
            spread_re, spread_im = (spread_ref[part, here, :].astype(f32) for part in range(2))
            parts = (
                wave_re * spread_re + wave_im * spread_im,
                wave_re * spread_im - wave_im * spread_re,
            )
            for part in range(2):
                left = jnp.where(in_left, parts[part], 0.0)
                right = jnp.where(in_left, 0.0, parts[part])
                for side, value in enumerate((left, right)):
                    sums[4 * part + side] += jnp.where(in_mine, value, 0.0)
                    sums[4 * part + 2 + side] += jnp.where(in_mine, 0.0, value)
        for part in range(2):
            for side in range(2):
                cols = pl.ds(side * window, window)
                own_ref[part, pl.ds(at, tall), cols] = sums[4 * part + side]
                away_ref[part, pl.ds(at, tall), cols] = sums[4 * part + 2 + side].astype(bf16)
        return 0

    lax.fori_loop(0, rows // tall, one, 0)


def finish_kernel(*refs):
    out_ref = refs[-1]
    rows = refs[0].shape[1]
    for chunk in range(chunk_count):
        own_ref, come_ref = refs[2 * chunk : 2 * chunk + 2]
        out_ref[:, pl.ds(chunk * rows, rows), :] = own_ref[...] + come_ref[...].astype(f32)


def shape_of(dims, dtype):
    return jax.ShapeDtypeStruct(dims, dtype)


def on_device(obj_amp, obj_phase, forward_waves, exit_adjoint, offsets):
    sections = lax.axis_size("sec")
    count, _, window, _ = exit_adjoint.shape
    _, half, width = obj_amp.shape
    group_count = sections // count
    chunks = range(chunk_count)
    rows = half // chunk_count
    piece = (2, rows, width)
    wave = (2, window, window)
    corners = offsets.T

    def to_other_half(value):
        return lax.ppermute(value, "scan", [(0, 1), (1, 0)])

    def exchange(values):
        return [values[0]] + [
            lax.ppermute(values[d], "sec", [(s, s ^ d) for s in range(sections)]) for d in range(1, count)
        ]

    mine = call(code_kernel, [shape_of(piece, bf16)] * chunk_count)(obj_amp[0], obj_phase[0])
    windows = []
    for c in chunks:
        cut = call(
            functools.partial(cut_kernel, c * rows, count),
            [shape_of(wave, bf16)] * count,
            prefetch=1,
            aliases={3 + i: i for i in range(len(windows))},
        )
        windows = cut(corners, mine[c], to_other_half(mine[c]), *windows)
    windows = exchange(windows)
    ready = call(ready_kernel, [shape_of(wave, bf16)] + [shape_of((window, window), bf16)] * 2, prefetch=1)
    start, down, across = ready(corners, exit_adjoint)
    waves = call(turn_kernel, shape_of(forward_waves.shape[1:], bf16), prefetch=1)(corners, forward_waves[0])

    cost = (count * 16 * window**3, count * 2 * window**2)
    first = call(first_kernel, [shape_of(wave, bf16), shape_of((count,) + wave, bf16)], cost=cost, grant=12)
    leave, held = first(start, down, across, *windows)
    for stage in range(1, group_count):
        come = lax.ppermute(leave, "sec", [(s, s - count) for s in range(count, sections)])
        come, waves = lax.optimization_barrier((come, waves))
        is_last = stage == group_count - 1
        through = call(
            functools.partial(next_kernel, is_last),
            [shape_of(wave, bf16)] * count if is_last else shape_of(wave, bf16),
            scratch=[pltpu.VMEM((count,) + wave, bf16)] if is_last else [],
            cost=cost,
            grant=12,
        )
        leave = through(start, come, down, across, held)

    came = exchange(leave)
    sums = []
    for c in chunks:
        gradient = call(
            functools.partial(gradient_kernel, c * rows), [shape_of(piece, f32), shape_of(piece, bf16)], prefetch=1
        )
        keep, away = gradient(corners, waves, *came)
        sums += [keep, to_other_half(away)]
    return call(finish_kernel, shape_of((2, half, width), f32))(*sums)[None]


def solution(mesh):
    in_specs = (
        P("sec", "scan", None),
        P("sec", "scan", None),
        P("sec", "scan", None, None, None),
        P("scan", None, None, None),
        P("scan", None),
    )
    out_specs = P("sec", None, "scan", None)
    return jax.shard_map(
        on_device, mesh=mesh, in_specs=in_specs, out_specs=out_specs, check_vma=False
    )
```

time: 130 us -> 119 us (0.915)
  waiting for transfers between devices: 60.9 us -> 74.7 us
  local copies, waits for them, and re-layouts: 14.8 us -> 2.77 us
  starting transfers between devices: 28.7 us -> 18.4 us
  Pallas kernels: 24.5 us -> 22.4 us
    ppermute x32 -> x18, waiting for transfers between devices: 45.7 us -> 61.6 us  [the longest x14 41.5 us: exchange(): lax.ppermute(values[d], 'sec', [(s, s ^ d) for s in range(sections)])]
    unnamed x61 -> x12, local copies, waits for them, and re-layouts: 14.8 us -> 2.77 us
    ppermute x32 -> x18, starting transfers between devices: 27.2 us -> 17 us  [the longest x14 11.7 us: exchange(): lax.ppermute(values[d], 'sec', [(s, s ^ d) for s in range(sections)])]
    ppermute x1, waiting for transfers between devices: 15.2 us -> 13.1 us  [on_device(): lax.ppermute(leave, 'sec', [(s, s - count) for s in range(count, sections)])]
    pallas_call x10, Pallas kernels: 24.5 us -> 22.4 us  [run(): pl.pallas_call(kernel, grid_spec=pltpu.PrefetchScalarGridSpec(num_scalar_...]
  transfers between devices with their start and end apart: 33 -> 19, of which waited for: 20 -> 15; matrix products, arithmetic and copies ran while one was open for 1% -> 0% of each run, Pallas kernels for 8% -> 6%
where the time goes in v6:
time: 119 us; the launch traced here: 118 us
  waiting for transfers between devices  74.7 us (63%)
  Pallas kernels  22.4 us (19%)
  starting transfers between devices  18.4 us (15%)
  local copies, waits for them, and re-layouts  2.77 us (2%)
    ppermute x14, waiting for transfers between devices, exchange(): lax.ppermute(values[d], 'sec', [(s, s ^ d) for s in range(sections)])  41.5 us
    pallas_call x10, Pallas kernels, run(): pl.pallas_call(kernel, grid_spec=pltpu.PrefetchScalarGridSpec(num_scalar_...  22.4 us
    ppermute x4, waiting for transfers between devices, to_other_half(): return lax.ppermute(value, 'scan', [(0, 1), (1, 0)])  20.1 us
    ppermute x1, waiting for transfers between devices, on_device(): lax.ppermute(leave, 'sec', [(s, s - count) for s in range(count, sections)])  13.1 us
    ppermute x14, starting transfers between devices, exchange(): lax.ppermute(values[d], 'sec', [(s, s ^ d) for s in range(sections)])  11.7 us
    ppermute x4, starting transfers between devices, to_other_half(): return lax.ppermute(value, 'scan', [(0, 1), (1, 0)])  5.24 us
    unnamed x12, local copies, waits for them, and re-layouts  2.77 us
  transfers between devices with their start and end apart: 19, of which 15 were waited for; matrix products, arithmetic and copies ran while one was open for 0% of the time, Pallas kernels for 6%

profile of v6, /device:TPU:0, one launch (start us, length us, event | category | flops | bytes accessed | tf_op | source)
XLA Modules:
  0.0 118.5 jit_solution(18326212544523743801)
XLA Ops:
  2.8 3.0 %collective-permute-start.1 = (bf16[2,128,512]{2,1,0:T(8,128)(2,1)S(1)}, bf16[2,128,512]{2,1,0:T(8,128)(2,1)S(1)}, u32[]{:S(2)}, u32[]{:S(2)}) collective-permute-start(bf16[2,128,512]{2,1,0:T(8,128)(2,1)S(1)} %get-tuple-element.46.mine_ref), channel_id=1, source_target_pairs={{0,1},{1,0},{2,3},{3,2},{4,5},{5,4},{6,7},{7,6},{8,9},{9,8},{10,11... | collective-permute-start | bytes 786440 | tf_op jit(solution)/shard_map/ppermute | solution.py:259
  5.9 7.1 %collective-permute-done.1.other_ref = bf16[2,128,512]{2,1,0:T(8,128)(2,1)S(1)} collective-permute-done((bf16[2,128,512]{2,1,0:T(8,128)(2,1)S(1)}, bf16[2,128,512]{2,1,0:T(8,128)(2,1)S(1)}, u32[]{:S(2)}, u32[]{:S(2)}) %collective-permute-start.1) | collective-permute-done | bytes 262176 | tf_op jit(solution)/shard_map/ppermute | solution.py:259
  13.6 1.1 shard_map.57
  14.8 3.0 %collective-permute-done.other_ref = bf16[2,128,512]{2,1,0:T(8,128)(2,1)S(1)} collective-permute-done((bf16[2,128,512]{2,1,0:T(8,128)(2,1)S(1)}, bf16[2,128,512]{2,1,0:T(8,128)(2,1)S(1)}, u32[]{:S(2)}, u32[]{:S(2)}) %collective-permute-start) | collective-permute-done | bytes 262176 | tf_op jit(solution)/shard_map/ppermute | solution.py:259
  17.7 1.2 %shard_map.58 = (bf16[2,256,256]{2,1,0:T(8,128)(2,1)S(1)}, bf16[2,256,256]{2,1,0:T(8,128)(2,1)S(1)}, bf16[2,256,256]{2,1,0:T(8,128)(2,1)S(1)}, bf16[2,256,256]{2...) custom-call(s32[2,8]{1,0:T(2,128)S(1)} %bitcast.9, ...), custom_call_target="tpu_custom_call", output_to_operand_aliasing={{0}: (3, {}), {1}: (4, {}), {2}: (5, {}), {3}: (6, {}), {4}... | custom-call | bytes 4718656 | tf_op jit(solution)/shard_map/pallas_call | solution.py:26
  19.1 1.8 %collective-permute-start.3 = (bf16[2,256,256]{2,1,0:T(8,128)(2,1)S(1)}, bf16[2,256,256]{2,1,0:T(8,128)(2,1)S(1)}, u32[]{:S(2)}, u32[]{:S(2)}) collective-permute-start(bf16[2,256,256]{2,1,0:T(8,128)(2,1)S(1)} %get-tuple-element.57), channel_id=1, source_target_pairs={{0,4},{2,6},{4,0},{6,2},{8,12},{10,14},{12,8},{14,10},{16,20},{18,... | collective-permute-start | bytes 786440 | tf_op jit(solution)/shard_map/ppermute | solution.py:263
  21.0 1.8 %collective-permute-start.5 = (bf16[2,256,256]{2,1,0:T(8,128)(2,1)S(1)}, bf16[2,256,256]{2,1,0:T(8,128)(2,1)S(1)}, u32[]{:S(2)}, u32[]{:S(2)}) collective-permute-start(bf16[2,256,256]{2,1,0:T(8,128)(2,1)S(1)} %get-tuple-element.59), channel_id=1, source_target_pairs={{0,8},{2,10},{4,12},{6,14},{8,0},{10,2},{12,4},{14,6},{16,24},{18,... | collective-permute-start | bytes 786440 | tf_op jit(solution)/shard_map/ppermute | solution.py:263
  22.8 2.6 %collective-permute-start.7 = (bf16[2,256,256]{2,1,0:T(8,128)(2,1)S(1)}, bf16[2,256,256]{2,1,0:T(8,128)(2,1)S(1)}, u32[]{:S(2)}, u32[]{:S(2)}) collective-permute-start(bf16[2,256,256]{2,1,0:T(8,128)(2,1)S(1)} %get-tuple-element.61), channel_id=1, source_target_pairs={{0,12},{2,14},{4,8},{6,10},{8,4},{10,6},{12,0},{14,2},{16,28},{18,... | collective-permute-start | bytes 786440 | tf_op jit(solution)/shard_map/ppermute | solution.py:263
  25.4 2.8 %collective-permute-done.3.refs_2_ = bf16[2,256,256]{2,1,0:T(8,128)(2,1)S(1)} collective-permute-done((bf16[2,256,256]{2,1,0:T(8,128)(2,1)S(1)}, bf16[2,256,256]{2,1,0:T(8,128)(2,1)S(1)}, u32[]{:S(2)}, u32[]{:S(2)}) %collective-permute-start.3) | collective-permute-done | bytes 262176 | tf_op jit(solution)/shard_map/ppermute | solution.py:263
  28.2 1.6 %collective-permute-start.8 = (bf16[2,256,256]{2,1,0:T(8,128)(2,1)S(1)}, bf16[2,256,256]{2,1,0:T(8,128)(2,1)S(1)}, u32[]{:S(2)}, u32[]{:S(2)}) collective-permute-start(bf16[2,256,256]{2,1,0:T(8,128)(2,1)S(1)} %get-tuple-element.62), channel_id=1, source_target_pairs={{0,14},{2,12},{4,10},{6,8},{8,6},{10,4},{12,2},{14,0},{16,30},{18,... | collective-permute-start | bytes 786440 | tf_op jit(solution)/shard_map/ppermute | solution.py:263
  29.8 1.2 %shard_map.55 = (bf16[2,256,256]{2,1,0:T(8,128)(2,1)S(1)}, bf16[256,256]{1,0:T(8,128)(2,1)S(1)}, bf16[256,256]{1,0:T(8,128)(2,1)S(1)}) custom-call(s32[2,8]{1,0:T(2,128)S(1)} %bitcast.10, bf16[8,2,256,256]{3,2,1,0:T(8,128)(2,1)S(1)} %copy-done.1), custom_call_target="tpu_custom_call" | custom-call | bytes 2621504 | tf_op jit(solution)/shard_map/pallas_call | solution.py:26
  31.0 1.9 %collective-permute-done.4.refs_3_ = bf16[2,256,256]{2,1,0:T(8,128)(2,1)S(1)} collective-permute-done((bf16[2,256,256]{2,1,0:T(8,128)(2,1)S(1)}, bf16[2,256,256]{2,1,0:T(8,128)(2,1)S(1)}, u32[]{:S(2)}, u32[]{:S(2)}) %collective-permute-start.4) | collective-permute-done | bytes 262176 | tf_op jit(solution)/shard_map/ppermute | solution.py:263
  33.0 2.1 %collective-permute-done.6.refs_5_ = bf16[2,256,256]{2,1,0:T(8,128)(2,1)S(1)} collective-permute-done((bf16[2,256,256]{2,1,0:T(8,128)(2,1)S(1)}, bf16[2,256,256]{2,1,0:T(8,128)(2,1)S(1)}, u32[]{:S(2)}, u32[]{:S(2)}) %collective-permute-start.6) | collective-permute-done | bytes 262176 | tf_op jit(solution)/shard_map/ppermute | solution.py:263
  35.0 7.5 %collective-permute-done.7.refs_6_ = bf16[2,256,256]{2,1,0:T(8,128)(2,1)S(1)} collective-permute-done((bf16[2,256,256]{2,1,0:T(8,128)(2,1)S(1)}, bf16[2,256,256]{2,1,0:T(8,128)(2,1)S(1)}, u32[]{:S(2)}, u32[]{:S(2)}) %collective-permute-start.7) | collective-permute-done | bytes 262176 | tf_op jit(solution)/shard_map/ppermute | solution.py:263
  42.5 4.5 %collective-permute-done.8.refs_7_ = bf16[2,256,256]{2,1,0:T(8,128)(2,1)S(1)} collective-permute-done((bf16[2,256,256]{2,1,0:T(8,128)(2,1)S(1)}, bf16[2,256,256]{2,1,0:T(8,128)(2,1)S(1)}, u32[]{:S(2)}, u32[]{:S(2)}) %collective-permute-start.8) | collective-permute-done | bytes 262176 | tf_op jit(solution)/shard_map/ppermute | solution.py:263
  47.0 5.2 %shard_map.59 = (bf16[2,256,256]{2,1,0:T(8,128)(2,1)S(1)}, bf16[8,2,256,256]{3,2,1,0:T(8,128)(2,1)S(1)}) custom-call(bf16[2,256,256]{2,1,0:T(8,128)(2,1)S(1)} %get-tuple-element.42.start_ref, bf16[256,256]{1,0:T(8,128)(2,1)S(1)} %get-tuple-element.43.down_ref, bf16[256,256]{1,0:T(8,128)(2,1)S(1)} %get-tuple-element.44.across_ref, ...), custom_call_target="tpu_custom_call" | custom-call | flops 2147483648 | bytes 4980736 | tf_op jit(solution)/shard_map/pallas_call | solution.py:26
  52.2 1.5 %collective-permute-start.9 = (bf16[2,256,256]{2,1,0:T(8,128)(2,1)S(1)}, bf16[2,256,256]{2,1,0:T(8,128)(2,1)S(1)}, u32[]{:S(2)}, u32[]{:S(2)}) collective-permute-start(bf16[2,256,256]{2,1,0:T(8,128)(2,1)S(1)} %get-tuple-element.63), channel_id=1, source_target_pairs={{16,0},{18,2},{20,4},{22,6},{24,8},{26,10},{28,12},{30,14},{17,1},... | collective-permute-start | bytes 786440 | tf_op jit(solution)/shard_map/ppermute | solution.py:285
  53.7 2.5 %shard_map.60.wave_ref = bf16[8,2,256,256]{3,2,1,0:T(8,128)(2,1)S(1)} custom-call(s32[2,8]{1,0:T(2,128)S(1)} %bitcast.11, bf16[8,2,256,256]{3,2,1,0:T(8,128)(2,1)S(1)} %bitcast.5), custom_call_target="tpu_custom_call" | custom-call | bytes 4194368 | tf_op jit(solution)/shard_map/pallas_call | solution.py:26
  56.2 13.1 %collective-permute-done.9.come_ref = bf16[2,256,256]{2,1,0:T(8,128)(2,1)S(1)} collective-permute-done((bf16[2,256,256]{2,1,0:T(8,128)(2,1)S(1)}, bf16[2,256,256]{2,1,0:T(8,128)(2,1)S(1)}, u32[]{:S(2)}, u32[]{:S(2)}) %collective-permute-start.9) | collective-permute-done | bytes 262176 | tf_op jit(solution)/shard_map/ppermute | solution.py:285
  69.2 5.2 %shard_map.61 = (bf16[2,256,256]{2,1,0:T(8,128)(2,1)S(1)}, bf16[2,256,256]{2,1,0:T(8,128)(2,1)S(1)}, bf16[2,256,256]{2,1,0:T(8,128)(2,1)S(1)}, bf16[2,256,256]{2...) custom-call(bf16[2,256,256]{2,1,0:T(8,128)(2,1)S(1)} %get-tuple-elem, ...), custom_call_target="tpu_custom_call" | custom-call | flops 2147483648 | bytes 4980736 | tf_op jit(solution)/shard_map/pallas_call | solution.py:26
  74.9 1.5 %collective-permute-start.12 = (bf16[2,256,256]{2,1,0:T(8,128)(2,1)S(1)}, bf16[2,256,256]{2,1,0:T(8,128)(2,1)S(1)}, u32[]{:S(2)}, u32[]{:S(2)}) collective-permute-start(bf16[2,256,256]{2,1,0:T(8,128)(2,1)S(1)} %get-tuple-element.70), channel_id=1, source_target_pairs={{0,6},{2,4},{4,2},{6,0},{8,14},{10,12},{12,10},{14,8},{16,22},{18,... | collective-permute-start | bytes 786440 | tf_op jit(solution)/shard_map/ppermute | solution.py:263
  76.4 1.7 %collective-permute-start.14 = (bf16[2,256,256]{2,1,0:T(8,128)(2,1)S(1)}, bf16[2,256,256]{2,1,0:T(8,128)(2,1)S(1)}, u32[]{:S(2)}, u32[]{:S(2)}) collective-permute-start(bf16[2,256,256]{2,1,0:T(8,128)(2,1)S(1)} %get-tuple-element.72), channel_id=1, source_target_pairs={{0,10},{2,8},{4,14},{6,12},{8,2},{10,0},{12,6},{14,4},{16,26},{18,... | collective-permute-start | bytes 786440 | tf_op jit(solution)/shard_map/ppermute | solution.py:263
  78.2 5.5 %collective-permute-done.11.refs_2_ = bf16[2,256,256]{2,1,0:T(8,128)(2,1)S(1)} collective-permute-done((bf16[2,256,256]{2,1,0:T(8,128)(2,1)S(1)}, bf16[2,256,256]{2,1,0:T(8,128)(2,1)S(1)}, u32[]{:S(2)}, u32[]{:S(2)}) %collective-permute-start.11) | collective-permute-done | bytes 262176 | tf_op jit(solution)/shard_map/ppermute | solution.py:263
  83.7 4.7 %collective-permute-done.12.refs_3_ = bf16[2,256,256]{2,1,0:T(8,128)(2,1)S(1)} collective-permute-done((bf16[2,256,256]{2,1,0:T(8,128)(2,1)S(1)}, bf16[2,256,256]{2,1,0:T(8,128)(2,1)S(1)}, u32[]{:S(2)}, u32[]{:S(2)}) %collective-permute-start.12) | collective-permute-done | bytes 262176 | tf_op jit(solution)/shard_map/ppermute | solution.py:263
  88.4 1.6 %collective-permute-done.14.refs_5_ = bf16[2,256,256]{2,1,0:T(8,128)(2,1)S(1)} collective-permute-done((bf16[2,256,256]{2,1,0:T(8,128)(2,1)S(1)}, bf16[2,256,256]{2,1,0:T(8,128)(2,1)S(1)}, u32[]{:S(2)}, u32[]{:S(2)}) %collective-permute-start.14) | collective-permute-done | bytes 262176 | tf_op jit(solution)/shard_map/ppermute | solution.py:263
  90.0 6.5 %collective-permute-done.15.refs_6_ = bf16[2,256,256]{2,1,0:T(8,128)(2,1)S(1)} collective-permute-done((bf16[2,256,256]{2,1,0:T(8,128)(2,1)S(1)}, bf16[2,256,256]{2,1,0:T(8,128)(2,1)S(1)}, u32[]{:S(2)}, u32[]{:S(2)}) %collective-permute-start.15) | collective-permute-done | bytes 262176 | tf_op jit(solution)/shard_map/ppermute | solution.py:263
  96.5 4.4 %collective-permute-done.16.refs_7_ = bf16[2,256,256]{2,1,0:T(8,128)(2,1)S(1)} collective-permute-done((bf16[2,256,256]{2,1,0:T(8,128)(2,1)S(1)}, bf16[2,256,256]{2,1,0:T(8,128)(2,1)S(1)}, u32[]{:S(2)}, u32[]{:S(2)}) %collective-permute-start.16) | collective-permute-done | bytes 262176 | tf_op jit(solution)/shard_map/ppermute | solution.py:263
  101.0 2.1 %shard_map.63 = (f32[2,128,512]{2,1,0:T(8,128)S(1)}, bf16[2,128,512]{2,1,0:T(8,128)(2,1)S(1)}) custom-call(s32[2,8]{1,0:T(2,128)S(1)} %bitcast.12, bf16[8,2,256,256]{3,2,1,0:T(8,128)(2,1)S(1)} %shard_map.60.wave_ref, bf16[2,256,256]{2,1,0:T(8,128)(2,1)S(1)} %get-tuple-element.67.refs_0_, bf16[2,256,256]{2,1,0:T(8,128)(2,1)S(1)} %collective-permute-done.10.refs_1_, ...), custom_call_target="tpu_custom_call" | custom-call | bytes 4980800 | tf_op jit(solution)/shard_map/pallas_call | solution.py:26
  103.1 1.7 %collective-permute-start.18 = (bf16[2,128,512]{2,1,0:T(8,128)(2,1)S(1)}, bf16[2,128,512]{2,1,0:T(8,128)(2,1)S(1)}, u32[]{:S(2)}, u32[]{:S(2)}) collective-permute-start(bf16[2,128,512]{2,1,0:T(8,128)(2,1)S(1)} %get-tuple-element.78), channel_id=1, source_target_pairs={{0,1},{1,0},{2,3},{3,2},{4,5},{5,4},{6,7},{7,6},{8,9},{9,8},{10,11... | collective-permute-start | bytes 786440 | tf_op jit(solution)/shard_map/ppermute | solution.py:259
  104.8 2.1 %shard_map.62 = (f32[2,128,512]{2,1,0:T(8,128)S(1)}, bf16[2,128,512]{2,1,0:T(8,128)(2,1)S(1)}) custom-call(s32[2,8]{1,0:T(2,128)S(1)} %bitcast.13, bf16[8,2,256,256]{3,2,1,0:T(8,128)(2,1)S(1)} %shard_map.60.wave_ref, bf16[2,256,256]{2,1,0:T(8,128)(2,1)S(1)} %get-tuple-element.67.refs_0_, bf16[2,256,256]{2,1,0:T(8,128)(2,1)S(1)} %collective-permute-done.10.refs_1_, ...), custom_call_target="tpu_custom_call" | custom-call | bytes 4980800 | tf_op jit(solution)/shard_map/pallas_call | solution.py:26
  107.3 4.9 %collective-permute-done.18.refs_3_ = bf16[2,128,512]{2,1,0:T(8,128)(2,1)S(1)} collective-permute-done((bf16[2,128,512]{2,1,0:T(8,128)(2,1)S(1)}, bf16[2,128,512]{2,1,0:T(8,128)(2,1)S(1)}, u32[]{:S(2)}, u32[]{:S(2)}) %collective-permute-start.18) | collective-permute-done | bytes 262176 | tf_op jit(solution)/shard_map/ppermute | solution.py:259
  112.2 5.1 %collective-permute-done.17.refs_1_ = bf16[2,128,512]{2,1,0:T(8,128)(2,1)S(1)} collective-permute-done((bf16[2,128,512]{2,1,0:T(8,128)(2,1)S(1)}, bf16[2,128,512]{2,1,0:T(8,128)(2,1)S(1)}, u32[]{:S(2)}, u32[]{:S(2)}) %collective-permute-start.17) | collective-permute-done | bytes 262176 | tf_op jit(solution)/shard_map/ppermute | solution.py:259
  (28 shorter events, 5.8 us)
Async XLA Ops:
  0.0 1.0 copy-start.2
  1.0 1.0 copy-start.3
  2.1 27.7 %copy-start.1 = (bf16[8,2,256,256]{3,2,1,0:T(8,128)(2,1)S(1)}, bf16[8,2,256,256]{3,2,1,0:T(8,128)(2,1)}, u32[]{:S(2)}) copy-start(bf16[8,2,256,256]{3,2,1,0:T(8,128)(2,1)} %exit_ref.1) | copy-start | bytes 6291460
  2.8 10.1 %collective-permute-start.1 = (bf16[2,128,512]{2,1,0:T(8,128)(2,1)S(1)}, bf16[2,128,512]{2,1,0:T(8,128)(2,1)S(1)}, u32[]{:S(2)}, u32[]{:S(2)}) collective-permute-start(bf16[2,128,512]{2,1,0:T(8,128)(2,1)S(1)} %get-tuple-element.46.mine_ref), channel_id=1, source_target_pairs={{0,1},{1,0},{2,3},{3,2},{4,5},{5,4},{6,7},{7,6},{8,9},{9,8},{10,11... | collective-permute-start | bytes 786440 | tf_op jit(solution)/shard_map/ppermute | solution.py:259
  5.8 11.9 %collective-permute-start = (bf16[2,128,512]{2,1,0:T(8,128)(2,1)S(1)}, bf16[2,128,512]{2,1,0:T(8,128)(2,1)S(1)}, u32[]{:S(2)}, u32[]{:S(2)}) collective-permute-start(bf16[2,128,512]{2,1,0:T(8,128)(2,1)S(1)} %get-tuple-element.45.mine_ref), channel_id=1, source_target_pairs={{0,1},{1,0},{2,3},{3,2},{4,5},{5,4},{6,7},{7,6},{8,9},{9,8},{10,11... | collective-permute-start | bytes 786440 | tf_op jit(solution)/shard_map/ppermute | solution.py:259
  13.0 0.7 copy-start.4
  19.0 3.8 %collective-permute-start.2 = (bf16[2,256,256]{2,1,0:T(8,128)(2,1)S(1)}, bf16[2,256,256]{2,1,0:T(8,128)(2,1)S(1)}, u32[]{:S(2)}, u32[]{:S(2)}) collective-permute-start(bf16[2,256,256]{2,1,0:T(8,128)(2,1)S(1)} %get-tuple-element.56), channel_id=1, source_target_pairs={{0,2},{2,0},{4,6},{6,4},{8,10},{10,8},{12,14},{14,12},{16,18},{18,... | collective-permute-start | bytes 786440 | tf_op jit(solution)/shard_map/ppermute | solution.py:263
  19.1 9.2 %collective-permute-start.3 = (bf16[2,256,256]{2,1,0:T(8,128)(2,1)S(1)}, bf16[2,256,256]{2,1,0:T(8,128)(2,1)S(1)}, u32[]{:S(2)}, u32[]{:S(2)}) collective-permute-start(bf16[2,256,256]{2,1,0:T(8,128)(2,1)S(1)} %get-tuple-element.57), channel_id=1, source_target_pairs={{0,4},{2,6},{4,0},{6,2},{8,12},{10,14},{12,8},{14,10},{16,20},{18,... | collective-permute-start | bytes 786440 | tf_op jit(solution)/shard_map/ppermute | solution.py:263
  20.9 12.1 %collective-permute-start.4 = (bf16[2,256,256]{2,1,0:T(8,128)(2,1)S(1)}, bf16[2,256,256]{2,1,0:T(8,128)(2,1)S(1)}, u32[]{:S(2)}, u32[]{:S(2)}) collective-permute-start(bf16[2,256,256]{2,1,0:T(8,128)(2,1)S(1)} %get-tuple-element.58), channel_id=1, source_target_pairs={{0,6},{2,4},{4,2},{6,0},{8,14},{10,12},{12,10},{14,8},{16,22},{18,... | collective-permute-start | bytes 786440 | tf_op jit(solution)/shard_map/ppermute | solution.py:263
  21.0 12.0 %collective-permute-start.5 = (bf16[2,256,256]{2,1,0:T(8,128)(2,1)S(1)}, bf16[2,256,256]{2,1,0:T(8,128)(2,1)S(1)}, u32[]{:S(2)}, u32[]{:S(2)}) collective-permute-start(bf16[2,256,256]{2,1,0:T(8,128)(2,1)S(1)} %get-tuple-element.59), channel_id=1, source_target_pairs={{0,8},{2,10},{4,12},{6,14},{8,0},{10,2},{12,4},{14,6},{16,24},{18,... | collective-permute-start | bytes 786440 | tf_op jit(solution)/shard_map/ppermute | solution.py:263
  22.8 12.3 %collective-permute-start.6 = (bf16[2,256,256]{2,1,0:T(8,128)(2,1)S(1)}, bf16[2,256,256]{2,1,0:T(8,128)(2,1)S(1)}, u32[]{:S(2)}, u32[]{:S(2)}) collective-permute-start(bf16[2,256,256]{2,1,0:T(8,128)(2,1)S(1)} %get-tuple-element.60), channel_id=1, source_target_pairs={{0,10},{2,8},{4,14},{6,12},{8,2},{10,0},{12,6},{14,4},{16,26},{18,... | collective-permute-start | bytes 786440 | tf_op jit(solution)/shard_map/ppermute | solution.py:263
  22.8 19.7 %collective-permute-start.7 = (bf16[2,256,256]{2,1,0:T(8,128)(2,1)S(1)}, bf16[2,256,256]{2,1,0:T(8,128)(2,1)S(1)}, u32[]{:S(2)}, u32[]{:S(2)}) collective-permute-start(bf16[2,256,256]{2,1,0:T(8,128)(2,1)S(1)} %get-tuple-element.61), channel_id=1, source_target_pairs={{0,12},{2,14},{4,8},{6,10},{8,4},{10,6},{12,0},{14,2},{16,28},{18,... | collective-permute-start | bytes 786440 | tf_op jit(solution)/shard_map/ppermute | solution.py:263
  28.2 18.7 %collective-permute-start.8 = (bf16[2,256,256]{2,1,0:T(8,128)(2,1)S(1)}, bf16[2,256,256]{2,1,0:T(8,128)(2,1)S(1)}, u32[]{:S(2)}, u32[]{:S(2)}) collective-permute-start(bf16[2,256,256]{2,1,0:T(8,128)(2,1)S(1)} %get-tuple-element.62), channel_id=1, source_target_pairs={{0,14},{2,12},{4,10},{6,8},{8,6},{10,4},{12,2},{14,0},{16,30},{18,... | collective-permute-start | bytes 786440 | tf_op jit(solution)/shard_map/ppermute | solution.py:263
  47.0 6.7 %copy-start = (bf16[1,8,2,256,256]{4,3,2,1,0:T(8,128)(2,1)S(1)}, bf16[1,8,2,256,256]{4,3,2,1,0:T(8,128)(2,1)}, u32[]{:S(2)}) copy-start(bf16[1,8,2,256,256]{4,3,2,1,0:T(8,128)(2,1)} %param.7) | copy-start | bytes 6291460
  47.0 6.7 %copy-start.5 = (s32[8,2]{0,1:T(2,128)S(1)}, s32[8,2]{0,1:T(2,128)}, u32[]{:S(2)}) copy-start(s32[8,2]{0,1:T(2,128)} %param.9) | copy-start | bytes 196
  52.2 17.1 %collective-permute-start.9 = (bf16[2,256,256]{2,1,0:T(8,128)(2,1)S(1)}, bf16[2,256,256]{2,1,0:T(8,128)(2,1)S(1)}, u32[]{:S(2)}, u32[]{:S(2)}) collective-permute-start(bf16[2,256,256]{2,1,0:T(8,128)(2,1)S(1)} %get-tuple-element.63), channel_id=1, source_target_pairs={{16,0},{18,2},{20,4},{22,6},{24,8},{26,10},{28,12},{30,14},{17,1},... | collective-permute-start | bytes 786440 | tf_op jit(solution)/shard_map/ppermute | solution.py:285
  74.5 3.6 %collective-permute-start.10 = (bf16[2,256,256]{2,1,0:T(8,128)(2,1)S(1)}, bf16[2,256,256]{2,1,0:T(8,128)(2,1)S(1)}, u32[]{:S(2)}, u32[]{:S(2)}) collective-permute-start(bf16[2,256,256]{2,1,0:T(8,128)(2,1)S(1)} %get-tuple-element.68), channel_id=1, source_target_pairs={{0,2},{2,0},{4,6},{6,4},{8,10},{10,8},{12,14},{14,12},{16,18},{18,... | collective-permute-start | bytes 786440 | tf_op jit(solution)/shard_map/ppermute | solution.py:263
  74.5 9.2 %collective-permute-start.11 = (bf16[2,256,256]{2,1,0:T(8,128)(2,1)S(1)}, bf16[2,256,256]{2,1,0:T(8,128)(2,1)S(1)}, u32[]{:S(2)}, u32[]{:S(2)}) collective-permute-start(bf16[2,256,256]{2,1,0:T(8,128)(2,1)S(1)} %get-tuple-element.69), channel_id=1, source_target_pairs={{0,4},{2,6},{4,0},{6,2},{8,12},{10,14},{12,8},{14,10},{16,20},{18,... | collective-permute-start | bytes 786440 | tf_op jit(solution)/shard_map/ppermute | solution.py:263
  74.9 13.5 %collective-permute-start.12 = (bf16[2,256,256]{2,1,0:T(8,128)(2,1)S(1)}, bf16[2,256,256]{2,1,0:T(8,128)(2,1)S(1)}, u32[]{:S(2)}, u32[]{:S(2)}) collective-permute-start(bf16[2,256,256]{2,1,0:T(8,128)(2,1)S(1)} %get-tuple-element.70), channel_id=1, source_target_pairs={{0,6},{2,4},{4,2},{6,0},{8,14},{10,12},{12,10},{14,8},{16,22},{18,... | collective-permute-start | bytes 786440 | tf_op jit(solution)/shard_map/ppermute | solution.py:263
  76.4 12.0 %collective-permute-start.13 = (bf16[2,256,256]{2,1,0:T(8,128)(2,1)S(1)}, bf16[2,256,256]{2,1,0:T(8,128)(2,1)S(1)}, u32[]{:S(2)}, u32[]{:S(2)}) collective-permute-start(bf16[2,256,256]{2,1,0:T(8,128)(2,1)S(1)} %get-tuple-element.71), channel_id=1, source_target_pairs={{0,8},{2,10},{4,12},{6,14},{8,0},{10,2},{12,4},{14,6},{16,24},{18,... | collective-permute-start | bytes 786440 | tf_op jit(solution)/shard_map/ppermute | solution.py:263
  76.4 13.6 %collective-permute-start.14 = (bf16[2,256,256]{2,1,0:T(8,128)(2,1)S(1)}, bf16[2,256,256]{2,1,0:T(8,128)(2,1)S(1)}, u32[]{:S(2)}, u32[]{:S(2)}) collective-permute-start(bf16[2,256,256]{2,1,0:T(8,128)(2,1)S(1)} %get-tuple-element.72), channel_id=1, source_target_pairs={{0,10},{2,8},{4,14},{6,12},{8,2},{10,0},{12,6},{14,4},{16,26},{18,... | collective-permute-start | bytes 786440 | tf_op jit(solution)/shard_map/ppermute | solution.py:263
  78.1 18.4 %collective-permute-start.15 = (bf16[2,256,256]{2,1,0:T(8,128)(2,1)S(1)}, bf16[2,256,256]{2,1,0:T(8,128)(2,1)S(1)}, u32[]{:S(2)}, u32[]{:S(2)}) collective-permute-start(bf16[2,256,256]{2,1,0:T(8,128)(2,1)S(1)} %get-tuple-element.73), channel_id=1, source_target_pairs={{0,12},{2,14},{4,8},{6,10},{8,4},{10,6},{12,0},{14,2},{16,28},{18,... | collective-permute-start | bytes 786440 | tf_op jit(solution)/shard_map/ppermute | solution.py:263
  83.7 17.3 %collective-permute-start.16 = (bf16[2,256,256]{2,1,0:T(8,128)(2,1)S(1)}, bf16[2,256,256]{2,1,0:T(8,128)(2,1)S(1)}, u32[]{:S(2)}, u32[]{:S(2)}) collective-permute-start(bf16[2,256,256]{2,1,0:T(8,128)(2,1)S(1)} %get-tuple-element.74), channel_id=1, source_target_pairs={{0,14},{2,12},{4,10},{6,8},{8,6},{10,4},{12,2},{14,0},{16,30},{18,... | collective-permute-start | bytes 786440 | tf_op jit(solution)/shard_map/ppermute | solution.py:263
  103.1 9.2 %collective-permute-start.18 = (bf16[2,128,512]{2,1,0:T(8,128)(2,1)S(1)}, bf16[2,128,512]{2,1,0:T(8,128)(2,1)S(1)}, u32[]{:S(2)}, u32[]{:S(2)}) collective-permute-start(bf16[2,128,512]{2,1,0:T(8,128)(2,1)S(1)} %get-tuple-element.78), channel_id=1, source_target_pairs={{0,1},{1,0},{2,3},{3,2},{4,5},{5,4},{6,7},{7,6},{8,9},{9,8},{10,11... | collective-permute-start | bytes 786440 | tf_op jit(solution)/shard_map/ppermute | solution.py:259
  106.9 10.5 %collective-permute-start.17 = (bf16[2,128,512]{2,1,0:T(8,128)(2,1)S(1)}, bf16[2,128,512]{2,1,0:T(8,128)(2,1)S(1)}, u32[]{:S(2)}, u32[]{:S(2)}) collective-permute-start(bf16[2,128,512]{2,1,0:T(8,128)(2,1)S(1)} %get-tuple-element.76), channel_id=1, source_target_pairs={{0,1},{1,0},{2,3},{3,2},{4,5},{5,4},{6,7},{7,6},{8,9},{9,8},{10,11... | collective-permute-start | bytes 786440 | tf_op jit(solution)/shard_map/ppermute | solution.py:259

commit v7 on v6

--- a/solution.py
+++ b/solution.py
@@ -13,6 +13,7 @@
 turning = 0.011
 code_gain = 83.0
 chunk_count = 2
+far = 2
 f32 = jnp.float32
 bf16 = jnp.bfloat16
 
@@ -45,21 +46,19 @@
     return lax.rem(lax.axis_index("sec").astype(jnp.int32), count)
 
 
-def code_kernel(amp_ref, phase_ref, *code_refs):
-    rows = code_refs[0].shape[1]
-    for chunk, code_ref in enumerate(code_refs):
-        amp = amp_ref[pl.ds(chunk * rows, rows), :]
-        half = 0.5 * phase_ref[pl.ds(chunk * rows, rows), :]
-        square = half * half
-        sine = jnp.full_like(half, 1.0 / math.factorial(13))
-        cosine = jnp.full_like(half, 1.0 / math.factorial(12))
-        for power in (11, 9, 7, 5, 3, 1):
-            sign = -1.0 if power % 4 == 3 else 1.0
-            sine = sine * square + sign / math.factorial(power)
-            cosine = cosine * square + sign / math.factorial(power - 1)
-        sine = sine * half
-        code_ref[0] = jnp.exp((code_gain * amp) * (1.0 - 2.0 * sine * sine)).astype(bf16)
-        code_ref[1] = jnp.exp((code_gain * amp) * (2.0 * sine * cosine)).astype(bf16)
+def coded(amp, phase):
+    half = 0.5 * phase
+    square = half * half
+    sine = jnp.full_like(half, 1.0 / math.factorial(13))
+    cosine = jnp.full_like(half, 1.0 / math.factorial(12))
+    for power in (11, 9, 7, 5, 3, 1):
+        sign = -1.0 if power % 4 == 3 else 1.0
+        sine = sine * square + sign / math.factorial(power)
+        cosine = cosine * square + sign / math.factorial(power - 1)
+    sine = sine * half
+    trans_re = amp * (1.0 - 2.0 * sine * sine)
+    trans_im = amp * (2.0 * sine * cosine)
+    return jnp.stack([jnp.exp(code_gain * trans_re).astype(bf16), jnp.exp(code_gain * trans_im).astype(bf16)])
 
 
 def first_masks(corner_ref, position, base, shape):
@@ -70,20 +69,25 @@
     return at_first != place, col >= corner_ref[1, position]
 
 
+def distances(count):
+    return sorted(range(count), key=lambda d: (d >= count - far, d > 0, d == 1, d % 2, d))
+
+
 def cut_kernel(base, count, corner_ref, mine_ref, other_ref, *refs):
     own = place_in_group(count)
-    for apart, win_ref in enumerate(refs[-count:]):
-        _, rows, width = mine_ref.shape
-        window = width // 2
-        if base:
-            win_ref[:, :base] = refs[apart][:, :base]
+    _, rows, width = mine_ref.shape
+    window = width // 2
+    for i, (apart, win_ref) in enumerate(zip(distances(count), refs[-count:])):
+        here = pl.ds(0 if i >= count - far else base, rows)
+        if base and i < count - far:
+            win_ref[:, :base] = refs[i][:, :base]
         in_mine, in_left = first_masks(corner_ref, own ^ apart, base, (rows, window))
         for part in range(2):
             left, right = (
                 jnp.where(in_mine, mine_ref[part, :, cols].astype(f32), other_ref[part, :, cols].astype(f32))
                 for cols in (slice(0, window), slice(window, 2 * window))
             )
-            win_ref[part, pl.ds(base, rows), :] = jnp.where(in_left, left, right).astype(bf16)
+            win_ref[part, here, :] = jnp.where(in_left, left, right).astype(bf16)
 
 
 def turned(wave, row_at, col_at):
@@ -151,16 +155,23 @@
     return chi_re, chi_im
 
 
+def in_pieces(count, window):
+    rows = window // chunk_count
+    near = [(apart, slice(0, window)) for apart in distances(count)[:-far]]
+    cut = [(count - far + i, slice(c * rows, (c + 1) * rows)) for c in range(chunk_count) for i in range(far)]
+    return list(zip(*near, *cut))
+
+
 def decoded(held_ref, layer):
     return [jnp.log(held_ref[layer, part].astype(f32)) * (1.0 / code_gain) for part in range(2)]
 
 
 def first_kernel(start_ref, down_ref, across_ref, *refs):
     *win_refs, leave_ref, held_ref = refs
-    count = len(win_refs)
+    count, _, window, _ = held_ref.shape
     own = place_in_group(count)
-    for apart in range(count):
-        held_ref[own ^ apart] = win_refs[apart][...]
+    for win_ref, apart, here in zip(win_refs, *in_pieces(count, window)):
+        held_ref[own ^ apart, :, here] = win_ref[...]
     leave_ref[0], leave_ref[1] = pass_group(
         down_ref[...],
         across_ref[...],
@@ -192,8 +203,8 @@
     if not is_last:
         refs[0][0], refs[0][1] = chi
         return
-    for apart in range(count):
-        refs[apart][...] = refs[-1][own ^ apart]
+    for spread_ref, apart, here in zip(refs, *in_pieces(count, window)):
+        spread_ref[...] = refs[-1][own ^ apart, :, here]
 
 
 def gradient_kernel(base, corner_ref, wave_ref, *refs):
@@ -207,11 +218,12 @@
         at = pl.multiple_of(block * tall, tall)
         sums = [jnp.zeros((tall, window), f32) for _ in range(8)]
         here = pl.ds(base + at, tall)
-        for apart, spread_ref in enumerate(spread_refs):
+        for apart, spread_ref in zip(distances(len(spread_refs)), spread_refs):
             position = own ^ apart
+            there = pl.ds(at, tall) if apart >= len(spread_refs) - far else here
             in_mine, in_left = first_masks(corner_ref, position, base + at, (tall, window))
             wave_re, wave_im = (wave_ref[position, part, here, :].astype(f32) for part in range(2))
-            spread_re, spread_im = (spread_ref[part, here, :].astype(f32) for part in range(2))
+            spread_re, spread_im = (spread_ref[part, there, :].astype(f32) for part in range(2))
             parts = (
                 wave_re * spread_re + wave_im * spread_im,
                 wave_re * spread_im - wave_im * spread_re,
@@ -258,26 +270,37 @@
     def to_other_half(value):
         return lax.ppermute(value, "scan", [(0, 1), (1, 0)])
 
-    def exchange(values):
-        return [values[0]] + [
-            lax.ppermute(values[d], "sec", [(s, s ^ d) for s in range(sections)]) for d in range(1, count)
-        ]
-
-    mine = call(code_kernel, [shape_of(piece, bf16)] * chunk_count)(obj_amp[0], obj_phase[0])
-    windows = []
+    def to_distance(value, d):
+        return lax.ppermute(value, "sec", [(s, s ^ d) for s in range(sections)])
+
+    def exchange(near):
+        return [to_distance(value, d) if d else value for d, value in zip(distances(count), near)]
+
+    def exchange_far(values):
+        return [to_distance(value, count - far + i) for i, value in enumerate(values)]
+
+    mine = [coded(obj_amp[0, c * rows : (c + 1) * rows], obj_phase[0, c * rows : (c + 1) * rows]) for c in chunks]
+    other = [to_other_half(value) for value in mine]
+    ready = call(ready_kernel, [shape_of(wave, bf16)] + [shape_of((window, window), bf16)] * 2, prefetch=1)
+    start, down, across = ready(corners, exit_adjoint)
+    other[0], start, down, across = lax.optimization_barrier((other[0], start, down, across))
+    near, distant = [], []
     for c in chunks:
         cut = call(
             functools.partial(cut_kernel, c * rows, count),
-            [shape_of(wave, bf16)] * count,
+            [shape_of(wave, bf16)] * (count - far) + [shape_of((2, rows, window), bf16)] * far,
             prefetch=1,
-            aliases={3 + i: i for i in range(len(windows))},
+            aliases={3 + i: i for i in range(len(near))},
         )
-        windows = cut(corners, mine[c], to_other_half(mine[c]), *windows)
-    windows = exchange(windows)
-    ready = call(ready_kernel, [shape_of(wave, bf16)] + [shape_of((window, window), bf16)] * 2, prefetch=1)
-    start, down, across = ready(corners, exit_adjoint)
+        if distant:
+            other[c], distant[-far] = lax.optimization_barrier((other[c], distant[-far]))
+        cuts = cut(corners, mine[c], other[c], *near)
+        near = cuts[: count - far]
+        distant += exchange_far(cuts[count - far :])
+    windows = exchange(near) + distant
     waves = call(turn_kernel, shape_of(forward_waves.shape[1:], bf16), prefetch=1)(corners, forward_waves[0])
 
+    pieces = [shape_of(wave, bf16)] * (count - far) + [shape_of((2, rows, window), bf16)] * (far * chunk_count)
     cost = (count * 16 * window**3, count * 2 * window**2)
     first = call(first_kernel, [shape_of(wave, bf16), shape_of((count,) + wave, bf16)], cost=cost, grant=12)
     leave, held = first(start, down, across, *windows)
@@ -287,20 +310,23 @@
         is_last = stage == group_count - 1
         through = call(
             functools.partial(next_kernel, is_last),
-            [shape_of(wave, bf16)] * count if is_last else shape_of(wave, bf16),
+            pieces if is_last else shape_of(wave, bf16),
             scratch=[pltpu.VMEM((count,) + wave, bf16)] if is_last else [],
             cost=cost,
             grant=12,
         )
         leave = through(start, come, down, across, held)
 
-    came = exchange(leave)
+    near, distant = leave[: count - far], leave[count - far :]
+    came_far = [exchange_far(distant[:far])]
+    came = exchange(near)
+    came_far += [exchange_far(distant[c * far : (c + 1) * far]) for c in chunks[1:]]
     sums = []
     for c in chunks:
         gradient = call(
             functools.partial(gradient_kernel, c * rows), [shape_of(piece, f32), shape_of(piece, bf16)], prefetch=1
         )
-        keep, away = gradient(corners, waves, *came)
+        keep, away = gradient(corners, waves, *came, *came_far[c])
         sums += [keep, to_other_half(away)]
     return call(finish_kernel, shape_of((2, half, width), f32))(*sums)[None]
 

time: 119 us -> 108 us (0.908)
  waiting for transfers between devices: 74.7 us -> 58.3 us
  starting transfers between devices: 18.4 us -> 25.2 us
  local copies, waits for them, and re-layouts: 2.77 us -> 0.01 us
  other arithmetic: 0 us -> 2.08 us
    ppermute x14 -> x18, waiting for transfers between devices: 41.5 us -> 29.6 us  [to_distance(): return lax.ppermute(value, 'sec', [(s, s ^ d) for s in range(sections)])]
    ppermute x14 -> x18, starting transfers between devices: 11.7 us -> 18.1 us  [to_distance(): return lax.ppermute(value, 'sec', [(s, s ^ d) for s in range(sections)])]
    ppermute x4, waiting for transfers between devices: 20.1 us -> 15.9 us  [to_other_half(): return lax.ppermute(value, 'scan', [(0, 1), (1, 0)])]
    unnamed x12 -> x6, local copies, waits for them, and re-layouts: 2.77 us -> 0.01 us
    convert_element_type x0 -> x1, other arithmetic: none -> 2.03 us  [coded(): jnp.exp(code_gain * trans_re).astype(bf16)]
    pallas_call x10 -> x9, Pallas kernels: 22.4 us -> 21.8 us  [run(): pl.pallas_call(kernel, grid_spec=pltpu.PrefetchScalarGridSpec(num_scalar_...]
  transfers between devices with their start and end apart: 19 -> 23, of which waited for: 15 -> 15; matrix products, arithmetic and copies ran while one was open for 0% -> 0% of each run, Pallas kernels for 6% -> 9%
where the time goes in v7:
time: 108 us; the launch traced here: 107 us
  waiting for transfers between devices  58.3 us (54%)
  starting transfers between devices  25.2 us (23%)
  Pallas kernels  21.8 us (20%)
  other arithmetic  2.08 us (2%)
    ppermute x18, waiting for transfers between devices, to_distance(): return lax.ppermute(value, 'sec', [(s, s ^ d) for s in range(sections)])  29.6 us
    pallas_call x9, Pallas kernels, run(): pl.pallas_call(kernel, grid_spec=pltpu.PrefetchScalarGridSpec(num_scalar_...  21.8 us
    ppermute x18, starting transfers between devices, to_distance(): return lax.ppermute(value, 'sec', [(s, s ^ d) for s in range(sections)])  18.1 us
    ppermute x4, waiting for transfers between devices, to_other_half(): return lax.ppermute(value, 'scan', [(0, 1), (1, 0)])  15.9 us
    ppermute x1, waiting for transfers between devices, on_device(): lax.ppermute(leave, 'sec', [(s, s - count) for s in range(count, sections)])  12.8 us
    ppermute x4, starting transfers between devices, to_other_half(): return lax.ppermute(value, 'scan', [(0, 1), (1, 0)])  5.63 us
  transfers between devices with their start and end apart: 23, of which 15 were waited for; matrix products, arithmetic and copies ran while one was open for 0% of the time, Pallas kernels for 9%

profile of v7, /device:TPU:0, one launch (start us, length us, event | category | flops | bytes accessed | tf_op | source)
XLA Modules:
  0.0 107.4 jit_solution(8502395637968579143)
XLA Ops:
  0.0 2.0 %fusion.13 = (bf16[1,128,512]{2,1,0:T(8,128)(2,1)S(1)}, bf16[1,128,512]{2,1,0:T(8,128)(2,1)S(1)}, bf16[1,128,512]{2,1,0:T(8,128)(2,1)S(1)}, bf16[1,128,512]{2,1,0:T(8,128)(2,1)S(1)}) fusion(f32[1,256,512]{2,1,0:T(8,128)} %param.5, f32[1,256,512]{2,1,0:T(8,128)} %param.6), kind=kLoop, calls=%fused_computation.17 | loop fusion | flops 4849664 | bytes 1572864 | tf_op jit(solution)/shard_map/convert_element_type | solution.py:61
  2.1 3.0 %collective-permute-start = (bf16[2,128,512]{2,1,0:T(8,128)(2,1)S(1)}, bf16[2,128,512]{2,1,0:T(8,128)(2,1)S(1)}, u32[]{:S(2)}, u32[]{:S(2)}) collective-permute-start(bf16[2,128,512]{2,1,0:T(8,128)(2,1)S(1)} %pad_maximum_fusion.mine_ref), channel_id=1, source_target_pairs={{0,1},{1,0},{2,3},{3,2},{4,5},{5,4},{6,7},{7,6},{8,9},{9,8},{10,11... | collective-permute-start | bytes 786440 | tf_op jit(solution)/shard_map/ppermute | solution.py:271
  5.2 1.2 %shard_map.55 = (bf16[2,256,256]{2,1,0:T(8,128)(2,1)S(1)}, bf16[256,256]{1,0:T(8,128)(2,1)S(1)}, bf16[256,256]{1,0:T(8,128)(2,1)S(1)}) custom-call(s32[2,8]{1,0:T(2,128)S(1)} %bitcast.4, bf16[8,2,256,256]{3,2,1,0:T(8,128)(2,1)S(1)} %copy-done.1), custom_call_target="tpu_custom_call" | custom-call | bytes 2621504 | tf_op jit(solution)/shard_map/pallas_call | solution.py:27
  6.4 5.8 %collective-permute-done.other_ref = bf16[2,128,512]{2,1,0:T(8,128)(2,1)S(1)} collective-permute-done((bf16[2,128,512]{2,1,0:T(8,128)(2,1)S(1)}, bf16[2,128,512]{2,1,0:T(8,128)(2,1)S(1)}, u32[]{:S(2)}, u32[]{:S(2)}) %collective-permute-start) | collective-permute-done | bytes 262176 | tf_op jit(solution)/shard_map/ppermute | solution.py:271
  12.2 1.1 %shard_map.56 = (bf16[2,256,256]{2,1,0:T(8,128)(2,1)S(1)}, bf16[2,256,256]{2,1,0:T(8,128)(2,1)S(1)}, bf16[2,256,256]{2,1,0:T(8,128)(2,1)S(1)}, bf16[2,256,256]{2...) custom-call(s32[2,8]{1,0:T(2,128)S(1)} %bitcast.5, ...), custom_call_target="tpu_custom_call" | custom-call | bytes 2359360 | tf_op jit(solution)/shard_map/pallas_call | solution.py:27
  13.4 3.2 %collective-permute-start.2 = (bf16[2,128,256]{2,1,0:T(8,128)(2,1)S(1)}, bf16[2,128,256]{2,1,0:T(8,128)(2,1)S(1)}, u32[]{:S(2)}, u32[]{:S(2)}) collective-permute-start(bf16[2,128,256]{2,1,0:T(8,128)(2,1)S(1)} %get-tuple-element.55), channel_id=1, source_target_pairs={{0,12},{2,14},{4,8},{6,10},{8,4},{10,6},{12,0},{14,2},{16,28},{18,... | collective-permute-start | bytes 393224 | tf_op jit(solution)/shard_map/ppermute | solution.py:274
  17.0 2.9 %collective-permute-done.2.refs_6_ = bf16[2,128,256]{2,1,0:T(8,128)(2,1)S(1)} collective-permute-done((bf16[2,128,256]{2,1,0:T(8,128)(2,1)S(1)}, bf16[2,128,256]{2,1,0:T(8,128)(2,1)S(1)}, u32[]{:S(2)}, u32[]{:S(2)}) %collective-permute-start.2) | collective-permute-done | bytes 131104 | tf_op jit(solution)/shard_map/ppermute | solution.py:274
  19.9 1.2 %shard_map.57 = (bf16[2,256,256]{2,1,0:T(8,128)(2,1)S(1)}, bf16[2,256,256]{2,1,0:T(8,128)(2,1)S(1)}, bf16[2,256,256]{2,1,0:T(8,128)(2,1)S(1)}, bf16[2,256,256]{2...) custom-call(s32[2,8]{1,0:T(2,128)S(1)} %bitcast.6, ...), custom_call_target="tpu_custom_call", output_to_operand_aliasing={{0}: (3, {}), {1}: (4, {}), {2}: (5, {}), {3}: (6, {}), {4}... | custom-call | bytes 3932224 | tf_op jit(solution)/shard_map/pallas_call | solution.py:27
  21.1 3.4 %collective-permute-start.9 = (bf16[2,128,256]{2,1,0:T(8,128)(2,1)S(1)}, bf16[2,128,256]{2,1,0:T(8,128)(2,1)S(1)}, u32[]{:S(2)}, u32[]{:S(2)}) collective-permute-start(bf16[2,128,256]{2,1,0:T(8,128)(2,1)S(1)} %get-tuple-element.71), channel_id=1, source_target_pairs={{0,12},{2,14},{4,8},{6,10},{8,4},{10,6},{12,0},{14,2},{16,28},{18,... | collective-permute-start | bytes 393224 | tf_op jit(solution)/shard_map/ppermute | solution.py:274
  25.3 2.2 %collective-permute-start.5 = (bf16[2,256,256]{2,1,0:T(8,128)(2,1)S(1)}, bf16[2,256,256]{2,1,0:T(8,128)(2,1)S(1)}, u32[]{:S(2)}, u32[]{:S(2)}) collective-permute-start(bf16[2,256,256]{2,1,0:T(8,128)(2,1)S(1)} %get-tuple-element.66), channel_id=1, source_target_pairs={{0,6},{2,4},{4,2},{6,0},{8,14},{10,12},{12,10},{14,8},{16,22},{18,... | collective-permute-start | bytes 786440 | tf_op jit(solution)/shard_map/ppermute | solution.py:274
  28.4 2.8 %collective-permute-done.10.refs_9_ = bf16[2,128,256]{2,1,0:T(8,128)(2,1)S(1)} collective-permute-done((bf16[2,128,256]{2,1,0:T(8,128)(2,1)S(1)}, bf16[2,128,256]{2,1,0:T(8,128)(2,1)S(1)}, u32[]{:S(2)}, u32[]{:S(2)}) %collective-permute-start.10) | collective-permute-done | bytes 131104 | tf_op jit(solution)/shard_map/ppermute | solution.py:274
  31.1 4.9 %collective-permute-done.3.refs_1_ = bf16[2,256,256]{2,1,0:T(8,128)(2,1)S(1)} collective-permute-done((bf16[2,256,256]{2,1,0:T(8,128)(2,1)S(1)}, bf16[2,256,256]{2,1,0:T(8,128)(2,1)S(1)}, u32[]{:S(2)}, u32[]{:S(2)}) %collective-permute-start.3) | collective-permute-done | bytes 262176 | tf_op jit(solution)/shard_map/ppermute | solution.py:274
  36.4 5.1 %collective-permute-done.5.refs_3_ = bf16[2,256,256]{2,1,0:T(8,128)(2,1)S(1)} collective-permute-done((bf16[2,256,256]{2,1,0:T(8,128)(2,1)S(1)}, bf16[2,256,256]{2,1,0:T(8,128)(2,1)S(1)}, u32[]{:S(2)}, u32[]{:S(2)}) %collective-permute-start.5) | collective-permute-done | bytes 262176 | tf_op jit(solution)/shard_map/ppermute | solution.py:274
  41.5 5.2 %shard_map.58 = (bf16[2,256,256]{2,1,0:T(8,128)(2,1)S(1)}, bf16[8,2,256,256]{3,2,1,0:T(8,128)(2,1)S(1)}) custom-call(bf16[2,256,256]{2,1,0:T(8,128)(2,1)S(1)} %get-tuple-element.51.start_ref, bf16[256,256]{1,0:T(8,128)(2,1)S(1)} %get-tuple-element.52.down_ref, bf16[256,256]{1,0:T(8,128)(2,1)S(1)} %get-tuple-element.53.across_ref, ...), custom_call_target="tpu_custom_call" | custom-call | flops 2147483648 | bytes 4980736 | tf_op jit(solution)/shard_map/pallas_call | solution.py:27
  46.8 1.5 %collective-permute-start.11 = (bf16[2,256,256]{2,1,0:T(8,128)(2,1)S(1)}, bf16[2,256,256]{2,1,0:T(8,128)(2,1)S(1)}, u32[]{:S(2)}, u32[]{:S(2)}) collective-permute-start(bf16[2,256,256]{2,1,0:T(8,128)(2,1)S(1)} %get-tuple-element.73), channel_id=1, source_target_pairs={{16,0},{18,2},{20,4},{22,6},{24,8},{26,10},{28,12},{30,14},{17,1},... | collective-permute-start | bytes 786440 | tf_op jit(solution)/shard_map/ppermute | solution.py:308
  48.2 2.5 %shard_map.59.wave_ref = bf16[8,2,256,256]{3,2,1,0:T(8,128)(2,1)S(1)} custom-call(s32[2,8]{1,0:T(2,128)S(1)} %bitcast.7, bf16[8,2,256,256]{3,2,1,0:T(8,128)(2,1)S(1)} %bitcast.3), custom_call_target="tpu_custom_call" | custom-call | bytes 4194368 | tf_op jit(solution)/shard_map/pallas_call | solution.py:27
  50.7 12.8 %collective-permute-done.11.come_ref = bf16[2,256,256]{2,1,0:T(8,128)(2,1)S(1)} collective-permute-done((bf16[2,256,256]{2,1,0:T(8,128)(2,1)S(1)}, bf16[2,256,256]{2,1,0:T(8,128)(2,1)S(1)}, u32[]{:S(2)}, u32[]{:S(2)}) %collective-permute-start.11) | collective-permute-done | bytes 262176 | tf_op jit(solution)/shard_map/ppermute | solution.py:308
  63.5 5.3 %shard_map.60 = (bf16[2,256,256]{2,1,0:T(8,128)(2,1)S(1)}, bf16[2,256,256]{2,1,0:T(8,128)(2,1)S(1)}, bf16[2,256,256]{2,1,0:T(8,128)(2,1)S(1)}, bf16[2,256,256]{2...) custom-call(bf16[2,256,256]{2,1,0:T(8,128)(2,1)S(1)} %get-tuple-elem, ...), custom_call_target="tpu_custom_call" | custom-call | flops 2147483648 | bytes 4980736 | tf_op jit(solution)/shard_map/pallas_call | solution.py:27
  68.8 1.5 %collective-permute-start.21 = (bf16[2,128,256]{2,1,0:T(8,128)(2,1)S(1)}, bf16[2,128,256]{2,1,0:T(8,128)(2,1)S(1)}, u32[]{:S(2)}, u32[]{:S(2)}) collective-permute-start(bf16[2,128,256]{2,1,0:T(8,128)(2,1)S(1)} %get-tuple-element.88), channel_id=1, source_target_pairs={{0,14},{2,12},{4,10},{6,8},{8,6},{10,4},{12,2},{14,0},{16,30},{18,... | collective-permute-start | bytes 393224 | tf_op jit(solution)/shard_map/ppermute | solution.py:274
  70.4 1.9 %collective-permute-start.12 = (bf16[2,256,256]{2,1,0:T(8,128)(2,1)S(1)}, bf16[2,256,256]{2,1,0:T(8,128)(2,1)S(1)}, u32[]{:S(2)}, u32[]{:S(2)}) collective-permute-start(bf16[2,256,256]{2,1,0:T(8,128)(2,1)S(1)} %get-tuple-element.78), channel_id=1, source_target_pairs={{0,4},{2,6},{4,0},{6,2},{8,12},{10,14},{12,8},{14,10},{16,20},{18,... | collective-permute-start | bytes 786440 | tf_op jit(solution)/shard_map/ppermute | solution.py:274
  72.3 0.9 collective-permute-start.14
  73.2 2.8 %collective-permute-done.20.refs_6_ = bf16[2,128,256]{2,1,0:T(8,128)(2,1)S(1)} collective-permute-done((bf16[2,128,256]{2,1,0:T(8,128)(2,1)S(1)}, bf16[2,128,256]{2,1,0:T(8,128)(2,1)S(1)}, u32[]{:S(2)}, u32[]{:S(2)}) %collective-permute-start.20) | collective-permute-done | bytes 131104 | tf_op jit(solution)/shard_map/ppermute | solution.py:274
  76.0 2.6 %collective-permute-start.16 = (bf16[2,256,256]{2,1,0:T(8,128)(2,1)S(1)}, bf16[2,256,256]{2,1,0:T(8,128)(2,1)S(1)}, u32[]{:S(2)}, u32[]{:S(2)}) collective-permute-start(bf16[2,256,256]{2,1,0:T(8,128)(2,1)S(1)} %get-tuple-element.82), channel_id=1, source_target_pairs={{0,2},{2,0},{4,6},{6,4},{8,10},{10,8},{12,14},{14,12},{16,18},{18,... | collective-permute-start | bytes 786440 | tf_op jit(solution)/shard_map/ppermute | solution.py:274
  78.6 4.2 %collective-permute-done.12.refs_1_ = bf16[2,256,256]{2,1,0:T(8,128)(2,1)S(1)} collective-permute-done((bf16[2,256,256]{2,1,0:T(8,128)(2,1)S(1)}, bf16[2,256,256]{2,1,0:T(8,128)(2,1)S(1)}, u32[]{:S(2)}, u32[]{:S(2)}) %collective-permute-start.12) | collective-permute-done | bytes 262176 | tf_op jit(solution)/shard_map/ppermute | solution.py:274
  83.3 1.4 %collective-permute-done.13.refs_2_ = bf16[2,256,256]{2,1,0:T(8,128)(2,1)S(1)} collective-permute-done((bf16[2,256,256]{2,1,0:T(8,128)(2,1)S(1)}, bf16[2,256,256]{2,1,0:T(8,128)(2,1)S(1)}, u32[]{:S(2)}, u32[]{:S(2)}) %collective-permute-start.13) | collective-permute-done | bytes 262176 | tf_op jit(solution)/shard_map/ppermute | solution.py:274
  85.3 4.7 %collective-permute-done.14.refs_3_ = bf16[2,256,256]{2,1,0:T(8,128)(2,1)S(1)} collective-permute-done((bf16[2,256,256]{2,1,0:T(8,128)(2,1)S(1)}, bf16[2,256,256]{2,1,0:T(8,128)(2,1)S(1)}, u32[]{:S(2)}, u32[]{:S(2)}) %collective-permute-start.14) | collective-permute-done | bytes 262176 | tf_op jit(solution)/shard_map/ppermute | solution.py:274
  90.0 2.1 %shard_map.62 = (f32[2,128,512]{2,1,0:T(8,128)S(1)}, bf16[2,128,512]{2,1,0:T(8,128)(2,1)S(1)}) custom-call(s32[2,8]{1,0:T(2,128)S(1)} %bitcast.8, bf16[8,2,256,256]{3,2,1,0:T(8,128)(2,1)S(1)} %shard_map.59.wave_ref, bf16[2,256,256]{2,1,0:T(8,128)(2,1)S(1)} %get-tuple-element.77.refs_0_, bf16[2,256,256]{2,1,0:T(8,128)(2,1)S(1)} %collective-permute-done.12.refs_1_, ...), custom_call_target="tpu_custom_call" | custom-call | bytes 4718656 | tf_op jit(solution)/shard_map/pallas_call | solution.py:27
  92.0 1.9 %collective-permute-start.22 = (bf16[2,128,512]{2,1,0:T(8,128)(2,1)S(1)}, bf16[2,128,512]{2,1,0:T(8,128)(2,1)S(1)}, u32[]{:S(2)}, u32[]{:S(2)}) collective-permute-start(bf16[2,128,512]{2,1,0:T(8,128)(2,1)S(1)} %get-tuple-element.90), channel_id=1, source_target_pairs={{0,1},{1,0},{2,3},{3,2},{4,5},{5,4},{6,7},{7,6},{8,9},{9,8},{10,11... | collective-permute-start | bytes 786440 | tf_op jit(solution)/shard_map/ppermute | solution.py:271
  94.0 2.1 %shard_map.61 = (f32[2,128,512]{2,1,0:T(8,128)S(1)}, bf16[2,128,512]{2,1,0:T(8,128)(2,1)S(1)}) custom-call(s32[2,8]{1,0:T(2,128)S(1)} %bitcast.9, bf16[8,2,256,256]{3,2,1,0:T(8,128)(2,1)S(1)} %shard_map.59.wave_ref, bf16[2,256,256]{2,1,0:T(8,128)(2,1)S(1)} %get-tuple-element.77.refs_0_, bf16[2,256,256]{2,1,0:T(8,128)(2,1)S(1)} %collective-permute-done.12.refs_1_, ...), custom_call_target="tpu_custom_call" | custom-call | bytes 4718656 | tf_op jit(solution)/shard_map/pallas_call | solution.py:27
  96.7 4.5 %collective-permute-done.22.refs_3_ = bf16[2,128,512]{2,1,0:T(8,128)(2,1)S(1)} collective-permute-done((bf16[2,128,512]{2,1,0:T(8,128)(2,1)S(1)}, bf16[2,128,512]{2,1,0:T(8,128)(2,1)S(1)}, u32[]{:S(2)}, u32[]{:S(2)}) %collective-permute-start.22) | collective-permute-done | bytes 262176 | tf_op jit(solution)/shard_map/ppermute | solution.py:271
  101.2 5.2 %collective-permute-done.19.refs_1_ = bf16[2,128,512]{2,1,0:T(8,128)(2,1)S(1)} collective-permute-done((bf16[2,128,512]{2,1,0:T(8,128)(2,1)S(1)}, bf16[2,128,512]{2,1,0:T(8,128)(2,1)S(1)}, u32[]{:S(2)}, u32[]{:S(2)}) %collective-permute-start.19) | collective-permute-done | bytes 262176 | tf_op jit(solution)/shard_map/ppermute | solution.py:271
  106.4 1.1 shard_map.63
  (32 shorter events, 4.5 us)
Async XLA Ops:
  0.0 5.2 %copy-start.2 = (s32[8,2]{0,1:T(2,128)S(1)}, s32[8,2]{0,1:T(2,128)}, u32[]{:S(2)}) copy-start(s32[8,2]{0,1:T(2,128)} %param.9) | copy-start | bytes 196
  0.0 5.2 %copy-start.1 = (bf16[8,2,256,256]{3,2,1,0:T(8,128)(2,1)S(1)}, bf16[8,2,256,256]{3,2,1,0:T(8,128)(2,1)}, u32[]{:S(2)}) copy-start(bf16[8,2,256,256]{3,2,1,0:T(8,128)(2,1)} %exit_ref.1) | copy-start | bytes 6291460
  2.1 10.1 %collective-permute-start = (bf16[2,128,512]{2,1,0:T(8,128)(2,1)S(1)}, bf16[2,128,512]{2,1,0:T(8,128)(2,1)S(1)}, u32[]{:S(2)}, u32[]{:S(2)}) collective-permute-start(bf16[2,128,512]{2,1,0:T(8,128)(2,1)S(1)} %pad_maximum_fusion.mine_ref), channel_id=1, source_target_pairs={{0,1},{1,0},{2,3},{3,2},{4,5},{5,4},{6,7},{7,6},{8,9},{9,8},{10,11... | collective-permute-start | bytes 786440 | tf_op jit(solution)/shard_map/ppermute | solution.py:271
  5.1 11.9 %collective-permute-start.1 = (bf16[2,128,512]{2,1,0:T(8,128)(2,1)S(1)}, bf16[2,128,512]{2,1,0:T(8,128)(2,1)S(1)}, u32[]{:S(2)}, u32[]{:S(2)}) collective-permute-start(bf16[2,128,512]{2,1,0:T(8,128)(2,1)S(1)} %pad_maximum_fusion.1.mine_ref), channel_id=1, source_target_pairs={{0,1},{1,0},{2,3},{3,2},{4,5},{5,4},{6,7},{7,6},{8,9},{9,8},{10,11... | collective-permute-start | bytes 786440 | tf_op jit(solution)/shard_map/ppermute | solution.py:271
  13.4 6.6 %collective-permute-start.2 = (bf16[2,128,256]{2,1,0:T(8,128)(2,1)S(1)}, bf16[2,128,256]{2,1,0:T(8,128)(2,1)S(1)}, u32[]{:S(2)}, u32[]{:S(2)}) collective-permute-start(bf16[2,128,256]{2,1,0:T(8,128)(2,1)S(1)} %get-tuple-element.55), channel_id=1, source_target_pairs={{0,12},{2,14},{4,8},{6,10},{8,4},{10,6},{12,0},{14,2},{16,28},{18,... | collective-permute-start | bytes 393224 | tf_op jit(solution)/shard_map/ppermute | solution.py:274
  16.5 8.8 %collective-permute-start.8 = (bf16[2,128,256]{2,1,0:T(8,128)(2,1)S(1)}, bf16[2,128,256]{2,1,0:T(8,128)(2,1)S(1)}, u32[]{:S(2)}, u32[]{:S(2)}) collective-permute-start(bf16[2,128,256]{2,1,0:T(8,128)(2,1)S(1)} %get-tuple-element.70), channel_id=1, source_target_pairs={{0,14},{2,12},{4,10},{6,8},{8,6},{10,4},{12,2},{14,0},{16,30},{18,... | collective-permute-start | bytes 393224 | tf_op jit(solution)/shard_map/ppermute | solution.py:274
  21.1 6.9 %collective-permute-start.9 = (bf16[2,128,256]{2,1,0:T(8,128)(2,1)S(1)}, bf16[2,128,256]{2,1,0:T(8,128)(2,1)S(1)}, u32[]{:S(2)}, u32[]{:S(2)}) collective-permute-start(bf16[2,128,256]{2,1,0:T(8,128)(2,1)S(1)} %get-tuple-element.71), channel_id=1, source_target_pairs={{0,12},{2,14},{4,8},{6,10},{8,4},{10,6},{12,0},{14,2},{16,28},{18,... | collective-permute-start | bytes 393224 | tf_op jit(solution)/shard_map/ppermute | solution.py:274
  24.6 6.6 %collective-permute-start.10 = (bf16[2,128,256]{2,1,0:T(8,128)(2,1)S(1)}, bf16[2,128,256]{2,1,0:T(8,128)(2,1)S(1)}, u32[]{:S(2)}, u32[]{:S(2)}) collective-permute-start(bf16[2,128,256]{2,1,0:T(8,128)(2,1)S(1)} %get-tuple-element.72), channel_id=1, source_target_pairs={{0,14},{2,12},{4,10},{6,8},{8,6},{10,4},{12,2},{14,0},{16,30},{18,... | collective-permute-start | bytes 393224 | tf_op jit(solution)/shard_map/ppermute | solution.py:274
  24.6 11.4 %collective-permute-start.3 = (bf16[2,256,256]{2,1,0:T(8,128)(2,1)S(1)}, bf16[2,256,256]{2,1,0:T(8,128)(2,1)S(1)}, u32[]{:S(2)}, u32[]{:S(2)}) collective-permute-start(bf16[2,256,256]{2,1,0:T(8,128)(2,1)S(1)} %get-tuple-element.64), channel_id=1, source_target_pairs={{0,4},{2,6},{4,0},{6,2},{8,12},{10,14},{12,8},{14,10},{16,20},{18,... | collective-permute-start | bytes 786440 | tf_op jit(solution)/shard_map/ppermute | solution.py:274
  24.8 11.6 %collective-permute-start.4 = (bf16[2,256,256]{2,1,0:T(8,128)(2,1)S(1)}, bf16[2,256,256]{2,1,0:T(8,128)(2,1)S(1)}, u32[]{:S(2)}, u32[]{:S(2)}) collective-permute-start(bf16[2,256,256]{2,1,0:T(8,128)(2,1)S(1)} %get-tuple-element.65), channel_id=1, source_target_pairs={{0,8},{2,10},{4,12},{6,14},{8,0},{10,2},{12,4},{14,6},{16,24},{18,... | collective-permute-start | bytes 786440 | tf_op jit(solution)/shard_map/ppermute | solution.py:274
  25.3 16.2 %collective-permute-start.5 = (bf16[2,256,256]{2,1,0:T(8,128)(2,1)S(1)}, bf16[2,256,256]{2,1,0:T(8,128)(2,1)S(1)}, u32[]{:S(2)}, u32[]{:S(2)}) collective-permute-start(bf16[2,256,256]{2,1,0:T(8,128)(2,1)S(1)} %get-tuple-element.66), channel_id=1, source_target_pairs={{0,6},{2,4},{4,2},{6,0},{8,14},{10,12},{12,10},{14,8},{16,22},{18,... | collective-permute-start | bytes 786440 | tf_op jit(solution)/shard_map/ppermute | solution.py:274
  28.0 13.5 %collective-permute-start.6 = (bf16[2,256,256]{2,1,0:T(8,128)(2,1)S(1)}, bf16[2,256,256]{2,1,0:T(8,128)(2,1)S(1)}, u32[]{:S(2)}, u32[]{:S(2)}) collective-permute-start(bf16[2,256,256]{2,1,0:T(8,128)(2,1)S(1)} %get-tuple-element.67), channel_id=1, source_target_pairs={{0,10},{2,8},{4,14},{6,12},{8,2},{10,0},{12,6},{14,4},{16,26},{18,... | collective-permute-start | bytes 786440 | tf_op jit(solution)/shard_map/ppermute | solution.py:274
  31.1 10.4 %collective-permute-start.7 = (bf16[2,256,256]{2,1,0:T(8,128)(2,1)S(1)}, bf16[2,256,256]{2,1,0:T(8,128)(2,1)S(1)}, u32[]{:S(2)}, u32[]{:S(2)}) collective-permute-start(bf16[2,256,256]{2,1,0:T(8,128)(2,1)S(1)} %get-tuple-element.68), channel_id=1, source_target_pairs={{0,2},{2,0},{4,6},{6,4},{8,10},{10,8},{12,14},{14,12},{16,18},{18,... | collective-permute-start | bytes 786440 | tf_op jit(solution)/shard_map/ppermute | solution.py:274
  41.5 6.7 %copy-start = (bf16[1,8,2,256,256]{4,3,2,1,0:T(8,128)(2,1)S(1)}, bf16[1,8,2,256,256]{4,3,2,1,0:T(8,128)(2,1)}, u32[]{:S(2)}) copy-start(bf16[1,8,2,256,256]{4,3,2,1,0:T(8,128)(2,1)} %param.7) | copy-start | bytes 6291460
  46.8 16.7 %collective-permute-start.11 = (bf16[2,256,256]{2,1,0:T(8,128)(2,1)S(1)}, bf16[2,256,256]{2,1,0:T(8,128)(2,1)S(1)}, u32[]{:S(2)}, u32[]{:S(2)}) collective-permute-start(bf16[2,256,256]{2,1,0:T(8,128)(2,1)S(1)} %get-tuple-element.73), channel_id=1, source_target_pairs={{16,0},{18,2},{20,4},{22,6},{24,8},{26,10},{28,12},{30,14},{17,1},... | collective-permute-start | bytes 786440 | tf_op jit(solution)/shard_map/ppermute | solution.py:308
  68.8 7.2 %collective-permute-start.20 = (bf16[2,128,256]{2,1,0:T(8,128)(2,1)S(1)}, bf16[2,128,256]{2,1,0:T(8,128)(2,1)S(1)}, u32[]{:S(2)}, u32[]{:S(2)}) collective-permute-start(bf16[2,128,256]{2,1,0:T(8,128)(2,1)S(1)} %get-tuple-element.87), channel_id=1, source_target_pairs={{0,12},{2,14},{4,8},{6,10},{8,4},{10,6},{12,0},{14,2},{16,28},{18,... | collective-permute-start | bytes 393224 | tf_op jit(solution)/shard_map/ppermute | solution.py:274
  68.8 7.1 %collective-permute-start.21 = (bf16[2,128,256]{2,1,0:T(8,128)(2,1)S(1)}, bf16[2,128,256]{2,1,0:T(8,128)(2,1)S(1)}, u32[]{:S(2)}, u32[]{:S(2)}) collective-permute-start(bf16[2,128,256]{2,1,0:T(8,128)(2,1)S(1)} %get-tuple-element.88), channel_id=1, source_target_pairs={{0,14},{2,12},{4,10},{6,8},{8,6},{10,4},{12,2},{14,0},{16,30},{18,... | collective-permute-start | bytes 393224 | tf_op jit(solution)/shard_map/ppermute | solution.py:274
  70.4 12.4 %collective-permute-start.12 = (bf16[2,256,256]{2,1,0:T(8,128)(2,1)S(1)}, bf16[2,256,256]{2,1,0:T(8,128)(2,1)S(1)}, u32[]{:S(2)}, u32[]{:S(2)}) collective-permute-start(bf16[2,256,256]{2,1,0:T(8,128)(2,1)S(1)} %get-tuple-element.78), channel_id=1, source_target_pairs={{0,4},{2,6},{4,0},{6,2},{8,12},{10,14},{12,8},{14,10},{16,20},{18,... | collective-permute-start | bytes 786440 | tf_op jit(solution)/shard_map/ppermute | solution.py:274
  72.2 12.4 %collective-permute-start.13 = (bf16[2,256,256]{2,1,0:T(8,128)(2,1)S(1)}, bf16[2,256,256]{2,1,0:T(8,128)(2,1)S(1)}, u32[]{:S(2)}, u32[]{:S(2)}) collective-permute-start(bf16[2,256,256]{2,1,0:T(8,128)(2,1)S(1)} %get-tuple-element.79), channel_id=1, source_target_pairs={{0,8},{2,10},{4,12},{6,14},{8,0},{10,2},{12,4},{14,6},{16,24},{18,... | collective-permute-start | bytes 786440 | tf_op jit(solution)/shard_map/ppermute | solution.py:274
  72.3 17.6 %collective-permute-start.14 = (bf16[2,256,256]{2,1,0:T(8,128)(2,1)S(1)}, bf16[2,256,256]{2,1,0:T(8,128)(2,1)S(1)}, u32[]{:S(2)}, u32[]{:S(2)}) collective-permute-start(bf16[2,256,256]{2,1,0:T(8,128)(2,1)S(1)} %get-tuple-element.80), channel_id=1, source_target_pairs={{0,6},{2,4},{4,2},{6,0},{8,14},{10,12},{12,10},{14,8},{16,22},{18,... | collective-permute-start | bytes 786440 | tf_op jit(solution)/shard_map/ppermute | solution.py:274
  76.0 14.0 %collective-permute-start.15 = (bf16[2,256,256]{2,1,0:T(8,128)(2,1)S(1)}, bf16[2,256,256]{2,1,0:T(8,128)(2,1)S(1)}, u32[]{:S(2)}, u32[]{:S(2)}) collective-permute-start(bf16[2,256,256]{2,1,0:T(8,128)(2,1)S(1)} %get-tuple-element.81), channel_id=1, source_target_pairs={{0,10},{2,8},{4,14},{6,12},{8,2},{10,0},{12,6},{14,4},{16,26},{18,... | collective-permute-start | bytes 786440 | tf_op jit(solution)/shard_map/ppermute | solution.py:274
  76.0 14.0 %collective-permute-start.16 = (bf16[2,256,256]{2,1,0:T(8,128)(2,1)S(1)}, bf16[2,256,256]{2,1,0:T(8,128)(2,1)S(1)}, u32[]{:S(2)}, u32[]{:S(2)}) collective-permute-start(bf16[2,256,256]{2,1,0:T(8,128)(2,1)S(1)} %get-tuple-element.82), channel_id=1, source_target_pairs={{0,2},{2,0},{4,6},{6,4},{8,10},{10,8},{12,14},{14,12},{16,18},{18,... | collective-permute-start | bytes 786440 | tf_op jit(solution)/shard_map/ppermute | solution.py:274
  82.8 11.2 %collective-permute-start.17 = (bf16[2,128,256]{2,1,0:T(8,128)(2,1)S(1)}, bf16[2,128,256]{2,1,0:T(8,128)(2,1)S(1)}, u32[]{:S(2)}, u32[]{:S(2)}) collective-permute-start(bf16[2,128,256]{2,1,0:T(8,128)(2,1)S(1)} %get-tuple-element.83), channel_id=1, source_target_pairs={{0,12},{2,14},{4,8},{6,10},{8,4},{10,6},{12,0},{14,2},{16,28},{18,... | collective-permute-start | bytes 393224 | tf_op jit(solution)/shard_map/ppermute | solution.py:274
  84.7 9.3 %collective-permute-start.18 = (bf16[2,128,256]{2,1,0:T(8,128)(2,1)S(1)}, bf16[2,128,256]{2,1,0:T(8,128)(2,1)S(1)}, u32[]{:S(2)}, u32[]{:S(2)}) collective-permute-start(bf16[2,128,256]{2,1,0:T(8,128)(2,1)S(1)} %get-tuple-element.84), channel_id=1, source_target_pairs={{0,14},{2,12},{4,10},{6,8},{8,6},{10,4},{12,2},{14,0},{16,30},{18,... | collective-permute-start | bytes 393224 | tf_op jit(solution)/shard_map/ppermute | solution.py:274
  92.0 9.2 %collective-permute-start.22 = (bf16[2,128,512]{2,1,0:T(8,128)(2,1)S(1)}, bf16[2,128,512]{2,1,0:T(8,128)(2,1)S(1)}, u32[]{:S(2)}, u32[]{:S(2)}) collective-permute-start(bf16[2,128,512]{2,1,0:T(8,128)(2,1)S(1)} %get-tuple-element.90), channel_id=1, source_target_pairs={{0,1},{1,0},{2,3},{3,2},{4,5},{5,4},{6,7},{7,6},{8,9},{9,8},{10,11... | collective-permute-start | bytes 786440 | tf_op jit(solution)/shard_map/ppermute | solution.py:271
  96.1 10.3 %collective-permute-start.19 = (bf16[2,128,512]{2,1,0:T(8,128)(2,1)S(1)}, bf16[2,128,512]{2,1,0:T(8,128)(2,1)S(1)}, u32[]{:S(2)}, u32[]{:S(2)}) collective-permute-start(bf16[2,128,512]{2,1,0:T(8,128)(2,1)S(1)} %get-tuple-element.86), channel_id=1, source_target_pairs={{0,1},{1,0},{2,3},{3,2},{4,5},{5,4},{6,7},{7,6},{8,9},{9,8},{10,11... | collective-permute-start | bytes 786440 | tf_op jit(solution)/shard_map/ppermute | solution.py:271

commit v8 on v7

--- a/solution.py
+++ b/solution.py
@@ -46,6 +46,11 @@
     return lax.rem(lax.axis_index("sec").astype(jnp.int32), count)
 
 
+def position_at(place, count):
+    hops = lax.axis_size("sec") // count - 1 - lax.axis_index("sec").astype(jnp.int32) // count
+    return place ^ (count // 2 * lax.rem(hops, 2) * lax.rem(place, 2))
+
+
 def coded(amp, phase):
     half = 0.5 * phase
     square = half * half
@@ -81,7 +86,7 @@
         here = pl.ds(0 if i >= count - far else base, rows)
         if base and i < count - far:
             win_ref[:, :base] = refs[i][:, :base]
-        in_mine, in_left = first_masks(corner_ref, own ^ apart, base, (rows, window))
+        in_mine, in_left = first_masks(corner_ref, position_at(own ^ apart, count), base, (rows, window))
         for part in range(2):
             left, right = (
                 jnp.where(in_mine, mine_ref[part, :, cols].astype(f32), other_ref[part, :, cols].astype(f32))
@@ -106,7 +111,8 @@
 
 
 def ready_kernel(corner_ref, exit_ref, start_ref, down_ref, across_ref):
-    own = place_in_group(exit_ref.shape[0])
+    count = exit_ref.shape[0]
+    own = position_at(place_in_group(count), count)
     row_at = corner_ref[0, own]
     col_at = corner_ref[1, own]
     size = start_ref.shape[-1]
@@ -129,30 +135,35 @@
     lax.fori_loop(0, count, one, 0)
 
 
-def back(down, across, chi_re, chi_im):
+def back(down, across, chi):
+    half = chi.shape[0] // 2
+
     def laplacian(field):
-        rows = jnp.dot(down, field, preferred_element_type=f32)
-        return rows + jnp.dot(field, across, preferred_element_type=f32)
-
-    lap_re = laplacian(chi_re)
-    lap_im = laplacian(chi_im)
-    lap2_re = laplacian(lap_re.astype(bf16))
-    lap2_im = laplacian(lap_im.astype(bf16))
+        columns = jnp.dot(field, across, preferred_element_type=f32)
+        return [
+            jnp.dot(down, field[here], preferred_element_type=f32) + columns[here]
+            for here in (slice(0, half), slice(half, 2 * half))
+        ]
+
+    lap_re, lap_im = laplacian(chi)
+    lap2_re, lap2_im = laplacian(jnp.concatenate([lap_re.astype(bf16), lap_im.astype(bf16)], axis=0))
     more_re = 2.0 * lap_re + (damping * lap2_re + turning * lap2_im)
     more_im = 2.0 * lap_im + (damping * lap2_im - turning * lap2_re)
-    spread_re = chi_re.astype(f32) + (damping * more_re + turning * more_im)
-    spread_im = chi_im.astype(f32) + (damping * more_im - turning * more_re)
+    spread_re = chi[:half].astype(f32) + (damping * more_re + turning * more_im)
+    spread_im = chi[half:].astype(f32) + (damping * more_im - turning * more_re)
     return spread_re, spread_im
 
 
-def pass_group(down, across, chi_re, chi_im, count, window_of, keep):
+def pass_group(down, across, chi, count, window_of, keep):
+    half = chi.shape[0] // 2
     for layer in range(count - 1, -1, -1):
-        spread_re, spread_im = back(down, across, chi_re, chi_im)
+        spread_re, spread_im = back(down, across, chi)
         keep(layer, spread_re, spread_im)
         win_re, win_im = window_of(layer)
         chi_re = (win_re * spread_re + win_im * spread_im).astype(bf16)
         chi_im = (win_re * spread_im - win_im * spread_re).astype(bf16)
-    return chi_re, chi_im
+        chi = jnp.concatenate([chi_re, chi_im], axis=0)
+    return chi[:half], chi[half:]
 
 
 def in_pieces(count, window):
@@ -175,8 +186,7 @@
     leave_ref[0], leave_ref[1] = pass_group(
         down_ref[...],
         across_ref[...],
-        start_ref[0],
-        start_ref[1],
+        jnp.concatenate([start_ref[0], start_ref[1]], axis=0),
         count,
         functools.partial(decoded, held_ref),
         lambda *_: None,
@@ -197,9 +207,8 @@
             refs[-1][layer, 0] = spread_re.astype(bf16)
             refs[-1][layer, 1] = spread_im.astype(bf16)
 
-    chi = pass_group(
-        down_ref[...], across_ref[...], chi_re, chi_im, count, functools.partial(decoded, held_ref), keep
-    )
+    chi = jnp.concatenate([chi_re, chi_im], axis=0)
+    chi = pass_group(down_ref[...], across_ref[...], chi, count, functools.partial(decoded, held_ref), keep)
     if not is_last:
         refs[0][0], refs[0][1] = chi
         return
@@ -219,7 +228,7 @@
         sums = [jnp.zeros((tall, window), f32) for _ in range(8)]
         here = pl.ds(base + at, tall)
         for apart, spread_ref in zip(distances(len(spread_refs)), spread_refs):
-            position = own ^ apart
+            position = position_at(own ^ apart, len(spread_refs))
             there = pl.ds(at, tall) if apart >= len(spread_refs) - far else here
             in_mine, in_left = first_masks(corner_ref, position, base + at, (tall, window))
             wave_re, wave_im = (wave_ref[position, part, here, :].astype(f32) for part in range(2))
@@ -229,16 +238,18 @@
                 wave_re * spread_im - wave_im * spread_re,
             )
             for part in range(2):
-                left = jnp.where(in_left, parts[part], 0.0)
-                right = jnp.where(in_left, 0.0, parts[part])
-                for side, value in enumerate((left, right)):
-                    sums[4 * part + side] += jnp.where(in_mine, value, 0.0)
-                    sums[4 * part + 2 + side] += jnp.where(in_mine, 0.0, value)
+                own_part = jnp.where(in_mine, parts[part], 0.0)
+                sums[4 * part] += parts[part]
+                sums[4 * part + 1] += own_part
+                sums[4 * part + 2] += jnp.where(in_left, parts[part], 0.0)
+                sums[4 * part + 3] += jnp.where(in_left, own_part, 0.0)
+        left, right = pl.ds(0, window), pl.ds(window, window)
         for part in range(2):
-            for side in range(2):
-                cols = pl.ds(side * window, window)
-                own_ref[part, pl.ds(at, tall), cols] = sums[4 * part + side]
-                away_ref[part, pl.ds(at, tall), cols] = sums[4 * part + 2 + side].astype(bf16)
+            every, mine, at_left, mine_left = sums[4 * part : 4 * part + 4]
+            own_ref[part, pl.ds(at, tall), left] = mine_left
+            own_ref[part, pl.ds(at, tall), right] = mine - mine_left
+            away_ref[part, pl.ds(at, tall), left] = (at_left - mine_left).astype(bf16)
+            away_ref[part, pl.ds(at, tall), right] = ((every - mine) - (at_left - mine_left)).astype(bf16)
         return 0
 
     lax.fori_loop(0, rows // tall, one, 0)
@@ -305,7 +316,9 @@
     first = call(first_kernel, [shape_of(wave, bf16), shape_of((count,) + wave, bf16)], cost=cost, grant=12)
     leave, held = first(start, down, across, *windows)
     for stage in range(1, group_count):
-        come = lax.ppermute(leave, "sec", [(s, s - count) for s in range(count, sections)])
+        come = lax.ppermute(
+            leave, "sec", [(s, (s - count) ^ (s % 2 * count // 2)) for s in range(count, sections)]
+        )
         come, waves = lax.optimization_barrier((come, waves))
         is_last = stage == group_count - 1
         through = call(

time: 108 us -> 109 us (level)
  waiting for transfers between devices: 58.3 us -> 55.1 us
  starting transfers between devices: 25.2 us -> 27.5 us
  Pallas kernels: 21.8 us -> 23.7 us
    ppermute x18, waiting for transfers between devices: 29.6 us -> 27 us  [to_distance(): return lax.ppermute(value, 'sec', [(s, s ^ d) for s in range(sections)])]
    pallas_call x9, Pallas kernels: 21.8 us -> 23.7 us  [run(): pl.pallas_call(kernel, grid_spec=pltpu.PrefetchScalarGridSpec(num_scalar_...]
    ppermute x18, starting transfers between devices: 18.1 us -> 19.7 us  [to_distance(): return lax.ppermute(value, 'sec', [(s, s ^ d) for s in range(sections)])]
where the time goes in v8:
time: 109 us
  waiting for transfers between devices  55.1 us (51%)
  starting transfers between devices  27.5 us (25%)
  Pallas kernels  23.7 us (22%)
  other arithmetic  2.08 us (2%)
    ppermute x18, waiting for transfers between devices, to_distance(): return lax.ppermute(value, 'sec', [(s, s ^ d) for s in range(sections)])  27 us
    pallas_call x9, Pallas kernels, run(): pl.pallas_call(kernel, grid_spec=pltpu.PrefetchScalarGridSpec(num_scalar_...  23.7 us
    ppermute x18, starting transfers between devices, to_distance(): return lax.ppermute(value, 'sec', [(s, s ^ d) for s in range(sections)])  19.7 us
    ppermute x4, waiting for transfers between devices, to_other_half(): return lax.ppermute(value, 'scan', [(0, 1), (1, 0)])  15.1 us
    ppermute x1, waiting for transfers between devices, on_device(): lax.ppermute(leave, 'sec', [(s, s - count ^ s % 2 * count // 2) for s in...  12.9 us
    ppermute x4, starting transfers between devices, to_other_half(): return lax.ppermute(value, 'scan', [(0, 1), (1, 0)])  6.35 us
  transfers between devices with their start and end apart: 23, of which 15 were waited for; matrix products, arithmetic and copies ran while one was open for 0% of the time, Pallas kernels for 9%

profile of v8, /device:TPU:0, one launch (start us, length us, event | category | flops | bytes accessed | tf_op | source)
XLA Modules:
  0.0 108.5 jit_solution(8884575745299968168)
XLA Ops:
  0.0 2.0 %fusion.13 = (bf16[1,128,512]{2,1,0:T(8,128)(2,1)S(1)}, bf16[1,128,512]{2,1,0:T(8,128)(2,1)S(1)}, bf16[1,128,512]{2,1,0:T(8,128)(2,1)S(1)}, bf16[1,128,512]{2,1,0:T(8,128)(2,1)S(1)}) fusion(f32[1,256,512]{2,1,0:T(8,128)} %param.5, f32[1,256,512]{2,1,0:T(8,128)} %param.6), kind=kLoop, calls=%fused_computation.17 | loop fusion | flops 4849664 | bytes 1572864 | tf_op jit(solution)/shard_map/convert_element_type | solution.py:66
  2.1 3.0 %collective-permute-start = (bf16[2,128,512]{2,1,0:T(8,128)(2,1)S(1)}, bf16[2,128,512]{2,1,0:T(8,128)(2,1)S(1)}, u32[]{:S(2)}, u32[]{:S(2)}) collective-permute-start(bf16[2,128,512]{2,1,0:T(8,128)(2,1)S(1)} %pad_maximum_fusion.mine_ref), channel_id=1, source_target_pairs={{0,1},{1,0},{2,3},{3,2},{4,5},{5,4},{6,7},{7,6},{8,9},{9,8},{10,11... | collective-permute-start | bytes 786440 | tf_op jit(solution)/shard_map/ppermute | solution.py:282
  5.2 1.2 %shard_map.55 = (bf16[2,256,256]{2,1,0:T(8,128)(2,1)S(1)}, bf16[256,256]{1,0:T(8,128)(2,1)S(1)}, bf16[256,256]{1,0:T(8,128)(2,1)S(1)}) custom-call(s32[2,8]{1,0:T(2,128)S(1)} %bitcast.4, bf16[8,2,256,256]{3,2,1,0:T(8,128)(2,1)S(1)} %copy-done.1), custom_call_target="tpu_custom_call" | custom-call | bytes 2621504 | tf_op jit(solution)/shard_map/pallas_call | solution.py:27
  6.4 5.8 %collective-permute-done.other_ref = bf16[2,128,512]{2,1,0:T(8,128)(2,1)S(1)} collective-permute-done((bf16[2,128,512]{2,1,0:T(8,128)(2,1)S(1)}, bf16[2,128,512]{2,1,0:T(8,128)(2,1)S(1)}, u32[]{:S(2)}, u32[]{:S(2)}) %collective-permute-start) | collective-permute-done | bytes 262176 | tf_op jit(solution)/shard_map/ppermute | solution.py:282
  12.2 1.2 %shard_map.56 = (bf16[2,256,256]{2,1,0:T(8,128)(2,1)S(1)}, bf16[2,256,256]{2,1,0:T(8,128)(2,1)S(1)}, bf16[2,256,256]{2,1,0:T(8,128)(2,1)S(1)}, bf16[2,256,256]{2...) custom-call(s32[2,8]{1,0:T(2,128)S(1)} %bitcast.5, ...), custom_call_target="tpu_custom_call" | custom-call | bytes 2359360 | tf_op jit(solution)/shard_map/pallas_call | solution.py:27
  13.4 3.2 %collective-permute-start.2 = (bf16[2,128,256]{2,1,0:T(8,128)(2,1)S(1)}, bf16[2,128,256]{2,1,0:T(8,128)(2,1)S(1)}, u32[]{:S(2)}, u32[]{:S(2)}) collective-permute-start(bf16[2,128,256]{2,1,0:T(8,128)(2,1)S(1)} %get-tuple-element.55), channel_id=1, source_target_pairs={{0,12},{2,14},{4,8},{6,10},{8,4},{10,6},{12,0},{14,2},{16,28},{18,... | collective-permute-start | bytes 393224 | tf_op jit(solution)/shard_map/ppermute | solution.py:285
  17.0 2.9 %collective-permute-done.2.refs_6_ = bf16[2,128,256]{2,1,0:T(8,128)(2,1)S(1)} collective-permute-done((bf16[2,128,256]{2,1,0:T(8,128)(2,1)S(1)}, bf16[2,128,256]{2,1,0:T(8,128)(2,1)S(1)}, u32[]{:S(2)}, u32[]{:S(2)}) %collective-permute-start.2) | collective-permute-done | bytes 131104 | tf_op jit(solution)/shard_map/ppermute | solution.py:285
  19.9 1.2 %shard_map.57 = (bf16[2,256,256]{2,1,0:T(8,128)(2,1)S(1)}, bf16[2,256,256]{2,1,0:T(8,128)(2,1)S(1)}, bf16[2,256,256]{2,1,0:T(8,128)(2,1)S(1)}, bf16[2,256,256]{2...) custom-call(s32[2,8]{1,0:T(2,128)S(1)} %bitcast.6, ...), custom_call_target="tpu_custom_call", output_to_operand_aliasing={{0}: (3, {}), {1}: (4, {}), {2}: (5, {}), {3}: (6, {}), {4}... | custom-call | bytes 3932224 | tf_op jit(solution)/shard_map/pallas_call | solution.py:27
  21.2 3.4 %collective-permute-start.9 = (bf16[2,128,256]{2,1,0:T(8,128)(2,1)S(1)}, bf16[2,128,256]{2,1,0:T(8,128)(2,1)S(1)}, u32[]{:S(2)}, u32[]{:S(2)}) collective-permute-start(bf16[2,128,256]{2,1,0:T(8,128)(2,1)S(1)} %get-tuple-element.71), channel_id=1, source_target_pairs={{0,12},{2,14},{4,8},{6,10},{8,4},{10,6},{12,0},{14,2},{16,28},{18,... | collective-permute-start | bytes 393224 | tf_op jit(solution)/shard_map/ppermute | solution.py:285
  25.3 2.2 %collective-permute-start.5 = (bf16[2,256,256]{2,1,0:T(8,128)(2,1)S(1)}, bf16[2,256,256]{2,1,0:T(8,128)(2,1)S(1)}, u32[]{:S(2)}, u32[]{:S(2)}) collective-permute-start(bf16[2,256,256]{2,1,0:T(8,128)(2,1)S(1)} %get-tuple-element.66), channel_id=1, source_target_pairs={{0,6},{2,4},{4,2},{6,0},{8,14},{10,12},{12,10},{14,8},{16,22},{18,... | collective-permute-start | bytes 786440 | tf_op jit(solution)/shard_map/ppermute | solution.py:285
  28.4 2.8 %collective-permute-done.10.refs_9_ = bf16[2,128,256]{2,1,0:T(8,128)(2,1)S(1)} collective-permute-done((bf16[2,128,256]{2,1,0:T(8,128)(2,1)S(1)}, bf16[2,128,256]{2,1,0:T(8,128)(2,1)S(1)}, u32[]{:S(2)}, u32[]{:S(2)}) %collective-permute-start.10) | collective-permute-done | bytes 131104 | tf_op jit(solution)/shard_map/ppermute | solution.py:285
  31.2 4.9 %collective-permute-done.3.refs_1_ = bf16[2,256,256]{2,1,0:T(8,128)(2,1)S(1)} collective-permute-done((bf16[2,256,256]{2,1,0:T(8,128)(2,1)S(1)}, bf16[2,256,256]{2,1,0:T(8,128)(2,1)S(1)}, u32[]{:S(2)}, u32[]{:S(2)}) %collective-permute-start.3) | collective-permute-done | bytes 262176 | tf_op jit(solution)/shard_map/ppermute | solution.py:285
  36.4 5.1 %collective-permute-done.5.refs_3_ = bf16[2,256,256]{2,1,0:T(8,128)(2,1)S(1)} collective-permute-done((bf16[2,256,256]{2,1,0:T(8,128)(2,1)S(1)}, bf16[2,256,256]{2,1,0:T(8,128)(2,1)S(1)}, u32[]{:S(2)}, u32[]{:S(2)}) %collective-permute-start.5) | collective-permute-done | bytes 262176 | tf_op jit(solution)/shard_map/ppermute | solution.py:285
  41.5 6.4 %shard_map.58 = (bf16[2,256,256]{2,1,0:T(8,128)(2,1)S(1)}, bf16[8,2,256,256]{3,2,1,0:T(8,128)(2,1)S(1)}) custom-call(bf16[2,256,256]{2,1,0:T(8,128)(2,1)S(1)} %get-tuple-element.51.start_ref, bf16[256,256]{1,0:T(8,128)(2,1)S(1)} %get-tuple-element.52.down_ref, bf16[256,256]{1,0:T(8,128)(2,1)S(1)} %get-tuple-element.53.across_ref, ...), custom_call_target="tpu_custom_call" | custom-call | flops 2147483648 | bytes 4980736 | tf_op jit(solution)/shard_map/pallas_call | solution.py:27
  48.0 1.5 %collective-permute-start.11 = (bf16[2,256,256]{2,1,0:T(8,128)(2,1)S(1)}, bf16[2,256,256]{2,1,0:T(8,128)(2,1)S(1)}, u32[]{:S(2)}, u32[]{:S(2)}) collective-permute-start(bf16[2,256,256]{2,1,0:T(8,128)(2,1)S(1)} %get-tuple-element.73), channel_id=1, source_target_pairs={{16,0},{18,10},{20,4},{22,14},{24,8},{26,2},{28,12},{30,6},{17,1},... | collective-permute-start | bytes 786440 | tf_op jit(solution)/shard_map/ppermute | solution.py:319
  49.5 2.5 %shard_map.59.wave_ref = bf16[8,2,256,256]{3,2,1,0:T(8,128)(2,1)S(1)} custom-call(s32[2,8]{1,0:T(2,128)S(1)} %bitcast.7, bf16[8,2,256,256]{3,2,1,0:T(8,128)(2,1)S(1)} %bitcast.3), custom_call_target="tpu_custom_call" | custom-call | bytes 4194368 | tf_op jit(solution)/shard_map/pallas_call | solution.py:27
  51.9 12.9 %collective-permute-done.11.come_ref = bf16[2,256,256]{2,1,0:T(8,128)(2,1)S(1)} collective-permute-done((bf16[2,256,256]{2,1,0:T(8,128)(2,1)S(1)}, bf16[2,256,256]{2,1,0:T(8,128)(2,1)S(1)}, u32[]{:S(2)}, u32[]{:S(2)}) %collective-permute-start.11) | collective-permute-done | bytes 262176 | tf_op jit(solution)/shard_map/ppermute | solution.py:319
  64.9 6.5 %shard_map.60 = (bf16[2,256,256]{2,1,0:T(8,128)(2,1)S(1)}, bf16[2,256,256]{2,1,0:T(8,128)(2,1)S(1)}, bf16[2,256,256]{2,1,0:T(8,128)(2,1)S(1)}, bf16[2,256,256]{2...) custom-call(bf16[2,256,256]{2,1,0:T(8,128)(2,1)S(1)} %get-tuple-elem, ...), custom_call_target="tpu_custom_call" | custom-call | flops 2147483648 | bytes 4980736 | tf_op jit(solution)/shard_map/pallas_call | solution.py:27
  72.4 2.5 %collective-permute-start.13 = (bf16[2,256,256]{2,1,0:T(8,128)(2,1)S(1)}, bf16[2,256,256]{2,1,0:T(8,128)(2,1)S(1)}, u32[]{:S(2)}, u32[]{:S(2)}) collective-permute-start(bf16[2,256,256]{2,1,0:T(8,128)(2,1)S(1)} %get-tuple-element.79), channel_id=1, source_target_pairs={{0,8},{2,10},{4,12},{6,14},{8,0},{10,2},{12,4},{14,6},{16,24},{18,... | collective-permute-start | bytes 786440 | tf_op jit(solution)/shard_map/ppermute | solution.py:285
  75.8 2.5 %collective-permute-done.20.refs_6_ = bf16[2,128,256]{2,1,0:T(8,128)(2,1)S(1)} collective-permute-done((bf16[2,128,256]{2,1,0:T(8,128)(2,1)S(1)}, bf16[2,128,256]{2,1,0:T(8,128)(2,1)S(1)}, u32[]{:S(2)}, u32[]{:S(2)}) %collective-permute-start.20) | collective-permute-done | bytes 131104 | tf_op jit(solution)/shard_map/ppermute | solution.py:285
  78.3 2.5 %collective-permute-start.16 = (bf16[2,256,256]{2,1,0:T(8,128)(2,1)S(1)}, bf16[2,256,256]{2,1,0:T(8,128)(2,1)S(1)}, u32[]{:S(2)}, u32[]{:S(2)}) collective-permute-start(bf16[2,256,256]{2,1,0:T(8,128)(2,1)S(1)} %get-tuple-element.82), channel_id=1, source_target_pairs={{0,2},{2,0},{4,6},{6,4},{8,10},{10,8},{12,14},{14,12},{16,18},{18,... | collective-permute-start | bytes 786440 | tf_op jit(solution)/shard_map/ppermute | solution.py:285
  80.8 3.8 %collective-permute-done.12.refs_1_ = bf16[2,256,256]{2,1,0:T(8,128)(2,1)S(1)} collective-permute-done((bf16[2,256,256]{2,1,0:T(8,128)(2,1)S(1)}, bf16[2,256,256]{2,1,0:T(8,128)(2,1)S(1)}, u32[]{:S(2)}, u32[]{:S(2)}) %collective-permute-start.12) | collective-permute-done | bytes 262176 | tf_op jit(solution)/shard_map/ppermute | solution.py:285
  84.6 1.2 %collective-permute-start.17 = (bf16[2,128,256]{2,1,0:T(8,128)(2,1)S(1)}, bf16[2,128,256]{2,1,0:T(8,128)(2,1)S(1)}, u32[]{:S(2)}, u32[]{:S(2)}) collective-permute-start(bf16[2,128,256]{2,1,0:T(8,128)(2,1)S(1)} %get-tuple-element.83), channel_id=1, source_target_pairs={{0,12},{2,14},{4,8},{6,10},{8,4},{10,6},{12,0},{14,2},{16,28},{18,... | collective-permute-start | bytes 393224 | tf_op jit(solution)/shard_map/ppermute | solution.py:285
  86.0 1.7 %collective-permute-start.18 = (bf16[2,128,256]{2,1,0:T(8,128)(2,1)S(1)}, bf16[2,128,256]{2,1,0:T(8,128)(2,1)S(1)}, u32[]{:S(2)}, u32[]{:S(2)}) collective-permute-start(bf16[2,128,256]{2,1,0:T(8,128)(2,1)S(1)} %get-tuple-element.84), channel_id=1, source_target_pairs={{0,14},{2,12},{4,10},{6,8},{8,6},{10,4},{12,2},{14,0},{16,30},{18,... | collective-permute-start | bytes 393224 | tf_op jit(solution)/shard_map/ppermute | solution.py:285
  87.7 4.0 %collective-permute-done.14.refs_3_ = bf16[2,256,256]{2,1,0:T(8,128)(2,1)S(1)} collective-permute-done((bf16[2,256,256]{2,1,0:T(8,128)(2,1)S(1)}, bf16[2,256,256]{2,1,0:T(8,128)(2,1)S(1)}, u32[]{:S(2)}, u32[]{:S(2)}) %collective-permute-start.14) | collective-permute-done | bytes 262176 | tf_op jit(solution)/shard_map/ppermute | solution.py:285
  91.6 1.8 %shard_map.62 = (f32[2,128,512]{2,1,0:T(8,128)S(1)}, bf16[2,128,512]{2,1,0:T(8,128)(2,1)S(1)}) custom-call(s32[2,8]{1,0:T(2,128)S(1)} %bitcast.8, bf16[8,2,256,256]{3,2,1,0:T(8,128)(2,1)S(1)} %shard_map.59.wave_ref, bf16[2,256,256]{2,1,0:T(8,128)(2,1)S(1)} %get-tuple-element.77.refs_0_, bf16[2,256,256]{2,1,0:T(8,128)(2,1)S(1)} %collective-permute-done.12.refs_1_, ...), custom_call_target="tpu_custom_call" | custom-call | bytes 4718656 | tf_op jit(solution)/shard_map/pallas_call | solution.py:27
  93.5 1.6 %collective-permute-start.22 = (bf16[2,128,512]{2,1,0:T(8,128)(2,1)S(1)}, bf16[2,128,512]{2,1,0:T(8,128)(2,1)S(1)}, u32[]{:S(2)}, u32[]{:S(2)}) collective-permute-start(bf16[2,128,512]{2,1,0:T(8,128)(2,1)S(1)} %get-tuple-element.90), channel_id=1, source_target_pairs={{0,1},{1,0},{2,3},{3,2},{4,5},{5,4},{6,7},{7,6},{8,9},{9,8},{10,11... | collective-permute-start | bytes 786440 | tf_op jit(solution)/shard_map/ppermute | solution.py:282
  95.1 1.8 %shard_map.61 = (f32[2,128,512]{2,1,0:T(8,128)S(1)}, bf16[2,128,512]{2,1,0:T(8,128)(2,1)S(1)}) custom-call(s32[2,8]{1,0:T(2,128)S(1)} %bitcast.9, bf16[8,2,256,256]{3,2,1,0:T(8,128)(2,1)S(1)} %shard_map.59.wave_ref, bf16[2,256,256]{2,1,0:T(8,128)(2,1)S(1)} %get-tuple-element.77.refs_0_, bf16[2,256,256]{2,1,0:T(8,128)(2,1)S(1)} %collective-permute-done.12.refs_1_, ...), custom_call_target="tpu_custom_call" | custom-call | bytes 4718656 | tf_op jit(solution)/shard_map/pallas_call | solution.py:27
  97.0 1.6 %collective-permute-start.19 = (bf16[2,128,512]{2,1,0:T(8,128)(2,1)S(1)}, bf16[2,128,512]{2,1,0:T(8,128)(2,1)S(1)}, u32[]{:S(2)}, u32[]{:S(2)}) collective-permute-start(bf16[2,128,512]{2,1,0:T(8,128)(2,1)S(1)} %get-tuple-element.86), channel_id=1, source_target_pairs={{0,1},{1,0},{2,3},{3,2},{4,5},{5,4},{6,7},{7,6},{8,9},{9,8},{10,11... | collective-permute-start | bytes 786440 | tf_op jit(solution)/shard_map/ppermute | solution.py:282
  98.6 4.1 %collective-permute-done.22.refs_3_ = bf16[2,128,512]{2,1,0:T(8,128)(2,1)S(1)} collective-permute-done((bf16[2,128,512]{2,1,0:T(8,128)(2,1)S(1)}, bf16[2,128,512]{2,1,0:T(8,128)(2,1)S(1)}, u32[]{:S(2)}, u32[]{:S(2)}) %collective-permute-start.22) | collective-permute-done | bytes 262176 | tf_op jit(solution)/shard_map/ppermute | solution.py:282
  102.7 4.7 %collective-permute-done.19.refs_1_ = bf16[2,128,512]{2,1,0:T(8,128)(2,1)S(1)} collective-permute-done((bf16[2,128,512]{2,1,0:T(8,128)(2,1)S(1)}, bf16[2,128,512]{2,1,0:T(8,128)(2,1)S(1)}, u32[]{:S(2)}, u32[]{:S(2)}) %collective-permute-start.19) | collective-permute-done | bytes 262176 | tf_op jit(solution)/shard_map/ppermute | solution.py:282
  107.4 1.1 shard_map.63
  (32 shorter events, 4.7 us)
Async XLA Ops:
  0.0 5.2 %copy-start.2 = (s32[8,2]{0,1:T(2,128)S(1)}, s32[8,2]{0,1:T(2,128)}, u32[]{:S(2)}) copy-start(s32[8,2]{0,1:T(2,128)} %param.9) | copy-start | bytes 196
  0.0 5.2 %copy-start.1 = (bf16[8,2,256,256]{3,2,1,0:T(8,128)(2,1)S(1)}, bf16[8,2,256,256]{3,2,1,0:T(8,128)(2,1)}, u32[]{:S(2)}) copy-start(bf16[8,2,256,256]{3,2,1,0:T(8,128)(2,1)} %exit_ref.1) | copy-start | bytes 6291460
  2.1 10.1 %collective-permute-start = (bf16[2,128,512]{2,1,0:T(8,128)(2,1)S(1)}, bf16[2,128,512]{2,1,0:T(8,128)(2,1)S(1)}, u32[]{:S(2)}, u32[]{:S(2)}) collective-permute-start(bf16[2,128,512]{2,1,0:T(8,128)(2,1)S(1)} %pad_maximum_fusion.mine_ref), channel_id=1, source_target_pairs={{0,1},{1,0},{2,3},{3,2},{4,5},{5,4},{6,7},{7,6},{8,9},{9,8},{10,11... | collective-permute-start | bytes 786440 | tf_op jit(solution)/shard_map/ppermute | solution.py:282
  5.1 11.9 %collective-permute-start.1 = (bf16[2,128,512]{2,1,0:T(8,128)(2,1)S(1)}, bf16[2,128,512]{2,1,0:T(8,128)(2,1)S(1)}, u32[]{:S(2)}, u32[]{:S(2)}) collective-permute-start(bf16[2,128,512]{2,1,0:T(8,128)(2,1)S(1)} %pad_maximum_fusion.1.mine_ref), channel_id=1, source_target_pairs={{0,1},{1,0},{2,3},{3,2},{4,5},{5,4},{6,7},{7,6},{8,9},{9,8},{10,11... | collective-permute-start | bytes 786440 | tf_op jit(solution)/shard_map/ppermute | solution.py:282
  13.4 6.6 %collective-permute-start.2 = (bf16[2,128,256]{2,1,0:T(8,128)(2,1)S(1)}, bf16[2,128,256]{2,1,0:T(8,128)(2,1)S(1)}, u32[]{:S(2)}, u32[]{:S(2)}) collective-permute-start(bf16[2,128,256]{2,1,0:T(8,128)(2,1)S(1)} %get-tuple-element.55), channel_id=1, source_target_pairs={{0,12},{2,14},{4,8},{6,10},{8,4},{10,6},{12,0},{14,2},{16,28},{18,... | collective-permute-start | bytes 393224 | tf_op jit(solution)/shard_map/ppermute | solution.py:285
  16.5 8.8 %collective-permute-start.8 = (bf16[2,128,256]{2,1,0:T(8,128)(2,1)S(1)}, bf16[2,128,256]{2,1,0:T(8,128)(2,1)S(1)}, u32[]{:S(2)}, u32[]{:S(2)}) collective-permute-start(bf16[2,128,256]{2,1,0:T(8,128)(2,1)S(1)} %get-tuple-element.70), channel_id=1, source_target_pairs={{0,14},{2,12},{4,10},{6,8},{8,6},{10,4},{12,2},{14,0},{16,30},{18,... | collective-permute-start | bytes 393224 | tf_op jit(solution)/shard_map/ppermute | solution.py:285
  21.2 6.9 %collective-permute-start.9 = (bf16[2,128,256]{2,1,0:T(8,128)(2,1)S(1)}, bf16[2,128,256]{2,1,0:T(8,128)(2,1)S(1)}, u32[]{:S(2)}, u32[]{:S(2)}) collective-permute-start(bf16[2,128,256]{2,1,0:T(8,128)(2,1)S(1)} %get-tuple-element.71), channel_id=1, source_target_pairs={{0,12},{2,14},{4,8},{6,10},{8,4},{10,6},{12,0},{14,2},{16,28},{18,... | collective-permute-start | bytes 393224 | tf_op jit(solution)/shard_map/ppermute | solution.py:285
  24.6 6.6 %collective-permute-start.10 = (bf16[2,128,256]{2,1,0:T(8,128)(2,1)S(1)}, bf16[2,128,256]{2,1,0:T(8,128)(2,1)S(1)}, u32[]{:S(2)}, u32[]{:S(2)}) collective-permute-start(bf16[2,128,256]{2,1,0:T(8,128)(2,1)S(1)} %get-tuple-element.72), channel_id=1, source_target_pairs={{0,14},{2,12},{4,10},{6,8},{8,6},{10,4},{12,2},{14,0},{16,30},{18,... | collective-permute-start | bytes 393224 | tf_op jit(solution)/shard_map/ppermute | solution.py:285
  24.6 11.4 %collective-permute-start.3 = (bf16[2,256,256]{2,1,0:T(8,128)(2,1)S(1)}, bf16[2,256,256]{2,1,0:T(8,128)(2,1)S(1)}, u32[]{:S(2)}, u32[]{:S(2)}) collective-permute-start(bf16[2,256,256]{2,1,0:T(8,128)(2,1)S(1)} %get-tuple-element.64), channel_id=1, source_target_pairs={{0,4},{2,6},{4,0},{6,2},{8,12},{10,14},{12,8},{14,10},{16,20},{18,... | collective-permute-start | bytes 786440 | tf_op jit(solution)/shard_map/ppermute | solution.py:285
  24.8 11.6 %collective-permute-start.4 = (bf16[2,256,256]{2,1,0:T(8,128)(2,1)S(1)}, bf16[2,256,256]{2,1,0:T(8,128)(2,1)S(1)}, u32[]{:S(2)}, u32[]{:S(2)}) collective-permute-start(bf16[2,256,256]{2,1,0:T(8,128)(2,1)S(1)} %get-tuple-element.65), channel_id=1, source_target_pairs={{0,8},{2,10},{4,12},{6,14},{8,0},{10,2},{12,4},{14,6},{16,24},{18,... | collective-permute-start | bytes 786440 | tf_op jit(solution)/shard_map/ppermute | solution.py:285
  25.3 16.2 %collective-permute-start.5 = (bf16[2,256,256]{2,1,0:T(8,128)(2,1)S(1)}, bf16[2,256,256]{2,1,0:T(8,128)(2,1)S(1)}, u32[]{:S(2)}, u32[]{:S(2)}) collective-permute-start(bf16[2,256,256]{2,1,0:T(8,128)(2,1)S(1)} %get-tuple-element.66), channel_id=1, source_target_pairs={{0,6},{2,4},{4,2},{6,0},{8,14},{10,12},{12,10},{14,8},{16,22},{18,... | collective-permute-start | bytes 786440 | tf_op jit(solution)/shard_map/ppermute | solution.py:285
  28.1 13.5 %collective-permute-start.6 = (bf16[2,256,256]{2,1,0:T(8,128)(2,1)S(1)}, bf16[2,256,256]{2,1,0:T(8,128)(2,1)S(1)}, u32[]{:S(2)}, u32[]{:S(2)}) collective-permute-start(bf16[2,256,256]{2,1,0:T(8,128)(2,1)S(1)} %get-tuple-element.67), channel_id=1, source_target_pairs={{0,10},{2,8},{4,14},{6,12},{8,2},{10,0},{12,6},{14,4},{16,26},{18,... | collective-permute-start | bytes 786440 | tf_op jit(solution)/shard_map/ppermute | solution.py:285
  31.2 10.4 %collective-permute-start.7 = (bf16[2,256,256]{2,1,0:T(8,128)(2,1)S(1)}, bf16[2,256,256]{2,1,0:T(8,128)(2,1)S(1)}, u32[]{:S(2)}, u32[]{:S(2)}) collective-permute-start(bf16[2,256,256]{2,1,0:T(8,128)(2,1)S(1)} %get-tuple-element.68), channel_id=1, source_target_pairs={{0,2},{2,0},{4,6},{6,4},{8,10},{10,8},{12,14},{14,12},{16,18},{18,... | collective-permute-start | bytes 786440 | tf_op jit(solution)/shard_map/ppermute | solution.py:285
  41.5 7.9 %copy-start = (bf16[1,8,2,256,256]{4,3,2,1,0:T(8,128)(2,1)S(1)}, bf16[1,8,2,256,256]{4,3,2,1,0:T(8,128)(2,1)}, u32[]{:S(2)}) copy-start(bf16[1,8,2,256,256]{4,3,2,1,0:T(8,128)(2,1)} %param.7) | copy-start | bytes 6291460
  48.0 16.9 %collective-permute-start.11 = (bf16[2,256,256]{2,1,0:T(8,128)(2,1)S(1)}, bf16[2,256,256]{2,1,0:T(8,128)(2,1)S(1)}, u32[]{:S(2)}, u32[]{:S(2)}) collective-permute-start(bf16[2,256,256]{2,1,0:T(8,128)(2,1)S(1)} %get-tuple-element.73), channel_id=1, source_target_pairs={{16,0},{18,10},{20,4},{22,14},{24,8},{26,2},{28,12},{30,6},{17,1},... | collective-permute-start | bytes 786440 | tf_op jit(solution)/shard_map/ppermute | solution.py:319
  71.3 6.9 %collective-permute-start.20 = (bf16[2,128,256]{2,1,0:T(8,128)(2,1)S(1)}, bf16[2,128,256]{2,1,0:T(8,128)(2,1)S(1)}, u32[]{:S(2)}, u32[]{:S(2)}) collective-permute-start(bf16[2,128,256]{2,1,0:T(8,128)(2,1)S(1)} %get-tuple-element.87), channel_id=1, source_target_pairs={{0,12},{2,14},{4,8},{6,10},{8,4},{10,6},{12,0},{14,2},{16,28},{18,... | collective-permute-start | bytes 393224 | tf_op jit(solution)/shard_map/ppermute | solution.py:285
  71.4 6.9 %collective-permute-start.21 = (bf16[2,128,256]{2,1,0:T(8,128)(2,1)S(1)}, bf16[2,128,256]{2,1,0:T(8,128)(2,1)S(1)}, u32[]{:S(2)}, u32[]{:S(2)}) collective-permute-start(bf16[2,128,256]{2,1,0:T(8,128)(2,1)S(1)} %get-tuple-element.88), channel_id=1, source_target_pairs={{0,14},{2,12},{4,10},{6,8},{8,6},{10,4},{12,2},{14,0},{16,30},{18,... | collective-permute-start | bytes 393224 | tf_op jit(solution)/shard_map/ppermute | solution.py:285
  71.5 13.1 %collective-permute-start.12 = (bf16[2,256,256]{2,1,0:T(8,128)(2,1)S(1)}, bf16[2,256,256]{2,1,0:T(8,128)(2,1)S(1)}, u32[]{:S(2)}, u32[]{:S(2)}) collective-permute-start(bf16[2,256,256]{2,1,0:T(8,128)(2,1)S(1)} %get-tuple-element.78), channel_id=1, source_target_pairs={{0,4},{2,6},{4,0},{6,2},{8,12},{10,14},{12,8},{14,10},{16,20},{18,... | collective-permute-start | bytes 786440 | tf_op jit(solution)/shard_map/ppermute | solution.py:285
  72.4 13.6 %collective-permute-start.13 = (bf16[2,256,256]{2,1,0:T(8,128)(2,1)S(1)}, bf16[2,256,256]{2,1,0:T(8,128)(2,1)S(1)}, u32[]{:S(2)}, u32[]{:S(2)}) collective-permute-start(bf16[2,256,256]{2,1,0:T(8,128)(2,1)S(1)} %get-tuple-element.79), channel_id=1, source_target_pairs={{0,8},{2,10},{4,12},{6,14},{8,0},{10,2},{12,4},{14,6},{16,24},{18,... | collective-permute-start | bytes 786440 | tf_op jit(solution)/shard_map/ppermute | solution.py:285
  74.9 16.7 %collective-permute-start.14 = (bf16[2,256,256]{2,1,0:T(8,128)(2,1)S(1)}, bf16[2,256,256]{2,1,0:T(8,128)(2,1)S(1)}, u32[]{:S(2)}, u32[]{:S(2)}) collective-permute-start(bf16[2,256,256]{2,1,0:T(8,128)(2,1)S(1)} %get-tuple-element.80), channel_id=1, source_target_pairs={{0,6},{2,4},{4,2},{6,0},{8,14},{10,12},{12,10},{14,8},{16,22},{18,... | collective-permute-start | bytes 786440 | tf_op jit(solution)/shard_map/ppermute | solution.py:285
  78.3 13.3 %collective-permute-start.15 = (bf16[2,256,256]{2,1,0:T(8,128)(2,1)S(1)}, bf16[2,256,256]{2,1,0:T(8,128)(2,1)S(1)}, u32[]{:S(2)}, u32[]{:S(2)}) collective-permute-start(bf16[2,256,256]{2,1,0:T(8,128)(2,1)S(1)} %get-tuple-element.81), channel_id=1, source_target_pairs={{0,10},{2,8},{4,14},{6,12},{8,2},{10,0},{12,6},{14,4},{16,26},{18,... | collective-permute-start | bytes 786440 | tf_op jit(solution)/shard_map/ppermute | solution.py:285
  78.3 13.3 %collective-permute-start.16 = (bf16[2,256,256]{2,1,0:T(8,128)(2,1)S(1)}, bf16[2,256,256]{2,1,0:T(8,128)(2,1)S(1)}, u32[]{:S(2)}, u32[]{:S(2)}) collective-permute-start(bf16[2,256,256]{2,1,0:T(8,128)(2,1)S(1)} %get-tuple-element.82), channel_id=1, source_target_pairs={{0,2},{2,0},{4,6},{6,4},{8,10},{10,8},{12,14},{14,12},{16,18},{18,... | collective-permute-start | bytes 786440 | tf_op jit(solution)/shard_map/ppermute | solution.py:285
  84.6 10.5 %collective-permute-start.17 = (bf16[2,128,256]{2,1,0:T(8,128)(2,1)S(1)}, bf16[2,128,256]{2,1,0:T(8,128)(2,1)S(1)}, u32[]{:S(2)}, u32[]{:S(2)}) collective-permute-start(bf16[2,128,256]{2,1,0:T(8,128)(2,1)S(1)} %get-tuple-element.83), channel_id=1, source_target_pairs={{0,12},{2,14},{4,8},{6,10},{8,4},{10,6},{12,0},{14,2},{16,28},{18,... | collective-permute-start | bytes 393224 | tf_op jit(solution)/shard_map/ppermute | solution.py:285
  86.0 9.2 %collective-permute-start.18 = (bf16[2,128,256]{2,1,0:T(8,128)(2,1)S(1)}, bf16[2,128,256]{2,1,0:T(8,128)(2,1)S(1)}, u32[]{:S(2)}, u32[]{:S(2)}) collective-permute-start(bf16[2,128,256]{2,1,0:T(8,128)(2,1)S(1)} %get-tuple-element.84), channel_id=1, source_target_pairs={{0,14},{2,12},{4,10},{6,8},{8,6},{10,4},{12,2},{14,0},{16,30},{18,... | collective-permute-start | bytes 393224 | tf_op jit(solution)/shard_map/ppermute | solution.py:285
  93.5 9.2 %collective-permute-start.22 = (bf16[2,128,512]{2,1,0:T(8,128)(2,1)S(1)}, bf16[2,128,512]{2,1,0:T(8,128)(2,1)S(1)}, u32[]{:S(2)}, u32[]{:S(2)}) collective-permute-start(bf16[2,128,512]{2,1,0:T(8,128)(2,1)S(1)} %get-tuple-element.90), channel_id=1, source_target_pairs={{0,1},{1,0},{2,3},{3,2},{4,5},{5,4},{6,7},{7,6},{8,9},{9,8},{10,11... | collective-permute-start | bytes 786440 | tf_op jit(solution)/shard_map/ppermute | solution.py:282
  97.0 10.5 %collective-permute-start.19 = (bf16[2,128,512]{2,1,0:T(8,128)(2,1)S(1)}, bf16[2,128,512]{2,1,0:T(8,128)(2,1)S(1)}, u32[]{:S(2)}, u32[]{:S(2)}) collective-permute-start(bf16[2,128,512]{2,1,0:T(8,128)(2,1)S(1)} %get-tuple-element.86), channel_id=1, source_target_pairs={{0,1},{1,0},{2,3},{3,2},{4,5},{5,4},{6,7},{7,6},{8,9},{9,8},{10,11... | collective-permute-start | bytes 786440 | tf_op jit(solution)/shard_map/ppermute | solution.py:282

commit v9 on v7

--- a/solution.py
+++ b/solution.py
@@ -46,6 +46,11 @@
     return lax.rem(lax.axis_index("sec").astype(jnp.int32), count)
 
 
+def position_at(place, count):
+    hops = lax.axis_size("sec") // count - 1 - lax.axis_index("sec").astype(jnp.int32) // count
+    return place ^ (count // 2 * lax.rem(hops, 2))
+
+
 def coded(amp, phase):
     half = 0.5 * phase
     square = half * half
@@ -81,7 +86,7 @@
         here = pl.ds(0 if i >= count - far else base, rows)
         if base and i < count - far:
             win_ref[:, :base] = refs[i][:, :base]
-        in_mine, in_left = first_masks(corner_ref, own ^ apart, base, (rows, window))
+        in_mine, in_left = first_masks(corner_ref, position_at(own ^ apart, count), base, (rows, window))
         for part in range(2):
             left, right = (
                 jnp.where(in_mine, mine_ref[part, :, cols].astype(f32), other_ref[part, :, cols].astype(f32))
@@ -106,7 +111,8 @@
 
 
 def ready_kernel(corner_ref, exit_ref, start_ref, down_ref, across_ref):
-    own = place_in_group(exit_ref.shape[0])
+    count = exit_ref.shape[0]
+    own = position_at(place_in_group(count), count)
     row_at = corner_ref[0, own]
     col_at = corner_ref[1, own]
     size = start_ref.shape[-1]
@@ -219,7 +225,7 @@
         sums = [jnp.zeros((tall, window), f32) for _ in range(8)]
         here = pl.ds(base + at, tall)
         for apart, spread_ref in zip(distances(len(spread_refs)), spread_refs):
-            position = own ^ apart
+            position = position_at(own ^ apart, len(spread_refs))
             there = pl.ds(at, tall) if apart >= len(spread_refs) - far else here
             in_mine, in_left = first_masks(corner_ref, position, base + at, (tall, window))
             wave_re, wave_im = (wave_ref[position, part, here, :].astype(f32) for part in range(2))
@@ -229,16 +235,18 @@
                 wave_re * spread_im - wave_im * spread_re,
             )
             for part in range(2):
-                left = jnp.where(in_left, parts[part], 0.0)
-                right = jnp.where(in_left, 0.0, parts[part])
-                for side, value in enumerate((left, right)):
-                    sums[4 * part + side] += jnp.where(in_mine, value, 0.0)
-                    sums[4 * part + 2 + side] += jnp.where(in_mine, 0.0, value)
+                own_part = jnp.where(in_mine, parts[part], 0.0)
+                sums[4 * part] += parts[part]
+                sums[4 * part + 1] += own_part
+                sums[4 * part + 2] += jnp.where(in_left, parts[part], 0.0)
+                sums[4 * part + 3] += jnp.where(in_left, own_part, 0.0)
+        left, right = pl.ds(0, window), pl.ds(window, window)
         for part in range(2):
-            for side in range(2):
-                cols = pl.ds(side * window, window)
-                own_ref[part, pl.ds(at, tall), cols] = sums[4 * part + side]
-                away_ref[part, pl.ds(at, tall), cols] = sums[4 * part + 2 + side].astype(bf16)
+            every, mine, at_left, mine_left = sums[4 * part : 4 * part + 4]
+            own_ref[part, pl.ds(at, tall), left] = mine_left
+            own_ref[part, pl.ds(at, tall), right] = mine - mine_left
+            away_ref[part, pl.ds(at, tall), left] = (at_left - mine_left).astype(bf16)
+            away_ref[part, pl.ds(at, tall), right] = ((every - mine) - (at_left - mine_left)).astype(bf16)
         return 0
 
     lax.fori_loop(0, rows // tall, one, 0)
@@ -305,7 +313,9 @@
     first = call(first_kernel, [shape_of(wave, bf16), shape_of((count,) + wave, bf16)], cost=cost, grant=12)
     leave, held = first(start, down, across, *windows)
     for stage in range(1, group_count):
-        come = lax.ppermute(leave, "sec", [(s, s - count) for s in range(count, sections)])
+        come = lax.ppermute(
+            leave, "sec", [(s, (s - count) ^ (count // 2)) for s in range(count, sections)]
+        )
         come, waves = lax.optimization_barrier((come, waves))
         is_last = stage == group_count - 1
         through = call(

time: 108 us -> 105 us (0.972)
  waiting for transfers between devices: 58.3 us -> 50.7 us
  starting transfers between devices: 25.2 us -> 30.3 us
    ppermute x1, waiting for transfers between devices: 12.8 us -> 8.15 us  [on_device(): lax.ppermute(leave, 'sec', [(s, s - count ^ count // 2) for s in range(co...]
    ppermute x18, starting transfers between devices: 18.1 us -> 22.1 us  [to_distance(): return lax.ppermute(value, 'sec', [(s, s ^ d) for s in range(sections)])]
    ppermute x4, waiting for transfers between devices: 15.9 us -> 13.5 us  [to_other_half(): return lax.ppermute(value, 'scan', [(0, 1), (1, 0)])]
    ppermute x4, starting transfers between devices: 5.63 us -> 6.73 us  [to_other_half(): return lax.ppermute(value, 'scan', [(0, 1), (1, 0)])]
  transfers between devices with their start and end apart: 23 -> 23, of which waited for: 15 -> 16; matrix products, arithmetic and copies ran while one was open for 0% -> 0% of each run, Pallas kernels for 9% -> 9%
where the time goes in v9:
time: 105 us
  waiting for transfers between devices  50.7 us (48%)
  starting transfers between devices  30.3 us (29%)
  Pallas kernels  21.3 us (20%)
  other arithmetic  2.08 us (2%)
    ppermute x18, waiting for transfers between devices, to_distance(): return lax.ppermute(value, 'sec', [(s, s ^ d) for s in range(sections)])  29 us
    ppermute x18, starting transfers between devices, to_distance(): return lax.ppermute(value, 'sec', [(s, s ^ d) for s in range(sections)])  22.1 us
    pallas_call x9, Pallas kernels, run(): pl.pallas_call(kernel, grid_spec=pltpu.PrefetchScalarGridSpec(num_scalar_...  21.3 us
    ppermute x4, waiting for transfers between devices, to_other_half(): return lax.ppermute(value, 'scan', [(0, 1), (1, 0)])  13.5 us
    ppermute x1, waiting for transfers between devices, on_device(): lax.ppermute(leave, 'sec', [(s, s - count ^ count // 2) for s in range(co...  8.15 us
    ppermute x4, starting transfers between devices, to_other_half(): return lax.ppermute(value, 'scan', [(0, 1), (1, 0)])  6.73 us
  transfers between devices with their start and end apart: 23, of which 16 were waited for; matrix products, arithmetic and copies ran while one was open for 0% of the time, Pallas kernels for 9%

profile of v9, /device:TPU:0, one launch (start us, length us, event | category | flops | bytes accessed | tf_op | source)
XLA Modules:
  0.0 104.6 jit_solution(10850056040396984623)
XLA Ops:
  0.0 2.0 %fusion.13 = (bf16[1,128,512]{2,1,0:T(8,128)(2,1)S(1)}, bf16[1,128,512]{2,1,0:T(8,128)(2,1)S(1)}, bf16[1,128,512]{2,1,0:T(8,128)(2,1)S(1)}, bf16[1,128,512]{2,1,0:T(8,128)(2,1)S(1)}) fusion(f32[1,256,512]{2,1,0:T(8,128)} %param.5, f32[1,256,512]{2,1,0:T(8,128)} %param.6), kind=kLoop, calls=%fused_computation.17 | loop fusion | flops 4849664 | bytes 1572864 | tf_op jit(solution)/shard_map/convert_element_type | solution.py:66
  2.1 3.0 %collective-permute-start = (bf16[2,128,512]{2,1,0:T(8,128)(2,1)S(1)}, bf16[2,128,512]{2,1,0:T(8,128)(2,1)S(1)}, u32[]{:S(2)}, u32[]{:S(2)}) collective-permute-start(bf16[2,128,512]{2,1,0:T(8,128)(2,1)S(1)} %pad_maximum_fusion.mine_ref), channel_id=1, source_target_pairs={{0,1},{1,0},{2,3},{3,2},{4,5},{5,4},{6,7},{7,6},{8,9},{9,8},{10,11... | collective-permute-start | bytes 786440 | tf_op jit(solution)/shard_map/ppermute | solution.py:279
  5.2 1.2 %shard_map.55 = (bf16[2,256,256]{2,1,0:T(8,128)(2,1)S(1)}, bf16[256,256]{1,0:T(8,128)(2,1)S(1)}, bf16[256,256]{1,0:T(8,128)(2,1)S(1)}) custom-call(s32[2,8]{1,0:T(2,128)S(1)} %bitcast.4, bf16[8,2,256,256]{3,2,1,0:T(8,128)(2,1)S(1)} %copy-done.1), custom_call_target="tpu_custom_call" | custom-call | bytes 2621504 | tf_op jit(solution)/shard_map/pallas_call | solution.py:27
  6.4 5.8 %collective-permute-done.other_ref = bf16[2,128,512]{2,1,0:T(8,128)(2,1)S(1)} collective-permute-done((bf16[2,128,512]{2,1,0:T(8,128)(2,1)S(1)}, bf16[2,128,512]{2,1,0:T(8,128)(2,1)S(1)}, u32[]{:S(2)}, u32[]{:S(2)}) %collective-permute-start) | collective-permute-done | bytes 262176 | tf_op jit(solution)/shard_map/ppermute | solution.py:279
  12.2 1.2 %shard_map.56 = (bf16[2,256,256]{2,1,0:T(8,128)(2,1)S(1)}, bf16[2,256,256]{2,1,0:T(8,128)(2,1)S(1)}, bf16[2,256,256]{2,1,0:T(8,128)(2,1)S(1)}, bf16[2,256,256]{2...) custom-call(s32[2,8]{1,0:T(2,128)S(1)} %bitcast.5, ...), custom_call_target="tpu_custom_call" | custom-call | bytes 2359360 | tf_op jit(solution)/shard_map/pallas_call | solution.py:27
  13.4 3.2 %collective-permute-start.2 = (bf16[2,128,256]{2,1,0:T(8,128)(2,1)S(1)}, bf16[2,128,256]{2,1,0:T(8,128)(2,1)S(1)}, u32[]{:S(2)}, u32[]{:S(2)}) collective-permute-start(bf16[2,128,256]{2,1,0:T(8,128)(2,1)S(1)} %get-tuple-element.55), channel_id=1, source_target_pairs={{0,12},{2,14},{4,8},{6,10},{8,4},{10,6},{12,0},{14,2},{16,28},{18,... | collective-permute-start | bytes 393224 | tf_op jit(solution)/shard_map/ppermute | solution.py:282
  17.0 2.9 %collective-permute-done.2.refs_6_ = bf16[2,128,256]{2,1,0:T(8,128)(2,1)S(1)} collective-permute-done((bf16[2,128,256]{2,1,0:T(8,128)(2,1)S(1)}, bf16[2,128,256]{2,1,0:T(8,128)(2,1)S(1)}, u32[]{:S(2)}, u32[]{:S(2)}) %collective-permute-start.2) | collective-permute-done | bytes 131104 | tf_op jit(solution)/shard_map/ppermute | solution.py:282
  19.9 1.2 %shard_map.57 = (bf16[2,256,256]{2,1,0:T(8,128)(2,1)S(1)}, bf16[2,256,256]{2,1,0:T(8,128)(2,1)S(1)}, bf16[2,256,256]{2,1,0:T(8,128)(2,1)S(1)}, bf16[2,256,256]{2...) custom-call(s32[2,8]{1,0:T(2,128)S(1)} %bitcast.6, ...), custom_call_target="tpu_custom_call", output_to_operand_aliasing={{0}: (3, {}), {1}: (4, {}), {2}: (5, {}), {3}: (6, {}), {4}... | custom-call | bytes 3932224 | tf_op jit(solution)/shard_map/pallas_call | solution.py:27
  21.2 3.4 %collective-permute-start.9 = (bf16[2,128,256]{2,1,0:T(8,128)(2,1)S(1)}, bf16[2,128,256]{2,1,0:T(8,128)(2,1)S(1)}, u32[]{:S(2)}, u32[]{:S(2)}) collective-permute-start(bf16[2,128,256]{2,1,0:T(8,128)(2,1)S(1)} %get-tuple-element.71), channel_id=1, source_target_pairs={{0,12},{2,14},{4,8},{6,10},{8,4},{10,6},{12,0},{14,2},{16,28},{18,... | collective-permute-start | bytes 393224 | tf_op jit(solution)/shard_map/ppermute | solution.py:282
  25.3 2.2 %collective-permute-start.5 = (bf16[2,256,256]{2,1,0:T(8,128)(2,1)S(1)}, bf16[2,256,256]{2,1,0:T(8,128)(2,1)S(1)}, u32[]{:S(2)}, u32[]{:S(2)}) collective-permute-start(bf16[2,256,256]{2,1,0:T(8,128)(2,1)S(1)} %get-tuple-element.66), channel_id=1, source_target_pairs={{0,6},{2,4},{4,2},{6,0},{8,14},{10,12},{12,10},{14,8},{16,22},{18,... | collective-permute-start | bytes 786440 | tf_op jit(solution)/shard_map/ppermute | solution.py:282
  28.4 2.8 %collective-permute-done.10.refs_9_ = bf16[2,128,256]{2,1,0:T(8,128)(2,1)S(1)} collective-permute-done((bf16[2,128,256]{2,1,0:T(8,128)(2,1)S(1)}, bf16[2,128,256]{2,1,0:T(8,128)(2,1)S(1)}, u32[]{:S(2)}, u32[]{:S(2)}) %collective-permute-start.10) | collective-permute-done | bytes 131104 | tf_op jit(solution)/shard_map/ppermute | solution.py:282
  31.2 4.9 %collective-permute-done.3.refs_1_ = bf16[2,256,256]{2,1,0:T(8,128)(2,1)S(1)} collective-permute-done((bf16[2,256,256]{2,1,0:T(8,128)(2,1)S(1)}, bf16[2,256,256]{2,1,0:T(8,128)(2,1)S(1)}, u32[]{:S(2)}, u32[]{:S(2)}) %collective-permute-start.3) | collective-permute-done | bytes 262176 | tf_op jit(solution)/shard_map/ppermute | solution.py:282
  36.4 5.1 %collective-permute-done.5.refs_3_ = bf16[2,256,256]{2,1,0:T(8,128)(2,1)S(1)} collective-permute-done((bf16[2,256,256]{2,1,0:T(8,128)(2,1)S(1)}, bf16[2,256,256]{2,1,0:T(8,128)(2,1)S(1)}, u32[]{:S(2)}, u32[]{:S(2)}) %collective-permute-start.5) | collective-permute-done | bytes 262176 | tf_op jit(solution)/shard_map/ppermute | solution.py:282
  41.5 5.2 %shard_map.58 = (bf16[2,256,256]{2,1,0:T(8,128)(2,1)S(1)}, bf16[8,2,256,256]{3,2,1,0:T(8,128)(2,1)S(1)}) custom-call(bf16[2,256,256]{2,1,0:T(8,128)(2,1)S(1)} %get-tuple-element.51.start_ref, bf16[256,256]{1,0:T(8,128)(2,1)S(1)} %get-tuple-element.52.down_ref, bf16[256,256]{1,0:T(8,128)(2,1)S(1)} %get-tuple-element.53.across_ref, ...), custom_call_target="tpu_custom_call" | custom-call | flops 2147483648 | bytes 4980736 | tf_op jit(solution)/shard_map/pallas_call | solution.py:27
  46.8 1.5 %collective-permute-start.11 = (bf16[2,256,256]{2,1,0:T(8,128)(2,1)S(1)}, bf16[2,256,256]{2,1,0:T(8,128)(2,1)S(1)}, u32[]{:S(2)}, u32[]{:S(2)}) collective-permute-start(bf16[2,256,256]{2,1,0:T(8,128)(2,1)S(1)} %get-tuple-element.73), channel_id=1, source_target_pairs={{16,8},{18,10},{20,12},{22,14},{24,0},{26,2},{28,4},{30,6},{17,9},... | collective-permute-start | bytes 786440 | tf_op jit(solution)/shard_map/ppermute | solution.py:316
  48.3 2.5 %shard_map.59.wave_ref = bf16[8,2,256,256]{3,2,1,0:T(8,128)(2,1)S(1)} custom-call(s32[2,8]{1,0:T(2,128)S(1)} %bitcast.7, bf16[8,2,256,256]{3,2,1,0:T(8,128)(2,1)S(1)} %bitcast.3), custom_call_target="tpu_custom_call" | custom-call | bytes 4194368 | tf_op jit(solution)/shard_map/pallas_call | solution.py:27
  50.8 8.2 %collective-permute-done.11.come_ref = bf16[2,256,256]{2,1,0:T(8,128)(2,1)S(1)} collective-permute-done((bf16[2,256,256]{2,1,0:T(8,128)(2,1)S(1)}, bf16[2,256,256]{2,1,0:T(8,128)(2,1)S(1)}, u32[]{:S(2)}, u32[]{:S(2)}) %collective-permute-start.11) | collective-permute-done | bytes 262176 | tf_op jit(solution)/shard_map/ppermute | solution.py:316
  58.9 5.3 %shard_map.60 = (bf16[2,256,256]{2,1,0:T(8,128)(2,1)S(1)}, bf16[2,256,256]{2,1,0:T(8,128)(2,1)S(1)}, bf16[2,256,256]{2,1,0:T(8,128)(2,1)S(1)}, bf16[2,256,256]{2...) custom-call(bf16[2,256,256]{2,1,0:T(8,128)(2,1)S(1)} %get-tuple-elem, ...), custom_call_target="tpu_custom_call" | custom-call | flops 2147483648 | bytes 4980736 | tf_op jit(solution)/shard_map/pallas_call | solution.py:27
  64.2 5.7 %collective-permute-start.20 = (bf16[2,128,256]{2,1,0:T(8,128)(2,1)S(1)}, bf16[2,128,256]{2,1,0:T(8,128)(2,1)S(1)}, u32[]{:S(2)}, u32[]{:S(2)}) collective-permute-start(bf16[2,128,256]{2,1,0:T(8,128)(2,1)S(1)} %get-tuple-element.87), channel_id=1, source_target_pairs={{0,12},{2,14},{4,8},{6,10},{8,4},{10,6},{12,0},{14,2},{16,28},{18,... | collective-permute-start | bytes 393224 | tf_op jit(solution)/shard_map/ppermute | solution.py:282
  69.9 1.2 %collective-permute-start.12 = (bf16[2,256,256]{2,1,0:T(8,128)(2,1)S(1)}, bf16[2,256,256]{2,1,0:T(8,128)(2,1)S(1)}, u32[]{:S(2)}, u32[]{:S(2)}) collective-permute-start(bf16[2,256,256]{2,1,0:T(8,128)(2,1)S(1)} %get-tuple-element.78), channel_id=1, source_target_pairs={{0,4},{2,6},{4,0},{6,2},{8,12},{10,14},{12,8},{14,10},{16,20},{18,... | collective-permute-start | bytes 786440 | tf_op jit(solution)/shard_map/ppermute | solution.py:282
  71.6 2.1 %collective-permute-start.14 = (bf16[2,256,256]{2,1,0:T(8,128)(2,1)S(1)}, bf16[2,256,256]{2,1,0:T(8,128)(2,1)S(1)}, u32[]{:S(2)}, u32[]{:S(2)}) collective-permute-start(bf16[2,256,256]{2,1,0:T(8,128)(2,1)S(1)} %get-tuple-element.80), channel_id=1, source_target_pairs={{0,6},{2,4},{4,2},{6,0},{8,14},{10,12},{12,10},{14,8},{16,22},{18,... | collective-permute-start | bytes 786440 | tf_op jit(solution)/shard_map/ppermute | solution.py:282
  73.7 2.7 %collective-permute-done.21.refs_7_ = bf16[2,128,256]{2,1,0:T(8,128)(2,1)S(1)} collective-permute-done((bf16[2,128,256]{2,1,0:T(8,128)(2,1)S(1)}, bf16[2,128,256]{2,1,0:T(8,128)(2,1)S(1)}, u32[]{:S(2)}, u32[]{:S(2)}) %collective-permute-start.21) | collective-permute-done | bytes 131104 | tf_op jit(solution)/shard_map/ppermute | solution.py:282
  76.9 4.4 %collective-permute-done.12.refs_1_ = bf16[2,256,256]{2,1,0:T(8,128)(2,1)S(1)} collective-permute-done((bf16[2,256,256]{2,1,0:T(8,128)(2,1)S(1)}, bf16[2,256,256]{2,1,0:T(8,128)(2,1)S(1)}, u32[]{:S(2)}, u32[]{:S(2)}) %collective-permute-start.12) | collective-permute-done | bytes 262176 | tf_op jit(solution)/shard_map/ppermute | solution.py:282
  81.3 2.3 %collective-permute-start.17 = (bf16[2,128,256]{2,1,0:T(8,128)(2,1)S(1)}, bf16[2,128,256]{2,1,0:T(8,128)(2,1)S(1)}, u32[]{:S(2)}, u32[]{:S(2)}) collective-permute-start(bf16[2,128,256]{2,1,0:T(8,128)(2,1)S(1)} %get-tuple-element.83), channel_id=1, source_target_pairs={{0,12},{2,14},{4,8},{6,10},{8,4},{10,6},{12,0},{14,2},{16,28},{18,... | collective-permute-start | bytes 393224 | tf_op jit(solution)/shard_map/ppermute | solution.py:282
  83.6 3.8 %collective-permute-done.14.refs_3_ = bf16[2,256,256]{2,1,0:T(8,128)(2,1)S(1)} collective-permute-done((bf16[2,256,256]{2,1,0:T(8,128)(2,1)S(1)}, bf16[2,256,256]{2,1,0:T(8,128)(2,1)S(1)}, u32[]{:S(2)}, u32[]{:S(2)}) %collective-permute-start.14) | collective-permute-done | bytes 262176 | tf_op jit(solution)/shard_map/ppermute | solution.py:282
  87.5 1.8 %shard_map.62 = (f32[2,128,512]{2,1,0:T(8,128)S(1)}, bf16[2,128,512]{2,1,0:T(8,128)(2,1)S(1)}) custom-call(s32[2,8]{1,0:T(2,128)S(1)} %bitcast.8, bf16[8,2,256,256]{3,2,1,0:T(8,128)(2,1)S(1)} %shard_map.59.wave_ref, bf16[2,256,256]{2,1,0:T(8,128)(2,1)S(1)} %get-tuple-element.77.refs_0_, bf16[2,256,256]{2,1,0:T(8,128)(2,1)S(1)} %collective-permute-done.12.refs_1_, ...), custom_call_target="tpu_custom_call" | custom-call | bytes 4718656 | tf_op jit(solution)/shard_map/pallas_call | solution.py:27
  89.3 1.8 %collective-permute-start.22 = (bf16[2,128,512]{2,1,0:T(8,128)(2,1)S(1)}, bf16[2,128,512]{2,1,0:T(8,128)(2,1)S(1)}, u32[]{:S(2)}, u32[]{:S(2)}) collective-permute-start(bf16[2,128,512]{2,1,0:T(8,128)(2,1)S(1)} %get-tuple-element.90), channel_id=1, source_target_pairs={{0,1},{1,0},{2,3},{3,2},{4,5},{5,4},{6,7},{7,6},{8,9},{9,8},{10,11... | collective-permute-start | bytes 786440 | tf_op jit(solution)/shard_map/ppermute | solution.py:279
  91.1 1.4 %collective-permute-done.18.refs_7_ = bf16[2,128,256]{2,1,0:T(8,128)(2,1)S(1)} collective-permute-done((bf16[2,128,256]{2,1,0:T(8,128)(2,1)S(1)}, bf16[2,128,256]{2,1,0:T(8,128)(2,1)S(1)}, u32[]{:S(2)}, u32[]{:S(2)}) %collective-permute-start.18) | collective-permute-done | bytes 131104 | tf_op jit(solution)/shard_map/ppermute | solution.py:282
  92.5 1.8 %shard_map.61 = (f32[2,128,512]{2,1,0:T(8,128)S(1)}, bf16[2,128,512]{2,1,0:T(8,128)(2,1)S(1)}) custom-call(s32[2,8]{1,0:T(2,128)S(1)} %bitcast.9, bf16[8,2,256,256]{3,2,1,0:T(8,128)(2,1)S(1)} %shard_map.59.wave_ref, bf16[2,256,256]{2,1,0:T(8,128)(2,1)S(1)} %get-tuple-element.77.refs_0_, bf16[2,256,256]{2,1,0:T(8,128)(2,1)S(1)} %collective-permute-done.12.refs_1_, ...), custom_call_target="tpu_custom_call" | custom-call | bytes 4718656 | tf_op jit(solution)/shard_map/pallas_call | solution.py:27
  94.4 1.9 %collective-permute-start.19 = (bf16[2,128,512]{2,1,0:T(8,128)(2,1)S(1)}, bf16[2,128,512]{2,1,0:T(8,128)(2,1)S(1)}, u32[]{:S(2)}, u32[]{:S(2)}) collective-permute-start(bf16[2,128,512]{2,1,0:T(8,128)(2,1)S(1)} %get-tuple-element.86), channel_id=1, source_target_pairs={{0,1},{1,0},{2,3},{3,2},{4,5},{5,4},{6,7},{7,6},{8,9},{9,8},{10,11... | collective-permute-start | bytes 786440 | tf_op jit(solution)/shard_map/ppermute | solution.py:279
  96.2 2.3 %collective-permute-done.22.refs_3_ = bf16[2,128,512]{2,1,0:T(8,128)(2,1)S(1)} collective-permute-done((bf16[2,128,512]{2,1,0:T(8,128)(2,1)S(1)}, bf16[2,128,512]{2,1,0:T(8,128)(2,1)S(1)}, u32[]{:S(2)}, u32[]{:S(2)}) %collective-permute-start.22) | collective-permute-done | bytes 262176 | tf_op jit(solution)/shard_map/ppermute | solution.py:279
  98.5 4.9 %collective-permute-done.19.refs_1_ = bf16[2,128,512]{2,1,0:T(8,128)(2,1)S(1)} collective-permute-done((bf16[2,128,512]{2,1,0:T(8,128)(2,1)S(1)}, bf16[2,128,512]{2,1,0:T(8,128)(2,1)S(1)}, u32[]{:S(2)}, u32[]{:S(2)}) %collective-permute-start.19) | collective-permute-done | bytes 262176 | tf_op jit(solution)/shard_map/ppermute | solution.py:279
  (32 shorter events, 4.7 us)
Async XLA Ops:
  0.0 5.2 %copy-start.2 = (s32[8,2]{0,1:T(2,128)S(1)}, s32[8,2]{0,1:T(2,128)}, u32[]{:S(2)}) copy-start(s32[8,2]{0,1:T(2,128)} %param.9) | copy-start | bytes 196
  0.0 5.2 %copy-start.1 = (bf16[8,2,256,256]{3,2,1,0:T(8,128)(2,1)S(1)}, bf16[8,2,256,256]{3,2,1,0:T(8,128)(2,1)}, u32[]{:S(2)}) copy-start(bf16[8,2,256,256]{3,2,1,0:T(8,128)(2,1)} %exit_ref.1) | copy-start | bytes 6291460
  2.1 10.1 %collective-permute-start = (bf16[2,128,512]{2,1,0:T(8,128)(2,1)S(1)}, bf16[2,128,512]{2,1,0:T(8,128)(2,1)S(1)}, u32[]{:S(2)}, u32[]{:S(2)}) collective-permute-start(bf16[2,128,512]{2,1,0:T(8,128)(2,1)S(1)} %pad_maximum_fusion.mine_ref), channel_id=1, source_target_pairs={{0,1},{1,0},{2,3},{3,2},{4,5},{5,4},{6,7},{7,6},{8,9},{9,8},{10,11... | collective-permute-start | bytes 786440 | tf_op jit(solution)/shard_map/ppermute | solution.py:279
  5.1 11.9 %collective-permute-start.1 = (bf16[2,128,512]{2,1,0:T(8,128)(2,1)S(1)}, bf16[2,128,512]{2,1,0:T(8,128)(2,1)S(1)}, u32[]{:S(2)}, u32[]{:S(2)}) collective-permute-start(bf16[2,128,512]{2,1,0:T(8,128)(2,1)S(1)} %pad_maximum_fusion.1.mine_ref), channel_id=1, source_target_pairs={{0,1},{1,0},{2,3},{3,2},{4,5},{5,4},{6,7},{7,6},{8,9},{9,8},{10,11... | collective-permute-start | bytes 786440 | tf_op jit(solution)/shard_map/ppermute | solution.py:279
  13.4 6.6 %collective-permute-start.2 = (bf16[2,128,256]{2,1,0:T(8,128)(2,1)S(1)}, bf16[2,128,256]{2,1,0:T(8,128)(2,1)S(1)}, u32[]{:S(2)}, u32[]{:S(2)}) collective-permute-start(bf16[2,128,256]{2,1,0:T(8,128)(2,1)S(1)} %get-tuple-element.55), channel_id=1, source_target_pairs={{0,12},{2,14},{4,8},{6,10},{8,4},{10,6},{12,0},{14,2},{16,28},{18,... | collective-permute-start | bytes 393224 | tf_op jit(solution)/shard_map/ppermute | solution.py:282
  16.5 8.8 %collective-permute-start.8 = (bf16[2,128,256]{2,1,0:T(8,128)(2,1)S(1)}, bf16[2,128,256]{2,1,0:T(8,128)(2,1)S(1)}, u32[]{:S(2)}, u32[]{:S(2)}) collective-permute-start(bf16[2,128,256]{2,1,0:T(8,128)(2,1)S(1)} %get-tuple-element.70), channel_id=1, source_target_pairs={{0,14},{2,12},{4,10},{6,8},{8,6},{10,4},{12,2},{14,0},{16,30},{18,... | collective-permute-start | bytes 393224 | tf_op jit(solution)/shard_map/ppermute | solution.py:282
  21.2 6.9 %collective-permute-start.9 = (bf16[2,128,256]{2,1,0:T(8,128)(2,1)S(1)}, bf16[2,128,256]{2,1,0:T(8,128)(2,1)S(1)}, u32[]{:S(2)}, u32[]{:S(2)}) collective-permute-start(bf16[2,128,256]{2,1,0:T(8,128)(2,1)S(1)} %get-tuple-element.71), channel_id=1, source_target_pairs={{0,12},{2,14},{4,8},{6,10},{8,4},{10,6},{12,0},{14,2},{16,28},{18,... | collective-permute-start | bytes 393224 | tf_op jit(solution)/shard_map/ppermute | solution.py:282
  24.6 6.6 %collective-permute-start.10 = (bf16[2,128,256]{2,1,0:T(8,128)(2,1)S(1)}, bf16[2,128,256]{2,1,0:T(8,128)(2,1)S(1)}, u32[]{:S(2)}, u32[]{:S(2)}) collective-permute-start(bf16[2,128,256]{2,1,0:T(8,128)(2,1)S(1)} %get-tuple-element.72), channel_id=1, source_target_pairs={{0,14},{2,12},{4,10},{6,8},{8,6},{10,4},{12,2},{14,0},{16,30},{18,... | collective-permute-start | bytes 393224 | tf_op jit(solution)/shard_map/ppermute | solution.py:282
  24.6 11.4 %collective-permute-start.3 = (bf16[2,256,256]{2,1,0:T(8,128)(2,1)S(1)}, bf16[2,256,256]{2,1,0:T(8,128)(2,1)S(1)}, u32[]{:S(2)}, u32[]{:S(2)}) collective-permute-start(bf16[2,256,256]{2,1,0:T(8,128)(2,1)S(1)} %get-tuple-element.64), channel_id=1, source_target_pairs={{0,4},{2,6},{4,0},{6,2},{8,12},{10,14},{12,8},{14,10},{16,20},{18,... | collective-permute-start | bytes 786440 | tf_op jit(solution)/shard_map/ppermute | solution.py:282
  24.8 11.6 %collective-permute-start.4 = (bf16[2,256,256]{2,1,0:T(8,128)(2,1)S(1)}, bf16[2,256,256]{2,1,0:T(8,128)(2,1)S(1)}, u32[]{:S(2)}, u32[]{:S(2)}) collective-permute-start(bf16[2,256,256]{2,1,0:T(8,128)(2,1)S(1)} %get-tuple-element.65), channel_id=1, source_target_pairs={{0,8},{2,10},{4,12},{6,14},{8,0},{10,2},{12,4},{14,6},{16,24},{18,... | collective-permute-start | bytes 786440 | tf_op jit(solution)/shard_map/ppermute | solution.py:282
  25.3 16.2 %collective-permute-start.5 = (bf16[2,256,256]{2,1,0:T(8,128)(2,1)S(1)}, bf16[2,256,256]{2,1,0:T(8,128)(2,1)S(1)}, u32[]{:S(2)}, u32[]{:S(2)}) collective-permute-start(bf16[2,256,256]{2,1,0:T(8,128)(2,1)S(1)} %get-tuple-element.66), channel_id=1, source_target_pairs={{0,6},{2,4},{4,2},{6,0},{8,14},{10,12},{12,10},{14,8},{16,22},{18,... | collective-permute-start | bytes 786440 | tf_op jit(solution)/shard_map/ppermute | solution.py:282
  28.1 13.5 %collective-permute-start.6 = (bf16[2,256,256]{2,1,0:T(8,128)(2,1)S(1)}, bf16[2,256,256]{2,1,0:T(8,128)(2,1)S(1)}, u32[]{:S(2)}, u32[]{:S(2)}) collective-permute-start(bf16[2,256,256]{2,1,0:T(8,128)(2,1)S(1)} %get-tuple-element.67), channel_id=1, source_target_pairs={{0,10},{2,8},{4,14},{6,12},{8,2},{10,0},{12,6},{14,4},{16,26},{18,... | collective-permute-start | bytes 786440 | tf_op jit(solution)/shard_map/ppermute | solution.py:282
  31.2 10.4 %collective-permute-start.7 = (bf16[2,256,256]{2,1,0:T(8,128)(2,1)S(1)}, bf16[2,256,256]{2,1,0:T(8,128)(2,1)S(1)}, u32[]{:S(2)}, u32[]{:S(2)}) collective-permute-start(bf16[2,256,256]{2,1,0:T(8,128)(2,1)S(1)} %get-tuple-element.68), channel_id=1, source_target_pairs={{0,2},{2,0},{4,6},{6,4},{8,10},{10,8},{12,14},{14,12},{16,18},{18,... | collective-permute-start | bytes 786440 | tf_op jit(solution)/shard_map/ppermute | solution.py:282
  41.5 6.7 %copy-start = (bf16[1,8,2,256,256]{4,3,2,1,0:T(8,128)(2,1)S(1)}, bf16[1,8,2,256,256]{4,3,2,1,0:T(8,128)(2,1)}, u32[]{:S(2)}) copy-start(bf16[1,8,2,256,256]{4,3,2,1,0:T(8,128)(2,1)} %param.7) | copy-start | bytes 6291460
  46.8 12.1 %collective-permute-start.11 = (bf16[2,256,256]{2,1,0:T(8,128)(2,1)S(1)}, bf16[2,256,256]{2,1,0:T(8,128)(2,1)S(1)}, u32[]{:S(2)}, u32[]{:S(2)}) collective-permute-start(bf16[2,256,256]{2,1,0:T(8,128)(2,1)S(1)} %get-tuple-element.73), channel_id=1, source_target_pairs={{16,8},{18,10},{20,12},{22,14},{24,0},{26,2},{28,4},{30,6},{17,9},... | collective-permute-start | bytes 786440 | tf_op jit(solution)/shard_map/ppermute | solution.py:316
  64.2 9.5 %collective-permute-start.20 = (bf16[2,128,256]{2,1,0:T(8,128)(2,1)S(1)}, bf16[2,128,256]{2,1,0:T(8,128)(2,1)S(1)}, u32[]{:S(2)}, u32[]{:S(2)}) collective-permute-start(bf16[2,128,256]{2,1,0:T(8,128)(2,1)S(1)} %get-tuple-element.87), channel_id=1, source_target_pairs={{0,12},{2,14},{4,8},{6,10},{8,4},{10,6},{12,0},{14,2},{16,28},{18,... | collective-permute-start | bytes 393224 | tf_op jit(solution)/shard_map/ppermute | solution.py:282
  69.9 6.6 %collective-permute-start.21 = (bf16[2,128,256]{2,1,0:T(8,128)(2,1)S(1)}, bf16[2,128,256]{2,1,0:T(8,128)(2,1)S(1)}, u32[]{:S(2)}, u32[]{:S(2)}) collective-permute-start(bf16[2,128,256]{2,1,0:T(8,128)(2,1)S(1)} %get-tuple-element.88), channel_id=1, source_target_pairs={{0,14},{2,12},{4,10},{6,8},{8,6},{10,4},{12,2},{14,0},{16,30},{18,... | collective-permute-start | bytes 393224 | tf_op jit(solution)/shard_map/ppermute | solution.py:282
  69.9 11.4 %collective-permute-start.12 = (bf16[2,256,256]{2,1,0:T(8,128)(2,1)S(1)}, bf16[2,256,256]{2,1,0:T(8,128)(2,1)S(1)}, u32[]{:S(2)}, u32[]{:S(2)}) collective-permute-start(bf16[2,256,256]{2,1,0:T(8,128)(2,1)S(1)} %get-tuple-element.78), channel_id=1, source_target_pairs={{0,4},{2,6},{4,0},{6,2},{8,12},{10,14},{12,8},{14,10},{16,20},{18,... | collective-permute-start | bytes 786440 | tf_op jit(solution)/shard_map/ppermute | solution.py:282
  71.1 12.5 %collective-permute-start.13 = (bf16[2,256,256]{2,1,0:T(8,128)(2,1)S(1)}, bf16[2,256,256]{2,1,0:T(8,128)(2,1)S(1)}, u32[]{:S(2)}, u32[]{:S(2)}) collective-permute-start(bf16[2,256,256]{2,1,0:T(8,128)(2,1)S(1)} %get-tuple-element.79), channel_id=1, source_target_pairs={{0,8},{2,10},{4,12},{6,14},{8,0},{10,2},{12,4},{14,6},{16,24},{18,... | collective-permute-start | bytes 786440 | tf_op jit(solution)/shard_map/ppermute | solution.py:282
  71.6 15.9 %collective-permute-start.14 = (bf16[2,256,256]{2,1,0:T(8,128)(2,1)S(1)}, bf16[2,256,256]{2,1,0:T(8,128)(2,1)S(1)}, u32[]{:S(2)}, u32[]{:S(2)}) collective-permute-start(bf16[2,256,256]{2,1,0:T(8,128)(2,1)S(1)} %get-tuple-element.80), channel_id=1, source_target_pairs={{0,6},{2,4},{4,2},{6,0},{8,14},{10,12},{12,10},{14,8},{16,22},{18,... | collective-permute-start | bytes 786440 | tf_op jit(solution)/shard_map/ppermute | solution.py:282
  73.7 13.8 %collective-permute-start.15 = (bf16[2,256,256]{2,1,0:T(8,128)(2,1)S(1)}, bf16[2,256,256]{2,1,0:T(8,128)(2,1)S(1)}, u32[]{:S(2)}, u32[]{:S(2)}) collective-permute-start(bf16[2,256,256]{2,1,0:T(8,128)(2,1)S(1)} %get-tuple-element.81), channel_id=1, source_target_pairs={{0,10},{2,8},{4,14},{6,12},{8,2},{10,0},{12,6},{14,4},{16,26},{18,... | collective-permute-start | bytes 786440 | tf_op jit(solution)/shard_map/ppermute | solution.py:282
  76.4 11.1 %collective-permute-start.16 = (bf16[2,256,256]{2,1,0:T(8,128)(2,1)S(1)}, bf16[2,256,256]{2,1,0:T(8,128)(2,1)S(1)}, u32[]{:S(2)}, u32[]{:S(2)}) collective-permute-start(bf16[2,256,256]{2,1,0:T(8,128)(2,1)S(1)} %get-tuple-element.82), channel_id=1, source_target_pairs={{0,2},{2,0},{4,6},{6,4},{8,10},{10,8},{12,14},{14,12},{16,18},{18,... | collective-permute-start | bytes 786440 | tf_op jit(solution)/shard_map/ppermute | solution.py:282
  81.3 9.8 %collective-permute-start.17 = (bf16[2,128,256]{2,1,0:T(8,128)(2,1)S(1)}, bf16[2,128,256]{2,1,0:T(8,128)(2,1)S(1)}, u32[]{:S(2)}, u32[]{:S(2)}) collective-permute-start(bf16[2,128,256]{2,1,0:T(8,128)(2,1)S(1)} %get-tuple-element.83), channel_id=1, source_target_pairs={{0,12},{2,14},{4,8},{6,10},{8,4},{10,6},{12,0},{14,2},{16,28},{18,... | collective-permute-start | bytes 393224 | tf_op jit(solution)/shard_map/ppermute | solution.py:282
  83.6 8.9 %collective-permute-start.18 = (bf16[2,128,256]{2,1,0:T(8,128)(2,1)S(1)}, bf16[2,128,256]{2,1,0:T(8,128)(2,1)S(1)}, u32[]{:S(2)}, u32[]{:S(2)}) collective-permute-start(bf16[2,128,256]{2,1,0:T(8,128)(2,1)S(1)} %get-tuple-element.84), channel_id=1, source_target_pairs={{0,14},{2,12},{4,10},{6,8},{8,6},{10,4},{12,2},{14,0},{16,30},{18,... | collective-permute-start | bytes 393224 | tf_op jit(solution)/shard_map/ppermute | solution.py:282
  89.3 9.2 %collective-permute-start.22 = (bf16[2,128,512]{2,1,0:T(8,128)(2,1)S(1)}, bf16[2,128,512]{2,1,0:T(8,128)(2,1)S(1)}, u32[]{:S(2)}, u32[]{:S(2)}) collective-permute-start(bf16[2,128,512]{2,1,0:T(8,128)(2,1)S(1)} %get-tuple-element.90), channel_id=1, source_target_pairs={{0,1},{1,0},{2,3},{3,2},{4,5},{5,4},{6,7},{7,6},{8,9},{9,8},{10,11... | collective-permute-start | bytes 786440 | tf_op jit(solution)/shard_map/ppermute | solution.py:279
  94.4 9.1 %collective-permute-start.19 = (bf16[2,128,512]{2,1,0:T(8,128)(2,1)S(1)}, bf16[2,128,512]{2,1,0:T(8,128)(2,1)S(1)}, u32[]{:S(2)}, u32[]{:S(2)}) collective-permute-start(bf16[2,128,512]{2,1,0:T(8,128)(2,1)S(1)} %get-tuple-element.86), channel_id=1, source_target_pairs={{0,1},{1,0},{2,3},{3,2},{4,5},{5,4},{6,7},{7,6},{8,9},{9,8},{10,11... | collective-permute-start | bytes 786440 | tf_op jit(solution)/shard_map/ppermute | solution.py:279

commit v10 on v9

--- a/solution.py
+++ b/solution.py
@@ -213,20 +213,21 @@
         spread_ref[...] = refs[-1][own ^ apart, :, here]
 
 
-def gradient_kernel(base, corner_ref, wave_ref, *refs):
-    *spread_refs, own_ref, away_ref = refs
-    rows = own_ref.shape[1]
-    window = wave_ref.shape[-1]
+def add_kernel(base, picks, begun, ends, corner_ref, wave_ref, *refs):
+    spread_refs, refs = refs[: len(picks)], refs[len(picks) :]
+    count, _, window, _ = wave_ref.shape
+    rows = window // chunk_count
     tall = 16
-    own = place_in_group(wave_ref.shape[0])
+    own = place_in_group(count)
 
     def one(block, _):
         at = pl.multiple_of(block * tall, tall)
-        sums = [jnp.zeros((tall, window), f32) for _ in range(8)]
+        rows_at = pl.ds(at, tall)
         here = pl.ds(base + at, tall)
-        for apart, spread_ref in zip(distances(len(spread_refs)), spread_refs):
-            position = position_at(own ^ apart, len(spread_refs))
-            there = pl.ds(at, tall) if apart >= len(spread_refs) - far else here
+        sums = [refs[0][i, rows_at, :] if begun else jnp.zeros((tall, window), f32) for i in range(8)]
+        for apart, spread_ref in zip(picks, spread_refs):
+            position = position_at(own ^ apart, count)
+            there = rows_at if apart >= count - far else here
             in_mine, in_left = first_masks(corner_ref, position, base + at, (tall, window))
             wave_re, wave_im = (wave_ref[position, part, here, :].astype(f32) for part in range(2))
             spread_re, spread_im = (spread_ref[part, there, :].astype(f32) for part in range(2))
@@ -240,24 +241,37 @@
                 sums[4 * part + 1] += own_part
                 sums[4 * part + 2] += jnp.where(in_left, parts[part], 0.0)
                 sums[4 * part + 3] += jnp.where(in_left, own_part, 0.0)
+        if not ends:
+            for i in range(8):
+                refs[-1][i, rows_at, :] = sums[i]
+            return 0
+        own_ref, away_ref = refs[-2:]
         left, right = pl.ds(0, window), pl.ds(window, window)
         for part in range(2):
             every, mine, at_left, mine_left = sums[4 * part : 4 * part + 4]
-            own_ref[part, pl.ds(at, tall), left] = mine_left
-            own_ref[part, pl.ds(at, tall), right] = mine - mine_left
-            away_ref[part, pl.ds(at, tall), left] = (at_left - mine_left).astype(bf16)
-            away_ref[part, pl.ds(at, tall), right] = ((every - mine) - (at_left - mine_left)).astype(bf16)
+            own_ref[part, rows_at, left] = mine_left
+            own_ref[part, rows_at, right] = mine - mine_left
+            away_ref[part, rows_at, left] = (at_left - mine_left).astype(bf16)
+            away_ref[part, rows_at, right] = ((every - mine) - (at_left - mine_left)).astype(bf16)
         return 0
 
     lax.fori_loop(0, rows // tall, one, 0)
 
 
-def finish_kernel(*refs):
-    out_ref = refs[-1]
-    rows = refs[0].shape[1]
-    for chunk in range(chunk_count):
-        own_ref, come_ref = refs[2 * chunk : 2 * chunk + 2]
-        out_ref[:, pl.ds(chunk * rows, rows), :] = own_ref[...] + come_ref[...].astype(f32)
+def finish(chunk, own, come, shape, before):
+    def kernel(own_ref, come_ref, *refs):
+        refs[-1][...] = own_ref[...] + come_ref[...].astype(f32)
+
+    vmem = pl.BlockSpec(memory_space=pltpu.VMEM)
+    return pl.pallas_call(
+        kernel,
+        grid=(1,),
+        in_specs=[vmem, vmem] + [pl.BlockSpec(memory_space=pl.ANY)] * len(before),
+        out_specs=pl.BlockSpec(own.shape, lambda _: (0, chunk, 0)),
+        out_shape=shape_of(shape, f32),
+        input_output_aliases={2: 0} if before else {},
+        compiler_params=pltpu.CompilerParams(vmem_limit_bytes=6 * 2**20),
+    )(own, come, *before)
 
 
 def shape_of(dims, dtype):
@@ -287,8 +301,13 @@
     def exchange_far(values):
         return [to_distance(value, count - far + i) for i, value in enumerate(values)]
 
-    mine = [coded(obj_amp[0, c * rows : (c + 1) * rows], obj_phase[0, c * rows : (c + 1) * rows]) for c in chunks]
-    other = [to_other_half(value) for value in mine]
+    mine, other = [], []
+    for c in chunks:
+        source = [array[0, c * rows : (c + 1) * rows] for array in (obj_amp, obj_phase)]
+        if c > 0:
+            source, mine[-1] = lax.optimization_barrier((source, mine[-1]))
+        mine.append(coded(*source))
+        other.append(to_other_half(mine[-1]))
     ready = call(ready_kernel, [shape_of(wave, bf16)] + [shape_of((window, window), bf16)] * 2, prefetch=1)
     start, down, across = ready(corners, exit_adjoint)
     other[0], start, down, across = lax.optimization_barrier((other[0], start, down, across))
@@ -331,14 +350,32 @@
     came_far = [exchange_far(distant[:far])]
     came = exchange(near)
     came_far += [exchange_far(distant[c * far : (c + 1) * far]) for c in chunks[1:]]
-    sums = []
+    order = distances(count)
+    early, late = order[: count // 2 - 1], order[count // 2 - 1 : count - far]
+    spread_at = dict(zip(order, came))
+
+    def add(c, picks, sums, ends):
+        spreads = [came_far[c][d - count + far] if d >= count - far else spread_at[d] for d in picks]
+        kernel = functools.partial(add_kernel, c * rows, picks, bool(sums), ends)
+        given = [shape_of(piece, f32), shape_of(piece, bf16)] if ends else shape_of((8, rows, window), f32)
+        return call(kernel, given, prefetch=1)(corners, waves, *spreads, *sums)
+
+    done = []
     for c in chunks:
-        gradient = call(
-            functools.partial(gradient_kernel, c * rows), [shape_of(piece, f32), shape_of(piece, bf16)], prefetch=1
-        )
-        keep, away = gradient(corners, waves, *came, *came_far[c])
-        sums += [keep, to_other_half(away)]
-    return call(finish_kernel, shape_of((2, half, width), f32))(*sums)[None]
+        if c == 0:
+            sums = add(c, early + order[-far:], [], False)
+            keep, away = add(c, late, [sums], True)
+        else:
+            sums = add(c, early, [], False)
+            sums, away = lax.optimization_barrier((sums, away))
+            sums = add(c, late, [sums], False)
+            done.append((keep, to_other_half(away)))
+            keep, away = add(c, order[-far:], [sums], True)
+    done.append((keep, to_other_half(away)))
+    result = []
+    for c in chunks:
+        result = [finish(c, *done[c], (2, half, width), result)]
+    return result[0][None]
 
 
 def solution(mesh):

time: 105 us -> 103 us (0.981)
  waiting for transfers between devices: 50.7 us -> 46.9 us
  Pallas kernels: 21.3 us -> 23.6 us
    ppermute x18, waiting for transfers between devices: 29 us -> 26.3 us  [to_distance(): return lax.ppermute(value, 'sec', [(s, s ^ d) for s in range(sections)])]
    pallas_call x0 -> x2, Pallas kernels: none -> 1.68 us  [finish(): pl.pallas_call(kernel, grid=(1,), in_specs=[vmem, vmem] + [pl.BlockSpec(m...]
    ppermute x4, waiting for transfers between devices: 13.5 us -> 12.5 us  [to_other_half(): return lax.ppermute(value, 'scan', [(0, 1), (1, 0)])]
    pallas_call x9 -> x11, Pallas kernels: 21.3 us -> 21.9 us  [run(): pl.pallas_call(kernel, grid_spec=pltpu.PrefetchScalarGridSpec(num_scalar_...]
  transfers between devices with their start and end apart: 23 -> 23, of which waited for: 16 -> 16; matrix products, arithmetic and copies ran while one was open for 0% -> 0% of each run, Pallas kernels for 9% -> 12%
where the time goes in v10:
time: 103 us
  waiting for transfers between devices  46.9 us (46%)
  starting transfers between devices  30.4 us (30%)
  Pallas kernels  23.6 us (23%)
  other arithmetic  2.09 us (2%)
    ppermute x18, waiting for transfers between devices, to_distance(): return lax.ppermute(value, 'sec', [(s, s ^ d) for s in range(sections)])  26.3 us
    ppermute x18, starting transfers between devices, to_distance(): return lax.ppermute(value, 'sec', [(s, s ^ d) for s in range(sections)])  22.2 us
    pallas_call x11, Pallas kernels, run(): pl.pallas_call(kernel, grid_spec=pltpu.PrefetchScalarGridSpec(num_scalar_...  21.9 us
    ppermute x4, waiting for transfers between devices, to_other_half(): return lax.ppermute(value, 'scan', [(0, 1), (1, 0)])  12.5 us
    ppermute x1, waiting for transfers between devices, on_device(): lax.ppermute(leave, 'sec', [(s, s - count ^ count // 2) for s in range(co...  8.16 us
    ppermute x4, starting transfers between devices, to_other_half(): return lax.ppermute(value, 'scan', [(0, 1), (1, 0)])  6.73 us
  transfers between devices with their start and end apart: 23, of which 16 were waited for; matrix products, arithmetic and copies ran while one was open for 0% of the time, Pallas kernels for 12%

profile of v10, /device:TPU:0, one launch (start us, length us, event | category | flops | bytes accessed | tf_op | source)
XLA Modules:
  0.0 103.2 jit_solution(6121399603492268191)
XLA Ops:
  0.0 1.7 %fusion.4 = (bf16[1,128,512]{2,1,0:T(8,128)(2,1)S(1)}, bf16[1,128,512]{2,1,0:T(8,128)(2,1)S(1)}, f32[128,512]{1,0:T(8,128)S(1)}, f32[128,512]{1,0:T(8,128)S(1)}) fusion(f32[1,256,512]{2,1,0:T(8,128)} %param.5, f32[1,256,512]{2,1,0:T(8,128)} %param.6), kind=kLoop, calls=%fused_computation.8 | loop fusion | flops 2424832 | bytes 1835008 | tf_op jit(solution)/shard_map/convert_element_type | solution.py:66
  1.7 3.0 %collective-permute-start = (bf16[2,128,512]{2,1,0:T(8,128)(2,1)S(1)}, bf16[2,128,512]{2,1,0:T(8,128)(2,1)S(1)}, u32[]{:S(2)}, u32[]{:S(2)}) collective-permute-start(bf16[2,128,512]{2,1,0:T(8,128)(2,1)S(1)} %pad_maximum_fusion.mine_ref), channel_id=1, source_target_pairs={{0,1},{1,0},{2,3},{3,2},{4,5},{5,4},{6,7},{7,6},{8,9},{9,8},{10,11... | collective-permute-start | bytes 786440 | tf_op jit(solution)/shard_map/ppermute | solution.py:293
  5.2 1.2 %shard_map.55 = (bf16[2,256,256]{2,1,0:T(8,128)(2,1)S(1)}, bf16[256,256]{1,0:T(8,128)(2,1)S(1)}, bf16[256,256]{1,0:T(8,128)(2,1)S(1)}) custom-call(s32[2,8]{1,0:T(2,128)S(1)} %bitcast.12, bf16[8,2,256,256]{3,2,1,0:T(8,128)(2,1)S(1)} %copy-done.1), custom_call_target="tpu_custom_call" | custom-call | bytes 2621504 | tf_op jit(solution)/shard_map/pallas_call | solution.py:27
  6.4 5.4 %collective-permute-done.other_ref = bf16[2,128,512]{2,1,0:T(8,128)(2,1)S(1)} collective-permute-done((bf16[2,128,512]{2,1,0:T(8,128)(2,1)S(1)}, bf16[2,128,512]{2,1,0:T(8,128)(2,1)S(1)}, u32[]{:S(2)}, u32[]{:S(2)}) %collective-permute-start) | collective-permute-done | bytes 262176 | tf_op jit(solution)/shard_map/ppermute | solution.py:293
  11.9 1.2 %shard_map.56 = (bf16[2,256,256]{2,1,0:T(8,128)(2,1)S(1)}, bf16[2,256,256]{2,1,0:T(8,128)(2,1)S(1)}, bf16[2,256,256]{2,1,0:T(8,128)(2,1)S(1)}, bf16[2,256,256]{2...) custom-call(s32[2,8]{1,0:T(2,128)S(1)} %bitcast.13, ...), custom_call_target="tpu_custom_call" | custom-call | bytes 2359360 | tf_op jit(solution)/shard_map/pallas_call | solution.py:27
  13.0 3.2 %collective-permute-start.2 = (bf16[2,128,256]{2,1,0:T(8,128)(2,1)S(1)}, bf16[2,128,256]{2,1,0:T(8,128)(2,1)S(1)}, u32[]{:S(2)}, u32[]{:S(2)}) collective-permute-start(bf16[2,128,256]{2,1,0:T(8,128)(2,1)S(1)} %get-tuple-element.63), channel_id=1, source_target_pairs={{0,12},{2,14},{4,8},{6,10},{8,4},{10,6},{12,0},{14,2},{16,28},{18,... | collective-permute-start | bytes 393224 | tf_op jit(solution)/shard_map/ppermute | solution.py:296
  16.7 2.9 %collective-permute-done.2.refs_6_ = bf16[2,128,256]{2,1,0:T(8,128)(2,1)S(1)} collective-permute-done((bf16[2,128,256]{2,1,0:T(8,128)(2,1)S(1)}, bf16[2,128,256]{2,1,0:T(8,128)(2,1)S(1)}, u32[]{:S(2)}, u32[]{:S(2)}) %collective-permute-start.2) | collective-permute-done | bytes 131104 | tf_op jit(solution)/shard_map/ppermute | solution.py:296
  19.6 1.2 %shard_map.57 = (bf16[2,256,256]{2,1,0:T(8,128)(2,1)S(1)}, bf16[2,256,256]{2,1,0:T(8,128)(2,1)S(1)}, bf16[2,256,256]{2,1,0:T(8,128)(2,1)S(1)}, bf16[2,256,256]{2...) custom-call(s32[2,8]{1,0:T(2,128)S(1)} %bitcast.14, ...), custom_call_target="tpu_custom_call", output_to_operand_aliasing={{0}: (3, {}), {1}: (4, {}), {2}: (5, {}), {3}: (6, {}), {4}... | custom-call | bytes 3932224 | tf_op jit(solution)/shard_map/pallas_call | solution.py:27
  20.8 3.4 %collective-permute-start.9 = (bf16[2,128,256]{2,1,0:T(8,128)(2,1)S(1)}, bf16[2,128,256]{2,1,0:T(8,128)(2,1)S(1)}, u32[]{:S(2)}, u32[]{:S(2)}) collective-permute-start(bf16[2,128,256]{2,1,0:T(8,128)(2,1)S(1)} %get-tuple-element.79), channel_id=1, source_target_pairs={{0,12},{2,14},{4,8},{6,10},{8,4},{10,6},{12,0},{14,2},{16,28},{18,... | collective-permute-start | bytes 393224 | tf_op jit(solution)/shard_map/ppermute | solution.py:296
  25.0 2.2 %collective-permute-start.5 = (bf16[2,256,256]{2,1,0:T(8,128)(2,1)S(1)}, bf16[2,256,256]{2,1,0:T(8,128)(2,1)S(1)}, u32[]{:S(2)}, u32[]{:S(2)}) collective-permute-start(bf16[2,256,256]{2,1,0:T(8,128)(2,1)S(1)} %get-tuple-element.74), channel_id=1, source_target_pairs={{0,6},{2,4},{4,2},{6,0},{8,14},{10,12},{12,10},{14,8},{16,22},{18,... | collective-permute-start | bytes 786440 | tf_op jit(solution)/shard_map/ppermute | solution.py:296
  28.1 2.8 %collective-permute-done.10.refs_9_ = bf16[2,128,256]{2,1,0:T(8,128)(2,1)S(1)} collective-permute-done((bf16[2,128,256]{2,1,0:T(8,128)(2,1)S(1)}, bf16[2,128,256]{2,1,0:T(8,128)(2,1)S(1)}, u32[]{:S(2)}, u32[]{:S(2)}) %collective-permute-start.10) | collective-permute-done | bytes 131104 | tf_op jit(solution)/shard_map/ppermute | solution.py:296
  30.8 4.9 %collective-permute-done.3.refs_1_ = bf16[2,256,256]{2,1,0:T(8,128)(2,1)S(1)} collective-permute-done((bf16[2,256,256]{2,1,0:T(8,128)(2,1)S(1)}, bf16[2,256,256]{2,1,0:T(8,128)(2,1)S(1)}, u32[]{:S(2)}, u32[]{:S(2)}) %collective-permute-start.3) | collective-permute-done | bytes 262176 | tf_op jit(solution)/shard_map/ppermute | solution.py:296
  36.1 5.1 %collective-permute-done.5.refs_3_ = bf16[2,256,256]{2,1,0:T(8,128)(2,1)S(1)} collective-permute-done((bf16[2,256,256]{2,1,0:T(8,128)(2,1)S(1)}, bf16[2,256,256]{2,1,0:T(8,128)(2,1)S(1)}, u32[]{:S(2)}, u32[]{:S(2)}) %collective-permute-start.5) | collective-permute-done | bytes 262176 | tf_op jit(solution)/shard_map/ppermute | solution.py:296
  41.2 5.2 %shard_map.58 = (bf16[2,256,256]{2,1,0:T(8,128)(2,1)S(1)}, bf16[8,2,256,256]{3,2,1,0:T(8,128)(2,1)S(1)}) custom-call(bf16[2,256,256]{2,1,0:T(8,128)(2,1)S(1)} %get-tuple-element.56.start_ref, bf16[256,256]{1,0:T(8,128)(2,1)S(1)} %get-tuple-element.57.down_ref, bf16[256,256]{1,0:T(8,128)(2,1)S(1)} %get-tuple-element.58.across_ref, ...), custom_call_target="tpu_custom_call" | custom-call | flops 2147483648 | bytes 4980736 | tf_op jit(solution)/shard_map/pallas_call | solution.py:27
  46.4 1.5 %collective-permute-start.11 = (bf16[2,256,256]{2,1,0:T(8,128)(2,1)S(1)}, bf16[2,256,256]{2,1,0:T(8,128)(2,1)S(1)}, u32[]{:S(2)}, u32[]{:S(2)}) collective-permute-start(bf16[2,256,256]{2,1,0:T(8,128)(2,1)S(1)} %get-tuple-element.81), channel_id=1, source_target_pairs={{16,8},{18,10},{20,12},{22,14},{24,0},{26,2},{28,4},{30,6},{17,9},... | collective-permute-start | bytes 786440 | tf_op jit(solution)/shard_map/ppermute | solution.py:335
  47.9 2.5 %shard_map.59.wave_ref = bf16[8,2,256,256]{3,2,1,0:T(8,128)(2,1)S(1)} custom-call(s32[2,8]{1,0:T(2,128)S(1)} %bitcast.15, bf16[8,2,256,256]{3,2,1,0:T(8,128)(2,1)S(1)} %bitcast.11), custom_call_target="tpu_custom_call" | custom-call | bytes 4194368 | tf_op jit(solution)/shard_map/pallas_call | solution.py:27
  50.4 8.2 %collective-permute-done.11.come_ref = bf16[2,256,256]{2,1,0:T(8,128)(2,1)S(1)} collective-permute-done((bf16[2,256,256]{2,1,0:T(8,128)(2,1)S(1)}, bf16[2,256,256]{2,1,0:T(8,128)(2,1)S(1)}, u32[]{:S(2)}, u32[]{:S(2)}) %collective-permute-start.11) | collective-permute-done | bytes 262176 | tf_op jit(solution)/shard_map/ppermute | solution.py:335
  58.5 5.2 %shard_map.60 = (bf16[2,256,256]{2,1,0:T(8,128)(2,1)S(1)}, bf16[2,256,256]{2,1,0:T(8,128)(2,1)S(1)}, bf16[2,256,256]{2,1,0:T(8,128)(2,1)S(1)}, bf16[2,256,256]{2...) custom-call(bf16[2,256,256]{2,1,0:T(8,128)(2,1)S(1)} %get-tuple-elem, ...), custom_call_target="tpu_custom_call" | custom-call | flops 2147483648 | bytes 4980736 | tf_op jit(solution)/shard_map/pallas_call | solution.py:27
  63.8 5.7 %collective-permute-start.19 = (bf16[2,128,256]{2,1,0:T(8,128)(2,1)S(1)}, bf16[2,128,256]{2,1,0:T(8,128)(2,1)S(1)}, u32[]{:S(2)}, u32[]{:S(2)}) collective-permute-start(bf16[2,128,256]{2,1,0:T(8,128)(2,1)S(1)} %get-tuple-element.93), channel_id=1, source_target_pairs={{0,12},{2,14},{4,8},{6,10},{8,4},{10,6},{12,0},{14,2},{16,28},{18,... | collective-permute-start | bytes 393224 | tf_op jit(solution)/shard_map/ppermute | solution.py:296
  69.5 1.2 %collective-permute-start.17 = (bf16[2,256,256]{2,1,0:T(8,128)(2,1)S(1)}, bf16[2,256,256]{2,1,0:T(8,128)(2,1)S(1)}, u32[]{:S(2)}, u32[]{:S(2)}) collective-permute-start(bf16[2,256,256]{2,1,0:T(8,128)(2,1)S(1)} %get-tuple-element.91), channel_id=1, source_target_pairs={{0,4},{2,6},{4,0},{6,2},{8,12},{10,14},{12,8},{14,10},{16,20},{18,... | collective-permute-start | bytes 786440 | tf_op jit(solution)/shard_map/ppermute | solution.py:296
  71.2 2.1 %collective-permute-start.14 = (bf16[2,256,256]{2,1,0:T(8,128)(2,1)S(1)}, bf16[2,256,256]{2,1,0:T(8,128)(2,1)S(1)}, u32[]{:S(2)}, u32[]{:S(2)}) collective-permute-start(bf16[2,256,256]{2,1,0:T(8,128)(2,1)S(1)} %get-tuple-element.87), channel_id=1, source_target_pairs={{0,6},{2,4},{4,2},{6,0},{8,14},{10,12},{12,10},{14,8},{16,22},{18,... | collective-permute-start | bytes 786440 | tf_op jit(solution)/shard_map/ppermute | solution.py:296
  73.3 2.7 %collective-permute-done.20.refs_4_ = bf16[2,128,256]{2,1,0:T(8,128)(2,1)S(1)} collective-permute-done((bf16[2,128,256]{2,1,0:T(8,128)(2,1)S(1)}, bf16[2,128,256]{2,1,0:T(8,128)(2,1)S(1)}, u32[]{:S(2)}, u32[]{:S(2)}) %collective-permute-start.20) | collective-permute-done | bytes 131104 | tf_op jit(solution)/shard_map/ppermute | solution.py:296
  76.5 4.4 %collective-permute-done.17.refs_1_ = bf16[2,256,256]{2,1,0:T(8,128)(2,1)S(1)} collective-permute-done((bf16[2,256,256]{2,1,0:T(8,128)(2,1)S(1)}, bf16[2,256,256]{2,1,0:T(8,128)(2,1)S(1)}, u32[]{:S(2)}, u32[]{:S(2)}) %collective-permute-start.17) | collective-permute-done | bytes 262176 | tf_op jit(solution)/shard_map/ppermute | solution.py:296
  80.9 2.3 %collective-permute-start.12 = (bf16[2,128,256]{2,1,0:T(8,128)(2,1)S(1)}, bf16[2,128,256]{2,1,0:T(8,128)(2,1)S(1)}, u32[]{:S(2)}, u32[]{:S(2)}) collective-permute-start(bf16[2,128,256]{2,1,0:T(8,128)(2,1)S(1)} %get-tuple-element.85), channel_id=1, source_target_pairs={{0,12},{2,14},{4,8},{6,10},{8,4},{10,6},{12,0},{14,2},{16,28},{18,... | collective-permute-start | bytes 393224 | tf_op jit(solution)/shard_map/ppermute | solution.py:296
  84.2 1.3 %shard_map.62.refs_3_ = f32[8,128,256]{2,1,0:T(8,128)S(1)} custom-call(s32[2,8]{1,0:T(2,128)S(1)} %bitcast.17, bf16[8,2,256,256]{3,2,1,0:T(8,128)(2,1)S(1)} %shard_map.59.wave_ref, bf16[2,256,256]{2,1,0:T(8,128)(2,1)S(1)} %get-tuple-element.90.refs_0_, bf16[2,256,256]{2,1,0:T(8,128)(2,1)S(1)} %collective-permute-done.17.refs_1_, ...), custom_call_target="tpu_custom_call" | custom-call | bytes 4194368 | tf_op jit(solution)/shard_map/pallas_call | solution.py:27
  85.5 1.5 %collective-permute-done.14.refs_0_ = bf16[2,256,256]{2,1,0:T(8,128)(2,1)S(1)} collective-permute-done((bf16[2,256,256]{2,1,0:T(8,128)(2,1)S(1)}, bf16[2,256,256]{2,1,0:T(8,128)(2,1)S(1)}, u32[]{:S(2)}, u32[]{:S(2)}) %collective-permute-start.14) | collective-permute-done | bytes 262176 | tf_op jit(solution)/shard_map/ppermute | solution.py:296
  87.1 1.1 %shard_map.63 = (f32[2,128,512]{2,1,0:T(8,128)S(1)}, bf16[2,128,512]{2,1,0:T(8,128)(2,1)S(1)}) custom-call(s32[2,8]{1,0:T(2,128)S(1)} %bitcast.18, bf16[8,2,256,256]{3,2,1,0:T(8,128)(2,1)S(1)} %shard_map.59.wave_ref, bf16[2,256,256]{2,1,0:T(8,128)(2,1)S(1)} %collective-permute-done.14.refs_0_, bf16[2,256,256]{2,1,0:T(8,128)(2,1)S(1)} %collective-permute-done.15.refs_1_, ...), custom_call_target="tpu_custom_call" | custom-call | bytes 4718656 | tf_op jit(solution)/shard_map/pallas_call | solution.py:27
  88.2 1.8 %collective-permute-start.22 = (bf16[2,128,512]{2,1,0:T(8,128)(2,1)S(1)}, bf16[2,128,512]{2,1,0:T(8,128)(2,1)S(1)}, u32[]{:S(2)}, u32[]{:S(2)}) collective-permute-start(bf16[2,128,512]{2,1,0:T(8,128)(2,1)S(1)} %get-tuple-element.100), channel_id=1, source_target_pairs={{0,1},{1,0},{2,3},{3,2},{4,5},{5,4},{6,7},{7,6},{8,9},{9,8},{10,11... | collective-permute-start | bytes 786440 | tf_op jit(solution)/shard_map/ppermute | solution.py:293
  91.1 1.1 %collective-permute-done.13.refs_1_ = bf16[2,128,256]{2,1,0:T(8,128)(2,1)S(1)} collective-permute-done((bf16[2,128,256]{2,1,0:T(8,128)(2,1)S(1)}, bf16[2,128,256]{2,1,0:T(8,128)(2,1)S(1)}, u32[]{:S(2)}, u32[]{:S(2)}) %collective-permute-start.13) | collective-permute-done | bytes 131104 | tf_op jit(solution)/shard_map/ppermute | solution.py:296
  93.1 1.9 %collective-permute-start.21 = (bf16[2,128,512]{2,1,0:T(8,128)(2,1)S(1)}, bf16[2,128,512]{2,1,0:T(8,128)(2,1)S(1)}, u32[]{:S(2)}, u32[]{:S(2)}) collective-permute-start(bf16[2,128,512]{2,1,0:T(8,128)(2,1)S(1)} %get-tuple-element.98), channel_id=1, source_target_pairs={{0,1},{1,0},{2,3},{3,2},{4,5},{5,4},{6,7},{7,6},{8,9},{9,8},{10,11... | collective-permute-start | bytes 786440 | tf_op jit(solution)/shard_map/ppermute | solution.py:293
  95.0 2.4 %collective-permute-done.22.come_ref = bf16[2,128,512]{2,1,0:T(8,128)(2,1)S(1)} collective-permute-done((bf16[2,128,512]{2,1,0:T(8,128)(2,1)S(1)}, bf16[2,128,512]{2,1,0:T(8,128)(2,1)S(1)}, u32[]{:S(2)}, u32[]{:S(2)}) %collective-permute-start.22) | collective-permute-done | bytes 262176 | tf_op jit(solution)/shard_map/ppermute | solution.py:293
  98.2 4.1 %collective-permute-done.21.come_ref = bf16[2,128,512]{2,1,0:T(8,128)(2,1)S(1)} collective-permute-done((bf16[2,128,512]{2,1,0:T(8,128)(2,1)S(1)}, bf16[2,128,512]{2,1,0:T(8,128)(2,1)S(1)}, u32[]{:S(2)}, u32[]{:S(2)}) %collective-permute-start.21) | collective-permute-done | bytes 262176 | tf_op jit(solution)/shard_map/ppermute | solution.py:293
  (37 shorter events, 8.7 us)
Async XLA Ops:
  0.0 5.2 %copy-start.2 = (s32[8,2]{0,1:T(2,128)S(1)}, s32[8,2]{0,1:T(2,128)}, u32[]{:S(2)}) copy-start(s32[8,2]{0,1:T(2,128)} %param.9) | copy-start | bytes 196
  0.0 5.2 %copy-start.1 = (bf16[8,2,256,256]{3,2,1,0:T(8,128)(2,1)S(1)}, bf16[8,2,256,256]{3,2,1,0:T(8,128)(2,1)}, u32[]{:S(2)}) copy-start(bf16[8,2,256,256]{3,2,1,0:T(8,128)(2,1)} %exit_ref.1) | copy-start | bytes 6291460
  1.7 10.1 %collective-permute-start = (bf16[2,128,512]{2,1,0:T(8,128)(2,1)S(1)}, bf16[2,128,512]{2,1,0:T(8,128)(2,1)S(1)}, u32[]{:S(2)}, u32[]{:S(2)}) collective-permute-start(bf16[2,128,512]{2,1,0:T(8,128)(2,1)S(1)} %pad_maximum_fusion.mine_ref), channel_id=1, source_target_pairs={{0,1},{1,0},{2,3},{3,2},{4,5},{5,4},{6,7},{7,6},{8,9},{9,8},{10,11... | collective-permute-start | bytes 786440 | tf_op jit(solution)/shard_map/ppermute | solution.py:293
  5.1 11.5 %collective-permute-start.1 = (bf16[2,128,512]{2,1,0:T(8,128)(2,1)S(1)}, bf16[2,128,512]{2,1,0:T(8,128)(2,1)S(1)}, u32[]{:S(2)}, u32[]{:S(2)}) collective-permute-start(bf16[2,128,512]{2,1,0:T(8,128)(2,1)S(1)} %pad_maximum_fusion.1.mine_ref), channel_id=1, source_target_pairs={{0,1},{1,0},{2,3},{3,2},{4,5},{5,4},{6,7},{7,6},{8,9},{9,8},{10,11... | collective-permute-start | bytes 786440 | tf_op jit(solution)/shard_map/ppermute | solution.py:293
  13.0 6.6 %collective-permute-start.2 = (bf16[2,128,256]{2,1,0:T(8,128)(2,1)S(1)}, bf16[2,128,256]{2,1,0:T(8,128)(2,1)S(1)}, u32[]{:S(2)}, u32[]{:S(2)}) collective-permute-start(bf16[2,128,256]{2,1,0:T(8,128)(2,1)S(1)} %get-tuple-element.63), channel_id=1, source_target_pairs={{0,12},{2,14},{4,8},{6,10},{8,4},{10,6},{12,0},{14,2},{16,28},{18,... | collective-permute-start | bytes 393224 | tf_op jit(solution)/shard_map/ppermute | solution.py:296
  16.2 8.8 %collective-permute-start.8 = (bf16[2,128,256]{2,1,0:T(8,128)(2,1)S(1)}, bf16[2,128,256]{2,1,0:T(8,128)(2,1)S(1)}, u32[]{:S(2)}, u32[]{:S(2)}) collective-permute-start(bf16[2,128,256]{2,1,0:T(8,128)(2,1)S(1)} %get-tuple-element.78), channel_id=1, source_target_pairs={{0,14},{2,12},{4,10},{6,8},{8,6},{10,4},{12,2},{14,0},{16,30},{18,... | collective-permute-start | bytes 393224 | tf_op jit(solution)/shard_map/ppermute | solution.py:296
  20.8 6.9 %collective-permute-start.9 = (bf16[2,128,256]{2,1,0:T(8,128)(2,1)S(1)}, bf16[2,128,256]{2,1,0:T(8,128)(2,1)S(1)}, u32[]{:S(2)}, u32[]{:S(2)}) collective-permute-start(bf16[2,128,256]{2,1,0:T(8,128)(2,1)S(1)} %get-tuple-element.79), channel_id=1, source_target_pairs={{0,12},{2,14},{4,8},{6,10},{8,4},{10,6},{12,0},{14,2},{16,28},{18,... | collective-permute-start | bytes 393224 | tf_op jit(solution)/shard_map/ppermute | solution.py:296
  24.3 6.6 %collective-permute-start.10 = (bf16[2,128,256]{2,1,0:T(8,128)(2,1)S(1)}, bf16[2,128,256]{2,1,0:T(8,128)(2,1)S(1)}, u32[]{:S(2)}, u32[]{:S(2)}) collective-permute-start(bf16[2,128,256]{2,1,0:T(8,128)(2,1)S(1)} %get-tuple-element.80), channel_id=1, source_target_pairs={{0,14},{2,12},{4,10},{6,8},{8,6},{10,4},{12,2},{14,0},{16,30},{18,... | collective-permute-start | bytes 393224 | tf_op jit(solution)/shard_map/ppermute | solution.py:296
  24.3 11.4 %collective-permute-start.3 = (bf16[2,256,256]{2,1,0:T(8,128)(2,1)S(1)}, bf16[2,256,256]{2,1,0:T(8,128)(2,1)S(1)}, u32[]{:S(2)}, u32[]{:S(2)}) collective-permute-start(bf16[2,256,256]{2,1,0:T(8,128)(2,1)S(1)} %get-tuple-element.72), channel_id=1, source_target_pairs={{0,4},{2,6},{4,0},{6,2},{8,12},{10,14},{12,8},{14,10},{16,20},{18,... | collective-permute-start | bytes 786440 | tf_op jit(solution)/shard_map/ppermute | solution.py:296
  24.5 11.6 %collective-permute-start.4 = (bf16[2,256,256]{2,1,0:T(8,128)(2,1)S(1)}, bf16[2,256,256]{2,1,0:T(8,128)(2,1)S(1)}, u32[]{:S(2)}, u32[]{:S(2)}) collective-permute-start(bf16[2,256,256]{2,1,0:T(8,128)(2,1)S(1)} %get-tuple-element.73), channel_id=1, source_target_pairs={{0,8},{2,10},{4,12},{6,14},{8,0},{10,2},{12,4},{14,6},{16,24},{18,... | collective-permute-start | bytes 786440 | tf_op jit(solution)/shard_map/ppermute | solution.py:296
  25.0 16.2 %collective-permute-start.5 = (bf16[2,256,256]{2,1,0:T(8,128)(2,1)S(1)}, bf16[2,256,256]{2,1,0:T(8,128)(2,1)S(1)}, u32[]{:S(2)}, u32[]{:S(2)}) collective-permute-start(bf16[2,256,256]{2,1,0:T(8,128)(2,1)S(1)} %get-tuple-element.74), channel_id=1, source_target_pairs={{0,6},{2,4},{4,2},{6,0},{8,14},{10,12},{12,10},{14,8},{16,22},{18,... | collective-permute-start | bytes 786440 | tf_op jit(solution)/shard_map/ppermute | solution.py:296
  27.7 13.5 %collective-permute-start.6 = (bf16[2,256,256]{2,1,0:T(8,128)(2,1)S(1)}, bf16[2,256,256]{2,1,0:T(8,128)(2,1)S(1)}, u32[]{:S(2)}, u32[]{:S(2)}) collective-permute-start(bf16[2,256,256]{2,1,0:T(8,128)(2,1)S(1)} %get-tuple-element.75), channel_id=1, source_target_pairs={{0,10},{2,8},{4,14},{6,12},{8,2},{10,0},{12,6},{14,4},{16,26},{18,... | collective-permute-start | bytes 786440 | tf_op jit(solution)/shard_map/ppermute | solution.py:296
  30.8 10.4 %collective-permute-start.7 = (bf16[2,256,256]{2,1,0:T(8,128)(2,1)S(1)}, bf16[2,256,256]{2,1,0:T(8,128)(2,1)S(1)}, u32[]{:S(2)}, u32[]{:S(2)}) collective-permute-start(bf16[2,256,256]{2,1,0:T(8,128)(2,1)S(1)} %get-tuple-element.76), channel_id=1, source_target_pairs={{0,2},{2,0},{4,6},{6,4},{8,10},{10,8},{12,14},{14,12},{16,18},{18,... | collective-permute-start | bytes 786440 | tf_op jit(solution)/shard_map/ppermute | solution.py:296
  41.2 6.7 %copy-start = (bf16[1,8,2,256,256]{4,3,2,1,0:T(8,128)(2,1)S(1)}, bf16[1,8,2,256,256]{4,3,2,1,0:T(8,128)(2,1)}, u32[]{:S(2)}) copy-start(bf16[1,8,2,256,256]{4,3,2,1,0:T(8,128)(2,1)} %param.7) | copy-start | bytes 6291460
  46.4 12.1 %collective-permute-start.11 = (bf16[2,256,256]{2,1,0:T(8,128)(2,1)S(1)}, bf16[2,256,256]{2,1,0:T(8,128)(2,1)S(1)}, u32[]{:S(2)}, u32[]{:S(2)}) collective-permute-start(bf16[2,256,256]{2,1,0:T(8,128)(2,1)S(1)} %get-tuple-element.81), channel_id=1, source_target_pairs={{16,8},{18,10},{20,12},{22,14},{24,0},{26,2},{28,4},{30,6},{17,9},... | collective-permute-start | bytes 786440 | tf_op jit(solution)/shard_map/ppermute | solution.py:335
  63.8 9.5 %collective-permute-start.19 = (bf16[2,128,256]{2,1,0:T(8,128)(2,1)S(1)}, bf16[2,128,256]{2,1,0:T(8,128)(2,1)S(1)}, u32[]{:S(2)}, u32[]{:S(2)}) collective-permute-start(bf16[2,128,256]{2,1,0:T(8,128)(2,1)S(1)} %get-tuple-element.93), channel_id=1, source_target_pairs={{0,12},{2,14},{4,8},{6,10},{8,4},{10,6},{12,0},{14,2},{16,28},{18,... | collective-permute-start | bytes 393224 | tf_op jit(solution)/shard_map/ppermute | solution.py:296
  69.5 6.6 %collective-permute-start.20 = (bf16[2,128,256]{2,1,0:T(8,128)(2,1)S(1)}, bf16[2,128,256]{2,1,0:T(8,128)(2,1)S(1)}, u32[]{:S(2)}, u32[]{:S(2)}) collective-permute-start(bf16[2,128,256]{2,1,0:T(8,128)(2,1)S(1)} %get-tuple-element.94), channel_id=1, source_target_pairs={{0,14},{2,12},{4,10},{6,8},{8,6},{10,4},{12,2},{14,0},{16,30},{18,... | collective-permute-start | bytes 393224 | tf_op jit(solution)/shard_map/ppermute | solution.py:296
  69.5 11.4 %collective-permute-start.17 = (bf16[2,256,256]{2,1,0:T(8,128)(2,1)S(1)}, bf16[2,256,256]{2,1,0:T(8,128)(2,1)S(1)}, u32[]{:S(2)}, u32[]{:S(2)}) collective-permute-start(bf16[2,256,256]{2,1,0:T(8,128)(2,1)S(1)} %get-tuple-element.91), channel_id=1, source_target_pairs={{0,4},{2,6},{4,0},{6,2},{8,12},{10,14},{12,8},{14,10},{16,20},{18,... | collective-permute-start | bytes 786440 | tf_op jit(solution)/shard_map/ppermute | solution.py:296
  70.7 12.5 %collective-permute-start.18 = (bf16[2,256,256]{2,1,0:T(8,128)(2,1)S(1)}, bf16[2,256,256]{2,1,0:T(8,128)(2,1)S(1)}, u32[]{:S(2)}, u32[]{:S(2)}) collective-permute-start(bf16[2,256,256]{2,1,0:T(8,128)(2,1)S(1)} %get-tuple-element.92), channel_id=1, source_target_pairs={{0,8},{2,10},{4,12},{6,14},{8,0},{10,2},{12,4},{14,6},{16,24},{18,... | collective-permute-start | bytes 786440 | tf_op jit(solution)/shard_map/ppermute | solution.py:296
  71.2 15.9 %collective-permute-start.14 = (bf16[2,256,256]{2,1,0:T(8,128)(2,1)S(1)}, bf16[2,256,256]{2,1,0:T(8,128)(2,1)S(1)}, u32[]{:S(2)}, u32[]{:S(2)}) collective-permute-start(bf16[2,256,256]{2,1,0:T(8,128)(2,1)S(1)} %get-tuple-element.87), channel_id=1, source_target_pairs={{0,6},{2,4},{4,2},{6,0},{8,14},{10,12},{12,10},{14,8},{16,22},{18,... | collective-permute-start | bytes 786440 | tf_op jit(solution)/shard_map/ppermute | solution.py:296
  73.3 13.8 %collective-permute-start.15 = (bf16[2,256,256]{2,1,0:T(8,128)(2,1)S(1)}, bf16[2,256,256]{2,1,0:T(8,128)(2,1)S(1)}, u32[]{:S(2)}, u32[]{:S(2)}) collective-permute-start(bf16[2,256,256]{2,1,0:T(8,128)(2,1)S(1)} %get-tuple-element.88), channel_id=1, source_target_pairs={{0,10},{2,8},{4,14},{6,12},{8,2},{10,0},{12,6},{14,4},{16,26},{18,... | collective-permute-start | bytes 786440 | tf_op jit(solution)/shard_map/ppermute | solution.py:296
  76.0 11.1 %collective-permute-start.16 = (bf16[2,256,256]{2,1,0:T(8,128)(2,1)S(1)}, bf16[2,256,256]{2,1,0:T(8,128)(2,1)S(1)}, u32[]{:S(2)}, u32[]{:S(2)}) collective-permute-start(bf16[2,256,256]{2,1,0:T(8,128)(2,1)S(1)} %get-tuple-element.89), channel_id=1, source_target_pairs={{0,2},{2,0},{4,6},{6,4},{8,10},{10,8},{12,14},{14,12},{16,18},{18,... | collective-permute-start | bytes 786440 | tf_op jit(solution)/shard_map/ppermute | solution.py:296
  80.9 10.1 %collective-permute-start.12 = (bf16[2,128,256]{2,1,0:T(8,128)(2,1)S(1)}, bf16[2,128,256]{2,1,0:T(8,128)(2,1)S(1)}, u32[]{:S(2)}, u32[]{:S(2)}) collective-permute-start(bf16[2,128,256]{2,1,0:T(8,128)(2,1)S(1)} %get-tuple-element.85), channel_id=1, source_target_pairs={{0,12},{2,14},{4,8},{6,10},{8,4},{10,6},{12,0},{14,2},{16,28},{18,... | collective-permute-start | bytes 393224 | tf_op jit(solution)/shard_map/ppermute | solution.py:296
  83.2 8.9 %collective-permute-start.13 = (bf16[2,128,256]{2,1,0:T(8,128)(2,1)S(1)}, bf16[2,128,256]{2,1,0:T(8,128)(2,1)S(1)}, u32[]{:S(2)}, u32[]{:S(2)}) collective-permute-start(bf16[2,128,256]{2,1,0:T(8,128)(2,1)S(1)} %get-tuple-element.86), channel_id=1, source_target_pairs={{0,14},{2,12},{4,10},{6,8},{8,6},{10,4},{12,2},{14,0},{16,30},{18,... | collective-permute-start | bytes 393224 | tf_op jit(solution)/shard_map/ppermute | solution.py:296
  88.2 9.2 %collective-permute-start.22 = (bf16[2,128,512]{2,1,0:T(8,128)(2,1)S(1)}, bf16[2,128,512]{2,1,0:T(8,128)(2,1)S(1)}, u32[]{:S(2)}, u32[]{:S(2)}) collective-permute-start(bf16[2,128,512]{2,1,0:T(8,128)(2,1)S(1)} %get-tuple-element.100), channel_id=1, source_target_pairs={{0,1},{1,0},{2,3},{3,2},{4,5},{5,4},{6,7},{7,6},{8,9},{9,8},{10,11... | collective-permute-start | bytes 786440 | tf_op jit(solution)/shard_map/ppermute | solution.py:293
  93.1 9.2 %collective-permute-start.21 = (bf16[2,128,512]{2,1,0:T(8,128)(2,1)S(1)}, bf16[2,128,512]{2,1,0:T(8,128)(2,1)S(1)}, u32[]{:S(2)}, u32[]{:S(2)}) collective-permute-start(bf16[2,128,512]{2,1,0:T(8,128)(2,1)S(1)} %get-tuple-element.98), channel_id=1, source_target_pairs={{0,1},{1,0},{2,3},{3,2},{4,5},{5,4},{6,7},{7,6},{8,9},{9,8},{10,11... | collective-permute-start | bytes 786440 | tf_op jit(solution)/shard_map/ppermute | solution.py:293

commit v11 on v10

--- a/solution.py
+++ b/solution.py
@@ -78,21 +78,36 @@
     return sorted(range(count), key=lambda d: (d >= count - far, d > 0, d == 1, d % 2, d))
 
 
+def select_window(corner_ref, position, base, mine_ref, other_ref):
+    _, rows, width = mine_ref.shape
+    window = width // 2
+    in_mine, in_left = first_masks(corner_ref, position, base, (rows, window))
+    for part in range(2):
+        left, right = (
+            jnp.where(in_mine, mine_ref[part, :, cols].astype(f32), other_ref[part, :, cols].astype(f32))
+            for cols in (slice(0, window), slice(window, 2 * window))
+        )
+        yield jnp.where(in_left, left, right).astype(bf16)
+
+
 def cut_kernel(base, count, corner_ref, mine_ref, other_ref, *refs):
     own = place_in_group(count)
-    _, rows, width = mine_ref.shape
-    window = width // 2
-    for i, (apart, win_ref) in enumerate(zip(distances(count), refs[-count:])):
-        here = pl.ds(0 if i >= count - far else base, rows)
-        if base and i < count - far:
+    here = pl.ds(base, mine_ref.shape[1])
+    near = distances(count)[:-far]
+    for i, (apart, win_ref) in enumerate(zip(near, refs[-len(near) :])):
+        if base:
             win_ref[:, :base] = refs[i][:, :base]
-        in_mine, in_left = first_masks(corner_ref, position_at(own ^ apart, count), base, (rows, window))
-        for part in range(2):
-            left, right = (
-                jnp.where(in_mine, mine_ref[part, :, cols].astype(f32), other_ref[part, :, cols].astype(f32))
-                for cols in (slice(0, window), slice(window, 2 * window))
-            )
-            win_ref[part, here, :] = jnp.where(in_left, left, right).astype(bf16)
+        position = position_at(own ^ apart, count)
+        for part, value in enumerate(select_window(corner_ref, position, base, mine_ref, other_ref)):
+            win_ref[part, here, :] = value
+
+
+def cut_far_kernel(base, count, corner_ref, mine_ref, other_ref, *win_refs):
+    own = place_in_group(count)
+    for apart, win_ref in enumerate(win_refs):
+        position = position_at(own ^ apart, count)
+        for part, value in enumerate(select_window(corner_ref, position, base, mine_ref, other_ref)):
+            win_ref[part] = value
 
 
 def turned(wave, row_at, col_at):
@@ -301,13 +316,14 @@
     def exchange_far(values):
         return [to_distance(value, count - far + i) for i, value in enumerate(values)]
 
-    mine, other = [], []
+    mine, other, far_mine = [], [], []
+    source = (obj_amp, obj_phase)
     for c in chunks:
-        source = [array[0, c * rows : (c + 1) * rows] for array in (obj_amp, obj_phase)]
         if c > 0:
             source, mine[-1] = lax.optimization_barrier((source, mine[-1]))
-        mine.append(coded(*source))
+        mine.append(coded(*(array[0, c * rows : (c + 1) * rows] for array in source)))
         other.append(to_other_half(mine[-1]))
+        far_mine.append(to_distance(mine[-1], count - far))
     ready = call(ready_kernel, [shape_of(wave, bf16)] + [shape_of((window, window), bf16)] * 2, prefetch=1)
     start, down, across = ready(corners, exit_adjoint)
     other[0], start, down, across = lax.optimization_barrier((other[0], start, down, across))
@@ -315,15 +331,18 @@
     for c in chunks:
         cut = call(
             functools.partial(cut_kernel, c * rows, count),
-            [shape_of(wave, bf16)] * (count - far) + [shape_of((2, rows, window), bf16)] * far,
+            [shape_of(wave, bf16)] * (count - far),
             prefetch=1,
             aliases={3 + i: i for i in range(len(near))},
         )
-        if distant:
-            other[c], distant[-far] = lax.optimization_barrier((other[c], distant[-far]))
-        cuts = cut(corners, mine[c], other[c], *near)
-        near = cuts[: count - far]
-        distant += exchange_far(cuts[count - far :])
+        near = cut(corners, mine[c], other[c], *near)
+    far_mine[-1], near = lax.optimization_barrier((far_mine[-1], near))
+    for c in chunks:
+        cut_far = call(
+            functools.partial(cut_far_kernel, c * rows, count), [shape_of((2, rows, window), bf16)] * far, prefetch=1
+        )
+        kept, given = cut_far(corners, far_mine[c], to_other_half(far_mine[c]))
+        distant += [kept, to_distance(given, 1)]
     windows = exchange(near) + distant
     waves = call(turn_kernel, shape_of(forward_waves.shape[1:], bf16), prefetch=1)(corners, forward_waves[0])
 

time: 103 us -> 97.2 us (0.944)
  waiting for transfers between devices: 46.9 us -> 42.7 us
  starting transfers between devices: 30.4 us -> 26.4 us
  Pallas kernels: 23.6 us -> 24.8 us
    ppermute x18, waiting for transfers between devices: 26.3 us -> 14.3 us  [to_distance(): return lax.ppermute(value, 'sec', [(s, s ^ d) for s in range(sections)])]
    ppermute x4 -> x6, waiting for transfers between devices: 12.5 us -> 19.7 us  [to_other_half(): return lax.ppermute(value, 'scan', [(0, 1), (1, 0)])]
    ppermute x18, starting transfers between devices: 22.2 us -> 18.4 us  [to_distance(): return lax.ppermute(value, 'sec', [(s, s ^ d) for s in range(sections)])]
    convert_element_type x1 -> x2, other arithmetic: 1.69 us -> 2.91 us  [coded(): jnp.exp(code_gain * trans_re).astype(bf16)]
    pallas_call x11 -> x13, Pallas kernels: 21.9 us -> 23.1 us  [run(): pl.pallas_call(kernel, grid_spec=pltpu.PrefetchScalarGridSpec(num_scalar_...]
    ppermute x4 -> x6, starting transfers between devices: 6.73 us -> 6.57 us  [to_other_half(): return lax.ppermute(value, 'scan', [(0, 1), (1, 0)])]
  transfers between devices with their start and end apart: 23 -> 25, of which waited for: 16 -> 16; matrix products, arithmetic and copies ran while one was open for 0% -> 1% of each run, Pallas kernels for 12% -> 14%
where the time goes in v11:
time: 97.2 us; the launch traced here: 97 us
  waiting for transfers between devices  42.7 us (44%)
  starting transfers between devices  26.4 us (27%)
  Pallas kernels  24.8 us (26%)
  other arithmetic  2.96 us (3%)
    pallas_call x13, Pallas kernels, run(): pl.pallas_call(kernel, grid_spec=pltpu.PrefetchScalarGridSpec(num_scalar_...  23.1 us
    ppermute x6, waiting for transfers between devices, to_other_half(): return lax.ppermute(value, 'scan', [(0, 1), (1, 0)])  19.7 us
    ppermute x18, starting transfers between devices, to_distance(): return lax.ppermute(value, 'sec', [(s, s ^ d) for s in range(sections)])  18.4 us
    ppermute x18, waiting for transfers between devices, to_distance(): return lax.ppermute(value, 'sec', [(s, s ^ d) for s in range(sections)])  14.3 us
    ppermute x1, waiting for transfers between devices, on_device(): lax.ppermute(leave, 'sec', [(s, s - count ^ count // 2) for s in range(co...  8.72 us
    ppermute x6, starting transfers between devices, to_other_half(): return lax.ppermute(value, 'scan', [(0, 1), (1, 0)])  6.57 us
    convert_element_type x2, other arithmetic, coded(): jnp.exp(code_gain * trans_re).astype(bf16)  2.91 us
  transfers between devices with their start and end apart: 25, of which 16 were waited for; matrix products, arithmetic and copies ran while one was open for 1% of the time, Pallas kernels for 14%

profile of v11, /device:TPU:0, one launch (start us, length us, event | category | flops | bytes accessed | tf_op | source)
XLA Modules:
  0.0 97.0 jit_solution(7053094307626701105)
XLA Ops:
  0.0 1.5 %fusion.4 = (bf16[1,128,512]{2,1,0:T(8,128)(2,1)S(1)}, bf16[1,128,512]{2,1,0:T(8,128)(2,1)S(1)}) fusion(f32[1,256,512]{2,1,0:T(8,128)} %param.5, f32[1,256,512]{2,1,0:T(8,128)} %param.6), kind=kLoop, calls=%fused_computation.8 | loop fusion | flops 2424832 | bytes 786432 | tf_op jit(solution)/shard_map/convert_element_type | solution.py:66
  1.6 4.0 %collective-permute-start.8 = (bf16[2,128,512]{2,1,0:T(8,128)(2,1)S(1)}, bf16[2,128,512]{2,1,0:T(8,128)(2,1)S(1)}, u32[]{:S(2)}, u32[]{:S(2)}) collective-permute-start(bf16[2,128,512]{2,1,0:T(8,128)(2,1)S(1)} %pad_maximum_fusion.mine_ref), channel_id=1, source_target_pairs={{0,12},{2,14},{4,8},{6,10},{8,4},{10,6},{12,0},{14,2},{16,28},{18,... | collective-permute-start | bytes 786440 | tf_op jit(solution)/shard_map/ppermute | solution.py:311
  5.6 1.5 %collective-permute-start = (bf16[2,128,512]{2,1,0:T(8,128)(2,1)S(1)}, bf16[2,128,512]{2,1,0:T(8,128)(2,1)S(1)}, u32[]{:S(2)}, u32[]{:S(2)}) collective-permute-start(bf16[2,128,512]{2,1,0:T(8,128)(2,1)S(1)} %pad_maximum_fusion.mine_ref), channel_id=1, source_target_pairs={{0,1},{1,0},{2,3},{3,2},{4,5},{5,4},{6,7},{7,6},{8,9},{9,8},{10,11... | collective-permute-start | bytes 786440 | tf_op jit(solution)/shard_map/ppermute | solution.py:308
  7.1 1.4 %fusion.13 = (bf16[1,128,512]{2,1,0:T(8,128)(2,1)S(1)}, bf16[1,128,512]{2,1,0:T(8,128)(2,1)S(1)}) fusion(f32[1,256,512]{2,1,0:T(8,128)} %param.5, f32[1,256,512]{2,1,0:T(8,128)} %param.6), kind=kLoop, calls=%fused_computation.17 | loop fusion | flops 2424832 | bytes 786432 | tf_op jit(solution)/shard_map/convert_element_type | solution.py:66
  9.2 1.2 %shard_map.55 = (bf16[2,256,256]{2,1,0:T(8,128)(2,1)S(1)}, bf16[256,256]{1,0:T(8,128)(2,1)S(1)}, bf16[256,256]{1,0:T(8,128)(2,1)S(1)}) custom-call(s32[2,8]{1,0:T(2,128)S(1)} %bitcast.4, bf16[8,2,256,256]{3,2,1,0:T(8,128)(2,1)S(1)} %copy-done.1), custom_call_target="tpu_custom_call" | custom-call | bytes 2621504 | tf_op jit(solution)/shard_map/pallas_call | solution.py:27
  10.4 4.4 %collective-permute-done.other_ref = bf16[2,128,512]{2,1,0:T(8,128)(2,1)S(1)} collective-permute-done((bf16[2,128,512]{2,1,0:T(8,128)(2,1)S(1)}, bf16[2,128,512]{2,1,0:T(8,128)(2,1)S(1)}, u32[]{:S(2)}, u32[]{:S(2)}) %collective-permute-start) | collective-permute-done | bytes 262176 | tf_op jit(solution)/shard_map/ppermute | solution.py:308
  14.8 1.0 %shard_map.56 = (bf16[2,256,256]{2,1,0:T(8,128)(2,1)S(1)}, bf16[2,256,256]{2,1,0:T(8,128)(2,1)S(1)}, bf16[2,256,256]{2,1,0:T(8,128)(2,1)S(1)}, bf16[2,256,256]{2...) custom-call(s32[2,8]{1,0:T(2,128)S(1)} %bitcast.5, ...), custom_call_target="tpu_custom_call" | custom-call | bytes 2097216 | tf_op jit(solution)/shard_map/pallas_call | solution.py:27
  15.9 1.6 %collective-permute-start.9 = (bf16[2,128,512]{2,1,0:T(8,128)(2,1)S(1)}, bf16[2,128,512]{2,1,0:T(8,128)(2,1)S(1)}, u32[]{:S(2)}, u32[]{:S(2)}) collective-permute-start(bf16[2,128,512]{2,1,0:T(8,128)(2,1)S(1)} %collective-permute-done.8.mine_ref), channel_id=1, source_target_pairs={{0,1},{1,0},{2,3},{3,2},{4,5},{5,4},{6,7},{7,6},{8,9},{9,8},{10,11... | collective-permute-start | bytes 786440 | tf_op jit(solution)/shard_map/ppermute | solution.py:308
  17.4 3.0 %collective-permute-done.2.other_ref = bf16[2,128,512]{2,1,0:T(8,128)(2,1)S(1)} collective-permute-done((bf16[2,128,512]{2,1,0:T(8,128)(2,1)S(1)}, bf16[2,128,512]{2,1,0:T(8,128)(2,1)S(1)}, u32[]{:S(2)}, u32[]{:S(2)}) %collective-permute-start.2) | collective-permute-done | bytes 262176 | tf_op jit(solution)/shard_map/ppermute | solution.py:308
  20.5 1.1 %shard_map.57 = (bf16[2,256,256]{2,1,0:T(8,128)(2,1)S(1)}, bf16[2,256,256]{2,1,0:T(8,128)(2,1)S(1)}, bf16[2,256,256]{2,1,0:T(8,128)(2,1)S(1)}, bf16[2,256,256]{2...) custom-call(s32[2,8]{1,0:T(2,128)S(1)} %bitcast.6, ...), custom_call_target="tpu_custom_call", output_to_operand_aliasing={{0}: (3, {}), {1}: (4, {}), {2}: (5, {}), {3}: (6, {}), {4}... | custom-call | bytes 3670080 | tf_op jit(solution)/shard_map/pallas_call | solution.py:27
  21.6 1.6 %collective-permute-start.11 = (bf16[2,128,512]{2,1,0:T(8,128)(2,1)S(1)}, bf16[2,128,512]{2,1,0:T(8,128)(2,1)S(1)}, u32[]{:S(2)}, u32[]{:S(2)}) collective-permute-start(bf16[2,128,512]{2,1,0:T(8,128)(2,1)S(1)} %collective-permute-done.1.mine_ref), channel_id=1, source_target_pairs={{0,1},{1,0},{2,3},{3,2},{4,5},{5,4},{6,7},{7,6},{8,9},{9,8},{10,11... | collective-permute-start | bytes 786440 | tf_op jit(solution)/shard_map/ppermute | solution.py:308
  24.1 2.0 %collective-permute-done.9.other_ref = bf16[2,128,512]{2,1,0:T(8,128)(2,1)S(1)} collective-permute-done((bf16[2,128,512]{2,1,0:T(8,128)(2,1)S(1)}, bf16[2,128,512]{2,1,0:T(8,128)(2,1)S(1)}, u32[]{:S(2)}, u32[]{:S(2)}) %collective-permute-start.9) | collective-permute-done | bytes 262176 | tf_op jit(solution)/shard_map/ppermute | solution.py:308
  26.9 3.3 %collective-permute-done.11.other_ref = bf16[2,128,512]{2,1,0:T(8,128)(2,1)S(1)} collective-permute-done((bf16[2,128,512]{2,1,0:T(8,128)(2,1)S(1)}, bf16[2,128,512]{2,1,0:T(8,128)(2,1)S(1)}, u32[]{:S(2)}, u32[]{:S(2)}) %collective-permute-start.11) | collective-permute-done | bytes 262176 | tf_op jit(solution)/shard_map/ppermute | solution.py:308
  33.1 1.6 %collective-permute-done.6.refs_4_ = bf16[2,256,256]{2,1,0:T(8,128)(2,1)S(1)} collective-permute-done((bf16[2,256,256]{2,1,0:T(8,128)(2,1)S(1)}, bf16[2,256,256]{2,1,0:T(8,128)(2,1)S(1)}, u32[]{:S(2)}, u32[]{:S(2)}) %collective-permute-start.6) | collective-permute-done | bytes 262176 | tf_op jit(solution)/shard_map/ppermute | solution.py:311
  34.8 5.2 %shard_map.60 = (bf16[2,256,256]{2,1,0:T(8,128)(2,1)S(1)}, bf16[8,2,256,256]{3,2,1,0:T(8,128)(2,1)S(1)}) custom-call(bf16[2,256,256]{2,1,0:T(8,128)(2,1)S(1)} %get-tuple-element.61.start_ref, bf16[256,256]{1,0:T(8,128)(2,1)S(1)} %get-tuple-element.62.down_ref, bf16[256,256]{1,0:T(8,128)(2,1)S(1)} %get-tuple-element.63.across_ref, ...), custom_call_target="tpu_custom_call" | custom-call | flops 2147483648 | bytes 4980736 | tf_op jit(solution)/shard_map/pallas_call | solution.py:27
  40.0 1.5 %collective-permute-start.13 = (bf16[2,256,256]{2,1,0:T(8,128)(2,1)S(1)}, bf16[2,256,256]{2,1,0:T(8,128)(2,1)S(1)}, u32[]{:S(2)}, u32[]{:S(2)}) collective-permute-start(bf16[2,256,256]{2,1,0:T(8,128)(2,1)S(1)} %get-tuple-element.91), channel_id=1, source_target_pairs={{16,8},{18,10},{20,12},{22,14},{24,0},{26,2},{28,4},{30,6},{17,9},... | collective-permute-start | bytes 786440 | tf_op jit(solution)/shard_map/ppermute | solution.py:354
  41.5 2.5 %shard_map.61.wave_ref = bf16[8,2,256,256]{3,2,1,0:T(8,128)(2,1)S(1)} custom-call(s32[2,8]{1,0:T(2,128)S(1)} %bitcast.9, bf16[8,2,256,256]{3,2,1,0:T(8,128)(2,1)S(1)} %bitcast.3), custom_call_target="tpu_custom_call" | custom-call | bytes 4194368 | tf_op jit(solution)/shard_map/pallas_call | solution.py:27
  44.0 8.7 %collective-permute-done.13.come_ref = bf16[2,256,256]{2,1,0:T(8,128)(2,1)S(1)} collective-permute-done((bf16[2,256,256]{2,1,0:T(8,128)(2,1)S(1)}, bf16[2,256,256]{2,1,0:T(8,128)(2,1)S(1)}, u32[]{:S(2)}, u32[]{:S(2)}) %collective-permute-start.13) | collective-permute-done | bytes 262176 | tf_op jit(solution)/shard_map/ppermute | solution.py:354
  52.7 5.2 %shard_map.62 = (bf16[2,256,256]{2,1,0:T(8,128)(2,1)S(1)}, bf16[2,256,256]{2,1,0:T(8,128)(2,1)S(1)}, bf16[2,256,256]{2,1,0:T(8,128)(2,1)S(1)}, bf16[2,256,256]{2...) custom-call(bf16[2,256,256]{2,1,0:T(8,128)(2,1)S(1)} %get-tuple-elem, ...), custom_call_target="tpu_custom_call" | custom-call | flops 2147483648 | bytes 4980736 | tf_op jit(solution)/shard_map/pallas_call | solution.py:27
  57.9 5.3 %collective-permute-start.21 = (bf16[2,128,256]{2,1,0:T(8,128)(2,1)S(1)}, bf16[2,128,256]{2,1,0:T(8,128)(2,1)S(1)}, u32[]{:S(2)}, u32[]{:S(2)}) collective-permute-start(bf16[2,128,256]{2,1,0:T(8,128)(2,1)S(1)} %get-tuple-element.103), channel_id=1, source_target_pairs={{0,12},{2,14},{4,8},{6,10},{8,4},{10,6},{12,0},{14,2},{16,28},{18,... | collective-permute-start | bytes 393224 | tf_op jit(solution)/shard_map/ppermute | solution.py:311
  64.0 2.3 %collective-permute-start.20 = (bf16[2,256,256]{2,1,0:T(8,128)(2,1)S(1)}, bf16[2,256,256]{2,1,0:T(8,128)(2,1)S(1)}, u32[]{:S(2)}, u32[]{:S(2)}) collective-permute-start(bf16[2,256,256]{2,1,0:T(8,128)(2,1)S(1)} %get-tuple-element.102), channel_id=1, source_target_pairs={{0,8},{2,10},{4,12},{6,14},{8,0},{10,2},{12,4},{14,6},{16,24},{18,... | collective-permute-start | bytes 786440 | tf_op jit(solution)/shard_map/ppermute | solution.py:311
  67.8 2.2 %collective-permute-done.22.refs_4_ = bf16[2,128,256]{2,1,0:T(8,128)(2,1)S(1)} collective-permute-done((bf16[2,128,256]{2,1,0:T(8,128)(2,1)S(1)}, bf16[2,128,256]{2,1,0:T(8,128)(2,1)S(1)}, u32[]{:S(2)}, u32[]{:S(2)}) %collective-permute-start.22) | collective-permute-done | bytes 131104 | tf_op jit(solution)/shard_map/ppermute | solution.py:311
  70.0 5.5 %collective-permute-done.19.refs_1_ = bf16[2,256,256]{2,1,0:T(8,128)(2,1)S(1)} collective-permute-done((bf16[2,256,256]{2,1,0:T(8,128)(2,1)S(1)}, bf16[2,256,256]{2,1,0:T(8,128)(2,1)S(1)}, u32[]{:S(2)}, u32[]{:S(2)}) %collective-permute-start.19) | collective-permute-done | bytes 262176 | tf_op jit(solution)/shard_map/ppermute | solution.py:311
  75.5 2.6 %collective-permute-start.14 = (bf16[2,128,256]{2,1,0:T(8,128)(2,1)S(1)}, bf16[2,128,256]{2,1,0:T(8,128)(2,1)S(1)}, u32[]{:S(2)}, u32[]{:S(2)}) collective-permute-start(bf16[2,128,256]{2,1,0:T(8,128)(2,1)S(1)} %get-tuple-element.95), channel_id=1, source_target_pairs={{0,12},{2,14},{4,8},{6,10},{8,4},{10,6},{12,0},{14,2},{16,28},{18,... | collective-permute-start | bytes 393224 | tf_op jit(solution)/shard_map/ppermute | solution.py:311
  78.1 1.0 %shard_map.63.refs_3_ = f32[8,128,256]{2,1,0:T(8,128)S(1)} custom-call(s32[2,8]{1,0:T(2,128)S(1)} %bitcast.10, bf16[8,2,256,256]{3,2,1,0:T(8,128)(2,1)S(1)} %shard_map.61.wave_ref, bf16[2,256,256]{2,1,0:T(8,128)(2,1)S(1)} %get-tuple-element.100.refs_0_, bf16[2,256,256]{2,1,0:T(8,128)(2,1)S(1)} %collective-permute-done.19.refs_1_, ...), custom_call_target="tpu_custom_call" | custom-call | bytes 3932224 | tf_op jit(solution)/shard_map/pallas_call | solution.py:27
  79.2 1.3 %shard_map.64.refs_3_ = f32[8,128,256]{2,1,0:T(8,128)S(1)} custom-call(s32[2,8]{1,0:T(2,128)S(1)} %bitcast.11, bf16[8,2,256,256]{3,2,1,0:T(8,128)(2,1)S(1)} %shard_map.61.wave_ref, bf16[2,256,256]{2,1,0:T(8,128)(2,1)S(1)} %get-tuple-element.100.refs_0_, bf16[2,256,256]{2,1,0:T(8,128)(2,1)S(1)} %collective-permute-done.19.refs_1_, ...), custom_call_target="tpu_custom_call" | custom-call | bytes 4194368 | tf_op jit(solution)/shard_map/pallas_call | solution.py:27
  81.2 1.1 %shard_map.65 = (f32[2,128,512]{2,1,0:T(8,128)S(1)}, bf16[2,128,512]{2,1,0:T(8,128)(2,1)S(1)}) custom-call(s32[2,8]{1,0:T(2,128)S(1)} %bitcast.12, bf16[8,2,256,256]{3,2,1,0:T(8,128)(2,1)S(1)} %shard_map.61.wave_ref, bf16[2,256,256]{2,1,0:T(8,128)(2,1)S(1)} %collective-permute-done.16.refs_0_, bf16[2,256,256]{2,1,0:T(8,128)(2,1)S(1)} %collective-permute-done.17.refs_1_, ...), custom_call_target="tpu_custom_call" | custom-call | bytes 4718656 | tf_op jit(solution)/shard_map/pallas_call | solution.py:27
  83.0 1.0 %shard_map.66.refs_2_ = f32[8,128,256]{2,1,0:T(8,128)S(1)} custom-call(s32[2,8]{1,0:T(2,128)S(1)} %bitcast.13, bf16[8,2,256,256]{3,2,1,0:T(8,128)(2,1)S(1)} %shard_map.61.wave_ref, bf16[2,256,256]{2,1,0:T(8,128)(2,1)S(1)} %collective-permute-done.16.refs_0_, bf16[2,256,256]{2,1,0:T(8,128)(2,1)S(1)} %collective-permute-done.17.refs_1_, ...), custom_call_target="tpu_custom_call" | custom-call | bytes 4980800 | tf_op jit(solution)/shard_map/pallas_call | solution.py:27
  84.1 2.7 %collective-permute-done.15.refs_1_ = bf16[2,128,256]{2,1,0:T(8,128)(2,1)S(1)} collective-permute-done((bf16[2,128,256]{2,1,0:T(8,128)(2,1)S(1)}, bf16[2,128,256]{2,1,0:T(8,128)(2,1)S(1)}, u32[]{:S(2)}, u32[]{:S(2)}) %collective-permute-start.15) | collective-permute-done | bytes 131104 | tf_op jit(solution)/shard_map/ppermute | solution.py:311
  86.8 1.0 shard_map.67
  88.4 2.1 %collective-permute-done.24.come_ref = bf16[2,128,512]{2,1,0:T(8,128)(2,1)S(1)} collective-permute-done((bf16[2,128,512]{2,1,0:T(8,128)(2,1)S(1)}, bf16[2,128,512]{2,1,0:T(8,128)(2,1)S(1)}, u32[]{:S(2)}, u32[]{:S(2)}) %collective-permute-start.24) | collective-permute-done | bytes 262176 | tf_op jit(solution)/shard_map/ppermute | solution.py:308
  91.4 4.8 %collective-permute-done.23.come_ref = bf16[2,128,512]{2,1,0:T(8,128)(2,1)S(1)} collective-permute-done((bf16[2,128,512]{2,1,0:T(8,128)(2,1)S(1)}, bf16[2,128,512]{2,1,0:T(8,128)(2,1)S(1)}, u32[]{:S(2)}, u32[]{:S(2)}) %collective-permute-start.23) | collective-permute-done | bytes 262176 | tf_op jit(solution)/shard_map/ppermute | solution.py:308
  (43 shorter events, 11.5 us)
Async XLA Ops:
  0.0 9.2 %copy-start.2 = (s32[8,2]{0,1:T(2,128)S(1)}, s32[8,2]{0,1:T(2,128)}, u32[]{:S(2)}) copy-start(s32[8,2]{0,1:T(2,128)} %param.9) | copy-start | bytes 196
  0.0 9.2 %copy-start.1 = (bf16[8,2,256,256]{3,2,1,0:T(8,128)(2,1)S(1)}, bf16[8,2,256,256]{3,2,1,0:T(8,128)(2,1)}, u32[]{:S(2)}) copy-start(bf16[8,2,256,256]{3,2,1,0:T(8,128)(2,1)} %exit_ref.1) | copy-start | bytes 6291460
  1.6 14.3 %collective-permute-start.8 = (bf16[2,128,512]{2,1,0:T(8,128)(2,1)S(1)}, bf16[2,128,512]{2,1,0:T(8,128)(2,1)S(1)}, u32[]{:S(2)}, u32[]{:S(2)}) collective-permute-start(bf16[2,128,512]{2,1,0:T(8,128)(2,1)S(1)} %pad_maximum_fusion.mine_ref), channel_id=1, source_target_pairs={{0,12},{2,14},{4,8},{6,10},{8,4},{10,6},{12,0},{14,2},{16,28},{18,... | collective-permute-start | bytes 786440 | tf_op jit(solution)/shard_map/ppermute | solution.py:311
  5.6 9.2 %collective-permute-start = (bf16[2,128,512]{2,1,0:T(8,128)(2,1)S(1)}, bf16[2,128,512]{2,1,0:T(8,128)(2,1)S(1)}, u32[]{:S(2)}, u32[]{:S(2)}) collective-permute-start(bf16[2,128,512]{2,1,0:T(8,128)(2,1)S(1)} %pad_maximum_fusion.mine_ref), channel_id=1, source_target_pairs={{0,1},{1,0},{2,3},{3,2},{4,5},{5,4},{6,7},{7,6},{8,9},{9,8},{10,11... | collective-permute-start | bytes 786440 | tf_op jit(solution)/shard_map/ppermute | solution.py:308
  8.5 11.9 %collective-permute-start.2 = (bf16[2,128,512]{2,1,0:T(8,128)(2,1)S(1)}, bf16[2,128,512]{2,1,0:T(8,128)(2,1)S(1)}, u32[]{:S(2)}, u32[]{:S(2)}) collective-permute-start(bf16[2,128,512]{2,1,0:T(8,128)(2,1)S(1)} %pad_maximum_fusion.1.mine_ref), channel_id=1, source_target_pairs={{0,1},{1,0},{2,3},{3,2},{4,5},{5,4},{6,7},{7,6},{8,9},{9,8},{10,11... | collective-permute-start | bytes 786440 | tf_op jit(solution)/shard_map/ppermute | solution.py:308
  9.1 12.4 %collective-permute-start.1 = (bf16[2,128,512]{2,1,0:T(8,128)(2,1)S(1)}, bf16[2,128,512]{2,1,0:T(8,128)(2,1)S(1)}, u32[]{:S(2)}, u32[]{:S(2)}) collective-permute-start(bf16[2,128,512]{2,1,0:T(8,128)(2,1)S(1)} %pad_maximum_fusion.1.mine_ref), channel_id=1, source_target_pairs={{0,12},{2,14},{4,8},{6,10},{8,4},{10,6},{12,0},{14,2},{16,28},{18,... | collective-permute-start | bytes 786440 | tf_op jit(solution)/shard_map/ppermute | solution.py:311
  15.9 10.2 %collective-permute-start.9 = (bf16[2,128,512]{2,1,0:T(8,128)(2,1)S(1)}, bf16[2,128,512]{2,1,0:T(8,128)(2,1)S(1)}, u32[]{:S(2)}, u32[]{:S(2)}) collective-permute-start(bf16[2,128,512]{2,1,0:T(8,128)(2,1)S(1)} %collective-permute-done.8.mine_ref), channel_id=1, source_target_pairs={{0,1},{1,0},{2,3},{3,2},{4,5},{5,4},{6,7},{7,6},{8,9},{9,8},{10,11... | collective-permute-start | bytes 786440 | tf_op jit(solution)/shard_map/ppermute | solution.py:308
  21.6 8.7 %collective-permute-start.11 = (bf16[2,128,512]{2,1,0:T(8,128)(2,1)S(1)}, bf16[2,128,512]{2,1,0:T(8,128)(2,1)S(1)}, u32[]{:S(2)}, u32[]{:S(2)}) collective-permute-start(bf16[2,128,512]{2,1,0:T(8,128)(2,1)S(1)} %collective-permute-done.1.mine_ref), channel_id=1, source_target_pairs={{0,1},{1,0},{2,3},{3,2},{4,5},{5,4},{6,7},{7,6},{8,9},{9,8},{10,11... | collective-permute-start | bytes 786440 | tf_op jit(solution)/shard_map/ppermute | solution.py:308
  23.1 8.9 %collective-permute-start.3 = (bf16[2,256,256]{2,1,0:T(8,128)(2,1)S(1)}, bf16[2,256,256]{2,1,0:T(8,128)(2,1)S(1)}, u32[]{:S(2)}, u32[]{:S(2)}) collective-permute-start(bf16[2,256,256]{2,1,0:T(8,128)(2,1)S(1)} %get-tuple-element.81), channel_id=1, source_target_pairs={{0,4},{2,6},{4,0},{6,2},{8,12},{10,14},{12,8},{14,10},{16,20},{18,... | collective-permute-start | bytes 786440 | tf_op jit(solution)/shard_map/ppermute | solution.py:311
  23.6 8.7 %collective-permute-start.4 = (bf16[2,256,256]{2,1,0:T(8,128)(2,1)S(1)}, bf16[2,256,256]{2,1,0:T(8,128)(2,1)S(1)}, u32[]{:S(2)}, u32[]{:S(2)}) collective-permute-start(bf16[2,256,256]{2,1,0:T(8,128)(2,1)S(1)} %get-tuple-element.82), channel_id=1, source_target_pairs={{0,8},{2,10},{4,12},{6,14},{8,0},{10,2},{12,4},{14,6},{16,24},{18,... | collective-permute-start | bytes 786440 | tf_op jit(solution)/shard_map/ppermute | solution.py:311
  24.1 9.1 %collective-permute-start.5 = (bf16[2,256,256]{2,1,0:T(8,128)(2,1)S(1)}, bf16[2,256,256]{2,1,0:T(8,128)(2,1)S(1)}, u32[]{:S(2)}, u32[]{:S(2)}) collective-permute-start(bf16[2,256,256]{2,1,0:T(8,128)(2,1)S(1)} %get-tuple-element.83), channel_id=1, source_target_pairs={{0,6},{2,4},{4,2},{6,0},{8,14},{10,12},{12,10},{14,8},{16,22},{18,... | collective-permute-start | bytes 786440 | tf_op jit(solution)/shard_map/ppermute | solution.py:311
  26.1 8.7 %collective-permute-start.6 = (bf16[2,256,256]{2,1,0:T(8,128)(2,1)S(1)}, bf16[2,256,256]{2,1,0:T(8,128)(2,1)S(1)}, u32[]{:S(2)}, u32[]{:S(2)}) collective-permute-start(bf16[2,256,256]{2,1,0:T(8,128)(2,1)S(1)} %get-tuple-element.84), channel_id=1, source_target_pairs={{0,10},{2,8},{4,14},{6,12},{8,2},{10,0},{12,6},{14,4},{16,26},{18,... | collective-permute-start | bytes 786440 | tf_op jit(solution)/shard_map/ppermute | solution.py:311
  30.2 4.5 %collective-permute-start.7 = (bf16[2,256,256]{2,1,0:T(8,128)(2,1)S(1)}, bf16[2,256,256]{2,1,0:T(8,128)(2,1)S(1)}, u32[]{:S(2)}, u32[]{:S(2)}) collective-permute-start(bf16[2,256,256]{2,1,0:T(8,128)(2,1)S(1)} %get-tuple-element.85), channel_id=1, source_target_pairs={{0,2},{2,0},{4,6},{6,4},{8,10},{10,8},{12,14},{14,12},{16,18},{18,... | collective-permute-start | bytes 786440 | tf_op jit(solution)/shard_map/ppermute | solution.py:311
  32.0 2.8 %collective-permute-start.10 = (bf16[2,128,256]{2,1,0:T(8,128)(2,1)S(1)}, bf16[2,128,256]{2,1,0:T(8,128)(2,1)S(1)}, u32[]{:S(2)}, u32[]{:S(2)}) collective-permute-start(bf16[2,128,256]{2,1,0:T(8,128)(2,1)S(1)} %get-tuple-element.87), channel_id=1, source_target_pairs={{0,2},{2,0},{4,6},{6,4},{8,10},{10,8},{12,14},{14,12},{16,18},{18,... | collective-permute-start | bytes 393224 | tf_op jit(solution)/shard_map/ppermute | solution.py:311
  32.3 2.5 %collective-permute-start.12 = (bf16[2,128,256]{2,1,0:T(8,128)(2,1)S(1)}, bf16[2,128,256]{2,1,0:T(8,128)(2,1)S(1)}, u32[]{:S(2)}, u32[]{:S(2)}) collective-permute-start(bf16[2,128,256]{2,1,0:T(8,128)(2,1)S(1)} %get-tuple-element.90), channel_id=1, source_target_pairs={{0,2},{2,0},{4,6},{6,4},{8,10},{10,8},{12,14},{14,12},{16,18},{18,... | collective-permute-start | bytes 393224 | tf_op jit(solution)/shard_map/ppermute | solution.py:311
  34.8 6.7 %copy-start = (bf16[1,8,2,256,256]{4,3,2,1,0:T(8,128)(2,1)S(1)}, bf16[1,8,2,256,256]{4,3,2,1,0:T(8,128)(2,1)}, u32[]{:S(2)}) copy-start(bf16[1,8,2,256,256]{4,3,2,1,0:T(8,128)(2,1)} %param.7) | copy-start | bytes 6291460
  40.0 12.7 %collective-permute-start.13 = (bf16[2,256,256]{2,1,0:T(8,128)(2,1)S(1)}, bf16[2,256,256]{2,1,0:T(8,128)(2,1)S(1)}, u32[]{:S(2)}, u32[]{:S(2)}) collective-permute-start(bf16[2,256,256]{2,1,0:T(8,128)(2,1)S(1)} %get-tuple-element.91), channel_id=1, source_target_pairs={{16,8},{18,10},{20,12},{22,14},{24,0},{26,2},{28,4},{30,6},{17,9},... | collective-permute-start | bytes 786440 | tf_op jit(solution)/shard_map/ppermute | solution.py:354
  57.9 9.2 %collective-permute-start.21 = (bf16[2,128,256]{2,1,0:T(8,128)(2,1)S(1)}, bf16[2,128,256]{2,1,0:T(8,128)(2,1)S(1)}, u32[]{:S(2)}, u32[]{:S(2)}) collective-permute-start(bf16[2,128,256]{2,1,0:T(8,128)(2,1)S(1)} %get-tuple-element.103), channel_id=1, source_target_pairs={{0,12},{2,14},{4,8},{6,10},{8,4},{10,6},{12,0},{14,2},{16,28},{18,... | collective-permute-start | bytes 393224 | tf_op jit(solution)/shard_map/ppermute | solution.py:311
  63.3 6.7 %collective-permute-start.22 = (bf16[2,128,256]{2,1,0:T(8,128)(2,1)S(1)}, bf16[2,128,256]{2,1,0:T(8,128)(2,1)S(1)}, u32[]{:S(2)}, u32[]{:S(2)}) collective-permute-start(bf16[2,128,256]{2,1,0:T(8,128)(2,1)S(1)} %get-tuple-element.104), channel_id=1, source_target_pairs={{0,14},{2,12},{4,10},{6,8},{8,6},{10,4},{12,2},{14,0},{16,30},{18,... | collective-permute-start | bytes 393224 | tf_op jit(solution)/shard_map/ppermute | solution.py:311
  63.3 12.3 %collective-permute-start.19 = (bf16[2,256,256]{2,1,0:T(8,128)(2,1)S(1)}, bf16[2,256,256]{2,1,0:T(8,128)(2,1)S(1)}, u32[]{:S(2)}, u32[]{:S(2)}) collective-permute-start(bf16[2,256,256]{2,1,0:T(8,128)(2,1)S(1)} %get-tuple-element.101), channel_id=1, source_target_pairs={{0,4},{2,6},{4,0},{6,2},{8,12},{10,14},{12,8},{14,10},{16,20},{18,... | collective-permute-start | bytes 786440 | tf_op jit(solution)/shard_map/ppermute | solution.py:311
  64.0 14.2 %collective-permute-start.20 = (bf16[2,256,256]{2,1,0:T(8,128)(2,1)S(1)}, bf16[2,256,256]{2,1,0:T(8,128)(2,1)S(1)}, u32[]{:S(2)}, u32[]{:S(2)}) collective-permute-start(bf16[2,256,256]{2,1,0:T(8,128)(2,1)S(1)} %get-tuple-element.102), channel_id=1, source_target_pairs={{0,8},{2,10},{4,12},{6,14},{8,0},{10,2},{12,4},{14,6},{16,24},{18,... | collective-permute-start | bytes 786440 | tf_op jit(solution)/shard_map/ppermute | solution.py:311
  66.2 14.8 %collective-permute-start.16 = (bf16[2,256,256]{2,1,0:T(8,128)(2,1)S(1)}, bf16[2,256,256]{2,1,0:T(8,128)(2,1)S(1)}, u32[]{:S(2)}, u32[]{:S(2)}) collective-permute-start(bf16[2,256,256]{2,1,0:T(8,128)(2,1)S(1)} %get-tuple-element.97), channel_id=1, source_target_pairs={{0,6},{2,4},{4,2},{6,0},{8,14},{10,12},{12,10},{14,8},{16,22},{18,... | collective-permute-start | bytes 786440 | tf_op jit(solution)/shard_map/ppermute | solution.py:311
  67.2 14.1 %collective-permute-start.17 = (bf16[2,256,256]{2,1,0:T(8,128)(2,1)S(1)}, bf16[2,256,256]{2,1,0:T(8,128)(2,1)S(1)}, u32[]{:S(2)}, u32[]{:S(2)}) collective-permute-start(bf16[2,256,256]{2,1,0:T(8,128)(2,1)S(1)} %get-tuple-element.98), channel_id=1, source_target_pairs={{0,10},{2,8},{4,14},{6,12},{8,2},{10,0},{12,6},{14,4},{16,26},{18,... | collective-permute-start | bytes 786440 | tf_op jit(solution)/shard_map/ppermute | solution.py:311
  70.0 11.2 %collective-permute-start.18 = (bf16[2,256,256]{2,1,0:T(8,128)(2,1)S(1)}, bf16[2,256,256]{2,1,0:T(8,128)(2,1)S(1)}, u32[]{:S(2)}, u32[]{:S(2)}) collective-permute-start(bf16[2,256,256]{2,1,0:T(8,128)(2,1)S(1)} %get-tuple-element.99), channel_id=1, source_target_pairs={{0,2},{2,0},{4,6},{6,4},{8,10},{10,8},{12,14},{14,12},{16,18},{18,... | collective-permute-start | bytes 786440 | tf_op jit(solution)/shard_map/ppermute | solution.py:311
  75.5 8.5 %collective-permute-start.14 = (bf16[2,128,256]{2,1,0:T(8,128)(2,1)S(1)}, bf16[2,128,256]{2,1,0:T(8,128)(2,1)S(1)}, u32[]{:S(2)}, u32[]{:S(2)}) collective-permute-start(bf16[2,128,256]{2,1,0:T(8,128)(2,1)S(1)} %get-tuple-element.95), channel_id=1, source_target_pairs={{0,12},{2,14},{4,8},{6,10},{8,4},{10,6},{12,0},{14,2},{16,28},{18,... | collective-permute-start | bytes 393224 | tf_op jit(solution)/shard_map/ppermute | solution.py:311
  78.1 8.6 %collective-permute-start.15 = (bf16[2,128,256]{2,1,0:T(8,128)(2,1)S(1)}, bf16[2,128,256]{2,1,0:T(8,128)(2,1)S(1)}, u32[]{:S(2)}, u32[]{:S(2)}) collective-permute-start(bf16[2,128,256]{2,1,0:T(8,128)(2,1)S(1)} %get-tuple-element.96), channel_id=1, source_target_pairs={{0,14},{2,12},{4,10},{6,8},{8,6},{10,4},{12,2},{14,0},{16,30},{18,... | collective-permute-start | bytes 393224 | tf_op jit(solution)/shard_map/ppermute | solution.py:311
  82.3 8.2 %collective-permute-start.24 = (bf16[2,128,512]{2,1,0:T(8,128)(2,1)S(1)}, bf16[2,128,512]{2,1,0:T(8,128)(2,1)S(1)}, u32[]{:S(2)}, u32[]{:S(2)}) collective-permute-start(bf16[2,128,512]{2,1,0:T(8,128)(2,1)S(1)} %get-tuple-element.110), channel_id=1, source_target_pairs={{0,1},{1,0},{2,3},{3,2},{4,5},{5,4},{6,7},{7,6},{8,9},{9,8},{10,11... | collective-permute-start | bytes 786440 | tf_op jit(solution)/shard_map/ppermute | solution.py:308
  87.7 8.4 %collective-permute-start.23 = (bf16[2,128,512]{2,1,0:T(8,128)(2,1)S(1)}, bf16[2,128,512]{2,1,0:T(8,128)(2,1)S(1)}, u32[]{:S(2)}, u32[]{:S(2)}) collective-permute-start(bf16[2,128,512]{2,1,0:T(8,128)(2,1)S(1)} %get-tuple-element.108), channel_id=1, source_target_pairs={{0,1},{1,0},{2,3},{3,2},{4,5},{5,4},{6,7},{7,6},{8,9},{9,8},{10,11... | collective-permute-start | bytes 786440 | tf_op jit(solution)/shard_map/ppermute | solution.py:308

commit v12 on v11

--- a/solution.py
+++ b/solution.py
@@ -137,7 +137,7 @@
     across_ref[...] = second_difference(size, col_at)
 
 
-def turn_kernel(corner_ref, wave_ref, turned_ref):
+def turn_kernel(corner_ref, wave_ref, turned_ref, given_ref):
     count = wave_ref.shape[0]
 
     def one(position, _):
@@ -148,6 +148,9 @@
         return 0
 
     lax.fori_loop(0, count, one, 0)
+    own = place_in_group(count)
+    for i in range(far):
+        given_ref[i] = turned_ref[position_at(own ^ (count - far + i), count)]
 
 
 def back(down, across, chi_re, chi_im):
@@ -224,13 +227,13 @@
     if not is_last:
         refs[0][0], refs[0][1] = chi
         return
-    for spread_ref, apart, here in zip(refs, *in_pieces(count, window)):
-        spread_ref[...] = refs[-1][own ^ apart, :, here]
-
-
-def add_kernel(base, picks, begun, ends, corner_ref, wave_ref, *refs):
+    for spread_ref, apart in zip(refs, distances(count)):
+        spread_ref[...] = refs[-1][own ^ apart]
+
+
+def add_kernel(base, count, picks, begun, ends, corner_ref, wave_ref, *refs):
     spread_refs, refs = refs[: len(picks)], refs[len(picks) :]
-    count, _, window, _ = wave_ref.shape
+    window = wave_ref.shape[-1]
     rows = window // chunk_count
     tall = 16
     own = place_in_group(count)
@@ -242,10 +245,10 @@
         sums = [refs[0][i, rows_at, :] if begun else jnp.zeros((tall, window), f32) for i in range(8)]
         for apart, spread_ref in zip(picks, spread_refs):
             position = position_at(own ^ apart, count)
-            there = rows_at if apart >= count - far else here
+            slot = position if wave_ref.shape[0] == count else apart
             in_mine, in_left = first_masks(corner_ref, position, base + at, (tall, window))
-            wave_re, wave_im = (wave_ref[position, part, here, :].astype(f32) for part in range(2))
-            spread_re, spread_im = (spread_ref[part, there, :].astype(f32) for part in range(2))
+            wave_re, wave_im = (wave_ref[slot, part, here, :].astype(f32) for part in range(2))
+            spread_re, spread_im = (spread_ref[part, here, :].astype(f32) for part in range(2))
             parts = (
                 wave_re * spread_re + wave_im * spread_im,
                 wave_re * spread_im - wave_im * spread_re,
@@ -273,20 +276,20 @@
     lax.fori_loop(0, rows // tall, one, 0)
 
 
-def finish(chunk, own, come, shape, before):
-    def kernel(own_ref, come_ref, *refs):
-        refs[-1][...] = own_ref[...] + come_ref[...].astype(f32)
+def finish(chunk, own, come, far_come, shape, before):
+    def kernel(own_ref, come_ref, far_ref, *refs):
+        refs[-1][...] = own_ref[...] + (come_ref[...].astype(f32) + far_ref[...].astype(f32))
 
     vmem = pl.BlockSpec(memory_space=pltpu.VMEM)
     return pl.pallas_call(
         kernel,
         grid=(1,),
-        in_specs=[vmem, vmem] + [pl.BlockSpec(memory_space=pl.ANY)] * len(before),
+        in_specs=[vmem] * 3 + [pl.BlockSpec(memory_space=pl.ANY)] * len(before),
         out_specs=pl.BlockSpec(own.shape, lambda _: (0, chunk, 0)),
         out_shape=shape_of(shape, f32),
-        input_output_aliases={2: 0} if before else {},
+        input_output_aliases={3: 0} if before else {},
         compiler_params=pltpu.CompilerParams(vmem_limit_bytes=6 * 2**20),
-    )(own, come, *before)
+    )(own, come, far_come, *before)
 
 
 def shape_of(dims, dtype):
@@ -344,57 +347,56 @@
         kept, given = cut_far(corners, far_mine[c], to_other_half(far_mine[c]))
         distant += [kept, to_distance(given, 1)]
     windows = exchange(near) + distant
-    waves = call(turn_kernel, shape_of(forward_waves.shape[1:], bf16), prefetch=1)(corners, forward_waves[0])
-
-    pieces = [shape_of(wave, bf16)] * (count - far) + [shape_of((2, rows, window), bf16)] * (far * chunk_count)
+    waves, given = call(
+        turn_kernel, [shape_of(forward_waves.shape[1:], bf16), shape_of((far,) + wave, bf16)], prefetch=1
+    )(corners, forward_waves[0])
+
     cost = (count * 16 * window**3, count * 2 * window**2)
     first = call(first_kernel, [shape_of(wave, bf16), shape_of((count,) + wave, bf16)], cost=cost, grant=12)
+    start, waves, given = lax.optimization_barrier((start, waves, given))
+    far_waves = to_distance(given, count - far)
     leave, held = first(start, down, across, *windows)
     for stage in range(1, group_count):
         come = lax.ppermute(
             leave, "sec", [(s, (s - count) ^ (count // 2)) for s in range(count, sections)]
         )
-        come, waves = lax.optimization_barrier((come, waves))
+        come, waves, far_waves = lax.optimization_barrier((come, waves, far_waves))
         is_last = stage == group_count - 1
         through = call(
             functools.partial(next_kernel, is_last),
-            pieces if is_last else shape_of(wave, bf16),
+            [shape_of(wave, bf16)] * count if is_last else shape_of(wave, bf16),
             scratch=[pltpu.VMEM((count,) + wave, bf16)] if is_last else [],
             cost=cost,
             grant=12,
         )
         leave = through(start, come, down, across, held)
 
-    near, distant = leave[: count - far], leave[count - far :]
-    came_far = [exchange_far(distant[:far])]
-    came = exchange(near)
-    came_far += [exchange_far(distant[c * far : (c + 1) * far]) for c in chunks[1:]]
+    def add(c, wave_set, picks, spreads, sums, ends):
+        kernel = functools.partial(add_kernel, c * rows, count, picks, bool(sums), ends)
+        given = [shape_of(piece, f32), shape_of(piece, bf16)] if ends else shape_of((8, rows, window), f32)
+        return call(kernel, given, prefetch=1)(corners, wave_set, *spreads, *sums)
+
+    far_kept, far_given = leave[count - far :]
+    far_spreads = [far_kept, to_distance(far_given, 1)]
+    came = exchange(leave[: count - far])
+    half_sums = []
+    for c in chunks:
+        keep, away = add(c, far_waves, [0, 1], far_spreads, [], True)
+        half_sums.append((keep + to_other_half(away).astype(f32)).astype(bf16))
+
     order = distances(count)
-    early, late = order[: count // 2 - 1], order[count // 2 - 1 : count - far]
-    spread_at = dict(zip(order, came))
-
-    def add(c, picks, sums, ends):
-        spreads = [came_far[c][d - count + far] if d >= count - far else spread_at[d] for d in picks]
-        kernel = functools.partial(add_kernel, c * rows, picks, bool(sums), ends)
-        given = [shape_of(piece, f32), shape_of(piece, bf16)] if ends else shape_of((8, rows, window), f32)
-        return call(kernel, given, prefetch=1)(corners, waves, *spreads, *sums)
-
-    done = []
-    for c in chunks:
-        if c == 0:
-            sums = add(c, early + order[-far:], [], False)
-            keep, away = add(c, late, [sums], True)
-        else:
-            sums = add(c, early, [], False)
-            sums, away = lax.optimization_barrier((sums, away))
-            sums = add(c, late, [sums], False)
-            done.append((keep, to_other_half(away)))
-            keep, away = add(c, order[-far:], [sums], True)
-    done.append((keep, to_other_half(away)))
+    cut_at = count // 2 - 1
+    early = [add(c, waves, order[:cut_at], came[:cut_at], [], False) for c in chunks]
     result = []
     for c in chunks:
-        result = [finish(c, *done[c], (2, half, width), result)]
-    return result[0][None]
+        half_sums[c], early[c] = lax.optimization_barrier((half_sums[c], early[c]))
+        far_come = to_distance(half_sums[c], count - far)
+        keep, away = add(c, waves, order[cut_at : count - far], came[cut_at:], [early[c]], True)
+        result.append((keep, to_other_half(away), far_come))
+    out = []
+    for c in chunks:
+        out = [finish(c, *result[c], (2, half, width), out)]
+    return out[0][None]
 
 
 def solution(mesh):

time: 97.2 us -> 97.5 us (level)
  starting transfers between devices: 26.4 us -> 24.4 us
  waiting for transfers between devices: 42.7 us -> 44.2 us
    ppermute x18, starting transfers between devices: 18.4 us -> 13.8 us  [to_distance(): return lax.ppermute(value, 'sec', [(s, s ^ d) for s in range(sections)])]
    ppermute x6 -> x8, starting transfers between devices: 6.57 us -> 9.13 us  [to_other_half(): return lax.ppermute(value, 'scan', [(0, 1), (1, 0)])]
    ppermute x6 -> x8, waiting for transfers between devices: 19.7 us -> 22.1 us  [to_other_half(): return lax.ppermute(value, 'scan', [(0, 1), (1, 0)])]
    ppermute x1, waiting for transfers between devices: 8.72 us -> 7.48 us  [on_device(): lax.ppermute(leave, 'sec', [(s, s - count ^ count // 2) for s in range(co...]
    pallas_call x13 -> x14, Pallas kernels: 23.1 us -> 23.6 us  [run(): pl.pallas_call(kernel, grid_spec=pltpu.PrefetchScalarGridSpec(num_scalar_...]
  transfers between devices with their start and end apart: 25 -> 27, of which waited for: 16 -> 16; matrix products, arithmetic and copies ran while one was open for 1% -> 2% of each run, Pallas kernels for 14% -> 19%
where the time goes in v12:
time: 97.5 us; the launch traced here: 97.4 us
  waiting for transfers between devices  44.2 us (45%)
  Pallas kernels  25.4 us (26%)
  starting transfers between devices  24.4 us (25%)
  other arithmetic  3.11 us (3%)
    pallas_call x14, Pallas kernels, run(): pl.pallas_call(kernel, grid_spec=pltpu.PrefetchScalarGridSpec(num_scalar_...  23.6 us
    ppermute x8, waiting for transfers between devices, to_other_half(): return lax.ppermute(value, 'scan', [(0, 1), (1, 0)])  22.1 us
    ppermute x18, waiting for transfers between devices, to_distance(): return lax.ppermute(value, 'sec', [(s, s ^ d) for s in range(sections)])  14.7 us
    ppermute x18, starting transfers between devices, to_distance(): return lax.ppermute(value, 'sec', [(s, s ^ d) for s in range(sections)])  13.8 us
    ppermute x8, starting transfers between devices, to_other_half(): return lax.ppermute(value, 'scan', [(0, 1), (1, 0)])  9.13 us
    ppermute x1, waiting for transfers between devices, on_device(): lax.ppermute(leave, 'sec', [(s, s - count ^ count // 2) for s in range(co...  7.48 us
    convert_element_type x2, other arithmetic, coded(): jnp.exp(code_gain * trans_re).astype(bf16)  2.91 us
  transfers between devices with their start and end apart: 27, of which 16 were waited for; matrix products, arithmetic and copies ran while one was open for 2% of the time, Pallas kernels for 19%

profile of v12, /device:TPU:0, one launch (start us, length us, event | category | flops | bytes accessed | tf_op | source)
XLA Modules:
  0.0 97.4 jit_solution(3508032438638746253)
XLA Ops:
  0.0 1.5 %fusion.4 = (bf16[1,128,512]{2,1,0:T(8,128)(2,1)S(1)}, bf16[1,128,512]{2,1,0:T(8,128)(2,1)S(1)}) fusion(f32[1,256,512]{2,1,0:T(8,128)} %param.5, f32[1,256,512]{2,1,0:T(8,128)} %param.6), kind=kLoop, calls=%fused_computation.10 | loop fusion | flops 2424832 | bytes 786432 | tf_op jit(solution)/shard_map/convert_element_type | solution.py:66
  1.6 4.0 %collective-permute-start.8 = (bf16[2,128,512]{2,1,0:T(8,128)(2,1)S(1)}, bf16[2,128,512]{2,1,0:T(8,128)(2,1)S(1)}, u32[]{:S(2)}, u32[]{:S(2)}) collective-permute-start(bf16[2,128,512]{2,1,0:T(8,128)(2,1)S(1)} %pad_maximum_fusion.mine_ref), channel_id=1, source_target_pairs={{0,12},{2,14},{4,8},{6,10},{8,4},{10,6},{12,0},{14,2},{16,28},{18,... | collective-permute-start | bytes 786440 | tf_op jit(solution)/shard_map/ppermute | solution.py:314
  5.6 1.5 %collective-permute-start = (bf16[2,128,512]{2,1,0:T(8,128)(2,1)S(1)}, bf16[2,128,512]{2,1,0:T(8,128)(2,1)S(1)}, u32[]{:S(2)}, u32[]{:S(2)}) collective-permute-start(bf16[2,128,512]{2,1,0:T(8,128)(2,1)S(1)} %pad_maximum_fusion.mine_ref), channel_id=1, source_target_pairs={{0,1},{1,0},{2,3},{3,2},{4,5},{5,4},{6,7},{7,6},{8,9},{9,8},{10,11... | collective-permute-start | bytes 786440 | tf_op jit(solution)/shard_map/ppermute | solution.py:311
  7.1 1.4 %fusion.13 = (bf16[1,128,512]{2,1,0:T(8,128)(2,1)S(1)}, bf16[1,128,512]{2,1,0:T(8,128)(2,1)S(1)}) fusion(f32[1,256,512]{2,1,0:T(8,128)} %param.5, f32[1,256,512]{2,1,0:T(8,128)} %param.6), kind=kLoop, calls=%fused_computation.19 | loop fusion | flops 2424832 | bytes 786432 | tf_op jit(solution)/shard_map/convert_element_type | solution.py:66
  9.2 1.2 %shard_map.55 = (bf16[2,256,256]{2,1,0:T(8,128)(2,1)S(1)}, bf16[256,256]{1,0:T(8,128)(2,1)S(1)}, bf16[256,256]{1,0:T(8,128)(2,1)S(1)}) custom-call(s32[2,8]{1,0:T(2,128)S(1)} %bitcast.4, bf16[8,2,256,256]{3,2,1,0:T(8,128)(2,1)S(1)} %copy-done), custom_call_target="tpu_custom_call" | custom-call | bytes 2621504 | tf_op jit(solution)/shard_map/pallas_call | solution.py:27
  10.4 4.4 %collective-permute-done.other_ref = bf16[2,128,512]{2,1,0:T(8,128)(2,1)S(1)} collective-permute-done((bf16[2,128,512]{2,1,0:T(8,128)(2,1)S(1)}, bf16[2,128,512]{2,1,0:T(8,128)(2,1)S(1)}, u32[]{:S(2)}, u32[]{:S(2)}) %collective-permute-start) | collective-permute-done | bytes 262176 | tf_op jit(solution)/shard_map/ppermute | solution.py:311
  14.8 1.0 %shard_map.57 = (bf16[2,256,256]{2,1,0:T(8,128)(2,1)S(1)}, bf16[2,256,256]{2,1,0:T(8,128)(2,1)S(1)}, bf16[2,256,256]{2,1,0:T(8,128)(2,1)S(1)}, bf16[2,256,256]{2...) custom-call(s32[2,8]{1,0:T(2,128)S(1)} %bitcast.5, ...), custom_call_target="tpu_custom_call" | custom-call | bytes 2097216 | tf_op jit(solution)/shard_map/pallas_call | solution.py:27
  15.9 1.6 %collective-permute-start.9 = (bf16[2,128,512]{2,1,0:T(8,128)(2,1)S(1)}, bf16[2,128,512]{2,1,0:T(8,128)(2,1)S(1)}, u32[]{:S(2)}, u32[]{:S(2)}) collective-permute-start(bf16[2,128,512]{2,1,0:T(8,128)(2,1)S(1)} %collective-permute-done.8.mine_ref), channel_id=1, source_target_pairs={{0,1},{1,0},{2,3},{3,2},{4,5},{5,4},{6,7},{7,6},{8,9},{9,8},{10,11... | collective-permute-start | bytes 786440 | tf_op jit(solution)/shard_map/ppermute | solution.py:311
  17.4 3.0 %collective-permute-done.2.other_ref = bf16[2,128,512]{2,1,0:T(8,128)(2,1)S(1)} collective-permute-done((bf16[2,128,512]{2,1,0:T(8,128)(2,1)S(1)}, bf16[2,128,512]{2,1,0:T(8,128)(2,1)S(1)}, u32[]{:S(2)}, u32[]{:S(2)}) %collective-permute-start.2) | collective-permute-done | bytes 262176 | tf_op jit(solution)/shard_map/ppermute | solution.py:311
  20.5 1.1 %shard_map.58 = (bf16[2,256,256]{2,1,0:T(8,128)(2,1)S(1)}, bf16[2,256,256]{2,1,0:T(8,128)(2,1)S(1)}, bf16[2,256,256]{2,1,0:T(8,128)(2,1)S(1)}, bf16[2,256,256]{2...) custom-call(s32[2,8]{1,0:T(2,128)S(1)} %bitcast.6, ...), custom_call_target="tpu_custom_call", output_to_operand_aliasing={{0}: (3, {}), {1}: (4, {}), {2}: (5, {}), {3}: (6, {}), {4}... | custom-call | bytes 3670080 | tf_op jit(solution)/shard_map/pallas_call | solution.py:27
  21.6 1.6 %collective-permute-start.11 = (bf16[2,128,512]{2,1,0:T(8,128)(2,1)S(1)}, bf16[2,128,512]{2,1,0:T(8,128)(2,1)S(1)}, u32[]{:S(2)}, u32[]{:S(2)}) collective-permute-start(bf16[2,128,512]{2,1,0:T(8,128)(2,1)S(1)} %collective-permute-done.1.mine_ref), channel_id=1, source_target_pairs={{0,1},{1,0},{2,3},{3,2},{4,5},{5,4},{6,7},{7,6},{8,9},{9,8},{10,11... | collective-permute-start | bytes 786440 | tf_op jit(solution)/shard_map/ppermute | solution.py:311
  24.1 2.0 %collective-permute-done.9.other_ref = bf16[2,128,512]{2,1,0:T(8,128)(2,1)S(1)} collective-permute-done((bf16[2,128,512]{2,1,0:T(8,128)(2,1)S(1)}, bf16[2,128,512]{2,1,0:T(8,128)(2,1)S(1)}, u32[]{:S(2)}, u32[]{:S(2)}) %collective-permute-start.9) | collective-permute-done | bytes 262176 | tf_op jit(solution)/shard_map/ppermute | solution.py:311
  26.9 3.3 %collective-permute-done.11.other_ref = bf16[2,128,512]{2,1,0:T(8,128)(2,1)S(1)} collective-permute-done((bf16[2,128,512]{2,1,0:T(8,128)(2,1)S(1)}, bf16[2,128,512]{2,1,0:T(8,128)(2,1)S(1)}, u32[]{:S(2)}, u32[]{:S(2)}) %collective-permute-start.11) | collective-permute-done | bytes 262176 | tf_op jit(solution)/shard_map/ppermute | solution.py:311
  32.5 2.5 %shard_map.56 = (bf16[8,2,256,256]{3,2,1,0:T(8,128)(2,1)S(1)}, bf16[2,2,256,256]{3,2,1,0:T(8,128)(2,1)S(1)}) custom-call(s32[2,8]{1,0:T(2,128)S(1)} %bitcast.9, bf16[8,2,256,256]{3,2,1,0:T(8,128)(2,1)S(1)} %bitcast.3), custom_call_target="tpu_custom_call" | custom-call | bytes 4718656 | tf_op jit(solution)/shard_map/pallas_call | solution.py:27
  35.8 5.2 %shard_map.61 = (bf16[2,256,256]{2,1,0:T(8,128)(2,1)S(1)}, bf16[8,2,256,256]{3,2,1,0:T(8,128)(2,1)S(1)}) custom-call(bf16[2,256,256]{2,1,0:T(8,128)(2,1)S(1)} %get-tuple-element.74.start_ref, bf16[256,256]{1,0:T(8,128)(2,1)S(1)} %get-tuple-element.75.down_ref, bf16[256,256]{1,0:T(8,128)(2,1)S(1)} %get-tuple-element.76.across_ref, ...), custom_call_target="tpu_custom_call" | custom-call | flops 2147483648 | bytes 4980736 | tf_op jit(solution)/shard_map/pallas_call | solution.py:27
  41.0 1.5 %collective-permute-start.13 = (bf16[2,256,256]{2,1,0:T(8,128)(2,1)S(1)}, bf16[2,256,256]{2,1,0:T(8,128)(2,1)S(1)}, u32[]{:S(2)}, u32[]{:S(2)}) collective-permute-start(bf16[2,256,256]{2,1,0:T(8,128)(2,1)S(1)} %get-tuple-element.104), channel_id=1, source_target_pairs={{16,8},{18,10},{20,12},{22,14},{24,0},{26,2},{28,4},{30,6},{17,9},... | collective-permute-start | bytes 786440 | tf_op jit(solution)/shard_map/ppermute | solution.py:360
  42.5 7.6 %collective-permute-done.14.wave_ref = bf16[2,2,256,256]{3,2,1,0:T(8,128)(2,1)S(1)} collective-permute-done((bf16[2,2,256,256]{3,2,1,0:T(8,128)(2,1)S(1)}, bf16[2,2,256,256]{3,2,1,0:T(8,128)(2,1)S(1)}, u32[]{:S(2)}, u32[]{:S(2)}) %collective-permute-start.14) | collective-permute-done | bytes 524320 | tf_op jit(solution)/shard_map/ppermute | solution.py:314
  50.1 7.5 %collective-permute-done.13.come_ref = bf16[2,256,256]{2,1,0:T(8,128)(2,1)S(1)} collective-permute-done((bf16[2,256,256]{2,1,0:T(8,128)(2,1)S(1)}, bf16[2,256,256]{2,1,0:T(8,128)(2,1)S(1)}, u32[]{:S(2)}, u32[]{:S(2)}) %collective-permute-start.13) | collective-permute-done | bytes 262176 | tf_op jit(solution)/shard_map/ppermute | solution.py:360
  57.6 5.2 %shard_map.62 = (bf16[2,256,256]{2,1,0:T(8,128)(2,1)S(1)}, bf16[2,256,256]{2,1,0:T(8,128)(2,1)S(1)}, bf16[2,256,256]{2,1,0:T(8,128)(2,1)S(1)}, bf16[2,256,256]{2...) custom-call(bf16[2,256,256]{2,1,0:T(8,128)(2,1)S(1)} %get-tuple-elem, ...), custom_call_target="tpu_custom_call" | custom-call | flops 2147483648 | bytes 4980736 | tf_op jit(solution)/shard_map/pallas_call | solution.py:27
  63.8 1.1 %collective-permute-start.21 = (bf16[2,256,256]{2,1,0:T(8,128)(2,1)S(1)}, bf16[2,256,256]{2,1,0:T(8,128)(2,1)S(1)}, u32[]{:S(2)}, u32[]{:S(2)}) collective-permute-start(bf16[2,256,256]{2,1,0:T(8,128)(2,1)S(1)} %get-tuple-element.120), channel_id=1, source_target_pairs={{0,8},{2,10},{4,12},{6,14},{8,0},{10,2},{12,4},{14,6},{16,24},{18,... | collective-permute-start | bytes 786440 | tf_op jit(solution)/shard_map/ppermute | solution.py:314
  65.8 1.6 %collective-permute-start.24 = (bf16[2,128,512]{2,1,0:T(8,128)(2,1)S(1)}, bf16[2,128,512]{2,1,0:T(8,128)(2,1)S(1)}, u32[]{:S(2)}, u32[]{:S(2)}) collective-permute-start(bf16[2,128,512]{2,1,0:T(8,128)(2,1)S(1)} %get-tuple-element.126), channel_id=1, source_target_pairs={{0,1},{1,0},{2,3},{3,2},{4,5},{5,4},{6,7},{7,6},{8,9},{9,8},{10,11... | collective-permute-start | bytes 786440 | tf_op jit(solution)/shard_map/ppermute | solution.py:311
  69.0 2.6 %collective-permute-done.20.refs_1_ = bf16[2,256,256]{2,1,0:T(8,128)(2,1)S(1)} collective-permute-done((bf16[2,256,256]{2,1,0:T(8,128)(2,1)S(1)}, bf16[2,256,256]{2,1,0:T(8,128)(2,1)S(1)}, u32[]{:S(2)}, u32[]{:S(2)}) %collective-permute-start.20) | collective-permute-done | bytes 262176 | tf_op jit(solution)/shard_map/ppermute | solution.py:314
  75.1 4.4 %collective-permute-done.19 = bf16[2,128,512]{2,1,0:T(8,128)(2,1)S(1)} collective-permute-done((bf16[2,128,512]{2,1,0:T(8,128)(2,1)S(1)}, bf16[2,128,512]{2,1,0:T(8,128)(2,1)S(1)}, u32[]{:S(2)}, u32[]{:S(2)}) %collective-permute-start.19) | collective-permute-done | bytes 262176 | tf_op jit(solution)/shard_map/ppermute | solution.py:311
  80.1 1.1 %shard_map.68 = (f32[2,128,512]{2,1,0:T(8,128)S(1)}, bf16[2,128,512]{2,1,0:T(8,128)(2,1)S(1)}) custom-call(s32[2,8]{1,0:T(2,128)S(1)} %bitcast.14, bf16[8,2,256,256]{3,2,1,0:T(8,128)(2,1)S(1)} %get-tuple-element.107.wave_ref, bf16[2,256,256]{2,1,0:T(8,128)(2,1)S(1)} %collective-permute-done.15.refs_0_, ...), custom_call_target="tpu_custom_call" | custom-call | bytes 4718656 | tf_op jit(solution)/shard_map/pallas_call | solution.py:27
  81.2 1.2 %collective-permute-start.25 = (bf16[2,128,512]{2,1,0:T(8,128)(2,1)S(1)}, bf16[2,128,512]{2,1,0:T(8,128)(2,1)S(1)}, u32[]{:S(2)}, u32[]{:S(2)}) collective-permute-start(bf16[2,128,512]{2,1,0:T(8,128)(2,1)S(1)} %get-tuple-element.129), channel_id=1, source_target_pairs={{0,1},{1,0},{2,3},{3,2},{4,5},{5,4},{6,7},{7,6},{8,9},{9,8},{10,11... | collective-permute-start | bytes 786440 | tf_op jit(solution)/shard_map/ppermute | solution.py:311
  82.4 1.8 %collective-permute-start.26 = (bf16[2,128,512]{2,1,0:T(8,128)(2,1)S(1)}, bf16[2,128,512]{2,1,0:T(8,128)(2,1)S(1)}, u32[]{:S(2)}, u32[]{:S(2)}) collective-permute-start(bf16[2,128,512]{2,1,0:T(8,128)(2,1)S(1)} %add_convert_fusion), channel_id=1, source_target_pairs={{0,12},{2,14},{4,8},{6,10},{8,4},{10,6},{12,0},{14,2},{16,28},{18,... | collective-permute-start | bytes 786440 | tf_op jit(solution)/shard_map/ppermute | solution.py:314
  84.2 1.1 %shard_map.65 = (f32[2,128,512]{2,1,0:T(8,128)S(1)}, bf16[2,128,512]{2,1,0:T(8,128)(2,1)S(1)}) custom-call(s32[2,8]{1,0:T(2,128)S(1)} %bitcast.15, bf16[8,2,256,256]{3,2,1,0:T(8,128)(2,1)S(1)} %get-tuple-element.107.wave_ref, bf16[2,256,256]{2,1,0:T(8,128)(2,1)S(1)} %collective-permute-done.15.refs_0_, ...), custom_call_target="tpu_custom_call" | custom-call | bytes 4718656 | tf_op jit(solution)/shard_map/pallas_call | solution.py:27
  85.9 1.5 %collective-permute-start.23 = (bf16[2,128,512]{2,1,0:T(8,128)(2,1)S(1)}, bf16[2,128,512]{2,1,0:T(8,128)(2,1)S(1)}, u32[]{:S(2)}, u32[]{:S(2)}) collective-permute-start(bf16[2,128,512]{2,1,0:T(8,128)(2,1)S(1)} %add_convert_fusion.1), channel_id=1, source_target_pairs={{0,12},{2,14},{4,8},{6,10},{8,4},{10,6},{12,0},{14,2},{16,28},{18,... | collective-permute-start | bytes 786440 | tf_op jit(solution)/shard_map/ppermute | solution.py:314
  87.4 3.0 %collective-permute-done.25.come_ref = bf16[2,128,512]{2,1,0:T(8,128)(2,1)S(1)} collective-permute-done((bf16[2,128,512]{2,1,0:T(8,128)(2,1)S(1)}, bf16[2,128,512]{2,1,0:T(8,128)(2,1)S(1)}, u32[]{:S(2)}, u32[]{:S(2)}) %collective-permute-start.25) | collective-permute-done | bytes 262176 | tf_op jit(solution)/shard_map/ppermute | solution.py:311
  90.4 2.1 %collective-permute-done.26.far_ref = bf16[2,128,512]{2,1,0:T(8,128)(2,1)S(1)} collective-permute-done((bf16[2,128,512]{2,1,0:T(8,128)(2,1)S(1)}, bf16[2,128,512]{2,1,0:T(8,128)(2,1)S(1)}, u32[]{:S(2)}, u32[]{:S(2)}) %collective-permute-start.26) | collective-permute-done | bytes 262176 | tf_op jit(solution)/shard_map/ppermute | solution.py:314
  93.4 1.6 %collective-permute-done.22.come_ref = bf16[2,128,512]{2,1,0:T(8,128)(2,1)S(1)} collective-permute-done((bf16[2,128,512]{2,1,0:T(8,128)(2,1)S(1)}, bf16[2,128,512]{2,1,0:T(8,128)(2,1)S(1)}, u32[]{:S(2)}, u32[]{:S(2)}) %collective-permute-start.22) | collective-permute-done | bytes 262176 | tf_op jit(solution)/shard_map/ppermute | solution.py:311
  95.0 1.4 %collective-permute-done.23.far_ref = bf16[2,128,512]{2,1,0:T(8,128)(2,1)S(1)} collective-permute-done((bf16[2,128,512]{2,1,0:T(8,128)(2,1)S(1)}, bf16[2,128,512]{2,1,0:T(8,128)(2,1)S(1)}, u32[]{:S(2)}, u32[]{:S(2)}) %collective-permute-start.23) | collective-permute-done | bytes 262176 | tf_op jit(solution)/shard_map/ppermute | solution.py:314
  (50 shorter events, 15.3 us)
Async XLA Ops:
  0.0 9.2 %copy-start.2 = (s32[8,2]{0,1:T(2,128)S(1)}, s32[8,2]{0,1:T(2,128)}, u32[]{:S(2)}) copy-start(s32[8,2]{0,1:T(2,128)} %param.9) | copy-start | bytes 196
  0.0 9.2 %copy-start = (bf16[8,2,256,256]{3,2,1,0:T(8,128)(2,1)S(1)}, bf16[8,2,256,256]{3,2,1,0:T(8,128)(2,1)}, u32[]{:S(2)}) copy-start(bf16[8,2,256,256]{3,2,1,0:T(8,128)(2,1)} %exit_ref.1) | copy-start | bytes 6291460
  1.6 14.3 %collective-permute-start.8 = (bf16[2,128,512]{2,1,0:T(8,128)(2,1)S(1)}, bf16[2,128,512]{2,1,0:T(8,128)(2,1)S(1)}, u32[]{:S(2)}, u32[]{:S(2)}) collective-permute-start(bf16[2,128,512]{2,1,0:T(8,128)(2,1)S(1)} %pad_maximum_fusion.mine_ref), channel_id=1, source_target_pairs={{0,12},{2,14},{4,8},{6,10},{8,4},{10,6},{12,0},{14,2},{16,28},{18,... | collective-permute-start | bytes 786440 | tf_op jit(solution)/shard_map/ppermute | solution.py:314
  5.6 9.2 %collective-permute-start = (bf16[2,128,512]{2,1,0:T(8,128)(2,1)S(1)}, bf16[2,128,512]{2,1,0:T(8,128)(2,1)S(1)}, u32[]{:S(2)}, u32[]{:S(2)}) collective-permute-start(bf16[2,128,512]{2,1,0:T(8,128)(2,1)S(1)} %pad_maximum_fusion.mine_ref), channel_id=1, source_target_pairs={{0,1},{1,0},{2,3},{3,2},{4,5},{5,4},{6,7},{7,6},{8,9},{9,8},{10,11... | collective-permute-start | bytes 786440 | tf_op jit(solution)/shard_map/ppermute | solution.py:311
  8.5 11.9 %collective-permute-start.2 = (bf16[2,128,512]{2,1,0:T(8,128)(2,1)S(1)}, bf16[2,128,512]{2,1,0:T(8,128)(2,1)S(1)}, u32[]{:S(2)}, u32[]{:S(2)}) collective-permute-start(bf16[2,128,512]{2,1,0:T(8,128)(2,1)S(1)} %pad_maximum_fusion.1.mine_ref), channel_id=1, source_target_pairs={{0,1},{1,0},{2,3},{3,2},{4,5},{5,4},{6,7},{7,6},{8,9},{9,8},{10,11... | collective-permute-start | bytes 786440 | tf_op jit(solution)/shard_map/ppermute | solution.py:311
  9.1 12.4 %collective-permute-start.1 = (bf16[2,128,512]{2,1,0:T(8,128)(2,1)S(1)}, bf16[2,128,512]{2,1,0:T(8,128)(2,1)S(1)}, u32[]{:S(2)}, u32[]{:S(2)}) collective-permute-start(bf16[2,128,512]{2,1,0:T(8,128)(2,1)S(1)} %pad_maximum_fusion.1.mine_ref), channel_id=1, source_target_pairs={{0,12},{2,14},{4,8},{6,10},{8,4},{10,6},{12,0},{14,2},{16,28},{18,... | collective-permute-start | bytes 786440 | tf_op jit(solution)/shard_map/ppermute | solution.py:314
  10.4 22.1 %copy-start.1 = (bf16[1,8,2,256,256]{4,3,2,1,0:T(8,128)(2,1)S(1)}, bf16[1,8,2,256,256]{4,3,2,1,0:T(8,128)(2,1)}, u32[]{:S(2)}) copy-start(bf16[1,8,2,256,256]{4,3,2,1,0:T(8,128)(2,1)} %param.7) | copy-start | bytes 6291460
  15.9 10.2 %collective-permute-start.9 = (bf16[2,128,512]{2,1,0:T(8,128)(2,1)S(1)}, bf16[2,128,512]{2,1,0:T(8,128)(2,1)S(1)}, u32[]{:S(2)}, u32[]{:S(2)}) collective-permute-start(bf16[2,128,512]{2,1,0:T(8,128)(2,1)S(1)} %collective-permute-done.8.mine_ref), channel_id=1, source_target_pairs={{0,1},{1,0},{2,3},{3,2},{4,5},{5,4},{6,7},{7,6},{8,9},{9,8},{10,11... | collective-permute-start | bytes 786440 | tf_op jit(solution)/shard_map/ppermute | solution.py:311
  21.6 8.7 %collective-permute-start.11 = (bf16[2,128,512]{2,1,0:T(8,128)(2,1)S(1)}, bf16[2,128,512]{2,1,0:T(8,128)(2,1)S(1)}, u32[]{:S(2)}, u32[]{:S(2)}) collective-permute-start(bf16[2,128,512]{2,1,0:T(8,128)(2,1)S(1)} %collective-permute-done.1.mine_ref), channel_id=1, source_target_pairs={{0,1},{1,0},{2,3},{3,2},{4,5},{5,4},{6,7},{7,6},{8,9},{9,8},{10,11... | collective-permute-start | bytes 786440 | tf_op jit(solution)/shard_map/ppermute | solution.py:311
  23.1 8.9 %collective-permute-start.3 = (bf16[2,256,256]{2,1,0:T(8,128)(2,1)S(1)}, bf16[2,256,256]{2,1,0:T(8,128)(2,1)S(1)}, u32[]{:S(2)}, u32[]{:S(2)}) collective-permute-start(bf16[2,256,256]{2,1,0:T(8,128)(2,1)S(1)} %get-tuple-element.94), channel_id=1, source_target_pairs={{0,4},{2,6},{4,0},{6,2},{8,12},{10,14},{12,8},{14,10},{16,20},{18,... | collective-permute-start | bytes 786440 | tf_op jit(solution)/shard_map/ppermute | solution.py:314
  23.6 8.7 %collective-permute-start.4 = (bf16[2,256,256]{2,1,0:T(8,128)(2,1)S(1)}, bf16[2,256,256]{2,1,0:T(8,128)(2,1)S(1)}, u32[]{:S(2)}, u32[]{:S(2)}) collective-permute-start(bf16[2,256,256]{2,1,0:T(8,128)(2,1)S(1)} %get-tuple-element.95), channel_id=1, source_target_pairs={{0,8},{2,10},{4,12},{6,14},{8,0},{10,2},{12,4},{14,6},{16,24},{18,... | collective-permute-start | bytes 786440 | tf_op jit(solution)/shard_map/ppermute | solution.py:314
  24.1 11.0 %collective-permute-start.5 = (bf16[2,256,256]{2,1,0:T(8,128)(2,1)S(1)}, bf16[2,256,256]{2,1,0:T(8,128)(2,1)S(1)}, u32[]{:S(2)}, u32[]{:S(2)}) collective-permute-start(bf16[2,256,256]{2,1,0:T(8,128)(2,1)S(1)} %get-tuple-element.96), channel_id=1, source_target_pairs={{0,6},{2,4},{4,2},{6,0},{8,14},{10,12},{12,10},{14,8},{16,22},{18,... | collective-permute-start | bytes 786440 | tf_op jit(solution)/shard_map/ppermute | solution.py:314
  26.1 9.7 %collective-permute-start.6 = (bf16[2,256,256]{2,1,0:T(8,128)(2,1)S(1)}, bf16[2,256,256]{2,1,0:T(8,128)(2,1)S(1)}, u32[]{:S(2)}, u32[]{:S(2)}) collective-permute-start(bf16[2,256,256]{2,1,0:T(8,128)(2,1)S(1)} %get-tuple-element.97), channel_id=1, source_target_pairs={{0,10},{2,8},{4,14},{6,12},{8,2},{10,0},{12,6},{14,4},{16,26},{18,... | collective-permute-start | bytes 786440 | tf_op jit(solution)/shard_map/ppermute | solution.py:314
  30.2 5.6 %collective-permute-start.7 = (bf16[2,256,256]{2,1,0:T(8,128)(2,1)S(1)}, bf16[2,256,256]{2,1,0:T(8,128)(2,1)S(1)}, u32[]{:S(2)}, u32[]{:S(2)}) collective-permute-start(bf16[2,256,256]{2,1,0:T(8,128)(2,1)S(1)} %get-tuple-element.98), channel_id=1, source_target_pairs={{0,2},{2,0},{4,6},{6,4},{8,10},{10,8},{12,14},{14,12},{16,18},{18,... | collective-permute-start | bytes 786440 | tf_op jit(solution)/shard_map/ppermute | solution.py:314
  32.0 3.8 %collective-permute-start.10 = (bf16[2,128,256]{2,1,0:T(8,128)(2,1)S(1)}, bf16[2,128,256]{2,1,0:T(8,128)(2,1)S(1)}, u32[]{:S(2)}, u32[]{:S(2)}) collective-permute-start(bf16[2,128,256]{2,1,0:T(8,128)(2,1)S(1)} %get-tuple-element.100), channel_id=1, source_target_pairs={{0,2},{2,0},{4,6},{6,4},{8,10},{10,8},{12,14},{14,12},{16,18},{18,... | collective-permute-start | bytes 393224 | tf_op jit(solution)/shard_map/ppermute | solution.py:314
  32.3 3.5 %collective-permute-start.12 = (bf16[2,128,256]{2,1,0:T(8,128)(2,1)S(1)}, bf16[2,128,256]{2,1,0:T(8,128)(2,1)S(1)}, u32[]{:S(2)}, u32[]{:S(2)}) collective-permute-start(bf16[2,128,256]{2,1,0:T(8,128)(2,1)S(1)} %get-tuple-element.103), channel_id=1, source_target_pairs={{0,2},{2,0},{4,6},{6,4},{8,10},{10,8},{12,14},{14,12},{16,18},{18,... | collective-permute-start | bytes 393224 | tf_op jit(solution)/shard_map/ppermute | solution.py:314
  35.1 15.1 %collective-permute-start.14 = (bf16[2,2,256,256]{3,2,1,0:T(8,128)(2,1)S(1)}, bf16[2,2,256,256]{3,2,1,0:T(8,128)(2,1)S(1)}, u32[]{:S(2)}, u32[]{:S(2)}) collective-permute-start(bf16[2,2,256,256]{3,2,1,0:T(8,128)(2,1)S(1)} %get-tuple-element.106), channel_id=1, source_target_pairs={{0,12},{2,14},{4,8},{6,10},{8,4},{10,6},{12,0},{14,2},{16,28},{18,... | collective-permute-start | bytes 1572872 | tf_op jit(solution)/shard_map/ppermute | solution.py:314
  41.0 16.6 %collective-permute-start.13 = (bf16[2,256,256]{2,1,0:T(8,128)(2,1)S(1)}, bf16[2,256,256]{2,1,0:T(8,128)(2,1)S(1)}, u32[]{:S(2)}, u32[]{:S(2)}) collective-permute-start(bf16[2,256,256]{2,1,0:T(8,128)(2,1)S(1)} %get-tuple-element.104), channel_id=1, source_target_pairs={{16,8},{18,10},{20,12},{22,14},{24,0},{26,2},{28,4},{30,6},{17,9},... | collective-permute-start | bytes 786440 | tf_op jit(solution)/shard_map/ppermute | solution.py:360
  62.8 2.1 %collective-permute-start.18 = (bf16[2,256,256]{2,1,0:T(8,128)(2,1)S(1)}, bf16[2,256,256]{2,1,0:T(8,128)(2,1)S(1)}, u32[]{:S(2)}, u32[]{:S(2)}) collective-permute-start(bf16[2,256,256]{2,1,0:T(8,128)(2,1)S(1)} %get-tuple-element.115), channel_id=1, source_target_pairs={{0,2},{2,0},{4,6},{6,4},{8,10},{10,8},{12,14},{14,12},{16,18},{18,... | collective-permute-start | bytes 786440 | tf_op jit(solution)/shard_map/ppermute | solution.py:314
  62.9 8.7 %collective-permute-start.20 = (bf16[2,256,256]{2,1,0:T(8,128)(2,1)S(1)}, bf16[2,256,256]{2,1,0:T(8,128)(2,1)S(1)}, u32[]{:S(2)}, u32[]{:S(2)}) collective-permute-start(bf16[2,256,256]{2,1,0:T(8,128)(2,1)S(1)} %get-tuple-element.119), channel_id=1, source_target_pairs={{0,4},{2,6},{4,0},{6,2},{8,12},{10,14},{12,8},{14,10},{16,20},{18,... | collective-permute-start | bytes 786440 | tf_op jit(solution)/shard_map/ppermute | solution.py:314
  63.8 8.4 %collective-permute-start.21 = (bf16[2,256,256]{2,1,0:T(8,128)(2,1)S(1)}, bf16[2,256,256]{2,1,0:T(8,128)(2,1)S(1)}, u32[]{:S(2)}, u32[]{:S(2)}) collective-permute-start(bf16[2,256,256]{2,1,0:T(8,128)(2,1)S(1)} %get-tuple-element.120), channel_id=1, source_target_pairs={{0,8},{2,10},{4,12},{6,14},{8,0},{10,2},{12,4},{14,6},{16,24},{18,... | collective-permute-start | bytes 786440 | tf_op jit(solution)/shard_map/ppermute | solution.py:314
  65.8 9.3 %collective-permute-start.24 = (bf16[2,128,512]{2,1,0:T(8,128)(2,1)S(1)}, bf16[2,128,512]{2,1,0:T(8,128)(2,1)S(1)}, u32[]{:S(2)}, u32[]{:S(2)}) collective-permute-start(bf16[2,128,512]{2,1,0:T(8,128)(2,1)S(1)} %get-tuple-element.126), channel_id=1, source_target_pairs={{0,1},{1,0},{2,3},{3,2},{4,5},{5,4},{6,7},{7,6},{8,9},{9,8},{10,11... | collective-permute-start | bytes 786440 | tf_op jit(solution)/shard_map/ppermute | solution.py:311
  68.3 11.3 %collective-permute-start.19 = (bf16[2,128,512]{2,1,0:T(8,128)(2,1)S(1)}, bf16[2,128,512]{2,1,0:T(8,128)(2,1)S(1)}, u32[]{:S(2)}, u32[]{:S(2)}) collective-permute-start(bf16[2,128,512]{2,1,0:T(8,128)(2,1)S(1)} %get-tuple-element.117), channel_id=1, source_target_pairs={{0,1},{1,0},{2,3},{3,2},{4,5},{5,4},{6,7},{7,6},{8,9},{9,8},{10,11... | collective-permute-start | bytes 786440 | tf_op jit(solution)/shard_map/ppermute | solution.py:311
  68.9 10.8 %collective-permute-start.15 = (bf16[2,256,256]{2,1,0:T(8,128)(2,1)S(1)}, bf16[2,256,256]{2,1,0:T(8,128)(2,1)S(1)}, u32[]{:S(2)}, u32[]{:S(2)}) collective-permute-start(bf16[2,256,256]{2,1,0:T(8,128)(2,1)S(1)} %get-tuple-element.110), channel_id=1, source_target_pairs={{0,6},{2,4},{4,2},{6,0},{8,14},{10,12},{12,10},{14,8},{16,22},{18,... | collective-permute-start | bytes 786440 | tf_op jit(solution)/shard_map/ppermute | solution.py:314
  71.6 8.4 %collective-permute-start.16 = (bf16[2,256,256]{2,1,0:T(8,128)(2,1)S(1)}, bf16[2,256,256]{2,1,0:T(8,128)(2,1)S(1)}, u32[]{:S(2)}, u32[]{:S(2)}) collective-permute-start(bf16[2,256,256]{2,1,0:T(8,128)(2,1)S(1)} %get-tuple-element.111), channel_id=1, source_target_pairs={{0,10},{2,8},{4,14},{6,12},{8,2},{10,0},{12,6},{14,4},{16,26},{18,... | collective-permute-start | bytes 786440 | tf_op jit(solution)/shard_map/ppermute | solution.py:314
  72.2 7.9 %collective-permute-start.17 = (bf16[2,256,256]{2,1,0:T(8,128)(2,1)S(1)}, bf16[2,256,256]{2,1,0:T(8,128)(2,1)S(1)}, u32[]{:S(2)}, u32[]{:S(2)}) collective-permute-start(bf16[2,256,256]{2,1,0:T(8,128)(2,1)S(1)} %get-tuple-element.112), channel_id=1, source_target_pairs={{0,2},{2,0},{4,6},{6,4},{8,10},{10,8},{12,14},{14,12},{16,18},{18,... | collective-permute-start | bytes 786440 | tf_op jit(solution)/shard_map/ppermute | solution.py:314
  81.2 9.2 %collective-permute-start.25 = (bf16[2,128,512]{2,1,0:T(8,128)(2,1)S(1)}, bf16[2,128,512]{2,1,0:T(8,128)(2,1)S(1)}, u32[]{:S(2)}, u32[]{:S(2)}) collective-permute-start(bf16[2,128,512]{2,1,0:T(8,128)(2,1)S(1)} %get-tuple-element.129), channel_id=1, source_target_pairs={{0,1},{1,0},{2,3},{3,2},{4,5},{5,4},{6,7},{7,6},{8,9},{9,8},{10,11... | collective-permute-start | bytes 786440 | tf_op jit(solution)/shard_map/ppermute | solution.py:311
  82.4 10.1 %collective-permute-start.26 = (bf16[2,128,512]{2,1,0:T(8,128)(2,1)S(1)}, bf16[2,128,512]{2,1,0:T(8,128)(2,1)S(1)}, u32[]{:S(2)}, u32[]{:S(2)}) collective-permute-start(bf16[2,128,512]{2,1,0:T(8,128)(2,1)S(1)} %add_convert_fusion), channel_id=1, source_target_pairs={{0,12},{2,14},{4,8},{6,10},{8,4},{10,6},{12,0},{14,2},{16,28},{18,... | collective-permute-start | bytes 786440 | tf_op jit(solution)/shard_map/ppermute | solution.py:314
  85.3 9.8 %collective-permute-start.22 = (bf16[2,128,512]{2,1,0:T(8,128)(2,1)S(1)}, bf16[2,128,512]{2,1,0:T(8,128)(2,1)S(1)}, u32[]{:S(2)}, u32[]{:S(2)}) collective-permute-start(bf16[2,128,512]{2,1,0:T(8,128)(2,1)S(1)} %get-tuple-element.123), channel_id=1, source_target_pairs={{0,1},{1,0},{2,3},{3,2},{4,5},{5,4},{6,7},{7,6},{8,9},{9,8},{10,11... | collective-permute-start | bytes 786440 | tf_op jit(solution)/shard_map/ppermute | solution.py:311
  85.9 10.6 %collective-permute-start.23 = (bf16[2,128,512]{2,1,0:T(8,128)(2,1)S(1)}, bf16[2,128,512]{2,1,0:T(8,128)(2,1)S(1)}, u32[]{:S(2)}, u32[]{:S(2)}) collective-permute-start(bf16[2,128,512]{2,1,0:T(8,128)(2,1)S(1)} %add_convert_fusion.1), channel_id=1, source_target_pairs={{0,12},{2,14},{4,8},{6,10},{8,4},{10,6},{12,0},{14,2},{16,28},{18,... | collective-permute-start | bytes 786440 | tf_op jit(solution)/shard_map/ppermute | solution.py:314

commit v13 on v12

--- a/solution.py
+++ b/solution.py
@@ -231,7 +231,10 @@
         spread_ref[...] = refs[-1][own ^ apart]
 
 
-def add_kernel(base, count, picks, begun, ends, corner_ref, wave_ref, *refs):
+def add_kernel(base, count, picks, begun, ends, corner_ref, *refs):
+    more = 1 if refs[0].shape[0] == count else 2
+    wave_refs, refs = refs[:more], refs[more:]
+    wave_ref = wave_refs[0]
     spread_refs, refs = refs[: len(picks)], refs[len(picks) :]
     window = wave_ref.shape[-1]
     rows = window // chunk_count
@@ -245,9 +248,13 @@
         sums = [refs[0][i, rows_at, :] if begun else jnp.zeros((tall, window), f32) for i in range(8)]
         for apart, spread_ref in zip(picks, spread_refs):
             position = position_at(own ^ apart, count)
-            slot = position if wave_ref.shape[0] == count else apart
+            slot = position if more == 1 else apart
             in_mine, in_left = first_masks(corner_ref, position, base + at, (tall, window))
             wave_re, wave_im = (wave_ref[slot, part, here, :].astype(f32) for part in range(2))
+            if more == 2:
+                in_last = jnp.full((tall, window), lax.axis_index("sec").astype(jnp.int32), jnp.int32) < count
+                wave_re = jnp.where(in_last, wave_re, wave_refs[1][slot, 0, here, :].astype(f32))
+                wave_im = jnp.where(in_last, wave_im, wave_refs[1][slot, 1, here, :].astype(f32))
             spread_re, spread_im = (spread_ref[part, here, :].astype(f32) for part in range(2))
             parts = (
                 wave_re * spread_re + wave_im * spread_im,
@@ -307,6 +314,11 @@
     wave = (2, window, window)
     corners = offsets.T
 
+    def far_permute(value, in_last):
+        return lax.ppermute(
+            value, "sec", [(s, s ^ (count - far) if (s < count) == in_last else s) for s in range(sections)]
+        )
+
     def to_other_half(value):
         return lax.ppermute(value, "scan", [(0, 1), (1, 0)])
 
@@ -354,13 +366,13 @@
     cost = (count * 16 * window**3, count * 2 * window**2)
     first = call(first_kernel, [shape_of(wave, bf16), shape_of((count,) + wave, bf16)], cost=cost, grant=12)
     start, waves, given = lax.optimization_barrier((start, waves, given))
-    far_waves = to_distance(given, count - far)
+    far_waves = [far_permute(given, True)]
     leave, held = first(start, down, across, *windows)
     for stage in range(1, group_count):
         come = lax.ppermute(
             leave, "sec", [(s, (s - count) ^ (count // 2)) for s in range(count, sections)]
         )
-        come, waves, far_waves = lax.optimization_barrier((come, waves, far_waves))
+        come, waves, far_waves, given = lax.optimization_barrier((come, waves, far_waves, given))
         is_last = stage == group_count - 1
         through = call(
             functools.partial(next_kernel, is_last),
@@ -374,8 +386,9 @@
     def add(c, wave_set, picks, spreads, sums, ends):
         kernel = functools.partial(add_kernel, c * rows, count, picks, bool(sums), ends)
         given = [shape_of(piece, f32), shape_of(piece, bf16)] if ends else shape_of((8, rows, window), f32)
-        return call(kernel, given, prefetch=1)(corners, wave_set, *spreads, *sums)
-
+        return call(kernel, given, prefetch=1)(corners, *wave_set, *spreads, *sums)
+
+    far_waves.append(far_permute(given, False))
     far_kept, far_given = leave[count - far :]
     far_spreads = [far_kept, to_distance(far_given, 1)]
     came = exchange(leave[: count - far])
@@ -386,12 +399,12 @@
 
     order = distances(count)
     cut_at = count // 2 - 1
-    early = [add(c, waves, order[:cut_at], came[:cut_at], [], False) for c in chunks]
+    early = [add(c, [waves], order[:cut_at], came[:cut_at], [], False) for c in chunks]
     result = []
     for c in chunks:
         half_sums[c], early[c] = lax.optimization_barrier((half_sums[c], early[c]))
         far_come = to_distance(half_sums[c], count - far)
-        keep, away = add(c, waves, order[cut_at : count - far], came[cut_at:], [early[c]], True)
+        keep, away = add(c, [waves], order[cut_at : count - far], came[cut_at:], [early[c]], True)
         result.append((keep, to_other_half(away), far_come))
     out = []
     for c in chunks:

time: 97.5 us -> 103 us (1.056)
  the two profiles are of different devices: /device:TPU:0 before, /device:TPU:16 now
where the time goes in v13:
time: 103 us
  waiting for transfers between devices  44.8 us (43%)
  starting transfers between devices  29.6 us (29%)
  Pallas kernels  25.5 us (25%)
  other arithmetic  3.12 us (3%)
    pallas_call x14, Pallas kernels, run(): pl.pallas_call(kernel, grid_spec=pltpu.PrefetchScalarGridSpec(num_scalar_...  23.7 us
    ppermute x8, waiting for transfers between devices, to_other_half(): return lax.ppermute(value, 'scan', [(0, 1), (1, 0)])  22 us
    ppermute x17, starting transfers between devices, to_distance(): return lax.ppermute(value, 'sec', [(s, s ^ d) for s in range(sections)])  12.5 us
    ppermute x1, waiting for transfers between devices, on_device(): lax.ppermute(leave, 'sec', [(s, s - count ^ count // 2) for s in range(co...  11.5 us
    ppermute x8, starting transfers between devices, to_other_half(): return lax.ppermute(value, 'scan', [(0, 1), (1, 0)])  9.89 us
    ppermute x2, waiting for transfers between devices, far_permute(): lax.ppermute(value, 'sec', [(s, s ^ count - far if (s < count) == in_last...  6.73 us
    ppermute x17, waiting for transfers between devices, to_distance(): return lax.ppermute(value, 'sec', [(s, s ^ d) for s in range(sections)])  4.54 us
    ppermute x1, starting transfers between devices, on_device(): lax.ppermute(leave, 'sec', [(s, s - count ^ count // 2) for s in range(co...  4.43 us
  transfers between devices with their start and end apart: 28, of which 14 were waited for; matrix products, arithmetic and copies ran while one was open for 2% of the time, Pallas kernels for 23%

profile of v13, /device:TPU:16, one launch (start us, length us, event | category | flops | bytes accessed | tf_op | source)
XLA Modules:
  0.0 103.2 jit_solution(9457589260904410245)
XLA Ops:
  0.0 1.5 %fusion.4 = (bf16[1,128,512]{2,1,0:T(8,128)(2,1)S(1)}, bf16[1,128,512]{2,1,0:T(8,128)(2,1)S(1)}) fusion(f32[1,256,512]{2,1,0:T(8,128)} %param.5, f32[1,256,512]{2,1,0:T(8,128)} %param.6), kind=kLoop, calls=%fused_computation.10 | loop fusion | flops 2424832 | bytes 786432 | tf_op jit(solution)/shard_map/convert_element_type | solution.py:66
  1.6 2.6 %collective-permute-start.8 = (bf16[2,128,512]{2,1,0:T(8,128)(2,1)S(1)}, bf16[2,128,512]{2,1,0:T(8,128)(2,1)S(1)}, u32[]{:S(2)}, u32[]{:S(2)}) collective-permute-start(bf16[2,128,512]{2,1,0:T(8,128)(2,1)S(1)} %pad_maximum_fusion.mine_ref), channel_id=1, source_target_pairs={{0,12},{2,14},{4,8},{6,10},{8,4},{10,6},{12,0},{14,2},{16,28},{18,... | collective-permute-start | bytes 786440 | tf_op jit(solution)/shard_map/ppermute | solution.py:326
  4.2 1.5 %collective-permute-start = (bf16[2,128,512]{2,1,0:T(8,128)(2,1)S(1)}, bf16[2,128,512]{2,1,0:T(8,128)(2,1)S(1)}, u32[]{:S(2)}, u32[]{:S(2)}) collective-permute-start(bf16[2,128,512]{2,1,0:T(8,128)(2,1)S(1)} %pad_maximum_fusion.mine_ref), channel_id=1, source_target_pairs={{0,1},{1,0},{2,3},{3,2},{4,5},{5,4},{6,7},{7,6},{8,9},{9,8},{10,11... | collective-permute-start | bytes 786440 | tf_op jit(solution)/shard_map/ppermute | solution.py:323
  5.7 1.4 %fusion.13 = (bf16[1,128,512]{2,1,0:T(8,128)(2,1)S(1)}, bf16[1,128,512]{2,1,0:T(8,128)(2,1)S(1)}) fusion(f32[1,256,512]{2,1,0:T(8,128)} %param.5, f32[1,256,512]{2,1,0:T(8,128)} %param.6), kind=kLoop, calls=%fused_computation.19 | loop fusion | flops 2424832 | bytes 786432 | tf_op jit(solution)/shard_map/convert_element_type | solution.py:66
  8.1 1.2 %shard_map.55 = (bf16[2,256,256]{2,1,0:T(8,128)(2,1)S(1)}, bf16[256,256]{1,0:T(8,128)(2,1)S(1)}, bf16[256,256]{1,0:T(8,128)(2,1)S(1)}) custom-call(s32[2,8]{1,0:T(2,128)S(1)} %bitcast.4, bf16[8,2,256,256]{3,2,1,0:T(8,128)(2,1)S(1)} %copy-done), custom_call_target="tpu_custom_call" | custom-call | bytes 2621504 | tf_op jit(solution)/shard_map/pallas_call | solution.py:27
  9.3 4.1 %collective-permute-done.other_ref = bf16[2,128,512]{2,1,0:T(8,128)(2,1)S(1)} collective-permute-done((bf16[2,128,512]{2,1,0:T(8,128)(2,1)S(1)}, bf16[2,128,512]{2,1,0:T(8,128)(2,1)S(1)}, u32[]{:S(2)}, u32[]{:S(2)}) %collective-permute-start) | collective-permute-done | bytes 262176 | tf_op jit(solution)/shard_map/ppermute | solution.py:323
  14.4 1.6 %collective-permute-start.9 = (bf16[2,128,512]{2,1,0:T(8,128)(2,1)S(1)}, bf16[2,128,512]{2,1,0:T(8,128)(2,1)S(1)}, u32[]{:S(2)}, u32[]{:S(2)}) collective-permute-start(bf16[2,128,512]{2,1,0:T(8,128)(2,1)S(1)} %collective-permute-done.8.mine_ref), channel_id=1, source_target_pairs={{0,1},{1,0},{2,3},{3,2},{4,5},{5,4},{6,7},{7,6},{8,9},{9,8},{10,11... | collective-permute-start | bytes 786440 | tf_op jit(solution)/shard_map/ppermute | solution.py:323
  16.0 3.0 %collective-permute-done.2.other_ref = bf16[2,128,512]{2,1,0:T(8,128)(2,1)S(1)} collective-permute-done((bf16[2,128,512]{2,1,0:T(8,128)(2,1)S(1)}, bf16[2,128,512]{2,1,0:T(8,128)(2,1)S(1)}, u32[]{:S(2)}, u32[]{:S(2)}) %collective-permute-start.2) | collective-permute-done | bytes 262176 | tf_op jit(solution)/shard_map/ppermute | solution.py:323
  20.1 1.6 %collective-permute-start.11 = (bf16[2,128,512]{2,1,0:T(8,128)(2,1)S(1)}, bf16[2,128,512]{2,1,0:T(8,128)(2,1)S(1)}, u32[]{:S(2)}, u32[]{:S(2)}) collective-permute-start(bf16[2,128,512]{2,1,0:T(8,128)(2,1)S(1)} %collective-permute-done.1.mine_ref), channel_id=1, source_target_pairs={{0,1},{1,0},{2,3},{3,2},{4,5},{5,4},{6,7},{7,6},{8,9},{9,8},{10,11... | collective-permute-start | bytes 786440 | tf_op jit(solution)/shard_map/ppermute | solution.py:323
  22.6 2.0 %collective-permute-done.9.other_ref = bf16[2,128,512]{2,1,0:T(8,128)(2,1)S(1)} collective-permute-done((bf16[2,128,512]{2,1,0:T(8,128)(2,1)S(1)}, bf16[2,128,512]{2,1,0:T(8,128)(2,1)S(1)}, u32[]{:S(2)}, u32[]{:S(2)}) %collective-permute-start.9) | collective-permute-done | bytes 262176 | tf_op jit(solution)/shard_map/ppermute | solution.py:323
  25.4 3.3 %collective-permute-done.11.other_ref = bf16[2,128,512]{2,1,0:T(8,128)(2,1)S(1)} collective-permute-done((bf16[2,128,512]{2,1,0:T(8,128)(2,1)S(1)}, bf16[2,128,512]{2,1,0:T(8,128)(2,1)S(1)}, u32[]{:S(2)}, u32[]{:S(2)}) %collective-permute-start.11) | collective-permute-done | bytes 262176 | tf_op jit(solution)/shard_map/ppermute | solution.py:323
  31.1 2.5 %shard_map.56 = (bf16[8,2,256,256]{3,2,1,0:T(8,128)(2,1)S(1)}, bf16[2,2,256,256]{3,2,1,0:T(8,128)(2,1)S(1)}) custom-call(s32[2,8]{1,0:T(2,128)S(1)} %bitcast.9, bf16[8,2,256,256]{3,2,1,0:T(8,128)(2,1)S(1)} %bitcast.3), custom_call_target="tpu_custom_call" | custom-call | bytes 4718656 | tf_op jit(solution)/shard_map/pallas_call | solution.py:27
  34.4 5.2 %shard_map.61 = (bf16[2,256,256]{2,1,0:T(8,128)(2,1)S(1)}, bf16[8,2,256,256]{3,2,1,0:T(8,128)(2,1)S(1)}) custom-call(bf16[2,256,256]{2,1,0:T(8,128)(2,1)S(1)} %get-tuple-element.75.start_ref, bf16[256,256]{1,0:T(8,128)(2,1)S(1)} %get-tuple-element.76.down_ref, bf16[256,256]{1,0:T(8,128)(2,1)S(1)} %get-tuple-element.77.across_ref, ...), custom_call_target="tpu_custom_call" | custom-call | flops 2147483648 | bytes 4980736 | tf_op jit(solution)/shard_map/pallas_call | solution.py:27
  39.6 4.4 %collective-permute-start.13 = (bf16[2,256,256]{2,1,0:T(8,128)(2,1)S(1)}, bf16[2,256,256]{2,1,0:T(8,128)(2,1)S(1)}, u32[]{:S(2)}, u32[]{:S(2)}) collective-permute-start(bf16[2,256,256]{2,1,0:T(8,128)(2,1)S(1)} %get-tuple-element.105), channel_id=1, source_target_pairs={{16,8},{18,10},{20,12},{22,14},{24,0},{26,2},{28,4},{30,6},{17,9},... | collective-permute-start | bytes 786440 | tf_op jit(solution)/shard_map/ppermute | solution.py:372
  44.0 11.5 %collective-permute-done.13.come_ref = bf16[2,256,256]{2,1,0:T(8,128)(2,1)S(1)} collective-permute-done((bf16[2,256,256]{2,1,0:T(8,128)(2,1)S(1)}, bf16[2,256,256]{2,1,0:T(8,128)(2,1)S(1)}, u32[]{:S(2)}, u32[]{:S(2)}) %collective-permute-start.13) | collective-permute-done | bytes 262176 | tf_op jit(solution)/shard_map/ppermute | solution.py:372
  55.6 2.1 %collective-permute-start.18 = (bf16[2,2,256,256]{3,2,1,0:T(8,128)(2,1)S(1)}, bf16[2,2,256,256]{3,2,1,0:T(8,128)(2,1)S(1)}, u32[]{:S(2)}, u32[]{:S(2)}) collective-permute-start(bf16[2,2,256,256]{3,2,1,0:T(8,128)(2,1)S(1)} %get-tuple-element.115), channel_id=1, source_target_pairs={{0,0},{2,2},{4,4},{6,6},{8,8},{10,10},{12,12},{14,14},{16,28},{18,... | collective-permute-start | bytes 1572872 | tf_op jit(solution)/shard_map/ppermute | solution.py:318
  57.6 5.2 %shard_map.62 = (bf16[2,256,256]{2,1,0:T(8,128)(2,1)S(1)}, bf16[2,256,256]{2,1,0:T(8,128)(2,1)S(1)}, bf16[2,256,256]{2,1,0:T(8,128)(2,1)S(1)}, bf16[2,256,256]{2...) custom-call(bf16[2,256,256]{2,1,0:T(8,128)(2,1)S(1)} %get-tuple-elem, ...), custom_call_target="tpu_custom_call" | custom-call | flops 2147483648 | bytes 4980736 | tf_op jit(solution)/shard_map/pallas_call | solution.py:27
  63.9 2.7 %collective-permute-start.22 = (bf16[2,256,256]{2,1,0:T(8,128)(2,1)S(1)}, bf16[2,256,256]{2,1,0:T(8,128)(2,1)S(1)}, u32[]{:S(2)}, u32[]{:S(2)}) collective-permute-start(bf16[2,256,256]{2,1,0:T(8,128)(2,1)S(1)} %get-tuple-element.122), channel_id=1, source_target_pairs={{0,8},{2,10},{4,12},{6,14},{8,0},{10,2},{12,4},{14,6},{16,24},{18,... | collective-permute-start | bytes 786440 | tf_op jit(solution)/shard_map/ppermute | solution.py:326
  66.5 6.7 %collective-permute-done.18.refs_1_ = bf16[2,2,256,256]{3,2,1,0:T(8,128)(2,1)S(1)} collective-permute-done((bf16[2,2,256,256]{3,2,1,0:T(8,128)(2,1)S(1)}, bf16[2,2,256,256]{3,2,1,0:T(8,128)(2,1)S(1)}, u32[]{:S(2)}, u32[]{:S(2)}) %collective-permute-start.18) | collective-permute-done | bytes 524320 | tf_op jit(solution)/shard_map/ppermute | solution.py:318
  76.0 1.3 %collective-permute-start.20 = (bf16[2,128,512]{2,1,0:T(8,128)(2,1)S(1)}, bf16[2,128,512]{2,1,0:T(8,128)(2,1)S(1)}, u32[]{:S(2)}, u32[]{:S(2)}) collective-permute-start(bf16[2,128,512]{2,1,0:T(8,128)(2,1)S(1)} %get-tuple-element.119), channel_id=1, source_target_pairs={{0,1},{1,0},{2,3},{3,2},{4,5},{5,4},{6,7},{7,6},{8,9},{9,8},{10,11... | collective-permute-start | bytes 786440 | tf_op jit(solution)/shard_map/ppermute | solution.py:323
  80.3 1.9 %collective-permute-done.25 = bf16[2,128,512]{2,1,0:T(8,128)(2,1)S(1)} collective-permute-done((bf16[2,128,512]{2,1,0:T(8,128)(2,1)S(1)}, bf16[2,128,512]{2,1,0:T(8,128)(2,1)S(1)}, u32[]{:S(2)}, u32[]{:S(2)}) %collective-permute-start.25) | collective-permute-done | bytes 262176 | tf_op jit(solution)/shard_map/ppermute | solution.py:323
  82.2 2.7 %collective-permute-done.20 = bf16[2,128,512]{2,1,0:T(8,128)(2,1)S(1)} collective-permute-done((bf16[2,128,512]{2,1,0:T(8,128)(2,1)S(1)}, bf16[2,128,512]{2,1,0:T(8,128)(2,1)S(1)}, u32[]{:S(2)}, u32[]{:S(2)}) %collective-permute-start.20) | collective-permute-done | bytes 262176 | tf_op jit(solution)/shard_map/ppermute | solution.py:323
  85.2 1.1 %shard_map.68 = (f32[2,128,512]{2,1,0:T(8,128)S(1)}, bf16[2,128,512]{2,1,0:T(8,128)(2,1)S(1)}) custom-call(s32[2,8]{1,0:T(2,128)S(1)} %bitcast.14, bf16[8,2,256,256]{3,2,1,0:T(8,128)(2,1)S(1)} %get-tuple-element.108.refs_0_, bf16[2,256,256]{2,1,0:T(8,128)(2,1)S(1)} %collective-permute-done.15.refs_1_, ...), custom_call_target="tpu_custom_call" | custom-call | bytes 4718656 | tf_op jit(solution)/shard_map/pallas_call | solution.py:27
  86.3 1.4 %collective-permute-start.26 = (bf16[2,128,512]{2,1,0:T(8,128)(2,1)S(1)}, bf16[2,128,512]{2,1,0:T(8,128)(2,1)S(1)}, u32[]{:S(2)}, u32[]{:S(2)}) collective-permute-start(bf16[2,128,512]{2,1,0:T(8,128)(2,1)S(1)} %get-tuple-element.131), channel_id=1, source_target_pairs={{0,1},{1,0},{2,3},{3,2},{4,5},{5,4},{6,7},{7,6},{8,9},{9,8},{10,11... | collective-permute-start | bytes 786440 | tf_op jit(solution)/shard_map/ppermute | solution.py:323
  87.8 1.2 %collective-permute-start.27 = (bf16[2,128,512]{2,1,0:T(8,128)(2,1)S(1)}, bf16[2,128,512]{2,1,0:T(8,128)(2,1)S(1)}, u32[]{:S(2)}, u32[]{:S(2)}) collective-permute-start(bf16[2,128,512]{2,1,0:T(8,128)(2,1)S(1)} %add_convert_fusion), channel_id=1, source_target_pairs={{0,12},{2,14},{4,8},{6,10},{8,4},{10,6},{12,0},{14,2},{16,28},{18,... | collective-permute-start | bytes 786440 | tf_op jit(solution)/shard_map/ppermute | solution.py:326
  89.0 1.1 %shard_map.65 = (f32[2,128,512]{2,1,0:T(8,128)S(1)}, bf16[2,128,512]{2,1,0:T(8,128)(2,1)S(1)}) custom-call(s32[2,8]{1,0:T(2,128)S(1)} %bitcast.15, bf16[8,2,256,256]{3,2,1,0:T(8,128)(2,1)S(1)} %get-tuple-element.108.refs_0_, bf16[2,256,256]{2,1,0:T(8,128)(2,1)S(1)} %collective-permute-done.15.refs_1_, ...), custom_call_target="tpu_custom_call" | custom-call | bytes 4718656 | tf_op jit(solution)/shard_map/pallas_call | solution.py:27
  90.1 1.1 %collective-permute-start.23 = (bf16[2,128,512]{2,1,0:T(8,128)(2,1)S(1)}, bf16[2,128,512]{2,1,0:T(8,128)(2,1)S(1)}, u32[]{:S(2)}, u32[]{:S(2)}) collective-permute-start(bf16[2,128,512]{2,1,0:T(8,128)(2,1)S(1)} %get-tuple-element.125), channel_id=1, source_target_pairs={{0,1},{1,0},{2,3},{3,2},{4,5},{5,4},{6,7},{7,6},{8,9},{9,8},{10,11... | collective-permute-start | bytes 786440 | tf_op jit(solution)/shard_map/ppermute | solution.py:323
  91.2 1.3 %collective-permute-start.24 = (bf16[2,128,512]{2,1,0:T(8,128)(2,1)S(1)}, bf16[2,128,512]{2,1,0:T(8,128)(2,1)S(1)}, u32[]{:S(2)}, u32[]{:S(2)}) collective-permute-start(bf16[2,128,512]{2,1,0:T(8,128)(2,1)S(1)} %add_convert_fusion.1), channel_id=1, source_target_pairs={{0,12},{2,14},{4,8},{6,10},{8,4},{10,6},{12,0},{14,2},{16,28},{18,... | collective-permute-start | bytes 786440 | tf_op jit(solution)/shard_map/ppermute | solution.py:326
  92.5 3.0 %collective-permute-done.26.come_ref = bf16[2,128,512]{2,1,0:T(8,128)(2,1)S(1)} collective-permute-done((bf16[2,128,512]{2,1,0:T(8,128)(2,1)S(1)}, bf16[2,128,512]{2,1,0:T(8,128)(2,1)S(1)}, u32[]{:S(2)}, u32[]{:S(2)}) %collective-permute-start.26) | collective-permute-done | bytes 262176 | tf_op jit(solution)/shard_map/ppermute | solution.py:323
  95.5 2.4 %collective-permute-done.27.far_ref = bf16[2,128,512]{2,1,0:T(8,128)(2,1)S(1)} collective-permute-done((bf16[2,128,512]{2,1,0:T(8,128)(2,1)S(1)}, bf16[2,128,512]{2,1,0:T(8,128)(2,1)S(1)}, u32[]{:S(2)}, u32[]{:S(2)}) %collective-permute-start.27) | collective-permute-done | bytes 262176 | tf_op jit(solution)/shard_map/ppermute | solution.py:326
  98.7 1.9 %collective-permute-done.23.come_ref = bf16[2,128,512]{2,1,0:T(8,128)(2,1)S(1)} collective-permute-done((bf16[2,128,512]{2,1,0:T(8,128)(2,1)S(1)}, bf16[2,128,512]{2,1,0:T(8,128)(2,1)S(1)}, u32[]{:S(2)}, u32[]{:S(2)}) %collective-permute-start.23) | collective-permute-done | bytes 262176 | tf_op jit(solution)/shard_map/ppermute | solution.py:323
  100.7 1.7 %collective-permute-done.24.far_ref = bf16[2,128,512]{2,1,0:T(8,128)(2,1)S(1)} collective-permute-done((bf16[2,128,512]{2,1,0:T(8,128)(2,1)S(1)}, bf16[2,128,512]{2,1,0:T(8,128)(2,1)S(1)}, u32[]{:S(2)}, u32[]{:S(2)}) %collective-permute-start.24) | collective-permute-done | bytes 262176 | tf_op jit(solution)/shard_map/ppermute | solution.py:326
  (52 shorter events, 16.7 us)
Async XLA Ops:
  0.0 8.1 %copy-start.2 = (s32[8,2]{0,1:T(2,128)S(1)}, s32[8,2]{0,1:T(2,128)}, u32[]{:S(2)}) copy-start(s32[8,2]{0,1:T(2,128)} %param.9) | copy-start | bytes 196
  0.0 8.1 %copy-start = (bf16[8,2,256,256]{3,2,1,0:T(8,128)(2,1)S(1)}, bf16[8,2,256,256]{3,2,1,0:T(8,128)(2,1)}, u32[]{:S(2)}) copy-start(bf16[8,2,256,256]{3,2,1,0:T(8,128)(2,1)} %exit_ref.1) | copy-start | bytes 6291460
  1.6 12.9 %collective-permute-start.8 = (bf16[2,128,512]{2,1,0:T(8,128)(2,1)S(1)}, bf16[2,128,512]{2,1,0:T(8,128)(2,1)S(1)}, u32[]{:S(2)}, u32[]{:S(2)}) collective-permute-start(bf16[2,128,512]{2,1,0:T(8,128)(2,1)S(1)} %pad_maximum_fusion.mine_ref), channel_id=1, source_target_pairs={{0,12},{2,14},{4,8},{6,10},{8,4},{10,6},{12,0},{14,2},{16,28},{18,... | collective-permute-start | bytes 786440 | tf_op jit(solution)/shard_map/ppermute | solution.py:326
  4.2 9.2 %collective-permute-start = (bf16[2,128,512]{2,1,0:T(8,128)(2,1)S(1)}, bf16[2,128,512]{2,1,0:T(8,128)(2,1)S(1)}, u32[]{:S(2)}, u32[]{:S(2)}) collective-permute-start(bf16[2,128,512]{2,1,0:T(8,128)(2,1)S(1)} %pad_maximum_fusion.mine_ref), channel_id=1, source_target_pairs={{0,1},{1,0},{2,3},{3,2},{4,5},{5,4},{6,7},{7,6},{8,9},{9,8},{10,11... | collective-permute-start | bytes 786440 | tf_op jit(solution)/shard_map/ppermute | solution.py:323
  7.1 11.9 %collective-permute-start.2 = (bf16[2,128,512]{2,1,0:T(8,128)(2,1)S(1)}, bf16[2,128,512]{2,1,0:T(8,128)(2,1)S(1)}, u32[]{:S(2)}, u32[]{:S(2)}) collective-permute-start(bf16[2,128,512]{2,1,0:T(8,128)(2,1)S(1)} %pad_maximum_fusion.1.mine_ref), channel_id=1, source_target_pairs={{0,1},{1,0},{2,3},{3,2},{4,5},{5,4},{6,7},{7,6},{8,9},{9,8},{10,11... | collective-permute-start | bytes 786440 | tf_op jit(solution)/shard_map/ppermute | solution.py:323
  7.7 12.4 %collective-permute-start.1 = (bf16[2,128,512]{2,1,0:T(8,128)(2,1)S(1)}, bf16[2,128,512]{2,1,0:T(8,128)(2,1)S(1)}, u32[]{:S(2)}, u32[]{:S(2)}) collective-permute-start(bf16[2,128,512]{2,1,0:T(8,128)(2,1)S(1)} %pad_maximum_fusion.1.mine_ref), channel_id=1, source_target_pairs={{0,12},{2,14},{4,8},{6,10},{8,4},{10,6},{12,0},{14,2},{16,28},{18,... | collective-permute-start | bytes 786440 | tf_op jit(solution)/shard_map/ppermute | solution.py:326
  9.3 21.8 %copy-start.1 = (bf16[1,8,2,256,256]{4,3,2,1,0:T(8,128)(2,1)S(1)}, bf16[1,8,2,256,256]{4,3,2,1,0:T(8,128)(2,1)}, u32[]{:S(2)}) copy-start(bf16[1,8,2,256,256]{4,3,2,1,0:T(8,128)(2,1)} %param.7) | copy-start | bytes 6291460
  14.4 10.2 %collective-permute-start.9 = (bf16[2,128,512]{2,1,0:T(8,128)(2,1)S(1)}, bf16[2,128,512]{2,1,0:T(8,128)(2,1)S(1)}, u32[]{:S(2)}, u32[]{:S(2)}) collective-permute-start(bf16[2,128,512]{2,1,0:T(8,128)(2,1)S(1)} %collective-permute-done.8.mine_ref), channel_id=1, source_target_pairs={{0,1},{1,0},{2,3},{3,2},{4,5},{5,4},{6,7},{7,6},{8,9},{9,8},{10,11... | collective-permute-start | bytes 786440 | tf_op jit(solution)/shard_map/ppermute | solution.py:323
  20.1 8.7 %collective-permute-start.11 = (bf16[2,128,512]{2,1,0:T(8,128)(2,1)S(1)}, bf16[2,128,512]{2,1,0:T(8,128)(2,1)S(1)}, u32[]{:S(2)}, u32[]{:S(2)}) collective-permute-start(bf16[2,128,512]{2,1,0:T(8,128)(2,1)S(1)} %collective-permute-done.1.mine_ref), channel_id=1, source_target_pairs={{0,1},{1,0},{2,3},{3,2},{4,5},{5,4},{6,7},{7,6},{8,9},{9,8},{10,11... | collective-permute-start | bytes 786440 | tf_op jit(solution)/shard_map/ppermute | solution.py:323
  21.7 8.9 %collective-permute-start.3 = (bf16[2,256,256]{2,1,0:T(8,128)(2,1)S(1)}, bf16[2,256,256]{2,1,0:T(8,128)(2,1)S(1)}, u32[]{:S(2)}, u32[]{:S(2)}) collective-permute-start(bf16[2,256,256]{2,1,0:T(8,128)(2,1)S(1)} %get-tuple-element.95), channel_id=1, source_target_pairs={{0,4},{2,6},{4,0},{6,2},{8,12},{10,14},{12,8},{14,10},{16,20},{18,... | collective-permute-start | bytes 786440 | tf_op jit(solution)/shard_map/ppermute | solution.py:326
  22.2 8.7 %collective-permute-start.4 = (bf16[2,256,256]{2,1,0:T(8,128)(2,1)S(1)}, bf16[2,256,256]{2,1,0:T(8,128)(2,1)S(1)}, u32[]{:S(2)}, u32[]{:S(2)}) collective-permute-start(bf16[2,256,256]{2,1,0:T(8,128)(2,1)S(1)} %get-tuple-element.96), channel_id=1, source_target_pairs={{0,8},{2,10},{4,12},{6,14},{8,0},{10,2},{12,4},{14,6},{16,24},{18,... | collective-permute-start | bytes 786440 | tf_op jit(solution)/shard_map/ppermute | solution.py:326
  22.6 11.0 %collective-permute-start.5 = (bf16[2,256,256]{2,1,0:T(8,128)(2,1)S(1)}, bf16[2,256,256]{2,1,0:T(8,128)(2,1)S(1)}, u32[]{:S(2)}, u32[]{:S(2)}) collective-permute-start(bf16[2,256,256]{2,1,0:T(8,128)(2,1)S(1)} %get-tuple-element.97), channel_id=1, source_target_pairs={{0,6},{2,4},{4,2},{6,0},{8,14},{10,12},{12,10},{14,8},{16,22},{18,... | collective-permute-start | bytes 786440 | tf_op jit(solution)/shard_map/ppermute | solution.py:326
  24.6 9.7 %collective-permute-start.6 = (bf16[2,256,256]{2,1,0:T(8,128)(2,1)S(1)}, bf16[2,256,256]{2,1,0:T(8,128)(2,1)S(1)}, u32[]{:S(2)}, u32[]{:S(2)}) collective-permute-start(bf16[2,256,256]{2,1,0:T(8,128)(2,1)S(1)} %get-tuple-element.98), channel_id=1, source_target_pairs={{0,10},{2,8},{4,14},{6,12},{8,2},{10,0},{12,6},{14,4},{16,26},{18,... | collective-permute-start | bytes 786440 | tf_op jit(solution)/shard_map/ppermute | solution.py:326
  28.8 5.5 %collective-permute-start.7 = (bf16[2,256,256]{2,1,0:T(8,128)(2,1)S(1)}, bf16[2,256,256]{2,1,0:T(8,128)(2,1)S(1)}, u32[]{:S(2)}, u32[]{:S(2)}) collective-permute-start(bf16[2,256,256]{2,1,0:T(8,128)(2,1)S(1)} %get-tuple-element.99), channel_id=1, source_target_pairs={{0,2},{2,0},{4,6},{6,4},{8,10},{10,8},{12,14},{14,12},{16,18},{18,... | collective-permute-start | bytes 786440 | tf_op jit(solution)/shard_map/ppermute | solution.py:326
  30.6 3.8 %collective-permute-start.10 = (bf16[2,128,256]{2,1,0:T(8,128)(2,1)S(1)}, bf16[2,128,256]{2,1,0:T(8,128)(2,1)S(1)}, u32[]{:S(2)}, u32[]{:S(2)}) collective-permute-start(bf16[2,128,256]{2,1,0:T(8,128)(2,1)S(1)} %get-tuple-element.101), channel_id=1, source_target_pairs={{0,2},{2,0},{4,6},{6,4},{8,10},{10,8},{12,14},{14,12},{16,18},{18,... | collective-permute-start | bytes 393224 | tf_op jit(solution)/shard_map/ppermute | solution.py:326
  30.8 3.5 %collective-permute-start.12 = (bf16[2,128,256]{2,1,0:T(8,128)(2,1)S(1)}, bf16[2,128,256]{2,1,0:T(8,128)(2,1)S(1)}, u32[]{:S(2)}, u32[]{:S(2)}) collective-permute-start(bf16[2,128,256]{2,1,0:T(8,128)(2,1)S(1)} %get-tuple-element.104), channel_id=1, source_target_pairs={{0,2},{2,0},{4,6},{6,4},{8,10},{10,8},{12,14},{14,12},{16,18},{18,... | collective-permute-start | bytes 393224 | tf_op jit(solution)/shard_map/ppermute | solution.py:326
  33.6 10.4 %collective-permute-start.14 = (bf16[2,2,256,256]{3,2,1,0:T(8,128)(2,1)S(1)}, bf16[2,2,256,256]{3,2,1,0:T(8,128)(2,1)S(1)}, u32[]{:S(2)}, u32[]{:S(2)}) collective-permute-start(bf16[2,2,256,256]{3,2,1,0:T(8,128)(2,1)S(1)} %get-tuple-element.115), channel_id=1, source_target_pairs={{0,12},{2,14},{4,8},{6,10},{8,4},{10,6},{12,0},{14,2},{16,16},{18,... | collective-permute-start | bytes 1572872 | tf_op jit(solution)/shard_map/ppermute | solution.py:318
  39.6 16.0 %collective-permute-start.13 = (bf16[2,256,256]{2,1,0:T(8,128)(2,1)S(1)}, bf16[2,256,256]{2,1,0:T(8,128)(2,1)S(1)}, u32[]{:S(2)}, u32[]{:S(2)}) collective-permute-start(bf16[2,256,256]{2,1,0:T(8,128)(2,1)S(1)} %get-tuple-element.105), channel_id=1, source_target_pairs={{16,8},{18,10},{20,12},{22,14},{24,0},{26,2},{28,4},{30,6},{17,9},... | collective-permute-start | bytes 786440 | tf_op jit(solution)/shard_map/ppermute | solution.py:372
  55.6 17.7 %collective-permute-start.18 = (bf16[2,2,256,256]{3,2,1,0:T(8,128)(2,1)S(1)}, bf16[2,2,256,256]{3,2,1,0:T(8,128)(2,1)S(1)}, u32[]{:S(2)}, u32[]{:S(2)}) collective-permute-start(bf16[2,2,256,256]{3,2,1,0:T(8,128)(2,1)S(1)} %get-tuple-element.115), channel_id=1, source_target_pairs={{0,0},{2,2},{4,4},{6,6},{8,8},{10,10},{12,12},{14,14},{16,28},{18,... | collective-permute-start | bytes 1572872 | tf_op jit(solution)/shard_map/ppermute | solution.py:318
  62.9 3.6 %collective-permute-start.19 = (bf16[2,256,256]{2,1,0:T(8,128)(2,1)S(1)}, bf16[2,256,256]{2,1,0:T(8,128)(2,1)S(1)}, u32[]{:S(2)}, u32[]{:S(2)}) collective-permute-start(bf16[2,256,256]{2,1,0:T(8,128)(2,1)S(1)} %get-tuple-element.117), channel_id=1, source_target_pairs={{0,2},{2,0},{4,6},{6,4},{8,10},{10,8},{12,14},{14,12},{16,18},{18,... | collective-permute-start | bytes 786440 | tf_op jit(solution)/shard_map/ppermute | solution.py:326
  63.0 14.3 %collective-permute-start.21 = (bf16[2,256,256]{2,1,0:T(8,128)(2,1)S(1)}, bf16[2,256,256]{2,1,0:T(8,128)(2,1)S(1)}, u32[]{:S(2)}, u32[]{:S(2)}) collective-permute-start(bf16[2,256,256]{2,1,0:T(8,128)(2,1)S(1)} %get-tuple-element.121), channel_id=1, source_target_pairs={{0,4},{2,6},{4,0},{6,2},{8,12},{10,14},{12,8},{14,10},{16,20},{18,... | collective-permute-start | bytes 786440 | tf_op jit(solution)/shard_map/ppermute | solution.py:326
  63.9 13.6 %collective-permute-start.22 = (bf16[2,256,256]{2,1,0:T(8,128)(2,1)S(1)}, bf16[2,256,256]{2,1,0:T(8,128)(2,1)S(1)}, u32[]{:S(2)}, u32[]{:S(2)}) collective-permute-start(bf16[2,256,256]{2,1,0:T(8,128)(2,1)S(1)} %get-tuple-element.122), channel_id=1, source_target_pairs={{0,8},{2,10},{4,12},{6,14},{8,0},{10,2},{12,4},{14,6},{16,24},{18,... | collective-permute-start | bytes 786440 | tf_op jit(solution)/shard_map/ppermute | solution.py:326
  74.1 8.0 %collective-permute-start.25 = (bf16[2,128,512]{2,1,0:T(8,128)(2,1)S(1)}, bf16[2,128,512]{2,1,0:T(8,128)(2,1)S(1)}, u32[]{:S(2)}, u32[]{:S(2)}) collective-permute-start(bf16[2,128,512]{2,1,0:T(8,128)(2,1)S(1)} %get-tuple-element.128), channel_id=1, source_target_pairs={{0,1},{1,0},{2,3},{3,2},{4,5},{5,4},{6,7},{7,6},{8,9},{9,8},{10,11... | collective-permute-start | bytes 786440 | tf_op jit(solution)/shard_map/ppermute | solution.py:323
  76.0 9.0 %collective-permute-start.20 = (bf16[2,128,512]{2,1,0:T(8,128)(2,1)S(1)}, bf16[2,128,512]{2,1,0:T(8,128)(2,1)S(1)}, u32[]{:S(2)}, u32[]{:S(2)}) collective-permute-start(bf16[2,128,512]{2,1,0:T(8,128)(2,1)S(1)} %get-tuple-element.119), channel_id=1, source_target_pairs={{0,1},{1,0},{2,3},{3,2},{4,5},{5,4},{6,7},{7,6},{8,9},{9,8},{10,11... | collective-permute-start | bytes 786440 | tf_op jit(solution)/shard_map/ppermute | solution.py:323
  77.2 8.0 %collective-permute-start.15 = (bf16[2,256,256]{2,1,0:T(8,128)(2,1)S(1)}, bf16[2,256,256]{2,1,0:T(8,128)(2,1)S(1)}, u32[]{:S(2)}, u32[]{:S(2)}) collective-permute-start(bf16[2,256,256]{2,1,0:T(8,128)(2,1)S(1)} %get-tuple-element.111), channel_id=1, source_target_pairs={{0,6},{2,4},{4,2},{6,0},{8,14},{10,12},{12,10},{14,8},{16,22},{18,... | collective-permute-start | bytes 786440 | tf_op jit(solution)/shard_map/ppermute | solution.py:326
  77.2 8.0 %collective-permute-start.16 = (bf16[2,256,256]{2,1,0:T(8,128)(2,1)S(1)}, bf16[2,256,256]{2,1,0:T(8,128)(2,1)S(1)}, u32[]{:S(2)}, u32[]{:S(2)}) collective-permute-start(bf16[2,256,256]{2,1,0:T(8,128)(2,1)S(1)} %get-tuple-element.112), channel_id=1, source_target_pairs={{0,10},{2,8},{4,14},{6,12},{8,2},{10,0},{12,6},{14,4},{16,26},{18,... | collective-permute-start | bytes 786440 | tf_op jit(solution)/shard_map/ppermute | solution.py:326
  77.5 7.7 %collective-permute-start.17 = (bf16[2,256,256]{2,1,0:T(8,128)(2,1)S(1)}, bf16[2,256,256]{2,1,0:T(8,128)(2,1)S(1)}, u32[]{:S(2)}, u32[]{:S(2)}) collective-permute-start(bf16[2,256,256]{2,1,0:T(8,128)(2,1)S(1)} %get-tuple-element.113), channel_id=1, source_target_pairs={{0,2},{2,0},{4,6},{6,4},{8,10},{10,8},{12,14},{14,12},{16,18},{18,... | collective-permute-start | bytes 786440 | tf_op jit(solution)/shard_map/ppermute | solution.py:326
  86.3 9.2 %collective-permute-start.26 = (bf16[2,128,512]{2,1,0:T(8,128)(2,1)S(1)}, bf16[2,128,512]{2,1,0:T(8,128)(2,1)S(1)}, u32[]{:S(2)}, u32[]{:S(2)}) collective-permute-start(bf16[2,128,512]{2,1,0:T(8,128)(2,1)S(1)} %get-tuple-element.131), channel_id=1, source_target_pairs={{0,1},{1,0},{2,3},{3,2},{4,5},{5,4},{6,7},{7,6},{8,9},{9,8},{10,11... | collective-permute-start | bytes 786440 | tf_op jit(solution)/shard_map/ppermute | solution.py:323
  87.8 10.1 %collective-permute-start.27 = (bf16[2,128,512]{2,1,0:T(8,128)(2,1)S(1)}, bf16[2,128,512]{2,1,0:T(8,128)(2,1)S(1)}, u32[]{:S(2)}, u32[]{:S(2)}) collective-permute-start(bf16[2,128,512]{2,1,0:T(8,128)(2,1)S(1)} %add_convert_fusion), channel_id=1, source_target_pairs={{0,12},{2,14},{4,8},{6,10},{8,4},{10,6},{12,0},{14,2},{16,28},{18,... | collective-permute-start | bytes 786440 | tf_op jit(solution)/shard_map/ppermute | solution.py:326
  90.1 10.6 %collective-permute-start.23 = (bf16[2,128,512]{2,1,0:T(8,128)(2,1)S(1)}, bf16[2,128,512]{2,1,0:T(8,128)(2,1)S(1)}, u32[]{:S(2)}, u32[]{:S(2)}) collective-permute-start(bf16[2,128,512]{2,1,0:T(8,128)(2,1)S(1)} %get-tuple-element.125), channel_id=1, source_target_pairs={{0,1},{1,0},{2,3},{3,2},{4,5},{5,4},{6,7},{7,6},{8,9},{9,8},{10,11... | collective-permute-start | bytes 786440 | tf_op jit(solution)/shard_map/ppermute | solution.py:323
  91.2 11.1 %collective-permute-start.24 = (bf16[2,128,512]{2,1,0:T(8,128)(2,1)S(1)}, bf16[2,128,512]{2,1,0:T(8,128)(2,1)S(1)}, u32[]{:S(2)}, u32[]{:S(2)}) collective-permute-start(bf16[2,128,512]{2,1,0:T(8,128)(2,1)S(1)} %add_convert_fusion.1), channel_id=1, source_target_pairs={{0,12},{2,14},{4,8},{6,10},{8,4},{10,6},{12,0},{14,2},{16,28},{18,... | collective-permute-start | bytes 786440 | tf_op jit(solution)/shard_map/ppermute | solution.py:326

commit v14 on v11

--- a/solution.py
+++ b/solution.py
@@ -316,14 +316,15 @@
     def exchange_far(values):
         return [to_distance(value, count - far + i) for i, value in enumerate(values)]
 
-    mine, other, far_mine = [], [], []
+    mine, other = [], []
     source = (obj_amp, obj_phase)
     for c in chunks:
         if c > 0:
             source, mine[-1] = lax.optimization_barrier((source, mine[-1]))
         mine.append(coded(*(array[0, c * rows : (c + 1) * rows] for array in source)))
         other.append(to_other_half(mine[-1]))
-        far_mine.append(to_distance(mine[-1], count - far))
+    mine = list(lax.optimization_barrier(mine))
+    far_mine = [to_distance(value, count - far) for value in mine]
     ready = call(ready_kernel, [shape_of(wave, bf16)] + [shape_of((window, window), bf16)] * 2, prefetch=1)
     start, down, across = ready(corners, exit_adjoint)
     other[0], start, down, across = lax.optimization_barrier((other[0], start, down, across))

time: 97.2 us -> 95.7 us (0.985)
  waiting for transfers between devices: 42.7 us -> 40.2 us
  starting transfers between devices: 26.4 us -> 27.5 us
    ppermute x6, waiting for transfers between devices: 19.7 us -> 11.4 us  [to_other_half(): return lax.ppermute(value, 'scan', [(0, 1), (1, 0)])]
    ppermute x18, waiting for transfers between devices: 14.3 us -> 20 us  [to_distance(): return lax.ppermute(value, 'sec', [(s, s ^ d) for s in range(sections)])]
  transfers between devices with their start and end apart: 25 -> 25, of which waited for: 16 -> 17; matrix products, arithmetic and copies ran while one was open for 1% -> 1% of each run, Pallas kernels for 14% -> 14%
where the time goes in v14:
time: 95.7 us; the launch traced here: 95.6 us
  waiting for transfers between devices  40.2 us (42%)
  starting transfers between devices  27.5 us (29%)
  Pallas kernels  24.8 us (26%)
  other arithmetic  2.96 us (3%)
    pallas_call x13, Pallas kernels, run(): pl.pallas_call(kernel, grid_spec=pltpu.PrefetchScalarGridSpec(num_scalar_...  23.1 us
    ppermute x18, waiting for transfers between devices, to_distance(): return lax.ppermute(value, 'sec', [(s, s ^ d) for s in range(sections)])  20 us
    ppermute x18, starting transfers between devices, to_distance(): return lax.ppermute(value, 'sec', [(s, s ^ d) for s in range(sections)])  18.8 us
    ppermute x6, waiting for transfers between devices, to_other_half(): return lax.ppermute(value, 'scan', [(0, 1), (1, 0)])  11.4 us
    ppermute x1, waiting for transfers between devices, on_device(): lax.ppermute(leave, 'sec', [(s, s - count ^ count // 2) for s in range(co...  8.76 us
    ppermute x6, starting transfers between devices, to_other_half(): return lax.ppermute(value, 'scan', [(0, 1), (1, 0)])  7.2 us
    convert_element_type x2, other arithmetic, coded(): jnp.exp(code_gain * trans_re).astype(bf16)  2.91 us
  transfers between devices with their start and end apart: 25, of which 17 were waited for; matrix products, arithmetic and copies ran while one was open for 1% of the time, Pallas kernels for 14%

profile of v14, /device:TPU:0, one launch (start us, length us, event | category | flops | bytes accessed | tf_op | source)
XLA Modules:
  0.0 95.6 jit_solution(14479598893588219080)
XLA Ops:
  0.0 1.5 %fusion.4 = (bf16[1,128,512]{2,1,0:T(8,128)(2,1)S(1)}, bf16[1,128,512]{2,1,0:T(8,128)(2,1)S(1)}) fusion(f32[1,256,512]{2,1,0:T(8,128)} %param.5, f32[1,256,512]{2,1,0:T(8,128)} %param.6), kind=kLoop, calls=%fused_computation.8 | loop fusion | flops 2424832 | bytes 786432 | tf_op jit(solution)/shard_map/convert_element_type | solution.py:66
  1.6 3.0 %collective-permute-start = (bf16[2,128,512]{2,1,0:T(8,128)(2,1)S(1)}, bf16[2,128,512]{2,1,0:T(8,128)(2,1)S(1)}, u32[]{:S(2)}, u32[]{:S(2)}) collective-permute-start(bf16[2,128,512]{2,1,0:T(8,128)(2,1)S(1)} %pad_maximum_fusion.mine_ref), channel_id=1, source_target_pairs={{0,1},{1,0},{2,3},{3,2},{4,5},{5,4},{6,7},{7,6},{8,9},{9,8},{10,11... | collective-permute-start | bytes 786440 | tf_op jit(solution)/shard_map/ppermute | solution.py:308
  4.6 1.4 %fusion.13 = (bf16[1,128,512]{2,1,0:T(8,128)(2,1)S(1)}, bf16[1,128,512]{2,1,0:T(8,128)(2,1)S(1)}) fusion(f32[1,256,512]{2,1,0:T(8,128)} %param.5, f32[1,256,512]{2,1,0:T(8,128)} %param.6), kind=kLoop, calls=%fused_computation.17 | loop fusion | flops 2424832 | bytes 786432 | tf_op jit(solution)/shard_map/convert_element_type | solution.py:66
  6.0 2.6 %collective-permute-start.8 = (bf16[2,128,512]{2,1,0:T(8,128)(2,1)S(1)}, bf16[2,128,512]{2,1,0:T(8,128)(2,1)S(1)}, u32[]{:S(2)}, u32[]{:S(2)}) collective-permute-start(bf16[2,128,512]{2,1,0:T(8,128)(2,1)S(1)} %pad_maximum_fusion.mine_ref), channel_id=1, source_target_pairs={{0,12},{2,14},{4,8},{6,10},{8,4},{10,6},{12,0},{14,2},{16,28},{18,... | collective-permute-start | bytes 786440 | tf_op jit(solution)/shard_map/ppermute | solution.py:311
  9.2 1.2 %shard_map.55 = (bf16[2,256,256]{2,1,0:T(8,128)(2,1)S(1)}, bf16[256,256]{1,0:T(8,128)(2,1)S(1)}, bf16[256,256]{1,0:T(8,128)(2,1)S(1)}) custom-call(s32[2,8]{1,0:T(2,128)S(1)} %bitcast.4, bf16[8,2,256,256]{3,2,1,0:T(8,128)(2,1)S(1)} %copy-done.1), custom_call_target="tpu_custom_call" | custom-call | bytes 2621504 | tf_op jit(solution)/shard_map/pallas_call | solution.py:27
  11.3 1.0 %shard_map.56 = (bf16[2,256,256]{2,1,0:T(8,128)(2,1)S(1)}, bf16[2,256,256]{2,1,0:T(8,128)(2,1)S(1)}, bf16[2,256,256]{2,1,0:T(8,128)(2,1)S(1)}, bf16[2,256,256]{2...) custom-call(s32[2,8]{1,0:T(2,128)S(1)} %bitcast.5, ...), custom_call_target="tpu_custom_call" | custom-call | bytes 2097216 | tf_op jit(solution)/shard_map/pallas_call | solution.py:27
  12.3 3.9 %collective-permute-done.8.mine_ref = bf16[2,128,512]{2,1,0:T(8,128)(2,1)S(1)} collective-permute-done((bf16[2,128,512]{2,1,0:T(8,128)(2,1)S(1)}, bf16[2,128,512]{2,1,0:T(8,128)(2,1)S(1)}, u32[]{:S(2)}, u32[]{:S(2)}) %collective-permute-start.8) | collective-permute-done | bytes 262176 | tf_op jit(solution)/shard_map/ppermute | solution.py:311
  17.0 1.1 %shard_map.57 = (bf16[2,256,256]{2,1,0:T(8,128)(2,1)S(1)}, bf16[2,256,256]{2,1,0:T(8,128)(2,1)S(1)}, bf16[2,256,256]{2,1,0:T(8,128)(2,1)S(1)}, bf16[2,256,256]{2...) custom-call(s32[2,8]{1,0:T(2,128)S(1)} %bitcast.6, ...), custom_call_target="tpu_custom_call", output_to_operand_aliasing={{0}: (3, {}), {1}: (4, {}), {2}: (5, {}), {3}: (6, {}), {4}... | custom-call | bytes 3670080 | tf_op jit(solution)/shard_map/pallas_call | solution.py:27
  18.1 2.3 %collective-permute-done.1.mine_ref = bf16[2,128,512]{2,1,0:T(8,128)(2,1)S(1)} collective-permute-done((bf16[2,128,512]{2,1,0:T(8,128)(2,1)S(1)}, bf16[2,128,512]{2,1,0:T(8,128)(2,1)S(1)}, u32[]{:S(2)}, u32[]{:S(2)}) %collective-permute-start.1) | collective-permute-done | bytes 262176 | tf_op jit(solution)/shard_map/ppermute | solution.py:311
  20.8 1.6 %collective-permute-start.3 = (bf16[2,256,256]{2,1,0:T(8,128)(2,1)S(1)}, bf16[2,256,256]{2,1,0:T(8,128)(2,1)S(1)}, u32[]{:S(2)}, u32[]{:S(2)}) collective-permute-start(bf16[2,256,256]{2,1,0:T(8,128)(2,1)S(1)} %get-tuple-element.85), channel_id=1, source_target_pairs={{0,4},{2,6},{4,0},{6,2},{8,12},{10,14},{12,8},{14,10},{16,20},{18,... | collective-permute-start | bytes 786440 | tf_op jit(solution)/shard_map/ppermute | solution.py:311
  22.4 1.6 %collective-permute-start.4 = (bf16[2,256,256]{2,1,0:T(8,128)(2,1)S(1)}, bf16[2,256,256]{2,1,0:T(8,128)(2,1)S(1)}, u32[]{:S(2)}, u32[]{:S(2)}) collective-permute-start(bf16[2,256,256]{2,1,0:T(8,128)(2,1)S(1)} %get-tuple-element.86), channel_id=1, source_target_pairs={{0,8},{2,10},{4,12},{6,14},{8,0},{10,2},{12,4},{14,6},{16,24},{18,... | collective-permute-start | bytes 786440 | tf_op jit(solution)/shard_map/ppermute | solution.py:311
  24.5 3.6 %collective-permute-done.11.other_ref = bf16[2,128,512]{2,1,0:T(8,128)(2,1)S(1)} collective-permute-done((bf16[2,128,512]{2,1,0:T(8,128)(2,1)S(1)}, bf16[2,128,512]{2,1,0:T(8,128)(2,1)S(1)}, u32[]{:S(2)}, u32[]{:S(2)}) %collective-permute-start.11) | collective-permute-done | bytes 262176 | tf_op jit(solution)/shard_map/ppermute | solution.py:308
  30.6 2.1 %collective-permute-done.5.refs_3_ = bf16[2,256,256]{2,1,0:T(8,128)(2,1)S(1)} collective-permute-done((bf16[2,256,256]{2,1,0:T(8,128)(2,1)S(1)}, bf16[2,256,256]{2,1,0:T(8,128)(2,1)S(1)}, u32[]{:S(2)}, u32[]{:S(2)}) %collective-permute-start.5) | collective-permute-done | bytes 262176 | tf_op jit(solution)/shard_map/ppermute | solution.py:311
  33.5 5.2 %shard_map.60 = (bf16[2,256,256]{2,1,0:T(8,128)(2,1)S(1)}, bf16[8,2,256,256]{3,2,1,0:T(8,128)(2,1)S(1)}) custom-call(bf16[2,256,256]{2,1,0:T(8,128)(2,1)S(1)} %get-tuple-element.63.start_ref, bf16[256,256]{1,0:T(8,128)(2,1)S(1)} %get-tuple-element.64.down_ref, bf16[256,256]{1,0:T(8,128)(2,1)S(1)} %get-tuple-element.65.across_ref, ...), custom_call_target="tpu_custom_call" | custom-call | flops 2147483648 | bytes 4980736 | tf_op jit(solution)/shard_map/pallas_call | solution.py:27
  38.7 1.5 %collective-permute-start.13 = (bf16[2,256,256]{2,1,0:T(8,128)(2,1)S(1)}, bf16[2,256,256]{2,1,0:T(8,128)(2,1)S(1)}, u32[]{:S(2)}, u32[]{:S(2)}) collective-permute-start(bf16[2,256,256]{2,1,0:T(8,128)(2,1)S(1)} %get-tuple-element.95), channel_id=1, source_target_pairs={{16,8},{18,10},{20,12},{22,14},{24,0},{26,2},{28,4},{30,6},{17,9},... | collective-permute-start | bytes 786440 | tf_op jit(solution)/shard_map/ppermute | solution.py:355
  40.2 2.5 %shard_map.61.wave_ref = bf16[8,2,256,256]{3,2,1,0:T(8,128)(2,1)S(1)} custom-call(s32[2,8]{1,0:T(2,128)S(1)} %bitcast.9, bf16[8,2,256,256]{3,2,1,0:T(8,128)(2,1)S(1)} %bitcast.3), custom_call_target="tpu_custom_call" | custom-call | bytes 4194368 | tf_op jit(solution)/shard_map/pallas_call | solution.py:27
  42.7 8.8 %collective-permute-done.13.come_ref = bf16[2,256,256]{2,1,0:T(8,128)(2,1)S(1)} collective-permute-done((bf16[2,256,256]{2,1,0:T(8,128)(2,1)S(1)}, bf16[2,256,256]{2,1,0:T(8,128)(2,1)S(1)}, u32[]{:S(2)}, u32[]{:S(2)}) %collective-permute-start.13) | collective-permute-done | bytes 262176 | tf_op jit(solution)/shard_map/ppermute | solution.py:355
  51.5 5.2 %shard_map.62 = (bf16[2,256,256]{2,1,0:T(8,128)(2,1)S(1)}, bf16[2,256,256]{2,1,0:T(8,128)(2,1)S(1)}, bf16[2,256,256]{2,1,0:T(8,128)(2,1)S(1)}, bf16[2,256,256]{2...) custom-call(bf16[2,256,256]{2,1,0:T(8,128)(2,1)S(1)} %get-tuple-elem, ...), custom_call_target="tpu_custom_call" | custom-call | flops 2147483648 | bytes 4980736 | tf_op jit(solution)/shard_map/pallas_call | solution.py:27
  56.7 5.1 %collective-permute-start.21 = (bf16[2,128,256]{2,1,0:T(8,128)(2,1)S(1)}, bf16[2,128,256]{2,1,0:T(8,128)(2,1)S(1)}, u32[]{:S(2)}, u32[]{:S(2)}) collective-permute-start(bf16[2,128,256]{2,1,0:T(8,128)(2,1)S(1)} %get-tuple-element.107), channel_id=1, source_target_pairs={{0,12},{2,14},{4,8},{6,10},{8,4},{10,6},{12,0},{14,2},{16,28},{18,... | collective-permute-start | bytes 393224 | tf_op jit(solution)/shard_map/ppermute | solution.py:311
  62.2 2.5 %collective-permute-start.20 = (bf16[2,256,256]{2,1,0:T(8,128)(2,1)S(1)}, bf16[2,256,256]{2,1,0:T(8,128)(2,1)S(1)}, u32[]{:S(2)}, u32[]{:S(2)}) collective-permute-start(bf16[2,256,256]{2,1,0:T(8,128)(2,1)S(1)} %get-tuple-element.106), channel_id=1, source_target_pairs={{0,8},{2,10},{4,12},{6,14},{8,0},{10,2},{12,4},{14,6},{16,24},{18,... | collective-permute-start | bytes 786440 | tf_op jit(solution)/shard_map/ppermute | solution.py:311
  65.7 1.1 %collective-permute-start.17 = (bf16[2,256,256]{2,1,0:T(8,128)(2,1)S(1)}, bf16[2,256,256]{2,1,0:T(8,128)(2,1)S(1)}, u32[]{:S(2)}, u32[]{:S(2)}) collective-permute-start(bf16[2,256,256]{2,1,0:T(8,128)(2,1)S(1)} %get-tuple-element.102), channel_id=1, source_target_pairs={{0,10},{2,8},{4,14},{6,12},{8,2},{10,0},{12,6},{14,4},{16,26},{18,... | collective-permute-start | bytes 786440 | tf_op jit(solution)/shard_map/ppermute | solution.py:311
  66.8 1.8 %collective-permute-done.22.refs_4_ = bf16[2,128,256]{2,1,0:T(8,128)(2,1)S(1)} collective-permute-done((bf16[2,128,256]{2,1,0:T(8,128)(2,1)S(1)}, bf16[2,128,256]{2,1,0:T(8,128)(2,1)S(1)}, u32[]{:S(2)}, u32[]{:S(2)}) %collective-permute-start.22) | collective-permute-done | bytes 131104 | tf_op jit(solution)/shard_map/ppermute | solution.py:311
  68.6 5.5 %collective-permute-done.19.refs_1_ = bf16[2,256,256]{2,1,0:T(8,128)(2,1)S(1)} collective-permute-done((bf16[2,256,256]{2,1,0:T(8,128)(2,1)S(1)}, bf16[2,256,256]{2,1,0:T(8,128)(2,1)S(1)}, u32[]{:S(2)}, u32[]{:S(2)}) %collective-permute-start.19) | collective-permute-done | bytes 262176 | tf_op jit(solution)/shard_map/ppermute | solution.py:311
  74.1 2.6 %collective-permute-start.14 = (bf16[2,128,256]{2,1,0:T(8,128)(2,1)S(1)}, bf16[2,128,256]{2,1,0:T(8,128)(2,1)S(1)}, u32[]{:S(2)}, u32[]{:S(2)}) collective-permute-start(bf16[2,128,256]{2,1,0:T(8,128)(2,1)S(1)} %get-tuple-element.99), channel_id=1, source_target_pairs={{0,12},{2,14},{4,8},{6,10},{8,4},{10,6},{12,0},{14,2},{16,28},{18,... | collective-permute-start | bytes 393224 | tf_op jit(solution)/shard_map/ppermute | solution.py:311
  77.7 1.3 %shard_map.64.refs_3_ = f32[8,128,256]{2,1,0:T(8,128)S(1)} custom-call(s32[2,8]{1,0:T(2,128)S(1)} %bitcast.11, bf16[8,2,256,256]{3,2,1,0:T(8,128)(2,1)S(1)} %shard_map.61.wave_ref, bf16[2,256,256]{2,1,0:T(8,128)(2,1)S(1)} %get-tuple-element.104.refs_0_, bf16[2,256,256]{2,1,0:T(8,128)(2,1)S(1)} %collective-permute-done.19.refs_1_, ...), custom_call_target="tpu_custom_call" | custom-call | bytes 4194368 | tf_op jit(solution)/shard_map/pallas_call | solution.py:27
  79.8 1.1 %shard_map.65 = (f32[2,128,512]{2,1,0:T(8,128)S(1)}, bf16[2,128,512]{2,1,0:T(8,128)(2,1)S(1)}) custom-call(s32[2,8]{1,0:T(2,128)S(1)} %bitcast.12, bf16[8,2,256,256]{3,2,1,0:T(8,128)(2,1)S(1)} %shard_map.61.wave_ref, bf16[2,256,256]{2,1,0:T(8,128)(2,1)S(1)} %collective-permute-done.16.refs_0_, bf16[2,256,256]{2,1,0:T(8,128)(2,1)S(1)} %collective-permute-done.17.refs_1_, ...), custom_call_target="tpu_custom_call" | custom-call | bytes 4718656 | tf_op jit(solution)/shard_map/pallas_call | solution.py:27
  80.9 1.8 %collective-permute-start.24 = (bf16[2,128,512]{2,1,0:T(8,128)(2,1)S(1)}, bf16[2,128,512]{2,1,0:T(8,128)(2,1)S(1)}, u32[]{:S(2)}, u32[]{:S(2)}) collective-permute-start(bf16[2,128,512]{2,1,0:T(8,128)(2,1)S(1)} %get-tuple-element.114), channel_id=1, source_target_pairs={{0,1},{1,0},{2,3},{3,2},{4,5},{5,4},{6,7},{7,6},{8,9},{9,8},{10,11... | collective-permute-start | bytes 786440 | tf_op jit(solution)/shard_map/ppermute | solution.py:308
  82.7 1.0 %shard_map.66.refs_2_ = f32[8,128,256]{2,1,0:T(8,128)S(1)} custom-call(s32[2,8]{1,0:T(2,128)S(1)} %bitcast.13, bf16[8,2,256,256]{3,2,1,0:T(8,128)(2,1)S(1)} %shard_map.61.wave_ref, bf16[2,256,256]{2,1,0:T(8,128)(2,1)S(1)} %collective-permute-done.16.refs_0_, bf16[2,256,256]{2,1,0:T(8,128)(2,1)S(1)} %collective-permute-done.17.refs_1_, ...), custom_call_target="tpu_custom_call" | custom-call | bytes 4980800 | tf_op jit(solution)/shard_map/pallas_call | solution.py:27
  83.7 1.6 %collective-permute-done.15.refs_1_ = bf16[2,128,256]{2,1,0:T(8,128)(2,1)S(1)} collective-permute-done((bf16[2,128,256]{2,1,0:T(8,128)(2,1)S(1)}, bf16[2,128,256]{2,1,0:T(8,128)(2,1)S(1)}, u32[]{:S(2)}, u32[]{:S(2)}) %collective-permute-start.15) | collective-permute-done | bytes 131104 | tf_op jit(solution)/shard_map/ppermute | solution.py:311
  86.3 1.3 %collective-permute-start.23 = (bf16[2,128,512]{2,1,0:T(8,128)(2,1)S(1)}, bf16[2,128,512]{2,1,0:T(8,128)(2,1)S(1)}, u32[]{:S(2)}, u32[]{:S(2)}) collective-permute-start(bf16[2,128,512]{2,1,0:T(8,128)(2,1)S(1)} %get-tuple-element.112), channel_id=1, source_target_pairs={{0,1},{1,0},{2,3},{3,2},{4,5},{5,4},{6,7},{7,6},{8,9},{9,8},{10,11... | collective-permute-start | bytes 786440 | tf_op jit(solution)/shard_map/ppermute | solution.py:308
  87.7 1.4 %collective-permute-done.24.come_ref = bf16[2,128,512]{2,1,0:T(8,128)(2,1)S(1)} collective-permute-done((bf16[2,128,512]{2,1,0:T(8,128)(2,1)S(1)}, bf16[2,128,512]{2,1,0:T(8,128)(2,1)S(1)}, u32[]{:S(2)}, u32[]{:S(2)}) %collective-permute-start.24) | collective-permute-done | bytes 262176 | tf_op jit(solution)/shard_map/ppermute | solution.py:308
  89.9 4.8 %collective-permute-done.23.come_ref = bf16[2,128,512]{2,1,0:T(8,128)(2,1)S(1)} collective-permute-done((bf16[2,128,512]{2,1,0:T(8,128)(2,1)S(1)}, bf16[2,128,512]{2,1,0:T(8,128)(2,1)S(1)}, u32[]{:S(2)}, u32[]{:S(2)}) %collective-permute-start.23) | collective-permute-done | bytes 262176 | tf_op jit(solution)/shard_map/ppermute | solution.py:308
  (43 shorter events, 12.4 us)
Async XLA Ops:
  0.0 9.2 %copy-start.2 = (s32[8,2]{0,1:T(2,128)S(1)}, s32[8,2]{0,1:T(2,128)}, u32[]{:S(2)}) copy-start(s32[8,2]{0,1:T(2,128)} %param.9) | copy-start | bytes 196
  0.0 9.2 %copy-start.1 = (bf16[8,2,256,256]{3,2,1,0:T(8,128)(2,1)S(1)}, bf16[8,2,256,256]{3,2,1,0:T(8,128)(2,1)}, u32[]{:S(2)}) copy-start(bf16[8,2,256,256]{3,2,1,0:T(8,128)(2,1)} %exit_ref.1) | copy-start | bytes 6291460
  1.6 9.7 %collective-permute-start = (bf16[2,128,512]{2,1,0:T(8,128)(2,1)S(1)}, bf16[2,128,512]{2,1,0:T(8,128)(2,1)S(1)}, u32[]{:S(2)}, u32[]{:S(2)}) collective-permute-start(bf16[2,128,512]{2,1,0:T(8,128)(2,1)S(1)} %pad_maximum_fusion.mine_ref), channel_id=1, source_target_pairs={{0,1},{1,0},{2,3},{3,2},{4,5},{5,4},{6,7},{7,6},{8,9},{9,8},{10,11... | collective-permute-start | bytes 786440 | tf_op jit(solution)/shard_map/ppermute | solution.py:308
  6.0 10.2 %collective-permute-start.8 = (bf16[2,128,512]{2,1,0:T(8,128)(2,1)S(1)}, bf16[2,128,512]{2,1,0:T(8,128)(2,1)S(1)}, u32[]{:S(2)}, u32[]{:S(2)}) collective-permute-start(bf16[2,128,512]{2,1,0:T(8,128)(2,1)S(1)} %pad_maximum_fusion.mine_ref), channel_id=1, source_target_pairs={{0,12},{2,14},{4,8},{6,10},{8,4},{10,6},{12,0},{14,2},{16,28},{18,... | collective-permute-start | bytes 786440 | tf_op jit(solution)/shard_map/ppermute | solution.py:311
  8.6 8.4 %collective-permute-start.2 = (bf16[2,128,512]{2,1,0:T(8,128)(2,1)S(1)}, bf16[2,128,512]{2,1,0:T(8,128)(2,1)S(1)}, u32[]{:S(2)}, u32[]{:S(2)}) collective-permute-start(bf16[2,128,512]{2,1,0:T(8,128)(2,1)S(1)} %pad_maximum_fusion.1.mine_ref), channel_id=1, source_target_pairs={{0,1},{1,0},{2,3},{3,2},{4,5},{5,4},{6,7},{7,6},{8,9},{9,8},{10,11... | collective-permute-start | bytes 786440 | tf_op jit(solution)/shard_map/ppermute | solution.py:308
  9.1 11.2 %collective-permute-start.1 = (bf16[2,128,512]{2,1,0:T(8,128)(2,1)S(1)}, bf16[2,128,512]{2,1,0:T(8,128)(2,1)S(1)}, u32[]{:S(2)}, u32[]{:S(2)}) collective-permute-start(bf16[2,128,512]{2,1,0:T(8,128)(2,1)S(1)} %pad_maximum_fusion.1.mine_ref), channel_id=1, source_target_pairs={{0,12},{2,14},{4,8},{6,10},{8,4},{10,6},{12,0},{14,2},{16,28},{18,... | collective-permute-start | bytes 786440 | tf_op jit(solution)/shard_map/ppermute | solution.py:311
  16.2 7.8 %collective-permute-start.9 = (bf16[2,128,512]{2,1,0:T(8,128)(2,1)S(1)}, bf16[2,128,512]{2,1,0:T(8,128)(2,1)S(1)}, u32[]{:S(2)}, u32[]{:S(2)}) collective-permute-start(bf16[2,128,512]{2,1,0:T(8,128)(2,1)S(1)} %collective-permute-done.8.mine_ref), channel_id=1, source_target_pairs={{0,1},{1,0},{2,3},{3,2},{4,5},{5,4},{6,7},{7,6},{8,9},{9,8},{10,11... | collective-permute-start | bytes 786440 | tf_op jit(solution)/shard_map/ppermute | solution.py:308
  20.3 7.8 %collective-permute-start.11 = (bf16[2,128,512]{2,1,0:T(8,128)(2,1)S(1)}, bf16[2,128,512]{2,1,0:T(8,128)(2,1)S(1)}, u32[]{:S(2)}, u32[]{:S(2)}) collective-permute-start(bf16[2,128,512]{2,1,0:T(8,128)(2,1)S(1)} %collective-permute-done.1.mine_ref), channel_id=1, source_target_pairs={{0,1},{1,0},{2,3},{3,2},{4,5},{5,4},{6,7},{7,6},{8,9},{9,8},{10,11... | collective-permute-start | bytes 786440 | tf_op jit(solution)/shard_map/ppermute | solution.py:308
  20.8 8.9 %collective-permute-start.3 = (bf16[2,256,256]{2,1,0:T(8,128)(2,1)S(1)}, bf16[2,256,256]{2,1,0:T(8,128)(2,1)S(1)}, u32[]{:S(2)}, u32[]{:S(2)}) collective-permute-start(bf16[2,256,256]{2,1,0:T(8,128)(2,1)S(1)} %get-tuple-element.85), channel_id=1, source_target_pairs={{0,4},{2,6},{4,0},{6,2},{8,12},{10,14},{12,8},{14,10},{16,20},{18,... | collective-permute-start | bytes 786440 | tf_op jit(solution)/shard_map/ppermute | solution.py:311
  22.4 8.2 %collective-permute-start.4 = (bf16[2,256,256]{2,1,0:T(8,128)(2,1)S(1)}, bf16[2,256,256]{2,1,0:T(8,128)(2,1)S(1)}, u32[]{:S(2)}, u32[]{:S(2)}) collective-permute-start(bf16[2,256,256]{2,1,0:T(8,128)(2,1)S(1)} %get-tuple-element.86), channel_id=1, source_target_pairs={{0,8},{2,10},{4,12},{6,14},{8,0},{10,2},{12,4},{14,6},{16,24},{18,... | collective-permute-start | bytes 786440 | tf_op jit(solution)/shard_map/ppermute | solution.py:311
  24.0 8.7 %collective-permute-start.5 = (bf16[2,256,256]{2,1,0:T(8,128)(2,1)S(1)}, bf16[2,256,256]{2,1,0:T(8,128)(2,1)S(1)}, u32[]{:S(2)}, u32[]{:S(2)}) collective-permute-start(bf16[2,256,256]{2,1,0:T(8,128)(2,1)S(1)} %get-tuple-element.87), channel_id=1, source_target_pairs={{0,6},{2,4},{4,2},{6,0},{8,14},{10,12},{12,10},{14,8},{16,22},{18,... | collective-permute-start | bytes 786440 | tf_op jit(solution)/shard_map/ppermute | solution.py:311
  24.0 9.5 %collective-permute-start.6 = (bf16[2,256,256]{2,1,0:T(8,128)(2,1)S(1)}, bf16[2,256,256]{2,1,0:T(8,128)(2,1)S(1)}, u32[]{:S(2)}, u32[]{:S(2)}) collective-permute-start(bf16[2,256,256]{2,1,0:T(8,128)(2,1)S(1)} %get-tuple-element.88), channel_id=1, source_target_pairs={{0,10},{2,8},{4,14},{6,12},{8,2},{10,0},{12,6},{14,4},{16,26},{18,... | collective-permute-start | bytes 786440 | tf_op jit(solution)/shard_map/ppermute | solution.py:311
  28.2 5.3 %collective-permute-start.7 = (bf16[2,256,256]{2,1,0:T(8,128)(2,1)S(1)}, bf16[2,256,256]{2,1,0:T(8,128)(2,1)S(1)}, u32[]{:S(2)}, u32[]{:S(2)}) collective-permute-start(bf16[2,256,256]{2,1,0:T(8,128)(2,1)S(1)} %get-tuple-element.89), channel_id=1, source_target_pairs={{0,2},{2,0},{4,6},{6,4},{8,10},{10,8},{12,14},{14,12},{16,18},{18,... | collective-permute-start | bytes 786440 | tf_op jit(solution)/shard_map/ppermute | solution.py:311
  29.6 3.8 %collective-permute-start.10 = (bf16[2,128,256]{2,1,0:T(8,128)(2,1)S(1)}, bf16[2,128,256]{2,1,0:T(8,128)(2,1)S(1)}, u32[]{:S(2)}, u32[]{:S(2)}) collective-permute-start(bf16[2,128,256]{2,1,0:T(8,128)(2,1)S(1)} %get-tuple-element.91), channel_id=1, source_target_pairs={{0,2},{2,0},{4,6},{6,4},{8,10},{10,8},{12,14},{14,12},{16,18},{18,... | collective-permute-start | bytes 393224 | tf_op jit(solution)/shard_map/ppermute | solution.py:311
  30.6 2.9 %collective-permute-start.12 = (bf16[2,128,256]{2,1,0:T(8,128)(2,1)S(1)}, bf16[2,128,256]{2,1,0:T(8,128)(2,1)S(1)}, u32[]{:S(2)}, u32[]{:S(2)}) collective-permute-start(bf16[2,128,256]{2,1,0:T(8,128)(2,1)S(1)} %get-tuple-element.94), channel_id=1, source_target_pairs={{0,2},{2,0},{4,6},{6,4},{8,10},{10,8},{12,14},{14,12},{16,18},{18,... | collective-permute-start | bytes 393224 | tf_op jit(solution)/shard_map/ppermute | solution.py:311
  33.5 6.7 %copy-start = (bf16[1,8,2,256,256]{4,3,2,1,0:T(8,128)(2,1)S(1)}, bf16[1,8,2,256,256]{4,3,2,1,0:T(8,128)(2,1)}, u32[]{:S(2)}) copy-start(bf16[1,8,2,256,256]{4,3,2,1,0:T(8,128)(2,1)} %param.7) | copy-start | bytes 6291460
  38.7 12.7 %collective-permute-start.13 = (bf16[2,256,256]{2,1,0:T(8,128)(2,1)S(1)}, bf16[2,256,256]{2,1,0:T(8,128)(2,1)S(1)}, u32[]{:S(2)}, u32[]{:S(2)}) collective-permute-start(bf16[2,256,256]{2,1,0:T(8,128)(2,1)S(1)} %get-tuple-element.95), channel_id=1, source_target_pairs={{16,8},{18,10},{20,12},{22,14},{24,0},{26,2},{28,4},{30,6},{17,9},... | collective-permute-start | bytes 786440 | tf_op jit(solution)/shard_map/ppermute | solution.py:355
  56.7 9.0 %collective-permute-start.21 = (bf16[2,128,256]{2,1,0:T(8,128)(2,1)S(1)}, bf16[2,128,256]{2,1,0:T(8,128)(2,1)S(1)}, u32[]{:S(2)}, u32[]{:S(2)}) collective-permute-start(bf16[2,128,256]{2,1,0:T(8,128)(2,1)S(1)} %get-tuple-element.107), channel_id=1, source_target_pairs={{0,12},{2,14},{4,8},{6,10},{8,4},{10,6},{12,0},{14,2},{16,28},{18,... | collective-permute-start | bytes 393224 | tf_op jit(solution)/shard_map/ppermute | solution.py:311
  61.8 6.7 %collective-permute-start.22 = (bf16[2,128,256]{2,1,0:T(8,128)(2,1)S(1)}, bf16[2,128,256]{2,1,0:T(8,128)(2,1)S(1)}, u32[]{:S(2)}, u32[]{:S(2)}) collective-permute-start(bf16[2,128,256]{2,1,0:T(8,128)(2,1)S(1)} %get-tuple-element.108), channel_id=1, source_target_pairs={{0,14},{2,12},{4,10},{6,8},{8,6},{10,4},{12,2},{14,0},{16,30},{18,... | collective-permute-start | bytes 393224 | tf_op jit(solution)/shard_map/ppermute | solution.py:311
  61.8 12.3 %collective-permute-start.19 = (bf16[2,256,256]{2,1,0:T(8,128)(2,1)S(1)}, bf16[2,256,256]{2,1,0:T(8,128)(2,1)S(1)}, u32[]{:S(2)}, u32[]{:S(2)}) collective-permute-start(bf16[2,256,256]{2,1,0:T(8,128)(2,1)S(1)} %get-tuple-element.105), channel_id=1, source_target_pairs={{0,4},{2,6},{4,0},{6,2},{8,12},{10,14},{12,8},{14,10},{16,20},{18,... | collective-permute-start | bytes 786440 | tf_op jit(solution)/shard_map/ppermute | solution.py:311
  62.2 14.4 %collective-permute-start.20 = (bf16[2,256,256]{2,1,0:T(8,128)(2,1)S(1)}, bf16[2,256,256]{2,1,0:T(8,128)(2,1)S(1)}, u32[]{:S(2)}, u32[]{:S(2)}) collective-permute-start(bf16[2,256,256]{2,1,0:T(8,128)(2,1)S(1)} %get-tuple-element.106), channel_id=1, source_target_pairs={{0,8},{2,10},{4,12},{6,14},{8,0},{10,2},{12,4},{14,6},{16,24},{18,... | collective-permute-start | bytes 786440 | tf_op jit(solution)/shard_map/ppermute | solution.py:311
  64.7 14.8 %collective-permute-start.16 = (bf16[2,256,256]{2,1,0:T(8,128)(2,1)S(1)}, bf16[2,256,256]{2,1,0:T(8,128)(2,1)S(1)}, u32[]{:S(2)}, u32[]{:S(2)}) collective-permute-start(bf16[2,256,256]{2,1,0:T(8,128)(2,1)S(1)} %get-tuple-element.101), channel_id=1, source_target_pairs={{0,6},{2,4},{4,2},{6,0},{8,14},{10,12},{12,10},{14,8},{16,22},{18,... | collective-permute-start | bytes 786440 | tf_op jit(solution)/shard_map/ppermute | solution.py:311
  65.7 14.1 %collective-permute-start.17 = (bf16[2,256,256]{2,1,0:T(8,128)(2,1)S(1)}, bf16[2,256,256]{2,1,0:T(8,128)(2,1)S(1)}, u32[]{:S(2)}, u32[]{:S(2)}) collective-permute-start(bf16[2,256,256]{2,1,0:T(8,128)(2,1)S(1)} %get-tuple-element.102), channel_id=1, source_target_pairs={{0,10},{2,8},{4,14},{6,12},{8,2},{10,0},{12,6},{14,4},{16,26},{18,... | collective-permute-start | bytes 786440 | tf_op jit(solution)/shard_map/ppermute | solution.py:311
  68.6 11.2 %collective-permute-start.18 = (bf16[2,256,256]{2,1,0:T(8,128)(2,1)S(1)}, bf16[2,256,256]{2,1,0:T(8,128)(2,1)S(1)}, u32[]{:S(2)}, u32[]{:S(2)}) collective-permute-start(bf16[2,256,256]{2,1,0:T(8,128)(2,1)S(1)} %get-tuple-element.103), channel_id=1, source_target_pairs={{0,2},{2,0},{4,6},{6,4},{8,10},{10,8},{12,14},{14,12},{16,18},{18,... | collective-permute-start | bytes 786440 | tf_op jit(solution)/shard_map/ppermute | solution.py:311
  74.1 9.6 %collective-permute-start.14 = (bf16[2,128,256]{2,1,0:T(8,128)(2,1)S(1)}, bf16[2,128,256]{2,1,0:T(8,128)(2,1)S(1)}, u32[]{:S(2)}, u32[]{:S(2)}) collective-permute-start(bf16[2,128,256]{2,1,0:T(8,128)(2,1)S(1)} %get-tuple-element.99), channel_id=1, source_target_pairs={{0,12},{2,14},{4,8},{6,10},{8,4},{10,6},{12,0},{14,2},{16,28},{18,... | collective-permute-start | bytes 393224 | tf_op jit(solution)/shard_map/ppermute | solution.py:311
  76.7 8.7 %collective-permute-start.15 = (bf16[2,128,256]{2,1,0:T(8,128)(2,1)S(1)}, bf16[2,128,256]{2,1,0:T(8,128)(2,1)S(1)}, u32[]{:S(2)}, u32[]{:S(2)}) collective-permute-start(bf16[2,128,256]{2,1,0:T(8,128)(2,1)S(1)} %get-tuple-element.100), channel_id=1, source_target_pairs={{0,14},{2,12},{4,10},{6,8},{8,6},{10,4},{12,2},{14,0},{16,30},{18,... | collective-permute-start | bytes 393224 | tf_op jit(solution)/shard_map/ppermute | solution.py:311
  80.9 8.2 %collective-permute-start.24 = (bf16[2,128,512]{2,1,0:T(8,128)(2,1)S(1)}, bf16[2,128,512]{2,1,0:T(8,128)(2,1)S(1)}, u32[]{:S(2)}, u32[]{:S(2)}) collective-permute-start(bf16[2,128,512]{2,1,0:T(8,128)(2,1)S(1)} %get-tuple-element.114), channel_id=1, source_target_pairs={{0,1},{1,0},{2,3},{3,2},{4,5},{5,4},{6,7},{7,6},{8,9},{9,8},{10,11... | collective-permute-start | bytes 786440 | tf_op jit(solution)/shard_map/ppermute | solution.py:308
  86.3 8.4 %collective-permute-start.23 = (bf16[2,128,512]{2,1,0:T(8,128)(2,1)S(1)}, bf16[2,128,512]{2,1,0:T(8,128)(2,1)S(1)}, u32[]{:S(2)}, u32[]{:S(2)}) collective-permute-start(bf16[2,128,512]{2,1,0:T(8,128)(2,1)S(1)} %get-tuple-element.112), channel_id=1, source_target_pairs={{0,1},{1,0},{2,3},{3,2},{4,5},{5,4},{6,7},{7,6},{8,9},{9,8},{10,11... | collective-permute-start | bytes 786440 | tf_op jit(solution)/shard_map/ppermute | solution.py:308

commit v15 on v14

--- a/solution.py
+++ b/solution.py
@@ -270,7 +270,7 @@
             away_ref[part, rows_at, right] = ((every - mine) - (at_left - mine_left)).astype(bf16)
         return 0
 
-    lax.fori_loop(0, rows // tall, one, 0)
+    lax.fori_loop(0, rows // tall, one, 0, unroll=2)
 
 
 def finish(chunk, own, come, shape, before):

time: 95.7 us -> 95.7 us (level)
  no operation moved by 1% of the time
where the time goes in v15:
time: 95.7 us; the launch traced here: 95.5 us
  waiting for transfers between devices  40.3 us (42%)
  starting transfers between devices  27.5 us (29%)
  Pallas kernels  24.6 us (26%)
  other arithmetic  2.96 us (3%)
    pallas_call x13, Pallas kernels, run(): pl.pallas_call(kernel, grid_spec=pltpu.PrefetchScalarGridSpec(num_scalar_...  22.9 us
    ppermute x18, waiting for transfers between devices, to_distance(): return lax.ppermute(value, 'sec', [(s, s ^ d) for s in range(sections)])  20.2 us
    ppermute x18, starting transfers between devices, to_distance(): return lax.ppermute(value, 'sec', [(s, s ^ d) for s in range(sections)])  18.8 us
    ppermute x6, waiting for transfers between devices, to_other_half(): return lax.ppermute(value, 'scan', [(0, 1), (1, 0)])  11.4 us
    ppermute x1, waiting for transfers between devices, on_device(): lax.ppermute(leave, 'sec', [(s, s - count ^ count // 2) for s in range(co...  8.76 us
    ppermute x6, starting transfers between devices, to_other_half(): return lax.ppermute(value, 'scan', [(0, 1), (1, 0)])  7.2 us
    convert_element_type x2, other arithmetic, coded(): jnp.exp(code_gain * trans_re).astype(bf16)  2.91 us
  transfers between devices with their start and end apart: 25, of which 17 were waited for; matrix products, arithmetic and copies ran while one was open for 1% of the time, Pallas kernels for 14%

profile of v15, /device:TPU:0, one launch (start us, length us, event | category | flops | bytes accessed | tf_op | source)
XLA Modules:
  0.0 95.5 jit_solution(1805466670302158568)
XLA Ops:
  0.0 1.5 %fusion.4 = (bf16[1,128,512]{2,1,0:T(8,128)(2,1)S(1)}, bf16[1,128,512]{2,1,0:T(8,128)(2,1)S(1)}) fusion(f32[1,256,512]{2,1,0:T(8,128)} %param.5, f32[1,256,512]{2,1,0:T(8,128)} %param.6), kind=kLoop, calls=%fused_computation.8 | loop fusion | flops 2424832 | bytes 786432 | tf_op jit(solution)/shard_map/convert_element_type | solution.py:66
  1.6 3.0 %collective-permute-start = (bf16[2,128,512]{2,1,0:T(8,128)(2,1)S(1)}, bf16[2,128,512]{2,1,0:T(8,128)(2,1)S(1)}, u32[]{:S(2)}, u32[]{:S(2)}) collective-permute-start(bf16[2,128,512]{2,1,0:T(8,128)(2,1)S(1)} %pad_maximum_fusion.mine_ref), channel_id=1, source_target_pairs={{0,1},{1,0},{2,3},{3,2},{4,5},{5,4},{6,7},{7,6},{8,9},{9,8},{10,11... | collective-permute-start | bytes 786440 | tf_op jit(solution)/shard_map/ppermute | solution.py:308
  4.6 1.4 %fusion.13 = (bf16[1,128,512]{2,1,0:T(8,128)(2,1)S(1)}, bf16[1,128,512]{2,1,0:T(8,128)(2,1)S(1)}) fusion(f32[1,256,512]{2,1,0:T(8,128)} %param.5, f32[1,256,512]{2,1,0:T(8,128)} %param.6), kind=kLoop, calls=%fused_computation.17 | loop fusion | flops 2424832 | bytes 786432 | tf_op jit(solution)/shard_map/convert_element_type | solution.py:66
  6.0 2.6 %collective-permute-start.8 = (bf16[2,128,512]{2,1,0:T(8,128)(2,1)S(1)}, bf16[2,128,512]{2,1,0:T(8,128)(2,1)S(1)}, u32[]{:S(2)}, u32[]{:S(2)}) collective-permute-start(bf16[2,128,512]{2,1,0:T(8,128)(2,1)S(1)} %pad_maximum_fusion.mine_ref), channel_id=1, source_target_pairs={{0,12},{2,14},{4,8},{6,10},{8,4},{10,6},{12,0},{14,2},{16,28},{18,... | collective-permute-start | bytes 786440 | tf_op jit(solution)/shard_map/ppermute | solution.py:311
  9.2 1.2 %shard_map.55 = (bf16[2,256,256]{2,1,0:T(8,128)(2,1)S(1)}, bf16[256,256]{1,0:T(8,128)(2,1)S(1)}, bf16[256,256]{1,0:T(8,128)(2,1)S(1)}) custom-call(s32[2,8]{1,0:T(2,128)S(1)} %bitcast.4, bf16[8,2,256,256]{3,2,1,0:T(8,128)(2,1)S(1)} %copy-done.1), custom_call_target="tpu_custom_call" | custom-call | bytes 2621504 | tf_op jit(solution)/shard_map/pallas_call | solution.py:27
  11.3 1.0 %shard_map.56 = (bf16[2,256,256]{2,1,0:T(8,128)(2,1)S(1)}, bf16[2,256,256]{2,1,0:T(8,128)(2,1)S(1)}, bf16[2,256,256]{2,1,0:T(8,128)(2,1)S(1)}, bf16[2,256,256]{2...) custom-call(s32[2,8]{1,0:T(2,128)S(1)} %bitcast.5, ...), custom_call_target="tpu_custom_call" | custom-call | bytes 2097216 | tf_op jit(solution)/shard_map/pallas_call | solution.py:27
  12.3 3.9 %collective-permute-done.8.mine_ref = bf16[2,128,512]{2,1,0:T(8,128)(2,1)S(1)} collective-permute-done((bf16[2,128,512]{2,1,0:T(8,128)(2,1)S(1)}, bf16[2,128,512]{2,1,0:T(8,128)(2,1)S(1)}, u32[]{:S(2)}, u32[]{:S(2)}) %collective-permute-start.8) | collective-permute-done | bytes 262176 | tf_op jit(solution)/shard_map/ppermute | solution.py:311
  17.0 1.1 %shard_map.57 = (bf16[2,256,256]{2,1,0:T(8,128)(2,1)S(1)}, bf16[2,256,256]{2,1,0:T(8,128)(2,1)S(1)}, bf16[2,256,256]{2,1,0:T(8,128)(2,1)S(1)}, bf16[2,256,256]{2...) custom-call(s32[2,8]{1,0:T(2,128)S(1)} %bitcast.6, ...), custom_call_target="tpu_custom_call", output_to_operand_aliasing={{0}: (3, {}), {1}: (4, {}), {2}: (5, {}), {3}: (6, {}), {4}... | custom-call | bytes 3670080 | tf_op jit(solution)/shard_map/pallas_call | solution.py:27
  18.1 2.3 %collective-permute-done.1.mine_ref = bf16[2,128,512]{2,1,0:T(8,128)(2,1)S(1)} collective-permute-done((bf16[2,128,512]{2,1,0:T(8,128)(2,1)S(1)}, bf16[2,128,512]{2,1,0:T(8,128)(2,1)S(1)}, u32[]{:S(2)}, u32[]{:S(2)}) %collective-permute-start.1) | collective-permute-done | bytes 262176 | tf_op jit(solution)/shard_map/ppermute | solution.py:311
  20.8 1.6 %collective-permute-start.3 = (bf16[2,256,256]{2,1,0:T(8,128)(2,1)S(1)}, bf16[2,256,256]{2,1,0:T(8,128)(2,1)S(1)}, u32[]{:S(2)}, u32[]{:S(2)}) collective-permute-start(bf16[2,256,256]{2,1,0:T(8,128)(2,1)S(1)} %get-tuple-element.85), channel_id=1, source_target_pairs={{0,4},{2,6},{4,0},{6,2},{8,12},{10,14},{12,8},{14,10},{16,20},{18,... | collective-permute-start | bytes 786440 | tf_op jit(solution)/shard_map/ppermute | solution.py:311
  22.4 1.6 %collective-permute-start.4 = (bf16[2,256,256]{2,1,0:T(8,128)(2,1)S(1)}, bf16[2,256,256]{2,1,0:T(8,128)(2,1)S(1)}, u32[]{:S(2)}, u32[]{:S(2)}) collective-permute-start(bf16[2,256,256]{2,1,0:T(8,128)(2,1)S(1)} %get-tuple-element.86), channel_id=1, source_target_pairs={{0,8},{2,10},{4,12},{6,14},{8,0},{10,2},{12,4},{14,6},{16,24},{18,... | collective-permute-start | bytes 786440 | tf_op jit(solution)/shard_map/ppermute | solution.py:311
  24.5 3.6 %collective-permute-done.11.other_ref = bf16[2,128,512]{2,1,0:T(8,128)(2,1)S(1)} collective-permute-done((bf16[2,128,512]{2,1,0:T(8,128)(2,1)S(1)}, bf16[2,128,512]{2,1,0:T(8,128)(2,1)S(1)}, u32[]{:S(2)}, u32[]{:S(2)}) %collective-permute-start.11) | collective-permute-done | bytes 262176 | tf_op jit(solution)/shard_map/ppermute | solution.py:308
  30.6 2.1 %collective-permute-done.5.refs_3_ = bf16[2,256,256]{2,1,0:T(8,128)(2,1)S(1)} collective-permute-done((bf16[2,256,256]{2,1,0:T(8,128)(2,1)S(1)}, bf16[2,256,256]{2,1,0:T(8,128)(2,1)S(1)}, u32[]{:S(2)}, u32[]{:S(2)}) %collective-permute-start.5) | collective-permute-done | bytes 262176 | tf_op jit(solution)/shard_map/ppermute | solution.py:311
  33.5 5.2 %shard_map.60 = (bf16[2,256,256]{2,1,0:T(8,128)(2,1)S(1)}, bf16[8,2,256,256]{3,2,1,0:T(8,128)(2,1)S(1)}) custom-call(bf16[2,256,256]{2,1,0:T(8,128)(2,1)S(1)} %get-tuple-element.63.start_ref, bf16[256,256]{1,0:T(8,128)(2,1)S(1)} %get-tuple-element.64.down_ref, bf16[256,256]{1,0:T(8,128)(2,1)S(1)} %get-tuple-element.65.across_ref, ...), custom_call_target="tpu_custom_call" | custom-call | flops 2147483648 | bytes 4980736 | tf_op jit(solution)/shard_map/pallas_call | solution.py:27
  38.7 1.5 %collective-permute-start.13 = (bf16[2,256,256]{2,1,0:T(8,128)(2,1)S(1)}, bf16[2,256,256]{2,1,0:T(8,128)(2,1)S(1)}, u32[]{:S(2)}, u32[]{:S(2)}) collective-permute-start(bf16[2,256,256]{2,1,0:T(8,128)(2,1)S(1)} %get-tuple-element.95), channel_id=1, source_target_pairs={{16,8},{18,10},{20,12},{22,14},{24,0},{26,2},{28,4},{30,6},{17,9},... | collective-permute-start | bytes 786440 | tf_op jit(solution)/shard_map/ppermute | solution.py:355
  40.2 2.5 %shard_map.61.wave_ref = bf16[8,2,256,256]{3,2,1,0:T(8,128)(2,1)S(1)} custom-call(s32[2,8]{1,0:T(2,128)S(1)} %bitcast.9, bf16[8,2,256,256]{3,2,1,0:T(8,128)(2,1)S(1)} %bitcast.3), custom_call_target="tpu_custom_call" | custom-call | bytes 4194368 | tf_op jit(solution)/shard_map/pallas_call | solution.py:27
  42.7 8.8 %collective-permute-done.13.come_ref = bf16[2,256,256]{2,1,0:T(8,128)(2,1)S(1)} collective-permute-done((bf16[2,256,256]{2,1,0:T(8,128)(2,1)S(1)}, bf16[2,256,256]{2,1,0:T(8,128)(2,1)S(1)}, u32[]{:S(2)}, u32[]{:S(2)}) %collective-permute-start.13) | collective-permute-done | bytes 262176 | tf_op jit(solution)/shard_map/ppermute | solution.py:355
  51.5 5.2 %shard_map.62 = (bf16[2,256,256]{2,1,0:T(8,128)(2,1)S(1)}, bf16[2,256,256]{2,1,0:T(8,128)(2,1)S(1)}, bf16[2,256,256]{2,1,0:T(8,128)(2,1)S(1)}, bf16[2,256,256]{2...) custom-call(bf16[2,256,256]{2,1,0:T(8,128)(2,1)S(1)} %get-tuple-elem, ...), custom_call_target="tpu_custom_call" | custom-call | flops 2147483648 | bytes 4980736 | tf_op jit(solution)/shard_map/pallas_call | solution.py:27
  56.7 5.1 %collective-permute-start.21 = (bf16[2,128,256]{2,1,0:T(8,128)(2,1)S(1)}, bf16[2,128,256]{2,1,0:T(8,128)(2,1)S(1)}, u32[]{:S(2)}, u32[]{:S(2)}) collective-permute-start(bf16[2,128,256]{2,1,0:T(8,128)(2,1)S(1)} %get-tuple-element.107), channel_id=1, source_target_pairs={{0,12},{2,14},{4,8},{6,10},{8,4},{10,6},{12,0},{14,2},{16,28},{18,... | collective-permute-start | bytes 393224 | tf_op jit(solution)/shard_map/ppermute | solution.py:311
  62.2 2.5 %collective-permute-start.20 = (bf16[2,256,256]{2,1,0:T(8,128)(2,1)S(1)}, bf16[2,256,256]{2,1,0:T(8,128)(2,1)S(1)}, u32[]{:S(2)}, u32[]{:S(2)}) collective-permute-start(bf16[2,256,256]{2,1,0:T(8,128)(2,1)S(1)} %get-tuple-element.106), channel_id=1, source_target_pairs={{0,8},{2,10},{4,12},{6,14},{8,0},{10,2},{12,4},{14,6},{16,24},{18,... | collective-permute-start | bytes 786440 | tf_op jit(solution)/shard_map/ppermute | solution.py:311
  65.7 1.1 %collective-permute-start.17 = (bf16[2,256,256]{2,1,0:T(8,128)(2,1)S(1)}, bf16[2,256,256]{2,1,0:T(8,128)(2,1)S(1)}, u32[]{:S(2)}, u32[]{:S(2)}) collective-permute-start(bf16[2,256,256]{2,1,0:T(8,128)(2,1)S(1)} %get-tuple-element.102), channel_id=1, source_target_pairs={{0,10},{2,8},{4,14},{6,12},{8,2},{10,0},{12,6},{14,4},{16,26},{18,... | collective-permute-start | bytes 786440 | tf_op jit(solution)/shard_map/ppermute | solution.py:311
  66.8 1.8 %collective-permute-done.22.refs_4_ = bf16[2,128,256]{2,1,0:T(8,128)(2,1)S(1)} collective-permute-done((bf16[2,128,256]{2,1,0:T(8,128)(2,1)S(1)}, bf16[2,128,256]{2,1,0:T(8,128)(2,1)S(1)}, u32[]{:S(2)}, u32[]{:S(2)}) %collective-permute-start.22) | collective-permute-done | bytes 131104 | tf_op jit(solution)/shard_map/ppermute | solution.py:311
  68.6 5.5 %collective-permute-done.19.refs_1_ = bf16[2,256,256]{2,1,0:T(8,128)(2,1)S(1)} collective-permute-done((bf16[2,256,256]{2,1,0:T(8,128)(2,1)S(1)}, bf16[2,256,256]{2,1,0:T(8,128)(2,1)S(1)}, u32[]{:S(2)}, u32[]{:S(2)}) %collective-permute-start.19) | collective-permute-done | bytes 262176 | tf_op jit(solution)/shard_map/ppermute | solution.py:311
  74.1 2.6 %collective-permute-start.14 = (bf16[2,128,256]{2,1,0:T(8,128)(2,1)S(1)}, bf16[2,128,256]{2,1,0:T(8,128)(2,1)S(1)}, u32[]{:S(2)}, u32[]{:S(2)}) collective-permute-start(bf16[2,128,256]{2,1,0:T(8,128)(2,1)S(1)} %get-tuple-element.99), channel_id=1, source_target_pairs={{0,12},{2,14},{4,8},{6,10},{8,4},{10,6},{12,0},{14,2},{16,28},{18,... | collective-permute-start | bytes 393224 | tf_op jit(solution)/shard_map/ppermute | solution.py:311
  77.7 1.2 %shard_map.64.refs_3_ = f32[8,128,256]{2,1,0:T(8,128)S(1)} custom-call(s32[2,8]{1,0:T(2,128)S(1)} %bitcast.11, bf16[8,2,256,256]{3,2,1,0:T(8,128)(2,1)S(1)} %shard_map.61.wave_ref, bf16[2,256,256]{2,1,0:T(8,128)(2,1)S(1)} %get-tuple-element.104.refs_0_, bf16[2,256,256]{2,1,0:T(8,128)(2,1)S(1)} %collective-permute-done.19.refs_1_, ...), custom_call_target="tpu_custom_call" | custom-call | bytes 4194368 | tf_op jit(solution)/shard_map/pallas_call | solution.py:27
  79.8 1.1 %shard_map.65 = (f32[2,128,512]{2,1,0:T(8,128)S(1)}, bf16[2,128,512]{2,1,0:T(8,128)(2,1)S(1)}) custom-call(s32[2,8]{1,0:T(2,128)S(1)} %bitcast.12, bf16[8,2,256,256]{3,2,1,0:T(8,128)(2,1)S(1)} %shard_map.61.wave_ref, bf16[2,256,256]{2,1,0:T(8,128)(2,1)S(1)} %collective-permute-done.16.refs_0_, bf16[2,256,256]{2,1,0:T(8,128)(2,1)S(1)} %collective-permute-done.17.refs_1_, ...), custom_call_target="tpu_custom_call" | custom-call | bytes 4718656 | tf_op jit(solution)/shard_map/pallas_call | solution.py:27
  80.8 1.8 %collective-permute-start.24 = (bf16[2,128,512]{2,1,0:T(8,128)(2,1)S(1)}, bf16[2,128,512]{2,1,0:T(8,128)(2,1)S(1)}, u32[]{:S(2)}, u32[]{:S(2)}) collective-permute-start(bf16[2,128,512]{2,1,0:T(8,128)(2,1)S(1)} %get-tuple-element.114), channel_id=1, source_target_pairs={{0,1},{1,0},{2,3},{3,2},{4,5},{5,4},{6,7},{7,6},{8,9},{9,8},{10,11... | collective-permute-start | bytes 786440 | tf_op jit(solution)/shard_map/ppermute | solution.py:308
  82.6 1.0 %shard_map.66.refs_2_ = f32[8,128,256]{2,1,0:T(8,128)S(1)} custom-call(s32[2,8]{1,0:T(2,128)S(1)} %bitcast.13, bf16[8,2,256,256]{3,2,1,0:T(8,128)(2,1)S(1)} %shard_map.61.wave_ref, bf16[2,256,256]{2,1,0:T(8,128)(2,1)S(1)} %collective-permute-done.16.refs_0_, bf16[2,256,256]{2,1,0:T(8,128)(2,1)S(1)} %collective-permute-done.17.refs_1_, ...), custom_call_target="tpu_custom_call" | custom-call | bytes 4980800 | tf_op jit(solution)/shard_map/pallas_call | solution.py:27
  83.7 1.7 %collective-permute-done.15.refs_1_ = bf16[2,128,256]{2,1,0:T(8,128)(2,1)S(1)} collective-permute-done((bf16[2,128,256]{2,1,0:T(8,128)(2,1)S(1)}, bf16[2,128,256]{2,1,0:T(8,128)(2,1)S(1)}, u32[]{:S(2)}, u32[]{:S(2)}) %collective-permute-start.15) | collective-permute-done | bytes 131104 | tf_op jit(solution)/shard_map/ppermute | solution.py:311
  86.3 1.3 %collective-permute-start.23 = (bf16[2,128,512]{2,1,0:T(8,128)(2,1)S(1)}, bf16[2,128,512]{2,1,0:T(8,128)(2,1)S(1)}, u32[]{:S(2)}, u32[]{:S(2)}) collective-permute-start(bf16[2,128,512]{2,1,0:T(8,128)(2,1)S(1)} %get-tuple-element.112), channel_id=1, source_target_pairs={{0,1},{1,0},{2,3},{3,2},{4,5},{5,4},{6,7},{7,6},{8,9},{9,8},{10,11... | collective-permute-start | bytes 786440 | tf_op jit(solution)/shard_map/ppermute | solution.py:308
  87.6 1.4 %collective-permute-done.24.come_ref = bf16[2,128,512]{2,1,0:T(8,128)(2,1)S(1)} collective-permute-done((bf16[2,128,512]{2,1,0:T(8,128)(2,1)S(1)}, bf16[2,128,512]{2,1,0:T(8,128)(2,1)S(1)}, u32[]{:S(2)}, u32[]{:S(2)}) %collective-permute-start.24) | collective-permute-done | bytes 262176 | tf_op jit(solution)/shard_map/ppermute | solution.py:308
  89.9 4.8 %collective-permute-done.23.come_ref = bf16[2,128,512]{2,1,0:T(8,128)(2,1)S(1)} collective-permute-done((bf16[2,128,512]{2,1,0:T(8,128)(2,1)S(1)}, bf16[2,128,512]{2,1,0:T(8,128)(2,1)S(1)}, u32[]{:S(2)}, u32[]{:S(2)}) %collective-permute-start.23) | collective-permute-done | bytes 262176 | tf_op jit(solution)/shard_map/ppermute | solution.py:308
  (43 shorter events, 12.4 us)
Async XLA Ops:
  0.0 9.2 %copy-start.2 = (s32[8,2]{0,1:T(2,128)S(1)}, s32[8,2]{0,1:T(2,128)}, u32[]{:S(2)}) copy-start(s32[8,2]{0,1:T(2,128)} %param.9) | copy-start | bytes 196
  0.0 9.2 %copy-start.1 = (bf16[8,2,256,256]{3,2,1,0:T(8,128)(2,1)S(1)}, bf16[8,2,256,256]{3,2,1,0:T(8,128)(2,1)}, u32[]{:S(2)}) copy-start(bf16[8,2,256,256]{3,2,1,0:T(8,128)(2,1)} %exit_ref.1) | copy-start | bytes 6291460
  1.6 9.7 %collective-permute-start = (bf16[2,128,512]{2,1,0:T(8,128)(2,1)S(1)}, bf16[2,128,512]{2,1,0:T(8,128)(2,1)S(1)}, u32[]{:S(2)}, u32[]{:S(2)}) collective-permute-start(bf16[2,128,512]{2,1,0:T(8,128)(2,1)S(1)} %pad_maximum_fusion.mine_ref), channel_id=1, source_target_pairs={{0,1},{1,0},{2,3},{3,2},{4,5},{5,4},{6,7},{7,6},{8,9},{9,8},{10,11... | collective-permute-start | bytes 786440 | tf_op jit(solution)/shard_map/ppermute | solution.py:308
  6.0 10.2 %collective-permute-start.8 = (bf16[2,128,512]{2,1,0:T(8,128)(2,1)S(1)}, bf16[2,128,512]{2,1,0:T(8,128)(2,1)S(1)}, u32[]{:S(2)}, u32[]{:S(2)}) collective-permute-start(bf16[2,128,512]{2,1,0:T(8,128)(2,1)S(1)} %pad_maximum_fusion.mine_ref), channel_id=1, source_target_pairs={{0,12},{2,14},{4,8},{6,10},{8,4},{10,6},{12,0},{14,2},{16,28},{18,... | collective-permute-start | bytes 786440 | tf_op jit(solution)/shard_map/ppermute | solution.py:311
  8.6 8.4 %collective-permute-start.2 = (bf16[2,128,512]{2,1,0:T(8,128)(2,1)S(1)}, bf16[2,128,512]{2,1,0:T(8,128)(2,1)S(1)}, u32[]{:S(2)}, u32[]{:S(2)}) collective-permute-start(bf16[2,128,512]{2,1,0:T(8,128)(2,1)S(1)} %pad_maximum_fusion.1.mine_ref), channel_id=1, source_target_pairs={{0,1},{1,0},{2,3},{3,2},{4,5},{5,4},{6,7},{7,6},{8,9},{9,8},{10,11... | collective-permute-start | bytes 786440 | tf_op jit(solution)/shard_map/ppermute | solution.py:308
  9.1 11.2 %collective-permute-start.1 = (bf16[2,128,512]{2,1,0:T(8,128)(2,1)S(1)}, bf16[2,128,512]{2,1,0:T(8,128)(2,1)S(1)}, u32[]{:S(2)}, u32[]{:S(2)}) collective-permute-start(bf16[2,128,512]{2,1,0:T(8,128)(2,1)S(1)} %pad_maximum_fusion.1.mine_ref), channel_id=1, source_target_pairs={{0,12},{2,14},{4,8},{6,10},{8,4},{10,6},{12,0},{14,2},{16,28},{18,... | collective-permute-start | bytes 786440 | tf_op jit(solution)/shard_map/ppermute | solution.py:311
  16.2 7.8 %collective-permute-start.9 = (bf16[2,128,512]{2,1,0:T(8,128)(2,1)S(1)}, bf16[2,128,512]{2,1,0:T(8,128)(2,1)S(1)}, u32[]{:S(2)}, u32[]{:S(2)}) collective-permute-start(bf16[2,128,512]{2,1,0:T(8,128)(2,1)S(1)} %collective-permute-done.8.mine_ref), channel_id=1, source_target_pairs={{0,1},{1,0},{2,3},{3,2},{4,5},{5,4},{6,7},{7,6},{8,9},{9,8},{10,11... | collective-permute-start | bytes 786440 | tf_op jit(solution)/shard_map/ppermute | solution.py:308
  20.3 7.8 %collective-permute-start.11 = (bf16[2,128,512]{2,1,0:T(8,128)(2,1)S(1)}, bf16[2,128,512]{2,1,0:T(8,128)(2,1)S(1)}, u32[]{:S(2)}, u32[]{:S(2)}) collective-permute-start(bf16[2,128,512]{2,1,0:T(8,128)(2,1)S(1)} %collective-permute-done.1.mine_ref), channel_id=1, source_target_pairs={{0,1},{1,0},{2,3},{3,2},{4,5},{5,4},{6,7},{7,6},{8,9},{9,8},{10,11... | collective-permute-start | bytes 786440 | tf_op jit(solution)/shard_map/ppermute | solution.py:308
  20.8 8.9 %collective-permute-start.3 = (bf16[2,256,256]{2,1,0:T(8,128)(2,1)S(1)}, bf16[2,256,256]{2,1,0:T(8,128)(2,1)S(1)}, u32[]{:S(2)}, u32[]{:S(2)}) collective-permute-start(bf16[2,256,256]{2,1,0:T(8,128)(2,1)S(1)} %get-tuple-element.85), channel_id=1, source_target_pairs={{0,4},{2,6},{4,0},{6,2},{8,12},{10,14},{12,8},{14,10},{16,20},{18,... | collective-permute-start | bytes 786440 | tf_op jit(solution)/shard_map/ppermute | solution.py:311
  22.4 8.2 %collective-permute-start.4 = (bf16[2,256,256]{2,1,0:T(8,128)(2,1)S(1)}, bf16[2,256,256]{2,1,0:T(8,128)(2,1)S(1)}, u32[]{:S(2)}, u32[]{:S(2)}) collective-permute-start(bf16[2,256,256]{2,1,0:T(8,128)(2,1)S(1)} %get-tuple-element.86), channel_id=1, source_target_pairs={{0,8},{2,10},{4,12},{6,14},{8,0},{10,2},{12,4},{14,6},{16,24},{18,... | collective-permute-start | bytes 786440 | tf_op jit(solution)/shard_map/ppermute | solution.py:311
  24.0 8.7 %collective-permute-start.5 = (bf16[2,256,256]{2,1,0:T(8,128)(2,1)S(1)}, bf16[2,256,256]{2,1,0:T(8,128)(2,1)S(1)}, u32[]{:S(2)}, u32[]{:S(2)}) collective-permute-start(bf16[2,256,256]{2,1,0:T(8,128)(2,1)S(1)} %get-tuple-element.87), channel_id=1, source_target_pairs={{0,6},{2,4},{4,2},{6,0},{8,14},{10,12},{12,10},{14,8},{16,22},{18,... | collective-permute-start | bytes 786440 | tf_op jit(solution)/shard_map/ppermute | solution.py:311
  24.0 9.5 %collective-permute-start.6 = (bf16[2,256,256]{2,1,0:T(8,128)(2,1)S(1)}, bf16[2,256,256]{2,1,0:T(8,128)(2,1)S(1)}, u32[]{:S(2)}, u32[]{:S(2)}) collective-permute-start(bf16[2,256,256]{2,1,0:T(8,128)(2,1)S(1)} %get-tuple-element.88), channel_id=1, source_target_pairs={{0,10},{2,8},{4,14},{6,12},{8,2},{10,0},{12,6},{14,4},{16,26},{18,... | collective-permute-start | bytes 786440 | tf_op jit(solution)/shard_map/ppermute | solution.py:311
  28.2 5.3 %collective-permute-start.7 = (bf16[2,256,256]{2,1,0:T(8,128)(2,1)S(1)}, bf16[2,256,256]{2,1,0:T(8,128)(2,1)S(1)}, u32[]{:S(2)}, u32[]{:S(2)}) collective-permute-start(bf16[2,256,256]{2,1,0:T(8,128)(2,1)S(1)} %get-tuple-element.89), channel_id=1, source_target_pairs={{0,2},{2,0},{4,6},{6,4},{8,10},{10,8},{12,14},{14,12},{16,18},{18,... | collective-permute-start | bytes 786440 | tf_op jit(solution)/shard_map/ppermute | solution.py:311
  29.6 3.8 %collective-permute-start.10 = (bf16[2,128,256]{2,1,0:T(8,128)(2,1)S(1)}, bf16[2,128,256]{2,1,0:T(8,128)(2,1)S(1)}, u32[]{:S(2)}, u32[]{:S(2)}) collective-permute-start(bf16[2,128,256]{2,1,0:T(8,128)(2,1)S(1)} %get-tuple-element.91), channel_id=1, source_target_pairs={{0,2},{2,0},{4,6},{6,4},{8,10},{10,8},{12,14},{14,12},{16,18},{18,... | collective-permute-start | bytes 393224 | tf_op jit(solution)/shard_map/ppermute | solution.py:311
  30.6 2.9 %collective-permute-start.12 = (bf16[2,128,256]{2,1,0:T(8,128)(2,1)S(1)}, bf16[2,128,256]{2,1,0:T(8,128)(2,1)S(1)}, u32[]{:S(2)}, u32[]{:S(2)}) collective-permute-start(bf16[2,128,256]{2,1,0:T(8,128)(2,1)S(1)} %get-tuple-element.94), channel_id=1, source_target_pairs={{0,2},{2,0},{4,6},{6,4},{8,10},{10,8},{12,14},{14,12},{16,18},{18,... | collective-permute-start | bytes 393224 | tf_op jit(solution)/shard_map/ppermute | solution.py:311
  33.5 6.7 %copy-start = (bf16[1,8,2,256,256]{4,3,2,1,0:T(8,128)(2,1)S(1)}, bf16[1,8,2,256,256]{4,3,2,1,0:T(8,128)(2,1)}, u32[]{:S(2)}) copy-start(bf16[1,8,2,256,256]{4,3,2,1,0:T(8,128)(2,1)} %param.7) | copy-start | bytes 6291460
  38.7 12.7 %collective-permute-start.13 = (bf16[2,256,256]{2,1,0:T(8,128)(2,1)S(1)}, bf16[2,256,256]{2,1,0:T(8,128)(2,1)S(1)}, u32[]{:S(2)}, u32[]{:S(2)}) collective-permute-start(bf16[2,256,256]{2,1,0:T(8,128)(2,1)S(1)} %get-tuple-element.95), channel_id=1, source_target_pairs={{16,8},{18,10},{20,12},{22,14},{24,0},{26,2},{28,4},{30,6},{17,9},... | collective-permute-start | bytes 786440 | tf_op jit(solution)/shard_map/ppermute | solution.py:355
  56.7 9.0 %collective-permute-start.21 = (bf16[2,128,256]{2,1,0:T(8,128)(2,1)S(1)}, bf16[2,128,256]{2,1,0:T(8,128)(2,1)S(1)}, u32[]{:S(2)}, u32[]{:S(2)}) collective-permute-start(bf16[2,128,256]{2,1,0:T(8,128)(2,1)S(1)} %get-tuple-element.107), channel_id=1, source_target_pairs={{0,12},{2,14},{4,8},{6,10},{8,4},{10,6},{12,0},{14,2},{16,28},{18,... | collective-permute-start | bytes 393224 | tf_op jit(solution)/shard_map/ppermute | solution.py:311
  61.8 6.7 %collective-permute-start.22 = (bf16[2,128,256]{2,1,0:T(8,128)(2,1)S(1)}, bf16[2,128,256]{2,1,0:T(8,128)(2,1)S(1)}, u32[]{:S(2)}, u32[]{:S(2)}) collective-permute-start(bf16[2,128,256]{2,1,0:T(8,128)(2,1)S(1)} %get-tuple-element.108), channel_id=1, source_target_pairs={{0,14},{2,12},{4,10},{6,8},{8,6},{10,4},{12,2},{14,0},{16,30},{18,... | collective-permute-start | bytes 393224 | tf_op jit(solution)/shard_map/ppermute | solution.py:311
  61.8 12.3 %collective-permute-start.19 = (bf16[2,256,256]{2,1,0:T(8,128)(2,1)S(1)}, bf16[2,256,256]{2,1,0:T(8,128)(2,1)S(1)}, u32[]{:S(2)}, u32[]{:S(2)}) collective-permute-start(bf16[2,256,256]{2,1,0:T(8,128)(2,1)S(1)} %get-tuple-element.105), channel_id=1, source_target_pairs={{0,4},{2,6},{4,0},{6,2},{8,12},{10,14},{12,8},{14,10},{16,20},{18,... | collective-permute-start | bytes 786440 | tf_op jit(solution)/shard_map/ppermute | solution.py:311
  62.2 14.4 %collective-permute-start.20 = (bf16[2,256,256]{2,1,0:T(8,128)(2,1)S(1)}, bf16[2,256,256]{2,1,0:T(8,128)(2,1)S(1)}, u32[]{:S(2)}, u32[]{:S(2)}) collective-permute-start(bf16[2,256,256]{2,1,0:T(8,128)(2,1)S(1)} %get-tuple-element.106), channel_id=1, source_target_pairs={{0,8},{2,10},{4,12},{6,14},{8,0},{10,2},{12,4},{14,6},{16,24},{18,... | collective-permute-start | bytes 786440 | tf_op jit(solution)/shard_map/ppermute | solution.py:311
  64.7 14.8 %collective-permute-start.16 = (bf16[2,256,256]{2,1,0:T(8,128)(2,1)S(1)}, bf16[2,256,256]{2,1,0:T(8,128)(2,1)S(1)}, u32[]{:S(2)}, u32[]{:S(2)}) collective-permute-start(bf16[2,256,256]{2,1,0:T(8,128)(2,1)S(1)} %get-tuple-element.101), channel_id=1, source_target_pairs={{0,6},{2,4},{4,2},{6,0},{8,14},{10,12},{12,10},{14,8},{16,22},{18,... | collective-permute-start | bytes 786440 | tf_op jit(solution)/shard_map/ppermute | solution.py:311
  65.7 14.1 %collective-permute-start.17 = (bf16[2,256,256]{2,1,0:T(8,128)(2,1)S(1)}, bf16[2,256,256]{2,1,0:T(8,128)(2,1)S(1)}, u32[]{:S(2)}, u32[]{:S(2)}) collective-permute-start(bf16[2,256,256]{2,1,0:T(8,128)(2,1)S(1)} %get-tuple-element.102), channel_id=1, source_target_pairs={{0,10},{2,8},{4,14},{6,12},{8,2},{10,0},{12,6},{14,4},{16,26},{18,... | collective-permute-start | bytes 786440 | tf_op jit(solution)/shard_map/ppermute | solution.py:311
  68.6 11.2 %collective-permute-start.18 = (bf16[2,256,256]{2,1,0:T(8,128)(2,1)S(1)}, bf16[2,256,256]{2,1,0:T(8,128)(2,1)S(1)}, u32[]{:S(2)}, u32[]{:S(2)}) collective-permute-start(bf16[2,256,256]{2,1,0:T(8,128)(2,1)S(1)} %get-tuple-element.103), channel_id=1, source_target_pairs={{0,2},{2,0},{4,6},{6,4},{8,10},{10,8},{12,14},{14,12},{16,18},{18,... | collective-permute-start | bytes 786440 | tf_op jit(solution)/shard_map/ppermute | solution.py:311
  74.1 9.6 %collective-permute-start.14 = (bf16[2,128,256]{2,1,0:T(8,128)(2,1)S(1)}, bf16[2,128,256]{2,1,0:T(8,128)(2,1)S(1)}, u32[]{:S(2)}, u32[]{:S(2)}) collective-permute-start(bf16[2,128,256]{2,1,0:T(8,128)(2,1)S(1)} %get-tuple-element.99), channel_id=1, source_target_pairs={{0,12},{2,14},{4,8},{6,10},{8,4},{10,6},{12,0},{14,2},{16,28},{18,... | collective-permute-start | bytes 393224 | tf_op jit(solution)/shard_map/ppermute | solution.py:311
  76.7 8.7 %collective-permute-start.15 = (bf16[2,128,256]{2,1,0:T(8,128)(2,1)S(1)}, bf16[2,128,256]{2,1,0:T(8,128)(2,1)S(1)}, u32[]{:S(2)}, u32[]{:S(2)}) collective-permute-start(bf16[2,128,256]{2,1,0:T(8,128)(2,1)S(1)} %get-tuple-element.100), channel_id=1, source_target_pairs={{0,14},{2,12},{4,10},{6,8},{8,6},{10,4},{12,2},{14,0},{16,30},{18,... | collective-permute-start | bytes 393224 | tf_op jit(solution)/shard_map/ppermute | solution.py:311
  80.8 8.2 %collective-permute-start.24 = (bf16[2,128,512]{2,1,0:T(8,128)(2,1)S(1)}, bf16[2,128,512]{2,1,0:T(8,128)(2,1)S(1)}, u32[]{:S(2)}, u32[]{:S(2)}) collective-permute-start(bf16[2,128,512]{2,1,0:T(8,128)(2,1)S(1)} %get-tuple-element.114), channel_id=1, source_target_pairs={{0,1},{1,0},{2,3},{3,2},{4,5},{5,4},{6,7},{7,6},{8,9},{9,8},{10,11... | collective-permute-start | bytes 786440 | tf_op jit(solution)/shard_map/ppermute | solution.py:308
  86.3 8.4 %collective-permute-start.23 = (bf16[2,128,512]{2,1,0:T(8,128)(2,1)S(1)}, bf16[2,128,512]{2,1,0:T(8,128)(2,1)S(1)}, u32[]{:S(2)}, u32[]{:S(2)}) collective-permute-start(bf16[2,128,512]{2,1,0:T(8,128)(2,1)S(1)} %get-tuple-element.112), channel_id=1, source_target_pairs={{0,1},{1,0},{2,3},{3,2},{4,5},{5,4},{6,7},{7,6},{8,9},{9,8},{10,11... | collective-permute-start | bytes 786440 | tf_op jit(solution)/shard_map/ppermute | solution.py:308
